TPU v7x, 128 devices: a whole 4x4x4 slice. The times are simulated.
128 devices in a mesh: dp: 16 (over x, z), seq: 8 (over y, core).
Axes of the slice: x: 4, y: 4, z: 4, core: 2. Of those that a mesh axis runs over, the one named last changes fastest.
Arguments:
- hidden: bfloat16 [16, 2048, 4096], P('dp', 'seq'), may hold values from -6 to 6
- frozen_queries: bfloat16 [16, 2048, 2048], P('dp', 'seq'), may hold values from -200 to 200
- frozen_keys: bfloat16 [16, 2048, 2048], P('dp', 'seq'), may hold values from -8 to 8
- frozen_values: bfloat16 [16, 2048, 2048], P('dp', 'seq'), may hold values from -6 to 6
- document_length_list: int32 [16, 8], P('dp'), may hold values from 1 to 1024, 2048 in all within a row
- query_down_weight: bfloat16 [4096, 64], replicated, may hold values from -0.09375 to 0.09375
- query_up_weight: bfloat16 [64, 2048], replicated, may hold values from -0.75 to 0.75
- value_down_weight: bfloat16 [4096, 64], replicated, may hold values from -0.09375 to 0.09375
- value_up_weight: bfloat16 [64, 2048], replicated, may hold values from -0.75 to 0.75
- output_gradient: bfloat16 [16, 2048, 2048], P('dp', 'seq'), may hold values from -0.59765625 to 0.59765625
Outputs:
- attn_out: bfloat16 [16, 2048, 2048], P('dp', 'seq')
- grad_a_q: float32 [4096, 64], replicated
- query_up_gradient: float32 [64, 2048], replicated
- grad_a_v: float32 [4096, 64], replicated
- value_up_gradient: float32 [64, 2048], replicated
Inputs may be any that keep to these rules, and one draw needn't show every extreme that they name: `document_length_list`: the 8 lengths of a micro-batch sum to 2048.
All inputs are finite; a program needn't handle non-finite values.
Results may differ from a plain program's by a relative error of at most 0.017.
Values may be sent and summed in bfloat16 or wider, within the bound.
No kernel may reach another device: no remote copies, remote signals or barrier semaphores. Data moves between devices by JAX's collectives and lax.ppermute only.
A program may use at most 128 MiB of HBM per device.

v0:
```python
import jax
import jax.numpy as jnp
from jax import lax
from jax.sharding import PartitionSpec as P

HEAD_COUNT = 16
HEAD_SIZE = 128


ADAPTER_SCALE = 2.0
NEG_FILL = -1e30


def document_ids(doc_sizes, length_all):
    doc_ends = jnp.cumsum(doc_sizes)
    position = jnp.arange(length_all, dtype=jnp.int32)
    return jnp.sum((position[:, None] >= doc_ends[None, :]).astype(jnp.int32), axis=1)


def per_device(
    hidden,
    frozen_queries,
    frozen_keys,
    frozen_values,
    document_length_list,
    query_down_weight,
    query_up_weight,
    value_down_weight,
    value_up_weight,
    output_gradient,
):
    token_total = hidden[0]
    query_reduced = jnp.dot(
        token_total, query_down_weight, preferred_element_type=jnp.float32
    ).astype(jnp.bfloat16)
    value_reduced = jnp.dot(
        token_total, value_down_weight, preferred_element_type=jnp.float32
    ).astype(jnp.bfloat16)
    query_tensor = (
        frozen_queries[0].astype(jnp.float32)
        + ADAPTER_SCALE
        * jnp.dot(query_reduced, query_up_weight, preferred_element_type=jnp.float32)
    ).astype(jnp.bfloat16)
    value_tensor = (
        frozen_values[0].astype(jnp.float32)
        + ADAPTER_SCALE
        * jnp.dot(value_reduced, value_up_weight, preferred_element_type=jnp.float32)
    ).astype(jnp.bfloat16)
    head_q, head_k, head_v, head_g = (
        lax.all_to_all(query_tensor, "seq", split_axis=1, concat_axis=0, tiled=True),
        lax.all_to_all(frozen_keys[0], "seq", split_axis=1, concat_axis=0, tiled=True),
        lax.all_to_all(value_tensor, "seq", split_axis=1, concat_axis=0, tiled=True),
        lax.all_to_all(output_gradient[0], "seq", split_axis=1, concat_axis=0, tiled=True),
    )
    length_all = head_q.shape[0]
    local_heads = HEAD_COUNT // lax.axis_size("seq")
    head_width = local_heads * HEAD_SIZE
    head_shape = (length_all, local_heads, HEAD_SIZE)
    head_q = head_q.reshape(head_shape)
    head_k = head_k.reshape(head_shape)
    head_v = head_v.reshape(head_shape)
    head_g = head_g.reshape(head_shape)
    documents = document_ids(document_length_list[0], length_all)
    position = jnp.arange(length_all, dtype=jnp.int32)
    scaling = HEAD_SIZE ** (-0.5)
    block_rows = min(length_all, max(512, length_all // 8))
    value_acc = jnp.zeros(head_shape, jnp.float32)
    result_parts = []
    query_parts = []
    for block_index in range(length_all // block_rows):
        begin_row = block_index * block_rows
        end_row = begin_row + block_rows
        q_block = head_q[begin_row:end_row]
        g_block = head_g[begin_row:end_row]
        scores = (
            jnp.einsum("qhd,khd->hqk", q_block, head_k, preferred_element_type=jnp.float32)
            * scaling
        )
        allowed = (position[None, :length_all] <= position[begin_row:end_row, None]) & (
            documents[None, :length_all] == documents[begin_row:end_row, None]
        )
        scores = jnp.where(allowed[None], scores, NEG_FILL)
        maximum = jnp.max(scores, axis=2, keepdims=True)
        powers = jnp.exp(scores - maximum)
        probability = powers / jnp.sum(powers, axis=2, keepdims=True)
        rounded_w = probability.astype(jnp.bfloat16)
        result_block = jnp.einsum(
            "hqk,khd->qhd", rounded_w, head_v, preferred_element_type=jnp.float32
        ).astype(jnp.bfloat16)
        row_dot = jnp.sum(g_block.astype(jnp.float32) * result_block.astype(jnp.float32), axis=2)
        prob_grad = jnp.einsum("qhd,khd->hqk", g_block, head_v, preferred_element_type=jnp.float32)
        score_grad = (probability * (prob_grad - row_dot.T[:, :, None])).astype(jnp.bfloat16)
        query_block = (
            jnp.einsum("hqk,khd->qhd", score_grad, head_k, preferred_element_type=jnp.float32)
            * scaling
        ).astype(jnp.bfloat16)
        value_acc = value_acc.at[:length_all].add(
            jnp.einsum("hqk,qhd->khd", rounded_w, g_block, preferred_element_type=jnp.float32)
        )
        result_parts.append(result_block)
        query_parts.append(query_block)
    result_heads = jnp.concatenate(result_parts, axis=0).reshape(length_all, head_width)
    query_heads = jnp.concatenate(query_parts, axis=0).reshape(length_all, head_width)
    value_heads = value_acc.astype(jnp.bfloat16).reshape(length_all, head_width)
    attended = lax.all_to_all(result_heads, "seq", split_axis=0, concat_axis=1, tiled=True)
    query_row_list, value_row_list = (
        lax.all_to_all(query_heads, "seq", split_axis=0, concat_axis=1, tiled=True),
        lax.all_to_all(value_heads, "seq", split_axis=0, concat_axis=1, tiled=True),
    )
    query_return = (
        ADAPTER_SCALE
        * jnp.dot(query_row_list, query_up_weight.T, preferred_element_type=jnp.float32)
    ).astype(jnp.bfloat16)
    value_return = (
        ADAPTER_SCALE
        * jnp.dot(value_row_list, value_up_weight.T, preferred_element_type=jnp.float32)
    ).astype(jnp.bfloat16)
    grad_a_q = jnp.dot(token_total.T, query_return, preferred_element_type=jnp.float32)
    grad_a_v = jnp.dot(token_total.T, value_return, preferred_element_type=jnp.float32)
    query_up_gradient = ADAPTER_SCALE * jnp.dot(
        query_reduced.T, query_row_list, preferred_element_type=jnp.float32
    )
    value_up_gradient = ADAPTER_SCALE * jnp.dot(
        value_reduced.T, value_row_list, preferred_element_type=jnp.float32
    )
    grad_a_q, query_up_gradient, grad_a_v, value_up_gradient = lax.psum(
        (grad_a_q, query_up_gradient, grad_a_v, value_up_gradient), ("dp", "seq")
    )
    return (attended[None], grad_a_q, query_up_gradient, grad_a_v, value_up_gradient)


def solution(mesh):
    in_specs = (
        P("dp", "seq", None),
        P("dp", "seq", None),
        P("dp", "seq", None),
        P("dp", "seq", None),
        P("dp", None),
        P(),
        P(),
        P(),
        P(),
        P("dp", "seq", None),
    )
    out_specs = (P("dp", "seq", None), P(), P(), P(), P())
    return jax.shard_map(
        per_device, mesh=mesh, in_specs=in_specs, out_specs=out_specs, check_vma=False
    )
```

profile of v0, /device:TPU:1, one launch (start us, length us, event | category | flops | bytes accessed | tf_op | source)
XLA Modules:
  0.0 434.5 jit_solution(1066890974343132014)
XLA Ops:
  13.4 6.0 %all-to-all-start = ((bf16[256,8,256]{2,0,1:T(8,128)(2,1)}), bf16[256,8,256]{2,0,1:T(8,128)(2,1)S(1)}, u32[]{:S(2)}, u32[]{:S(2)}) async-start(bf16[256,8,256]{2,0,1:T(8,128)(2,1)} %bitcast.201), calls=%async_computation | async-start | bytes 2097152 | tf_op jit(solution)/shard_map/all_to_all | solution.py:52
  23.9 10.6 %all-to-all-done = bf16[256,8,256]{2,0,1:T(8,128)(2,1)S(1)} async-done(((bf16[256,8,256]{2,0,1:T(8,128)(2,1)}), bf16[256,8,256]{2,0,1:T(8,128)(2,1)S(1)}, u32[]{:S(2)}, u32[]{:S(2)}) %all-to-all-start) | async-done | bytes 1048608 | tf_op jit(solution)/shard_map/all_to_all | solution.py:52
  34.5 5.1 %all-to-all-start.1 = ((bf16[256,8,256]{2,0,1:T(8,128)(2,1)}), bf16[256,8,256]{2,0,1:T(8,128)(2,1)}, u32[]{:S(2)}, u32[]{:S(2)}) async-start(bf16[256,8,256]{2,0,1:T(8,128)(2,1)} %bitcast.200), calls=%async_computation.1 | async-start | bytes 2097152 | tf_op jit(solution)/shard_map/all_to_all | solution.py:50
  39.6 2.3 copy.106
  41.9 13.0 %all-to-all-done.1 = bf16[256,8,256]{2,0,1:T(8,128)(2,1)} async-done(((bf16[256,8,256]{2,0,1:T(8,128)(2,1)}), bf16[256,8,256]{2,0,1:T(8,128)(2,1)}, u32[]{:S(2)}, u32[]{:S(2)}) %all-to-all-start.1) | async-done | bytes 1048608 | tf_op jit(solution)/shard_map/all_to_all | solution.py:50
  54.8 5.0 %all-to-all-start.2 = ((bf16[256,8,256]{0,2,1:T(8,128)(2,1)}), bf16[256,8,256]{0,2,1:T(8,128)(2,1)}, u32[]{:S(2)}, u32[]{:S(2)}) async-start(bf16[256,8,256]{0,2,1:T(8,128)(2,1)} %bitcast.199), calls=%async_computation.2 | async-start | bytes 2097152 | tf_op jit(solution)/shard_map/all_to_all | solution.py:51
  59.8 2.3 copy.117
  62.4 12.7 %all-to-all-done.2 = bf16[256,8,256]{0,2,1:T(8,128)(2,1)} async-done(((bf16[256,8,256]{0,2,1:T(8,128)(2,1)}), bf16[256,8,256]{0,2,1:T(8,128)(2,1)}, u32[]{:S(2)}, u32[]{:S(2)}) %all-to-all-start.2) | async-done | bytes 1048608 | tf_op jit(solution)/shard_map/all_to_all | solution.py:51
  75.1 5.0 %all-to-all-start.4 = ((bf16[256,8,256]{0,2,1:T(8,128)(2,1)}), bf16[256,8,256]{0,2,1:T(8,128)(2,1)}, u32[]{:S(2)}, u32[]{:S(2)}) async-start(bf16[256,8,256]{0,2,1:T(8,128)(2,1)} %bitcast.198), calls=%async_computation.4 | async-start | bytes 2097152 | tf_op jit(solution)/shard_map/all_to_all | solution.py:53
  80.0 5.0 %fusion.20 = (pred[512,2048]{1,0:T(8,128)(4,1)}, pred[512,2048]{1,0:T(8,128)(4,1)}, pred[512,2048]{1,0:T(8,128)(4,1)}, pred[512,2048]{1,0:T(8,128)(4,1)}) fusion(s32[2048]{0:T(1024)S(1)} %convert_reduce_fusion, s32[512]{0:T(512)S(1)} %get-tuple-element.134, s32[512]{0:T(512)S(1)} %get-tuple-element.111, s32[512]{0:T(512)S(1)} %get-tuple-element.114, ...), kind=kLoop, calls=%fused_computation.42 | loop fusion | flops 12582912 | bytes 4218880 | tf_op jit(solution)/shard_map/and | solution.py:79
  86.2 2.4 copy.179
  88.6 2.1 fusion.121
  96.6 2.8 copy.107
  99.4 2.5 reshape.417
  101.9 2.1 fusion.120
  110.3 1.9 copy.123
  114.0 8.0 %fusion.138 = (f32[2,512]{1,0:T(2,128)S(1)}, f32[2,512,2048]{2,1,0:T(8,128)}) fusion(pred[512,2048]{1,0:T(8,128)(4,1)} %get-tuple-element.107, bf16[2048,2,128]{0,2,1:T(8,128)(2,1)} %reshape.417, bf16[512,2,128]{2,1,0:T(2,128)(2,1)} %slice.151), kind=kOutput, calls=%fused_computation.151 | convolution fusion | flops 545261568 | bytes 10752000 | tf_op jit(solution)/shard_map/sub | solution.py:84
  122.0 4.7 %fusion.28 = bf16[2,512,2048]{2,1,0:T(8,128)(2,1)S(1)} fusion(f32[2,512,2048]{2,1,0:T(8,128)} %get-tuple-element.122, f32[2,512]{1,0:T(2,128)S(1)} %get-tuple-element.121), kind=kLoop, calls=%fused_computation.50 | loop fusion | flops 4194304 | bytes 12587008 | tf_op jit(solution)/shard_map/convert_element_type | solution.py:86
  126.7 3.1 fusion.143
  129.8 2.3 multiply_reduce_fusion.3
  132.1 7.0 %fusion.63 = bf16[512,2,128]{2,0,1:T(8,128)(2,1)} fusion(bf16[2048,2,128]{0,2,1:T(8,128)(2,1)} %reshape.417, bf16[2048,2,128]{0,2,1:T(8,128)(2,1)S(1)} %copy.179, bf16[512,2,128]{0,2,1:T(8,128)(2,1)} %slice.165, f32[2,512]{1,0:T(2,128)S(1)} %bitcast.209, f32[2,512,2048]{2,1,0:T(8,128)} %get-tuple-element.122, f32[2,512]{1,0:T(2,128)S(1)} %get-tuple-element.121), kind=kOutput, calls=%fused_computation.96 | convolution fusion | flops 1082392576 | bytes 11018240 | tf_op jit(solution)/shard_map/hqk,khd->qhd/dot_general | solution.py:94
  139.1 8.2 %fusion.133 = (f32[2,512]{1,0:T(2,128)S(1)}, f32[2,512,2048]{2,1,0:T(8,128)}) fusion(pred[512,2048]{1,0:T(8,128)(4,1)} %get-tuple-element.108, bf16[2048,2,128]{0,2,1:T(8,128)(2,1)} %reshape.417, bf16[512,2,128]{2,1,0:T(2,128)(2,1)} %slice.155), kind=kOutput, calls=%fused_computation.150 | convolution fusion | flops 545261568 | bytes 10752000 | tf_op jit(solution)/shard_map/sub | solution.py:84
  147.3 4.7 %fusion.29 = bf16[2,512,2048]{2,1,0:T(8,128)(2,1)S(1)} fusion(f32[2,512,2048]{2,1,0:T(8,128)} %get-tuple-element.120, f32[2,512]{1,0:T(2,128)S(1)} %get-tuple-element.119), kind=kLoop, calls=%fused_computation.51 | loop fusion | flops 4194304 | bytes 12587008 | tf_op jit(solution)/shard_map/convert_element_type | solution.py:86
  152.0 1.9 copy-done.1
  153.9 2.3 multiply_reduce_fusion.2
  156.2 6.9 %fusion.62 = bf16[512,2,128]{2,0,1:T(8,128)(2,1)} fusion(bf16[2048,2,128]{0,2,1:T(8,128)(2,1)} %reshape.417, bf16[2048,2,128]{0,2,1:T(8,128)(2,1)S(1)} %copy.179, bf16[512,2,128]{0,2,1:T(8,128)(2,1)} %slice.167, f32[2,512]{1,0:T(2,128)S(1)} %bitcast.211, f32[2,512,2048]{2,1,0:T(8,128)} %get-tuple-element.120, f32[2,512]{1,0:T(2,128)S(1)} %get-tuple-element.119), kind=kOutput, calls=%fused_computation.95 | convolution fusion | flops 1082392576 | bytes 11018240 | tf_op jit(solution)/shard_map/hqk,khd->qhd/dot_general | solution.py:94
  163.2 8.0 %fusion.128 = (f32[2,512]{1,0:T(2,128)S(1)}, f32[2,512,2048]{2,1,0:T(8,128)}) fusion(pred[512,2048]{1,0:T(8,128)(4,1)} %get-tuple-element.109, bf16[2048,2,128]{0,2,1:T(8,128)(2,1)} %reshape.417, bf16[512,2,128]{2,1,0:T(2,128)(2,1)} %slice.159), kind=kOutput, calls=%fused_computation.149 | convolution fusion | flops 545261568 | bytes 10752000 | tf_op jit(solution)/shard_map/sub | solution.py:84
  171.1 4.6 %fusion.30 = bf16[2,512,2048]{2,1,0:T(8,128)(2,1)S(1)} fusion(f32[2,512,2048]{2,1,0:T(8,128)} %get-tuple-element.118, f32[2,512]{1,0:T(2,128)S(1)} %get-tuple-element.117), kind=kLoop, calls=%fused_computation.52 | loop fusion | flops 4194304 | bytes 12587008 | tf_op jit(solution)/shard_map/convert_element_type | solution.py:86
  177.7 2.7 multiply_reduce_fusion.1
  180.4 6.9 %fusion.61 = bf16[512,2,128]{2,0,1:T(8,128)(2,1)} fusion(bf16[2048,2,128]{0,2,1:T(8,128)(2,1)} %reshape.417, bf16[2048,2,128]{0,2,1:T(8,128)(2,1)S(1)} %copy.179, bf16[512,2,128]{0,2,1:T(8,128)(2,1)S(1)} %slice.169, f32[2,512]{1,0:T(2,128)S(1)} %bitcast.212, f32[2,512,2048]{2,1,0:T(8,128)} %get-tuple-element.118, f32[2,512]{1,0:T(2,128)S(1)} %get-tuple-element.117), kind=kOutput, calls=%fused_computation.94 | convolution fusion | flops 1082392576 | bytes 11018240 | tf_op jit(solution)/shard_map/hqk,khd->qhd/dot_general | solution.py:94
  187.3 8.0 %fusion.123 = (f32[2,512]{1,0:T(2,128)S(1)}, f32[2,512,2048]{2,1,0:T(8,128)}) fusion(pred[512,2048]{1,0:T(8,128)(4,1)} %get-tuple-element.110, bf16[2048,2,128]{0,2,1:T(8,128)(2,1)} %reshape.417, bf16[512,2,128]{2,1,0:T(2,128)(2,1)} %slice.163), kind=kOutput, calls=%fused_computation.148 | convolution fusion | flops 545261568 | bytes 10752000 | tf_op jit(solution)/shard_map/sub | solution.py:84
  195.3 4.7 %fusion.31 = bf16[2,512,2048]{2,1,0:T(8,128)(2,1)S(1)} fusion(f32[2,512,2048]{2,1,0:T(8,128)} %get-tuple-element.116, f32[2,512]{1,0:T(2,128)S(1)} %get-tuple-element.115), kind=kLoop, calls=%fused_computation.53 | loop fusion | flops 4194304 | bytes 12587008 | tf_op jit(solution)/shard_map/convert_element_type | solution.py:86
  200.0 1.9 copy-done.4
  201.9 2.3 multiply_reduce_fusion
  204.2 6.9 %fusion.60 = bf16[512,2,128]{2,0,1:T(8,128)(2,1)} fusion(bf16[2048,2,128]{0,2,1:T(8,128)(2,1)} %reshape.417, bf16[2048,2,128]{0,2,1:T(8,128)(2,1)S(1)} %copy.179, bf16[512,2,128]{0,2,1:T(8,128)(2,1)} %slice.171, f32[2,512]{1,0:T(2,128)S(1)} %bitcast.210, f32[2,512,2048]{2,1,0:T(8,128)} %get-tuple-element.116, f32[2,512]{1,0:T(2,128)S(1)} %get-tuple-element.115), kind=kOutput, calls=%fused_computation.93 | convolution fusion | flops 1082392576 | bytes 11018240 | tf_op jit(solution)/shard_map/hqk,khd->qhd/dot_general | solution.py:94
  216.6 4.8 %all-to-all-start.5 = ((bf16[8,256,256]{1,2,0:T(8,128)(2,1)}), bf16[8,256,256]{1,2,0:T(8,128)(2,1)S(1)}, u32[]{:S(2)}, u32[]{:S(2)}) async-start(bf16[8,256,256]{1,2,0:T(8,128)(2,1)} %copy.139), calls=%async_computation.5 | async-start | bytes 2097152 | tf_op jit(solution)/shard_map/all_to_all | solution.py:107
  221.4 4.8 %convolution_add_fusion.2 = f32[2,2048,128]{2,1,0:T(8,128)S(1)} fusion(f32[2,2048,128]{2,1,0:T(8,128)} %fusion.143, bf16[2,512,2048]{2,1,0:T(8,128)(2,1)} %copy-done.1, bf16[512,2,128]{0,2,1:T(8,128)(2,1)} %slice.167), kind=kOutput, calls=%fused_computation.56 | convolution fusion | flops 537395200 | bytes 8650752 | tf_op jit(solution)/shard_map/hqk,qhd->khd/dot_general | solution.py:98
  228.4 2.8 fusion.37
  231.2 2.3 copy.148
  236.5 5.0 %all-to-all-start.6 = ((bf16[8,256,256]{1,2,0:T(8,128)(2,1)}), bf16[8,256,256]{1,2,0:T(8,128)(2,1)}, u32[]{:S(2)}, u32[]{:S(2)}) async-start(bf16[8,256,256]{1,2,0:T(8,128)(2,1)} %copy.149), calls=%async_computation.6 | async-start | bytes 2097152 | tf_op jit(solution)/shard_map/all_to_all | solution.py:108
  242.7 2.0 convolution_bitcast_fusion.1
  244.7 12.0 %all-to-all-done.6 = bf16[8,256,256]{1,2,0:T(8,128)(2,1)} async-done(((bf16[8,256,256]{1,2,0:T(8,128)(2,1)}), bf16[8,256,256]{1,2,0:T(8,128)(2,1)}, u32[]{:S(2)}, u32[]{:S(2)}) %all-to-all-start.6) | async-done | bytes 1048608 | tf_op jit(solution)/shard_map/all_to_all | solution.py:108
  256.7 2.5 convolution_multiply_fusion.2
  259.2 3.3 convolution_bitcast_fusion
  263.3 19.8 %all_to_all.115 = bf16[8,256,256]{1,2,0:T(8,128)(2,1)S(1)} all-to-all(bf16[8,256,256]{1,2,0:T(8,128)(2,1)S(1)} %copy.116), channel_id=1, replica_groups=mesh['dp'=16,'seq'=8] {'seq'}, dimensions={0} | all-to-all | bytes 2097152 | tf_op jit(solution)/shard_map/all_to_all | solution.py:105
  284.5 135.8 %all-reduce.3.cloned.1.call-done = (f32[4096,64]{0,1:T(8,128)}, f32[64,2048]{1,0:T(8,128)}, f32[4096,64]{0,1:T(8,128)}, f32[64,2048]{1,0:T(8,128)}) async-done(((f32[4096,64]{0,1:T(8,128)}, f32[64,2048]{1,0:T(8,128)}, f32[4096,64]{0,1:T(8,128)}, f32[64,2048]{1,0:T(8,128)}), (f32[4096,64]{0,1:T(8,128)}, f32[64,2048]{1,0:T(8,128)}, f32[4096,64]{0,1:T(8,128)}, ...) | async-done | bytes 3145744 | tf_op jit(solution)/shard_map/psum | solution.py:126
  420.2 2.3 copy.249
  424.4 2.3 copy.251
  (75 shorter events, 44.7 us)
Async XLA Ops:
  7.2 1.6 copy-start
  10.6 10.6 %copy-start.10 = (bf16[64,2048]{1,0:T(8,128)(2,1)S(1)}, bf16[64,2048]{1,0:T(8,128)(2,1)}, u32[]{:S(2)}) copy-start(bf16[64,2048]{1,0:T(8,128)(2,1)} %param.32) | copy-start | bytes 786436
  13.4 21.1 %all-to-all-start = ((bf16[256,8,256]{2,0,1:T(8,128)(2,1)}), bf16[256,8,256]{2,0,1:T(8,128)(2,1)S(1)}, u32[]{:S(2)}, u32[]{:S(2)}) async-start(bf16[256,8,256]{2,0,1:T(8,128)(2,1)} %bitcast.201), calls=%async_computation | async-start | bytes 2097152 | tf_op jit(solution)/shard_map/all_to_all | solution.py:52
  34.5 27.6 %copy-start.17 = (s32[1,8]{1,0:T(1,128)S(1)}, s32[1,8]{1,0:T(1,128)}, u32[]{:S(2)}) copy-start(s32[1,8]{1,0:T(1,128)} %param.30) | copy-start | bytes 100
  34.5 20.3 %all-to-all-start.1 = ((bf16[256,8,256]{2,0,1:T(8,128)(2,1)}), bf16[256,8,256]{2,0,1:T(8,128)(2,1)}, u32[]{:S(2)}, u32[]{:S(2)}) async-start(bf16[256,8,256]{2,0,1:T(8,128)(2,1)} %bitcast.200), calls=%async_computation.1 | async-start | bytes 2097152 | tf_op jit(solution)/shard_map/all_to_all | solution.py:50
  54.8 20.2 %all-to-all-start.2 = ((bf16[256,8,256]{0,2,1:T(8,128)(2,1)}), bf16[256,8,256]{0,2,1:T(8,128)(2,1)}, u32[]{:S(2)}, u32[]{:S(2)}) async-start(bf16[256,8,256]{0,2,1:T(8,128)(2,1)} %bitcast.199), calls=%async_computation.2 | async-start | bytes 2097152 | tf_op jit(solution)/shard_map/all_to_all | solution.py:51
  75.1 26.9 %all-to-all-start.4 = ((bf16[256,8,256]{0,2,1:T(8,128)(2,1)}), bf16[256,8,256]{0,2,1:T(8,128)(2,1)}, u32[]{:S(2)}, u32[]{:S(2)}) async-start(bf16[256,8,256]{0,2,1:T(8,128)(2,1)} %bitcast.198), calls=%async_computation.4 | async-start | bytes 2097152 | tf_op jit(solution)/shard_map/all_to_all | solution.py:53
  122.0 4.7 %copy-start.7 = (bf16[512,2,128]{0,2,1:T(8,128)(2,1)S(1)}, bf16[512,2,128]{0,2,1:T(8,128)(2,1)}, u32[]{:S(2)}) copy-start(bf16[512,2,128]{0,2,1:T(8,128)(2,1)} %slice.165) | copy-start | bytes 786436
  147.3 6.6 %copy-start.6 = (bf16[512,2,128]{0,2,1:T(8,128)(2,1)S(1)}, bf16[512,2,128]{0,2,1:T(8,128)(2,1)}, u32[]{:S(2)}) copy-start(bf16[512,2,128]{0,2,1:T(8,128)(2,1)} %slice.167) | copy-start | bytes 786436
  152.0 1.9 copy-start.1
  175.8 1.9 copy-start.2
  195.3 6.6 %copy-start.8 = (bf16[512,2,128]{0,2,1:T(8,128)(2,1)S(1)}, bf16[512,2,128]{0,2,1:T(8,128)(2,1)}, u32[]{:S(2)}) copy-start(bf16[512,2,128]{0,2,1:T(8,128)(2,1)} %slice.171) | copy-start | bytes 786436
  199.9 1.9 copy-start.4
  216.6 19.9 %all-to-all-start.5 = ((bf16[8,256,256]{1,2,0:T(8,128)(2,1)}), bf16[8,256,256]{1,2,0:T(8,128)(2,1)S(1)}, u32[]{:S(2)}, u32[]{:S(2)}) async-start(bf16[8,256,256]{1,2,0:T(8,128)(2,1)} %copy.139), calls=%async_computation.5 | async-start | bytes 2097152 | tf_op jit(solution)/shard_map/all_to_all | solution.py:107
  221.4 4.8 %copy-start.3 = (bf16[2,512,2048]{2,1,0:T(8,128)(2,1)S(1)}, bf16[2,512,2048]{2,1,0:T(8,128)(2,1)}, u32[]{:S(2)}) copy-start(bf16[2,512,2048]{2,1,0:T(8,128)(2,1)} %copy-done.2) | copy-start | bytes 12582916
  226.2 2.2 copy-start.5
  226.2 2.2 copy-start.9
  233.5 9.3 %copy-start.11 = (bf16[64,2048]{1,0:T(8,128)(2,1)S(1)}, bf16[64,2048]{1,0:T(8,128)(2,1)}, u32[]{:S(2)}) copy-start(bf16[64,2048]{1,0:T(8,128)(2,1)} %param.32) | copy-start | bytes 786436
  236.5 20.2 %all-to-all-start.6 = ((bf16[8,256,256]{1,2,0:T(8,128)(2,1)}), bf16[8,256,256]{1,2,0:T(8,128)(2,1)}, u32[]{:S(2)}, u32[]{:S(2)}) async-start(bf16[8,256,256]{1,2,0:T(8,128)(2,1)} %copy.149), calls=%async_computation.6 | async-start | bytes 2097152 | tf_op jit(solution)/shard_map/all_to_all | solution.py:108
  241.5 178.7 %all-reduce.3.cloned.1.call-start = ((), (), s32[]{:S(2)}) async-start(), calls=%async_computation.7 | async-start | bytes 6291456 | tf_op jit(solution)/shard_map/psum | solution.py:126
  259.2 3.4 copy-start.12
  259.2 3.4 copy-start.13
  259.2 3.4 copy-start.14
  259.2 3.4 copy-start.15
  420.2 6.5 %copy-start.16 = (f32[64,2048]{1,0:T(8,128)S(1)}, f32[64,2048]{1,0:T(8,128)}, u32[]{:S(2)}) copy-start(f32[64,2048]{1,0:T(8,128)} %get-tuple-element.139) | copy-start | bytes 1572868
Sparse Core Ops, SparseCore 0:
  262.7 157.5 all-reduce.2
where the time goes:
time: 441 us; the launch traced here: 435 us
  waiting for transfers between devices  184 us (42%)
  matrix products  98.1 us (22%)
  local copies, waits for them, and re-layouts  61.7 us (14%)
  starting transfers between devices  30.9 us (7%)
  other arithmetic  25.3 us (6%)
  blocking collectives  19.8 us (4%)
  between operations  14.5 us (3%)
    psum x1, waiting for transfers between devices, per_device(): lax.psum((grad_a_q, query_up_gradient, grad_a_v, value_up_gradient), ('dp...  136 us
    sub x4, matrix products, per_device(): powers = jnp.exp(scores - maximum)  32.1 us
    dot_general x4, matrix products, per_device(): jnp.einsum('hqk,khd->qhd', score_grad, head_k, preferred_element_type=jnp...  27.7 us
    unnamed x46, local copies, waits for them, and re-layouts  24.4 us
    all_to_all x1, blocking collectives, per_device(): lax.all_to_all(result_heads, 'seq', split_axis=0, concat_axis=1, tiled=True)  19.8 us
    convert_element_type x4, other arithmetic, per_device(): rounded_w = probability.astype(jnp.bfloat16)  18.6 us
    all_to_all x1, waiting for transfers between devices, per_device(): lax.all_to_all(query_tensor, 'seq', split_axis=1, concat_axis=0, tiled=True)  13 us
    all_to_all x1, waiting for transfers between devices, per_device(): lax.all_to_all(frozen_keys[0], 'seq', split_axis=1, concat_axis=0, tiled=...  12.7 us
  transfers between devices with their start and end apart: 7, of which 6 were waited for; matrix products, arithmetic and copies ran while one was open for 12% of the time, Pallas kernels for 0%

commit v1 on v0

v1 whole, which is shorter than its diff:
```python
import functools

import jax
import jax.numpy as jnp
from jax import lax
from jax.experimental import pallas as pl
from jax.experimental.pallas import tpu as pltpu
from jax.sharding import Mesh
from jax.sharding import PartitionSpec as P

HEAD_COUNT = 16
HEAD_SIZE = 128
RANK = 64
NDOC = 8
TILE = 256
MAX_TILES = 5
ADAPTER_SCALE = 2.0
NEG_FILL = -1e30
SCALING = HEAD_SIZE ** (-0.5)
LOG2_E = 1.4426950408889634

DOWN_ROWS, DOWN_COLS = 16, 256
UP_ROWS, UP_COLS = 16, 128

DP = ("x", "z")
SEQ = ("y", "core")
ALL = ("x", "z", "y", "core")
NT = (((1,), (1,)), ((), ()))


def dot(a, b):
    return jnp.dot(a, b, preferred_element_type=jnp.float32)


def dot_nt(a, b):
    return lax.dot_general(a, b, NT, preferred_element_type=jnp.float32)


def pack_kernel(hidden, wq_down, wv_down, fq, fk, fv, grad, wq_up, wv_up, out, low):
    width = fq.shape[1]

    @pl.when(pl.program_id(0) == 0)
    def _():
        low[:, :RANK] = dot_nt(hidden[...], wq_down[...]).astype(jnp.bfloat16)
        low[:, RANK:] = dot_nt(hidden[...], wv_down[...]).astype(jnp.bfloat16)

    q_add = ADAPTER_SCALE * dot(low[:, :RANK], wq_up[...])
    v_add = ADAPTER_SCALE * dot(low[:, RANK:], wv_up[...])
    out[0, :, 0:width] = (fq[...].astype(jnp.float32) + q_add).astype(jnp.bfloat16)
    out[0, :, width : 2 * width] = fk[...]
    out[0, :, 2 * width : 3 * width] = (fv[...].astype(jnp.float32) + v_add).astype(jnp.bfloat16)
    out[0, :, 3 * width : 4 * width] = grad[...]
    out[0, :, 4 * width :] = low[...]


def pack(hidden, wq_down_t, wv_down_t, fq, fk, fv, grad, wq_up, wv_up, seq_size):
    rows, model = hidden.shape
    width = fq.shape[1] // seq_size
    whole = lambda s: pl.BlockSpec(s, lambda d: (0, 0))
    column = lambda r: pl.BlockSpec((r, width), lambda d: (0, d))
    packed = 4 * width + 2 * RANK
    return pl.pallas_call(
        pack_kernel,
        grid=(seq_size,),
        in_specs=[
            whole((rows, model)),
            whole((RANK, model)),
            whole((RANK, model)),
            column(rows),
            column(rows),
            column(rows),
            column(rows),
            column(RANK),
            column(RANK),
        ],
        out_specs=pl.BlockSpec((1, rows, packed), lambda d: (d, 0, 0)),
        out_shape=jax.ShapeDtypeStruct((seq_size, rows, packed), jnp.bfloat16),
        scratch_shapes=[pltpu.VMEM((rows, 2 * RANK), jnp.bfloat16)],
        compiler_params=pltpu.CompilerParams(vmem_limit_bytes=40 << 20),
        name="pack",
    )(hidden, wq_down_t, wv_down_t, fq, fk, fv, grad, wq_up, wv_up)


def attention_kernel(
    meta, packed, wq_up, wv_up, out, back, up, q_t, k_t, v_t, g_t, dq_t, dv, dv_t
):
    length = packed.shape[0]
    heads = out.shape[1] // HEAD_SIZE
    width = heads * HEAD_SIZE
    blocks = length // TILE

    def columns(which, head):
        begin = which * width + head * HEAD_SIZE
        return slice(begin, begin + HEAD_SIZE)

    for head in range(heads):
        q_t[...] = packed[:, columns(0, head)].T
        k_t[...] = packed[:, columns(1, head)].T
        v_t[...] = packed[:, columns(2, head)].T
        g_t[...] = packed[:, columns(3, head)].T
        dv[...] = jnp.zeros_like(dv)

        def block(index, _, head=head):
            row0 = pl.multiple_of(index * TILE, TILE)
            q_rows = pl.ds(row0, TILE)
            position = row0 + lax.broadcasted_iota(jnp.int32, (1, TILE), 1)
            begin = jnp.zeros((1, TILE), jnp.int32)
            first = jnp.int32(0)
            end = jnp.int32(0)
            for doc in range(NDOC):
                end = end + meta[doc]
                begin = jnp.where(position >= end, end, begin)
                first = jnp.where(row0 >= end, end, first)
            first_tile = lax.div(first, TILE)
            tiles = index - first_tile + 1

            def body(count):
                key0 = pl.multiple_of((index + 1 - count) * TILE, TILE)
                k_rows = pl.ds(key0, count * TILE)
                keys = packed[k_rows, columns(1, head)]
                values = packed[k_rows, columns(2, head)]
                scores = dot(keys, q_t[:, q_rows])
                key_position = key0 + lax.broadcasted_iota(jnp.int32, (count * TILE, TILE), 0)
                allowed = (key_position >= begin) & (key_position <= position)
                scores = jnp.where(allowed, scores, NEG_FILL)
                maximum = jnp.max(scores, axis=0, keepdims=True)
                powers = jnp.exp2((scores - maximum) * (SCALING * LOG2_E))
                inverse = 1.0 / jnp.sum(powers, axis=0, keepdims=True)
                rounded = powers.astype(jnp.bfloat16)
                result = (dot(v_t[:, k_rows], rounded) * inverse).astype(jnp.bfloat16)
                g_block = g_t[:, q_rows]
                g_wide = g_block.astype(jnp.float32)
                row_dot = jnp.sum(g_wide * result.astype(jnp.float32), axis=0, keepdims=True)
                prob_grad = dot(values, g_block)
                score_grad = (powers * (prob_grad - row_dot)).astype(jnp.bfloat16)
                query_grad = dot(k_t[:, k_rows], score_grad) * (inverse * SCALING)
                dq_t[head * HEAD_SIZE : (head + 1) * HEAD_SIZE, q_rows] = query_grad.astype(
                    jnp.bfloat16
                )
                out[q_rows, head * HEAD_SIZE : (head + 1) * HEAD_SIZE] = result.T
                g_scaled = (g_wide * inverse).astype(jnp.bfloat16).T
                dv[k_rows, :] += dot(rounded, g_scaled)

            for count in range(1, min(MAX_TILES, blocks) + 1):
                pl.when(tiles == count)(functools.partial(body, count))
            return 0

        lax.fori_loop(0, blocks, block, 0)
        dv_t[head * HEAD_SIZE : (head + 1) * HEAD_SIZE, :] = dv[...].astype(jnp.bfloat16).T

    low = packed[:, 4 * width :]
    seq_size = back.shape[0]
    rows = back.shape[2]
    for part, (grads, weight) in enumerate(((dq_t, wq_up), (dv_t, wv_up))):
        returned = (ADAPTER_SCALE * dot(weight[...], grads[...])).astype(jnp.bfloat16)
        for device in range(seq_size):
            back[device, part * RANK : (part + 1) * RANK, :] = returned[
                :, device * rows : (device + 1) * rows
            ]
        up_t = dot(grads[...], low) * ADAPTER_SCALE
        up_part = up_t.T[part * RANK : (part + 1) * RANK, :].astype(jnp.bfloat16)
        across = width // UP_COLS
        for row in range(RANK // UP_ROWS):
            for column in range(across):
                up[(part * (RANK // UP_ROWS) + row) * across + column] = up_part[
                    row * UP_ROWS : (row + 1) * UP_ROWS, column * UP_COLS : (column + 1) * UP_COLS
                ]


def attention(meta, packed, wq_up, wv_up, seq_size):
    length = packed.shape[0]
    width = (packed.shape[1] - 2 * RANK) // 4
    rows = length // seq_size
    column = pl.BlockSpec((RANK, width), lambda i, meta: (0, meta[NDOC]))
    whole = lambda *s: pl.BlockSpec(s, lambda i, meta: (0,) * len(s))
    head_t = pltpu.VMEM((HEAD_SIZE, length), jnp.bfloat16)
    return pl.pallas_call(
        attention_kernel,
        grid_spec=pltpu.PrefetchScalarGridSpec(
            num_scalar_prefetch=1,
            grid=(1,),
            in_specs=[whole(*packed.shape), column, column],
            out_specs=[
                whole(length, width),
                whole(seq_size, 2 * RANK, rows),
                whole(2 * RANK * width // (UP_ROWS * UP_COLS), UP_ROWS, UP_COLS),
            ],
            scratch_shapes=[
                head_t,
                head_t,
                head_t,
                head_t,
                pltpu.VMEM((width, length), jnp.bfloat16),
                pltpu.VMEM((length, HEAD_SIZE), jnp.float32),
                pltpu.VMEM((width, length), jnp.bfloat16),
            ],
        ),
        out_shape=[
            jax.ShapeDtypeStruct((length, width), jnp.bfloat16),
            jax.ShapeDtypeStruct((seq_size, 2 * RANK, rows), jnp.bfloat16),
            jax.ShapeDtypeStruct(
                (2 * RANK * width // (UP_ROWS * UP_COLS), UP_ROWS, UP_COLS), jnp.bfloat16
            ),
        ],
        compiler_params=pltpu.CompilerParams(vmem_limit_bytes=56 << 20),
        name="attention",
    )(meta, packed, wq_up, wv_up)


def down_kernel(parts, hidden, out):
    total = parts[0].astype(jnp.float32)
    for source in range(1, parts.shape[0]):
        total += parts[source].astype(jnp.float32)
    back = total.astype(jnp.bfloat16)
    grad = dot(back, hidden[...]).astype(out.dtype)
    for column in range(out.shape[0]):
        for row in range(out.shape[1]):
            out[column, row] = grad[
                row * DOWN_ROWS : (row + 1) * DOWN_ROWS,
                column * DOWN_COLS : (column + 1) * DOWN_COLS,
            ]


def down_gradient(parts, hidden):
    seq_size, columns, rows = parts.shape
    model = hidden.shape[1]
    step = 1024
    tiles = (step // DOWN_COLS, columns // DOWN_ROWS, DOWN_ROWS, DOWN_COLS)
    return pl.pallas_call(
        down_kernel,
        grid=(model // step,),
        in_specs=[
            pl.BlockSpec((seq_size, columns, rows), lambda i: (0, 0, 0)),
            pl.BlockSpec((rows, step), lambda i: (0, i)),
        ],
        out_specs=pl.BlockSpec(tiles, lambda i: (i, 0, 0, 0)),
        out_shape=jax.ShapeDtypeStruct((model // DOWN_COLS,) + tiles[1:], jnp.bfloat16),
        compiler_params=pltpu.CompilerParams(vmem_limit_bytes=40 << 20),
        name="down_gradient",
    )(parts, hidden)


def place_kernel(parts, grad_a_q, up_q, grad_a_v, up_v):
    dp_size, seq_size = parts.shape[:2]
    half = RANK // DOWN_ROWS
    for p in range(dp_size):
        for s in range(seq_size):
            target = (grad_a_q, grad_a_v)[s // half]
            target[
                s % half * DOWN_ROWS : (s % half + 1) * DOWN_ROWS,
                p * DOWN_COLS : (p + 1) * DOWN_COLS,
            ] = parts[p, s, :, :DOWN_COLS].astype(jnp.float32)
            row, column = p // 2, p % 2
            target = (up_q, up_v)[row // half]
            target[
                row % half * UP_ROWS : (row % half + 1) * UP_ROWS,
                (2 * s + column) * UP_COLS : (2 * s + column + 1) * UP_COLS,
            ] = parts[p, s, :, DOWN_COLS:].astype(jnp.float32)


def place(parts, model, width):
    vmem = pl.BlockSpec(memory_space=pltpu.VMEM)
    shapes = [(RANK, model), (RANK, width), (RANK, model), (RANK, width)]
    return pl.pallas_call(
        place_kernel,
        in_specs=[vmem],
        out_specs=[vmem] * 4,
        out_shape=[jax.ShapeDtypeStruct(shape, jnp.float32) for shape in shapes],
        compiler_params=pltpu.CompilerParams(vmem_limit_bytes=40 << 20),
        name="place",
    )(parts)


def swap(x, axes):
    return lax.all_to_all(x, axes, 0, 0, tiled=True)


def spread(x, axes, size):
    return swap(jnp.broadcast_to(x[None], (size,) + x.shape), axes)


def per_device(
    sizes,
    hidden,
    frozen_queries,
    frozen_keys,
    frozen_values,
    document_length_list,
    query_down_weight,
    query_up_weight,
    value_down_weight,
    value_up_weight,
    output_gradient,
):
    dp_size, seq_size = sizes
    packed = pack(
        hidden[0],
        query_down_weight.T,
        value_down_weight.T,
        frozen_queries[0],
        frozen_keys[0],
        frozen_values[0],
        output_gradient[0],
        query_up_weight,
        value_up_weight,
        seq_size,
    )
    rows = packed.shape[1]
    received = swap(packed, SEQ)
    received = received.reshape(seq_size * rows, packed.shape[2])
    me = lax.axis_index(SEQ).astype(jnp.int32)
    meta = jnp.concatenate([document_length_list[0], me[None]])
    result, back, up = attention(meta, received, query_up_weight, value_up_weight, seq_size)
    width = result.shape[1]

    back = swap(back, SEQ)
    down = down_gradient(back, hidden[0])
    attended = swap(result.reshape(seq_size, rows, width), SEQ)
    attended = attended.transpose(1, 0, 2).reshape(1, rows, seq_size * width)

    up = swap(up, DP)
    up = jnp.sum(up.astype(jnp.float32), axis=0).astype(jnp.bfloat16)
    model = hidden.shape[2]
    devices = dp_size * seq_size
    down = swap(down.reshape(devices, DOWN_ROWS, DOWN_COLS), ALL)
    down = jnp.sum(down.astype(jnp.float32), axis=0).astype(jnp.bfloat16)
    both = jnp.concatenate([down, up], axis=1)
    both = spread(both, ALL, devices)
    both = both.reshape(dp_size, seq_size, DOWN_ROWS, DOWN_COLS + UP_COLS)
    grad_a_q, up_q, grad_a_v, up_v = place(both, model, seq_size * width)
    return attended, grad_a_q.T, up_q, grad_a_v.T, up_v


def solution(mesh):
    dp_size, seq_size = mesh.shape["dp"], mesh.shape["seq"]
    fine = Mesh(mesh.devices.reshape(4, 4, 4, 2), ALL)
    rows = P(DP, SEQ, None)
    in_specs = (rows, rows, rows, rows, P(DP, None), P(), P(), P(), P(), rows)
    out_specs = (rows, P(), P(), P(), P())
    return jax.shard_map(
        functools.partial(per_device, (dp_size, seq_size)),
        mesh=fine,
        in_specs=in_specs,
        out_specs=out_specs,
        check_vma=False,
    )
```

time: 441 us -> 208 us (0.47); the launches traced: 435 us -> 207 us
  matrix products: 98.1 us -> 0 us
  waiting for transfers between devices: 184 us -> 94 us
  local copies, waits for them, and re-layouts: 61.7 us -> 18.9 us
  Pallas kernels: 0 us -> 30.9 us
  other arithmetic: 25.3 us -> 0.81 us
  blocking collectives: 19.8 us -> 39.2 us
  between operations: 14.5 us -> 0.72 us
  starting transfers between devices: 30.9 us -> 22.9 us
    psum x1 -> x0, waiting for transfers between devices: 136 us -> none  [per_device(): lax.psum((grad_a_q, query_up_gradient, grad_a_v, value_up_gradient), ('dp...]
    dot_general x20 -> x0, matrix products: 65.9 us -> none  [the longest x4 27.7 us: per_device(): jnp.einsum('hqk,khd->qhd', score_grad, head_k, preferred_element_type=jnp...]
    all_to_all x6 -> x4, waiting for transfers between devices: 48.5 us -> 94 us  [swap(): return lax.all_to_all(x, axes, 0, 0, tiled=True)]
    sub x4 -> x0, matrix products: 32.1 us -> none  [per_device(): powers = jnp.exp(scores - maximum)]
    pallas_call x0 -> x4, Pallas kernels: none -> 30.9 us  [the longest x1 23.8 us: attention(): pl.pallas_call(attention_kernel, grid_spec=pltpu.PrefetchScalarGridSpec(n...]
    slice x15 -> x0, local copies, waits for them, and re-layouts: 20.1 us -> none  [the longest x9 12.1 us: per_device(): g_block = head_g[begin_row:end_row]]
    all_to_all x1 -> x2, blocking collectives: 19.8 us -> 39.2 us  [swap(): return lax.all_to_all(x, axes, 0, 0, tiled=True)]
    convert_element_type x4 -> x0, other arithmetic: 18.6 us -> none  [per_device(): rounded_w = probability.astype(jnp.bfloat16)]
  transfers between devices with their start and end apart: 7 -> 4, of which waited for: 6 -> 4; matrix products, arithmetic and copies ran while one was open for 12% -> 2% of each run, Pallas kernels for 0% -> 1%
where the time goes in v1:
time: 208 us; the launch traced here: 207 us
  waiting for transfers between devices  94 us (45%)
  blocking collectives  39.2 us (19%)
  Pallas kernels  30.9 us (15%)
  starting transfers between devices  22.9 us (11%)
  local copies, waits for them, and re-layouts  18.9 us (9%)
    all_to_all x4, waiting for transfers between devices, swap(): return lax.all_to_all(x, axes, 0, 0, tiled=True)  94 us
    all_to_all x2, blocking collectives, swap(): return lax.all_to_all(x, axes, 0, 0, tiled=True)  39.2 us
    pallas_call x1, Pallas kernels, attention(): pl.pallas_call(attention_kernel, grid_spec=pltpu.PrefetchScalarGridSpec(n...  23.8 us
    all_to_all x4, starting transfers between devices, swap(): return lax.all_to_all(x, axes, 0, 0, tiled=True)  22.9 us
    unnamed x26, local copies, waits for them, and re-layouts  13.7 us
  transfers between devices with their start and end apart: 4, of which 4 were waited for; matrix products, arithmetic and copies ran while one was open for 2% of the time, Pallas kernels for 1%

profile of v1, /device:TPU:1, one launch (start us, length us, event | category | flops | bytes accessed | tf_op | source)
XLA Modules:
  0.0 207.3 jit_solution(12050593305109423066)
XLA Ops:
  0.6 0.0 copy-start.1
  0.6 1.6 copy-done.1
  2.2 0.0 copy-start.4
  2.2 1.2 copy-done.4
  3.5 0.0 copy-start.5
  3.5 1.2 copy-done.5
  4.7 0.0 copy-start.6
  4.7 1.2 copy-done.6
  5.9 0.0 copy-start.7
  5.9 1.2 copy-done.7
  7.1 0.0 copy-start.8
  7.1 0.9 copy-done.8
  8.1 0.0 copy-start.9
  8.1 0.9 copy-done.9
  9.0 0.0 copy-start.10
  9.0 1.0 copy-done.10
  10.1 0.0 copy-start.11
  10.1 1.0 copy-done.11
  11.1 4.1 %pack.1 = bf16[8,256,1152]{2,1,0:T(8,128)(2,1)S(1)} custom-call(bf16[256,4096]{1,0:T(8,128)(2,1)S(1)} %bitcast.16, bf16[64,4096]{1,0:T(8,128)(2,1)S(1)} %bitcast.24, bf16[64,4096]{1,0:T(8,128)(2,1)S(1)} %bitcast.25, bf16[256,2048]{1,0:T(8,128)(2,1)S(1)} %bitcast.20, bf16[256,2048]{1,0:T(8,128)(2,1)S(1)} %bitcast.21, bf16[256,2048]{1,0:T(8,128)(2,1)S(1)} %bitcast.22, ...), custom_call_target="tpu_custom_call" | custom-call | tf_op jit(solution)/shard_map/pack/pallas_call | solution.py:62
  15.3 0.0 copy-start
  15.3 2.2 %copy-done = bf16[8,256,1152]{2,1,0:T(8,128)(2,1)} copy-done((bf16[8,256,1152]{2,1,0:T(8,128)(2,1)}, bf16[8,256,1152]{2,1,0:T(8,128)(2,1)S(1)}, u32[]{:S(2)}) %copy-start) | copy-done | bytes 4718616
  17.4 0.0 copy-start.12
  17.4 6.1 %all-to-all-start = ((bf16[8,256,1152]{2,1,0:T(8,128)(2,1)}), bf16[8,256,1152]{2,1,0:T(8,128)(2,1)}, u32[]{:S(2)}, u32[]{:S(2)}) async-start(bf16[8,256,1152]{2,1,0:T(8,128)(2,1)} %copy-done), calls=%async_computation | async-start | bytes 9437184 | tf_op jit(solution)/shard_map/all_to_all | solution.py:275
  23.5 0.0 copy-done.12
  23.5 0.6 pad_add_fusion.meta
  24.1 53.9 %all-to-all-done = bf16[8,256,1152]{2,1,0:T(8,128)(2,1)} async-done(((bf16[8,256,1152]{2,1,0:T(8,128)(2,1)}), bf16[8,256,1152]{2,1,0:T(8,128)(2,1)}, u32[]{:S(2)}, u32[]{:S(2)}) %all-to-all-start) | async-done | bytes 4718624 | tf_op jit(solution)/shard_map/all_to_all | solution.py:275
  78.1 0.0 copy-start.2
  78.1 23.8 %attention.1 = (bf16[2048,256]{1,0:T(8,128)(2,1)}, bf16[8,128,256]{2,1,0:T(8,128)(2,1)}, bf16[16,16,128]{2,1,0:T(8,128)(2,1)}) custom-call(s32[9]{0:T(128)} %pad_add_fusion.meta, bf16[2048,1152]{1,0:T(8,128)(2,1)} %bitcast.9.packed, bf16[64,2048]{1,0:T(8,128)(2,1)} %wq_up.3, bf16[64,2048]{1,0:T(8,128)(2,1)} %wv_up.3), custom_call_target="tpu_custom_call" | custom-call | tf_op jit(solution)/shard_map/attention/pallas_call | solution.py:177
  101.8 14.3 %all_to_all.30.parts = bf16[8,128,256]{2,1,0:T(8,128)(2,1)} all-to-all(bf16[8,128,256]{2,1,0:T(8,128)(2,1)} %get-tuple-element.13), channel_id=1, replica_groups=mesh['x'=4,'z'=4,'y'=4,'core'=2] {'y','core'}, dimensions={0} | all-to-all | bytes 1048576 | tf_op jit(solution)/shard_map/all_to_all | solution.py:275
  116.2 7.9 %all-to-all-start.4 = ((bf16[16,16,128]{2,1,0:T(8,128)(2,1)}), bf16[16,16,128]{2,1,0:T(8,128)(2,1)S(1)}, u32[]{:S(2)}, u32[]{:S(2)}) async-start(bf16[16,16,128]{2,1,0:T(8,128)(2,1)} %get-tuple-element.14), calls=%async_computation.4 | async-start | bytes 131072 | tf_op jit(solution)/shard_map/all_to_all | solution.py:275
  124.1 0.0 copy-done.2
  124.1 0.0 copy-start.3
  124.1 1.0 copy-done.3
  125.1 1.2 down_gradient.1
  126.4 4.2 %all-to-all-done.4 = bf16[16,16,128]{2,1,0:T(8,128)(2,1)S(1)} async-done(((bf16[16,16,128]{2,1,0:T(8,128)(2,1)}), bf16[16,16,128]{2,1,0:T(8,128)(2,1)S(1)}, u32[]{:S(2)}, u32[]{:S(2)}) %all-to-all-start.4) | async-done | bytes 65568 | tf_op jit(solution)/shard_map/all_to_all | solution.py:275
  130.6 24.8 %all_to_all.31 = bf16[128,16,256]{2,1,0:T(8,128)(2,1)S(1)} all-to-all(bf16[128,16,256]{2,1,0:T(8,128)(2,1)S(1)} %bitcast.19), channel_id=1, replica_groups=mesh['x'=4,'z'=4,'y'=4,'core'=2] {'x','z','y','core'}, dimensions={0} | all-to-all | bytes 2097152 | tf_op jit(solution)/shard_map/all_to_all | solution.py:275
  155.4 4.6 %all-to-all-start.1 = ((bf16[8,256,256]{2,1,0:T(8,128)(2,1)}), bf16[8,256,256]{2,1,0:T(8,128)(2,1)S(1)}, u32[]{:S(2)}, u32[]{:S(2)}) async-start(bf16[8,256,256]{2,1,0:T(8,128)(2,1)} %bitcast.27), calls=%async_computation.1 | async-start | bytes 2097152 | tf_op jit(solution)/shard_map/all_to_all | solution.py:275
  160.1 0.2 reduce_sum.24
  160.3 14.9 %all-to-all-done.1 = bf16[8,256,256]{2,1,0:T(8,128)(2,1)S(1)} async-done(((bf16[8,256,256]{2,1,0:T(8,128)(2,1)}), bf16[8,256,256]{2,1,0:T(8,128)(2,1)S(1)}, u32[]{:S(2)}, u32[]{:S(2)}) %all-to-all-start.1) | async-done | bytes 1048608 | tf_op jit(solution)/shard_map/all_to_all | solution.py:275
  175.2 1.3 broadcast_in_dim.10
  176.5 4.3 %all-to-all-start.5 = ((bf16[128,16,384]{2,1,0:T(8,128)(2,1)}), bf16[128,16,384]{2,1,0:T(8,128)(2,1)S(1)}, u32[]{:S(2)}, u32[]{:S(2)}) async-start(bf16[128,16,384]{2,1,0:T(8,128)(2,1)} %broadcast_in_dim.10), calls=%async_computation.5 | async-start | bytes 3145728 | tf_op jit(solution)/shard_map/all_to_all | solution.py:275
  180.8 1.6 copy.15
  182.3 2.3 %reshape.28 = bf16[1,256,2048]{2,1,0:T(8,128)(2,1)} reshape(bf16[256,8,256]{2,1,0:T(8,128)(2,1)} %copy.15) | data formatting | bytes 2097152 | tf_op jit(solution)/shard_map/reshape | solution.py:319
  184.7 21.0 %all-to-all-done.5 = bf16[128,16,384]{2,1,0:T(8,128)(2,1)S(1)} async-done(((bf16[128,16,384]{2,1,0:T(8,128)(2,1)}), bf16[128,16,384]{2,1,0:T(8,128)(2,1)S(1)}, u32[]{:S(2)}, u32[]{:S(2)}) %all-to-all-start.5) | async-done | bytes 1572896 | tf_op jit(solution)/shard_map/all_to_all | solution.py:275
  205.6 1.7 place.1
  (2 shorter events, 0.0 us)
Async XLA Ops:
  0.6 1.6 copy-start.1
  2.2 1.2 copy-start.4
  3.5 1.2 copy-start.5
  4.7 1.2 copy-start.6
  5.9 1.2 copy-start.7
  7.1 0.9 copy-start.8
  8.1 0.9 copy-start.9
  9.0 1.0 copy-start.10
  10.1 1.0 copy-start.11
  15.3 2.2 %copy-start = (bf16[8,256,1152]{2,1,0:T(8,128)(2,1)}, bf16[8,256,1152]{2,1,0:T(8,128)(2,1)S(1)}, u32[]{:S(2)}) copy-start(bf16[8,256,1152]{2,1,0:T(8,128)(2,1)S(1)} %pack.1) | copy-start | bytes 14155780
  17.4 6.1 %copy-start.12 = (s32[1,8]{1,0:T(1,128)S(1)}, s32[1,8]{1,0:T(1,128)}, u32[]{:S(2)}) copy-start(s32[1,8]{1,0:T(1,128)} %param.14) | copy-start | bytes 100
  17.4 60.6 %all-to-all-start = ((bf16[8,256,1152]{2,1,0:T(8,128)(2,1)}), bf16[8,256,1152]{2,1,0:T(8,128)(2,1)}, u32[]{:S(2)}, u32[]{:S(2)}) async-start(bf16[8,256,1152]{2,1,0:T(8,128)(2,1)} %copy-done), calls=%async_computation | async-start | bytes 9437184 | tf_op jit(solution)/shard_map/all_to_all | solution.py:275
  78.1 46.0 %copy-start.2 = (bf16[1,256,4096]{2,1,0:T(8,128)(2,1)S(1)}, bf16[1,256,4096]{2,1,0:T(8,128)(2,1)}, u32[]{:S(2)}) copy-start(bf16[1,256,4096]{2,1,0:T(8,128)(2,1)} %param.10) | copy-start | bytes 6291460
  116.2 14.4 %all-to-all-start.4 = ((bf16[16,16,128]{2,1,0:T(8,128)(2,1)}), bf16[16,16,128]{2,1,0:T(8,128)(2,1)S(1)}, u32[]{:S(2)}, u32[]{:S(2)}) async-start(bf16[16,16,128]{2,1,0:T(8,128)(2,1)} %get-tuple-element.14), calls=%async_computation.4 | async-start | bytes 131072 | tf_op jit(solution)/shard_map/all_to_all | solution.py:275
  124.1 1.0 copy-start.3
  155.4 19.7 %all-to-all-start.1 = ((bf16[8,256,256]{2,1,0:T(8,128)(2,1)}), bf16[8,256,256]{2,1,0:T(8,128)(2,1)S(1)}, u32[]{:S(2)}, u32[]{:S(2)}) async-start(bf16[8,256,256]{2,1,0:T(8,128)(2,1)} %bitcast.27), calls=%async_computation.1 | async-start | bytes 2097152 | tf_op jit(solution)/shard_map/all_to_all | solution.py:275
  176.5 29.1 %all-to-all-start.5 = ((bf16[128,16,384]{2,1,0:T(8,128)(2,1)}), bf16[128,16,384]{2,1,0:T(8,128)(2,1)S(1)}, u32[]{:S(2)}, u32[]{:S(2)}) async-start(bf16[128,16,384]{2,1,0:T(8,128)(2,1)} %broadcast_in_dim.10), calls=%async_computation.5 | async-start | bytes 3145728 | tf_op jit(solution)/shard_map/all_to_all | solution.py:275

commit v2 on v1

v2 whole, which is shorter than its diff:
```python
import functools

import jax
import jax.numpy as jnp
from jax import lax
from jax.experimental import pallas as pl
from jax.experimental.pallas import tpu as pltpu
from jax.sharding import Mesh
from jax.sharding import PartitionSpec as P

HEAD_COUNT = 16
HEAD_SIZE = 128
RANK = 64
NDOC = 8
TILE = 256
MAX_TILES = 5
ADAPTER_SCALE = 2.0
NEG_FILL = -1e30
SCALING = HEAD_SIZE ** (-0.5)
LOG2_E = 1.4426950408889634

SHARE_ROWS = 16
DOWN_COLS = 256
UP_COLS = 32

DP = ("x", "z")
SEQ = ("y", "core")
PLANE = ("x", "z", "y")
ALL = ("x", "z", "y", "core")
NT = (((1,), (1,)), ((), ()))


def dot(a, b):
    return jnp.dot(a, b, preferred_element_type=jnp.float32)


def dot_nt(a, b):
    return lax.dot_general(a, b, NT, preferred_element_type=jnp.float32)


def pack_kernel(hidden, wq_down, wv_down, fq, fk, fv, grad, wq_up, wv_up, out, low):
    width = fq.shape[1]

    @pl.when(pl.program_id(0) == 0)
    def _():
        low[:, :RANK] = dot_nt(hidden[...], wq_down[...]).astype(jnp.bfloat16)
        low[:, RANK:] = dot_nt(hidden[...], wv_down[...]).astype(jnp.bfloat16)

    q_add = ADAPTER_SCALE * dot(low[:, :RANK], wq_up[...])
    v_add = ADAPTER_SCALE * dot(low[:, RANK:], wv_up[...])
    out[0, :, 0:width] = (fq[...].astype(jnp.float32) + q_add).astype(jnp.bfloat16)
    out[0, :, width : 2 * width] = fk[...]
    out[0, :, 2 * width : 3 * width] = (fv[...].astype(jnp.float32) + v_add).astype(jnp.bfloat16)
    out[0, :, 3 * width : 4 * width] = grad[...]
    out[0, :, 4 * width :] = low[...]


def pack(hidden, wq_down_t, wv_down_t, fq, fk, fv, grad, wq_up, wv_up, seq_size):
    rows, model = hidden.shape
    width = fq.shape[1] // seq_size
    whole = lambda s: pl.BlockSpec(s, lambda d: (0, 0))
    column = lambda r: pl.BlockSpec((r, width), lambda d: (0, d))
    packed = 4 * width + 2 * RANK
    return pl.pallas_call(
        pack_kernel,
        grid=(seq_size,),
        in_specs=[
            whole((rows, model)),
            whole((RANK, model)),
            whole((RANK, model)),
            column(rows),
            column(rows),
            column(rows),
            column(rows),
            column(RANK),
            column(RANK),
        ],
        out_specs=pl.BlockSpec((1, rows, packed), lambda d: (d, 0, 0)),
        out_shape=jax.ShapeDtypeStruct((seq_size, rows, packed), jnp.bfloat16),
        scratch_shapes=[pltpu.VMEM((rows, 2 * RANK), jnp.bfloat16)],
        compiler_params=pltpu.CompilerParams(vmem_limit_bytes=60 << 20),
        name="pack",
    )(hidden, wq_down_t, wv_down_t, fq, fk, fv, grad, wq_up, wv_up)


def attention_kernel(
    meta, packed, wq_up, wv_up, out, back_0, back_1, back_2, back_3, up,
    q_t, k_t, v_t, g_t, dq_t, dv, dv_t, returned,
):
    length = packed.shape[0]
    heads = out.shape[1] // HEAD_SIZE
    width = heads * HEAD_SIZE
    blocks = length // TILE
    chip = meta[NDOC]
    span = [slice(head * HEAD_SIZE, (head + 1) * HEAD_SIZE) for head in range(heads)]

    def columns(which, head):
        begin = which * width + head * HEAD_SIZE
        return slice(begin, begin + HEAD_SIZE)

    for head in range(heads):
        q_t[span[head], :] = packed[:, columns(0, head)].T
        k_t[span[head], :] = packed[:, columns(1, head)].T
        v_t[span[head], :] = packed[:, columns(2, head)].T
        g_t[span[head], :] = packed[:, columns(3, head)].T
    dv[...] = jnp.zeros_like(dv)

    def block(index, _):
        row0 = pl.multiple_of(index * TILE, TILE)
        q_rows = pl.ds(row0, TILE)
        position = row0 + lax.broadcasted_iota(jnp.int32, (1, TILE), 1)
        begin = jnp.zeros((1, TILE), jnp.int32)
        first = jnp.int32(0)
        end = jnp.int32(0)
        for doc in range(NDOC):
            end = end + meta[doc]
            begin = jnp.where(position >= end, end, begin)
            first = jnp.where(row0 >= end, end, first)
        tiles = index - lax.div(first, TILE) + 1

        def body(count):
            key0 = pl.multiple_of((index + 1 - count) * TILE, TILE)
            k_rows = pl.ds(key0, count * TILE)
            key_index = lax.broadcasted_iota(jnp.int32, (count * TILE, TILE), 0)
            in_document = key_index >= begin - key0
            causal = lax.broadcasted_iota(jnp.int32, (TILE, TILE), 0) <= (
                lax.broadcasted_iota(jnp.int32, (TILE, TILE), 1)
            )
            held = []
            for head in range(heads):
                scores = dot(packed[k_rows, columns(1, head)], q_t[span[head], q_rows])
                prob_grad = dot(packed[k_rows, columns(2, head)], g_t[span[head], q_rows])
                scores = jnp.where(in_document, scores, NEG_FILL)
                last = jnp.where(causal, scores[(count - 1) * TILE :], NEG_FILL)
                if count > 1:
                    scores = jnp.concatenate([scores[: (count - 1) * TILE], last], axis=0)
                else:
                    scores = last
                maximum = jnp.max(scores, axis=0, keepdims=True)
                powers = jnp.exp2((scores - maximum) * (SCALING * LOG2_E))
                inverse = 1.0 / jnp.sum(powers, axis=0, keepdims=True)
                held.append((prob_grad, powers.astype(jnp.bfloat16), inverse))
            for head in range(heads):
                prob_grad, rounded, inverse = held[head]
                result = (dot(v_t[span[head], k_rows], rounded) * inverse).astype(jnp.bfloat16)
                g_wide = g_t[span[head], q_rows].astype(jnp.float32)
                row_dot = jnp.sum(g_wide * result.astype(jnp.float32), axis=0, keepdims=True)
                score_grad = rounded * (prob_grad - row_dot).astype(jnp.bfloat16)
                query_grad = dot(k_t[span[head], k_rows], score_grad) * (inverse * SCALING)
                dq_t[span[head], q_rows] = query_grad.astype(jnp.bfloat16)
                out[q_rows, span[head]] = result.T
                g_scaled = (g_wide * inverse).astype(jnp.bfloat16).T
                dv[head, k_rows, :] += dot(rounded, g_scaled)

        for count in range(1, min(MAX_TILES, blocks) + 1):
            pl.when(tiles == count)(functools.partial(body, count))
        return 0

    lax.fori_loop(0, blocks, block, 0)
    for head in range(heads):
        dv_t[span[head], :] = dv[head].astype(jnp.bfloat16).T

    for part, (grads, weight) in enumerate(((dq_t, wq_up), (dv_t, wv_up))):
        returned[part * RANK : (part + 1) * RANK, :] = (
            ADAPTER_SCALE * dot(weight[...], grads[...])
        ).astype(jnp.bfloat16)
    backs = (back_0, back_1, back_2, back_3)
    rows = back_0.shape[2]
    for step in range(len(backs)):
        target = lax.rem(chip + step, len(backs))
        for core in range(2):
            begin = pl.multiple_of((target * 2 + core) * rows, rows)
            backs[step][core] = returned[:, pl.ds(begin, rows)]

    low = packed[:, 4 * width :]
    lane = lax.broadcasted_iota(jnp.int32, (width, up.shape[1]), 1)
    source = lax.broadcasted_iota(jnp.int32, (width, up.shape[1]), 0)
    mine = (source == (lane // 128) * UP_COLS + lane % UP_COLS) & (
        (lane % 128) // UP_COLS == chip
    )
    mine = jnp.where(mine, 1.0, 0.0).astype(jnp.bfloat16)
    for part, grads in enumerate((dq_t, dv_t)):
        up_part = (dot(grads[...], low) * ADAPTER_SCALE).T[part * RANK : (part + 1) * RANK, :]
        up[part * RANK : (part + 1) * RANK, :] = dot(up_part.astype(jnp.bfloat16), mine).astype(
            jnp.bfloat16
        )


VMEM = pl.BlockSpec(memory_space=pltpu.VMEM)
SMEM = pl.BlockSpec(memory_space=pltpu.SMEM)


def attention(meta, packed, wq_up, wv_up, seq_size):
    length = packed.shape[0]
    width = (packed.shape[1] - 2 * RANK) // 4
    rows = length // seq_size
    heads = width // HEAD_SIZE
    chips = seq_size // 2
    wide_t = pltpu.VMEM((width, length), jnp.bfloat16)
    back = jax.ShapeDtypeStruct((2, 2 * RANK, rows), jnp.bfloat16)
    return pl.pallas_call(
        attention_kernel,
        in_specs=[SMEM, VMEM, VMEM, VMEM],
        out_specs=[VMEM] * (2 + chips),
        scratch_shapes=[
            wide_t,
            wide_t,
            wide_t,
            wide_t,
            wide_t,
            pltpu.VMEM((heads, length, HEAD_SIZE), jnp.float32),
            wide_t,
            pltpu.VMEM((2 * RANK, length), jnp.bfloat16),
        ],
        out_shape=[jax.ShapeDtypeStruct((length, width), jnp.bfloat16)]
        + [back] * chips
        + [jax.ShapeDtypeStruct((2 * RANK, width // UP_COLS * 128), jnp.bfloat16)],
        compiler_params=pltpu.CompilerParams(vmem_limit_bytes=40 << 20),
        name="attention",
    )(meta, packed, wq_up, wv_up)


def chips_kernel(part_0, part_1, part_2, part_3, out):
    total = part_0[...].astype(jnp.float32)
    for part in (part_1, part_2, part_3):
        total += part[...].astype(jnp.float32)
    out[...] = total.astype(out.dtype)


def sum_chips(parts):
    return pl.pallas_call(
        chips_kernel,
        in_specs=[VMEM] * len(parts),
        out_specs=VMEM,
        out_shape=jax.ShapeDtypeStruct(parts[0].shape, parts[0].dtype),
        name="sum_chips",
    )(*parts)


def down_kernel(core, own, other, hidden, hidden_other, up, out):
    total = (own[...].astype(jnp.float32) + other[...].astype(jnp.float32)).astype(jnp.bfloat16)
    first = core[0] == 0
    here = jnp.where(first, total[0], total[1])
    there = jnp.where(first, total[1], total[0])
    grad = (dot(here, hidden[...]) + dot(there, hidden_other[...])).astype(out.dtype)
    for row in range(out.shape[0]):
        across = slice(row * SHARE_ROWS, (row + 1) * SHARE_ROWS)
        for column in range(out.shape[1]):
            out[row, column, :, :DOWN_COLS] = grad[
                across, column * DOWN_COLS : (column + 1) * DOWN_COLS
            ]
            out[row, column, :, DOWN_COLS:] = up[across, column * 128 : (column + 1) * 128]


def down_gradient(core, own, other, hidden, hidden_other, up):
    rows, half = hidden_other.shape
    steps = 4
    step = half // steps
    columns = half // DOWN_COLS
    across = 2 * RANK // SHARE_ROWS
    return pl.pallas_call(
        down_kernel,
        grid_spec=pltpu.PrefetchScalarGridSpec(
            num_scalar_prefetch=1,
            grid=(steps,),
            in_specs=[
                pl.BlockSpec(own.shape, lambda i, core: (0, 0, 0)),
                pl.BlockSpec(own.shape, lambda i, core: (0, 0, 0)),
                pl.BlockSpec((rows, step), lambda i, core: (0, core[0] * steps + i)),
                pl.BlockSpec((rows, step), lambda i, core: (0, i)),
                pl.BlockSpec((2 * RANK, columns // steps * 128), lambda i, core: (0, i)),
            ],
            out_specs=pl.BlockSpec(
                (across, columns // steps, SHARE_ROWS, DOWN_COLS + 128),
                lambda i, core: (0, i, 0, 0),
            ),
        ),
        out_shape=jax.ShapeDtypeStruct(
            (across, columns, SHARE_ROWS, DOWN_COLS + 128), jnp.bfloat16
        ),
        compiler_params=pltpu.CompilerParams(vmem_limit_bytes=24 << 20),
        name="down_gradient",
    )(core, own, other, hidden, hidden_other, up)


def share_kernel(parts, out):
    total = parts[0].astype(jnp.float32)
    for part in range(1, parts.shape[0]):
        total += parts[part].astype(jnp.float32)
    total = total.astype(out.dtype)
    for part in range(out.shape[0]):
        out[part] = total


def sum_share(parts):
    return pl.pallas_call(
        share_kernel,
        in_specs=[VMEM],
        out_specs=VMEM,
        out_shape=jax.ShapeDtypeStruct(parts.shape, parts.dtype),
        name="sum_share",
    )(parts)


def place_kernel(core, own, other, grad_a_q, up_q, grad_a_v, up_v, wide):
    half = own.shape[0] // 2
    columns = own.shape[1]
    for part, shares in enumerate((own, other)):
        which = core[0] if part == 0 else 1 - core[0]
        for row in range(own.shape[0]):
            across = slice(row % half * SHARE_ROWS, (row % half + 1) * SHARE_ROWS)
            target = (grad_a_q, grad_a_v)[row // half]
            for column in range(columns):
                begin = pl.multiple_of((which * columns + column) * DOWN_COLS, DOWN_COLS)
                target[across, pl.ds(begin, DOWN_COLS)] = shares[
                    row, column, :, :DOWN_COLS
                ].astype(jnp.float32)
                wide[
                    row * SHARE_ROWS : (row + 1) * SHARE_ROWS, column * 128 : (column + 1) * 128
                ] = shares[row, column, :, DOWN_COLS:]
        width = columns * UP_COLS
        source = lax.broadcasted_iota(jnp.int32, (columns * 128, width), 0)
        lane = lax.broadcasted_iota(jnp.int32, (columns * 128, width), 1)
        lane = (lane // UP_COLS) * 128 + lane % UP_COLS
        for chip in range(128 // UP_COLS):
            pick = jnp.where(source == lane + chip * UP_COLS, 1.0, 0.0).astype(jnp.bfloat16)
            picked = dot(wide[...], pick)
            begin = pl.multiple_of((2 * chip + which) * width, width)
            up_q[:, pl.ds(begin, width)] = picked[:RANK]
            up_v[:, pl.ds(begin, width)] = picked[RANK:]


def place(core, own, other, model, width):
    shapes = [(RANK, model), (RANK, width), (RANK, model), (RANK, width)]
    return pl.pallas_call(
        place_kernel,
        in_specs=[SMEM, VMEM, VMEM],
        out_specs=[VMEM] * 4,
        out_shape=[jax.ShapeDtypeStruct(shape, jnp.float32) for shape in shapes],
        scratch_shapes=[pltpu.VMEM((2 * RANK, own.shape[1] * 128), jnp.bfloat16)],
        compiler_params=pltpu.CompilerParams(vmem_limit_bytes=30 << 20),
        name="place",
    )(core, own, other)


def swap(x, axes):
    return lax.all_to_all(x, axes, 0, 0, tiled=True)


def to_other_core(x):
    return lax.ppermute(x, "core", [(0, 1), (1, 0)])


def per_device(
    sizes,
    hidden,
    frozen_queries,
    frozen_keys,
    frozen_values,
    document_length_list,
    query_down_weight,
    query_up_weight,
    value_down_weight,
    value_up_weight,
    output_gradient,
):
    dp_size, seq_size = sizes
    chips = seq_size // 2
    rows, model = hidden.shape[1:]
    half = model // 2
    chip = lax.axis_index("y").astype(jnp.int32)
    core = lax.axis_index("core").astype(jnp.int32)
    packed = pack(
        hidden[0],
        query_down_weight.T,
        value_down_weight.T,
        frozen_queries[0],
        frozen_keys[0],
        frozen_values[0],
        output_gradient[0],
        query_up_weight,
        value_up_weight,
        seq_size,
    )
    received = swap(packed, SEQ).reshape(seq_size * rows, packed.shape[2])
    hidden_other = to_other_core(
        lax.dynamic_slice(hidden[0], (0, (1 - core) * half), (rows, half))
    )
    width = frozen_queries.shape[2] // seq_size
    own_columns = (0, (chip * 2 + core) * width)
    wq_up = lax.dynamic_slice(query_up_weight, own_columns, (RANK, width))
    wv_up = lax.dynamic_slice(value_up_weight, own_columns, (RANK, width))
    meta = jnp.concatenate([document_length_list[0], chip[None]])
    result, *backs, up = attention(meta, received, wq_up, wv_up, seq_size)

    arrived = [backs[0]] + [
        lax.ppermute(backs[step], "y", [(c, (c + step) % chips) for c in range(chips)])
        for step in range(1, chips)
    ]
    back = sum_chips(arrived)
    back_other = to_other_core(back)
    result, back_other = lax.optimization_barrier((result, back_other))
    down = down_gradient(core[None], back, back_other, hidden[0], hidden_other, up)
    attended = swap(result.reshape(seq_size, rows, width), SEQ)
    attended = attended.transpose(1, 0, 2).reshape(1, rows, seq_size * width)

    shares = swap(down.reshape((-1,) + down.shape[2:]), PLANE)
    shares = swap(sum_share(shares), PLANE).reshape(down.shape)
    shares_other = to_other_core(shares)
    grad_a_q, up_q, grad_a_v, up_v = place(
        core[None], shares, shares_other, model, seq_size * width
    )
    return attended, grad_a_q.T, up_q, grad_a_v.T, up_v


def solution(mesh):
    dp_size, seq_size = mesh.shape["dp"], mesh.shape["seq"]
    fine = Mesh(mesh.devices.reshape(4, 4, 4, 2), ALL)
    rows = P(DP, SEQ, None)
    in_specs = (rows, rows, rows, rows, P(DP, None), P(), P(), P(), P(), rows)
    out_specs = (rows, P(), P(), P(), P())
    return jax.shard_map(
        functools.partial(per_device, (dp_size, seq_size)),
        mesh=fine,
        in_specs=in_specs,
        out_specs=out_specs,
        check_vma=False,
    )
```

time: 208 us -> 181 us (0.87)
  waiting for transfers between devices: 94 us -> 74.5 us
  local copies, waits for them, and re-layouts: 18.9 us -> 7.96 us
  starting transfers between devices: 22.9 us -> 17.7 us
  Pallas kernels: 30.9 us -> 35.5 us
  blocking collectives: 39.2 us -> 43.6 us
    all_to_all x4 -> x2, waiting for transfers between devices: 94 us -> 67.4 us  [swap(): return lax.all_to_all(x, axes, 0, 0, tiled=True)]
    unnamed x26 -> x14, local copies, waits for them, and re-layouts: 13.7 us -> 2.22 us
    all_to_all x4 -> x2, starting transfers between devices: 22.9 us -> 12.6 us  [swap(): return lax.all_to_all(x, axes, 0, 0, tiled=True)]
    ppermute x0 -> x6, waiting for transfers between devices: none -> 7.03 us  [the longest x3 5.83 us: per_device(): lax.ppermute(backs[step], 'y', [(c, (c + step) % chips) for c in range(ch...]
    pallas_call x1, Pallas kernels: 4.13 us -> 10.2 us  [pack(): pl.pallas_call(pack_kernel, grid=(seq_size,), in_specs=[whole((rows, mode...]
    ppermute x0 -> x6, starting transfers between devices: none -> 5.04 us  [the longest x3 2.68 us: per_device(): lax.ppermute(backs[step], 'y', [(c, (c + step) % chips) for c in range(ch...]
    all_to_all x2, blocking collectives: 39.2 us -> 43.6 us  [swap(): return lax.all_to_all(x, axes, 0, 0, tiled=True)]
    pallas_call x3 -> x5, Pallas kernels: 26.7 us -> 25.2 us  [the longest x1 17.1 us: attention(): pl.pallas_call(attention_kernel, in_specs=[SMEM, VMEM, VMEM, VMEM], out_s...]
  transfers between devices with their start and end apart: 4 -> 8, of which waited for: 4 -> 6; matrix products, arithmetic and copies ran while one was open for 2% -> 3% of each run, Pallas kernels for 1% -> 11%
where the time goes in v2:
time: 181 us; the launch traced here: 180 us
  waiting for transfers between devices  74.5 us (41%)
  blocking collectives  43.6 us (24%)
  Pallas kernels  35.5 us (20%)
  starting transfers between devices  17.7 us (10%)
  local copies, waits for them, and re-layouts  7.96 us (4%)
    all_to_all x2, waiting for transfers between devices, swap(): return lax.all_to_all(x, axes, 0, 0, tiled=True)  67.4 us
    all_to_all x2, blocking collectives, swap(): return lax.all_to_all(x, axes, 0, 0, tiled=True)  43.6 us
    pallas_call x1, Pallas kernels, attention(): pl.pallas_call(attention_kernel, in_specs=[SMEM, VMEM, VMEM, VMEM], out_s...  17.1 us
    all_to_all x2, starting transfers between devices, swap(): return lax.all_to_all(x, axes, 0, 0, tiled=True)  12.6 us
    pallas_call x1, Pallas kernels, pack(): pl.pallas_call(pack_kernel, grid=(seq_size,), in_specs=[whole((rows, mode...  10.2 us
    ppermute x3, waiting for transfers between devices, per_device(): lax.ppermute(backs[step], 'y', [(c, (c + step) % chips) for c in range(ch...  5.83 us
  transfers between devices with their start and end apart: 8, of which 6 were waited for; matrix products, arithmetic and copies ran while one was open for 3% of the time, Pallas kernels for 11%

profile of v2, /device:TPU:1, one launch (start us, length us, event | category | flops | bytes accessed | tf_op | source)
XLA Modules:
  0.0 179.9 jit_solution(17857401362029419944)
XLA Ops:
  0.6 10.2 %pack.1 = bf16[8,256,1152]{2,1,0:T(8,128)(2,1)} custom-call(bf16[256,4096]{1,0:T(8,128)(2,1)} %bitcast.19, bf16[64,4096]{1,0:T(8,128)(2,1)} %bitcast.29, bf16[64,4096]{1,0:T(8,128)(2,1)} %bitcast.30, bf16[256,2048]{1,0:T(8,128)(2,1)} %bitcast.25, bf16[256,2048]{1,0:T(8,128)(2,1)} %bitcast.26, bf16[256,2048]{1,0:T(8,128)(2,1)} %bitcast.27, ...), custom_call_target="tpu_custom_call" | custom-call | tf_op jit(solution)/shard_map/pack/pallas_call | solution.py:64
  10.8 0.0 copy-start
  10.8 0.0 copy-start.6
  10.9 6.1 %all-to-all-start = ((bf16[8,256,1152]{2,1,0:T(8,128)(2,1)}), bf16[8,256,1152]{2,1,0:T(8,128)(2,1)}, u32[]{:S(2)}, u32[]{:S(2)}) async-start(bf16[8,256,1152]{2,1,0:T(8,128)(2,1)} %pack.1), calls=%async_computation | async-start | bytes 9437184 | tf_op jit(solution)/shard_map/all_to_all | solution.py:347
  17.0 0.0 copy-done
  17.0 1.1 dynamic-slice_bitcast_fusion
  18.1 0.1 collective-permute-start.4
  18.1 0.0 copy-done.6
  18.1 0.1 pad_add_fusion.meta
  18.2 0.8 constant_dynamic-slice_fusion
  19.0 52.5 %all-to-all-done = bf16[8,256,1152]{2,1,0:T(8,128)(2,1)} async-done(((bf16[8,256,1152]{2,1,0:T(8,128)(2,1)}), bf16[8,256,1152]{2,1,0:T(8,128)(2,1)}, u32[]{:S(2)}, u32[]{:S(2)}) %all-to-all-start) | async-done | bytes 4718624 | tf_op jit(solution)/shard_map/all_to_all | solution.py:347
  71.5 17.1 %attention.1 = (bf16[2048,256]{1,0:T(8,128)(2,1)}, bf16[2,128,256]{2,1,0:T(8,128)(2,1)S(1)}, bf16[2,128,256]{2,1,0:T(8,128)(2,1)S(1)}, bf16[2,128,256]{2,1,0:T(8...) custom-call(s32[9]{0:T(128)S(1)} %pad_add_fusion.meta, ...), custom_call_target="tpu_custom_call" | custom-call | tf_op jit(solution)/shard_map/attention/pallas_call | solution.py:201
  88.6 0.0 copy-start.2
  88.6 0.6 copy-done.2
  89.3 0.3 collective-permute-start
  89.6 1.8 collective-permute-start.1
  91.4 0.6 collective-permute-start.2
  92.0 3.7 %collective-permute-done.part_1 = bf16[2,128,256]{2,1,0:T(8,128)(2,1)S(1)} collective-permute-done((bf16[2,128,256]{2,1,0:T(8,128)(2,1)S(1)}, bf16[2,128,256]{2,1,0:T(8,128)(2,1)S(1)}, u32[]{:S(2)}, u32[]{:S(2)}) %collective-permute-start) | collective-permute-done | bytes 131104 | tf_op jit(solution)/shard_map/ppermute | solution.py:397
  95.7 0.0 copy-start.3
  95.7 1.2 collective-permute-done.1.part_2
  96.9 0.0 copy-start.4
  96.9 0.9 collective-permute-done.2.part_3
  97.8 0.0 copy-done.4
  97.8 0.0 copy-start.5
  97.8 0.7 copy-done.5
  98.5 0.0 copy-done.3
  98.5 1.8 %sum_chips.1.own = bf16[2,128,256]{2,1,0:T(8,128)(2,1)} custom-call(bf16[2,128,256]{2,1,0:T(8,128)(2,1)} %copy-done.2, bf16[2,128,256]{2,1,0:T(8,128)(2,1)} %copy-done.3, bf16[2,128,256]{2,1,0:T(8,128)(2,1)} %copy-done.4, bf16[2,128,256]{2,1,0:T(8,128)(2,1)} %copy-done.5), custom_call_target="tpu_custom_call" | custom-call | tf_op jit(solution)/shard_map/sum_chips/pallas_call | solution.py:231
  100.3 2.1 %collective-permute-start.3 = (bf16[2,128,256]{2,1,0:T(8,128)(2,1)}, bf16[2,128,256]{2,1,0:T(8,128)(2,1)S(1)}, u32[]{:S(2)}, u32[]{:S(2)}) collective-permute-start(bf16[2,128,256]{2,1,0:T(8,128)(2,1)} %sum_chips.1.own), channel_id=1, source_target_pairs={{0,1},{1,0},{2,3},{3,2},{4,5},{5,4},{6,7},{7,6},{8,9},{9,8},{10,11... | collective-permute-start | bytes 393224 | tf_op jit(solution)/shard_map/ppermute | solution.py:351
  102.4 1.2 collective-permute-done.3.other
  103.6 0.0 collective-permute-done.4.hidden_other
  103.6 0.0 copy-start.1
  103.6 0.9 copy-done.1
  104.5 1.3 down_gradient.1
  105.8 24.7 %all_to_all.20.parts = bf16[64,16,384]{2,1,0:T(8,128)(2,1)} all-to-all(bf16[64,16,384]{2,1,0:T(8,128)(2,1)S(1)} %bitcast.21), channel_id=1, replica_groups=mesh['x'=4,'z'=4,'y'=4,'core'=2] {'x','z','y'}, dimensions={0} | all-to-all | bytes 1572864 | tf_op jit(solution)/shard_map/all_to_all | solution.py:347
  130.5 2.2 %sum_share.1 = bf16[64,16,384]{2,1,0:T(8,128)(2,1)} custom-call(bf16[64,16,384]{2,1,0:T(8,128)(2,1)} %all_to_all.20.parts), custom_call_target="tpu_custom_call" | custom-call | tf_op jit(solution)/shard_map/sum_share/pallas_call | solution.py:296
  132.7 18.9 %all_to_all.21 = bf16[64,16,384]{2,1,0:T(8,128)(2,1)S(1)} all-to-all(bf16[64,16,384]{2,1,0:T(8,128)(2,1)} %sum_share.1), channel_id=1, replica_groups=mesh['x'=4,'z'=4,'y'=4,'core'=2] {'x','z','y'}, dimensions={0} | all-to-all | bytes 1572864 | tf_op jit(solution)/shard_map/all_to_all | solution.py:347
  151.5 6.5 %all-to-all-start.1 = ((bf16[8,256,256]{2,1,0:T(8,128)(2,1)}), bf16[8,256,256]{2,1,0:T(8,128)(2,1)S(1)}, u32[]{:S(2)}, u32[]{:S(2)}) async-start(bf16[8,256,256]{2,1,0:T(8,128)(2,1)} %bitcast.10), calls=%async_computation.1 | async-start | bytes 2097152 | tf_op jit(solution)/shard_map/all_to_all | solution.py:347
  158.1 0.2 collective-permute-start.5
  158.2 14.9 %all-to-all-done.1 = bf16[8,256,256]{2,1,0:T(8,128)(2,1)S(1)} async-done(((bf16[8,256,256]{2,1,0:T(8,128)(2,1)}), bf16[8,256,256]{2,1,0:T(8,128)(2,1)S(1)}, u32[]{:S(2)}, u32[]{:S(2)}) %all-to-all-start.1) | async-done | bytes 1048608 | tf_op jit(solution)/shard_map/all_to_all | solution.py:347
  173.2 1.6 copy.15
  174.7 2.3 %reshape.28 = bf16[1,256,2048]{2,1,0:T(8,128)(2,1)} reshape(bf16[256,8,256]{2,1,0:T(8,128)(2,1)} %copy.15) | data formatting | bytes 2097152 | tf_op jit(solution)/shard_map/reshape | solution.py:405
  177.1 0.0 collective-permute-done.5.other
  177.1 2.8 %place.1 = (f32[64,4096]{1,0:T(8,128)}, f32[64,2048]{1,0:T(8,128)}, f32[64,4096]{1,0:T(8,128)}, f32[64,2048]{1,0:T(8,128)}) custom-call(s32[1]{0:T(128)} %bitcast.12.core, bf16[8,8,16,384]{3,2,1,0:T(8,128)(2,1)S(1)} %bitcast.23, bf16[8,8,16,384]{3,2,1,0:T(8,128)(2,1)S(1)} %collective-permute-done.5.other), custom_call_target="tpu_custom_call" | custom-call | tf_op jit(solution)/shard_map/place/pallas_call | solution.py:335
Async XLA Ops:
  10.8 6.1 %copy-start = (bf16[1,256,4096]{2,1,0:T(8,128)(2,1)S(1)}, bf16[1,256,4096]{2,1,0:T(8,128)(2,1)}, u32[]{:S(2)}) copy-start(bf16[1,256,4096]{2,1,0:T(8,128)(2,1)} %param.10) | copy-start | bytes 6291460
  10.8 7.3 %copy-start.6 = (s32[1,8]{1,0:T(1,128)S(1)}, s32[1,8]{1,0:T(1,128)}, u32[]{:S(2)}) copy-start(s32[1,8]{1,0:T(1,128)} %param.14) | copy-start | bytes 100
  10.9 60.6 %all-to-all-start = ((bf16[8,256,1152]{2,1,0:T(8,128)(2,1)}), bf16[8,256,1152]{2,1,0:T(8,128)(2,1)}, u32[]{:S(2)}, u32[]{:S(2)}) async-start(bf16[8,256,1152]{2,1,0:T(8,128)(2,1)} %pack.1), calls=%async_computation | async-start | bytes 9437184 | tf_op jit(solution)/shard_map/all_to_all | solution.py:347
  18.1 85.5 %collective-permute-start.4 = (bf16[256,2048]{1,0:T(8,128)(2,1)}, bf16[256,2048]{1,0:T(8,128)(2,1)S(1)}, u32[]{:S(2)}, u32[]{:S(2)}) collective-permute-start(bf16[256,2048]{1,0:T(8,128)(2,1)} %dynamic-slice_bitcast_fusion), channel_id=1, source_target_pairs={{0,1},{1,0},{2,3},{3,2},{4,5},{5,4},{6,7},{7,6},{8,9},{9,8},{10,11... | collective-permute-start | bytes 3145736 | tf_op jit(solution)/shard_map/ppermute | solution.py:351
  88.6 0.7 copy-start.2
  89.3 6.4 %collective-permute-start = (bf16[2,128,256]{2,1,0:T(8,128)(2,1)S(1)}, bf16[2,128,256]{2,1,0:T(8,128)(2,1)S(1)}, u32[]{:S(2)}, u32[]{:S(2)}) collective-permute-start(bf16[2,128,256]{2,1,0:T(8,128)(2,1)S(1)} %get-tuple-element.19), channel_id=1, source_target_pairs={{0,2},{2,4},{4,6},{6,0},{1,3},{3,5},{5,7},{7,1},{8,10},{10,12},{12... | collective-permute-start | bytes 393224 | tf_op jit(solution)/shard_map/ppermute | solution.py:397
  89.6 7.3 %collective-permute-start.1 = (bf16[2,128,256]{2,1,0:T(8,128)(2,1)S(1)}, bf16[2,128,256]{2,1,0:T(8,128)(2,1)S(1)}, u32[]{:S(2)}, u32[]{:S(2)}) collective-permute-start(bf16[2,128,256]{2,1,0:T(8,128)(2,1)S(1)} %get-tuple-element.20), channel_id=1, source_target_pairs={{0,4},{2,6},{4,0},{6,2},{1,5},{3,7},{5,1},{7,3},{8,12},{10,14},{12... | collective-permute-start | bytes 393224 | tf_op jit(solution)/shard_map/ppermute | solution.py:397
  91.4 6.4 %collective-permute-start.2 = (bf16[2,128,256]{2,1,0:T(8,128)(2,1)S(1)}, bf16[2,128,256]{2,1,0:T(8,128)(2,1)S(1)}, u32[]{:S(2)}, u32[]{:S(2)}) collective-permute-start(bf16[2,128,256]{2,1,0:T(8,128)(2,1)S(1)} %get-tuple-element.21), channel_id=1, source_target_pairs={{0,6},{2,0},{4,2},{6,4},{1,7},{3,1},{5,3},{7,5},{8,14},{10,8},{12,... | collective-permute-start | bytes 393224 | tf_op jit(solution)/shard_map/ppermute | solution.py:397
  95.7 2.8 %copy-start.3 = (bf16[2,128,256]{2,1,0:T(8,128)(2,1)}, bf16[2,128,256]{2,1,0:T(8,128)(2,1)S(1)}, u32[]{:S(2)}) copy-start(bf16[2,128,256]{2,1,0:T(8,128)(2,1)S(1)} %collective-permute-done.part_1) | copy-start | bytes 393220
  96.9 1.0 copy-start.4
  97.8 0.7 copy-start.5
  100.3 3.3 %collective-permute-start.3 = (bf16[2,128,256]{2,1,0:T(8,128)(2,1)}, bf16[2,128,256]{2,1,0:T(8,128)(2,1)S(1)}, u32[]{:S(2)}, u32[]{:S(2)}) collective-permute-start(bf16[2,128,256]{2,1,0:T(8,128)(2,1)} %sum_chips.1.own), channel_id=1, source_target_pairs={{0,1},{1,0},{2,3},{3,2},{4,5},{5,4},{6,7},{7,6},{8,9},{9,8},{10,11... | collective-permute-start | bytes 393224 | tf_op jit(solution)/shard_map/ppermute | solution.py:351
  103.6 0.9 copy-start.1
  151.5 21.6 %all-to-all-start.1 = ((bf16[8,256,256]{2,1,0:T(8,128)(2,1)}), bf16[8,256,256]{2,1,0:T(8,128)(2,1)S(1)}, u32[]{:S(2)}, u32[]{:S(2)}) async-start(bf16[8,256,256]{2,1,0:T(8,128)(2,1)} %bitcast.10), calls=%async_computation.1 | async-start | bytes 2097152 | tf_op jit(solution)/shard_map/all_to_all | solution.py:347
  158.1 19.0 %collective-permute-start.5 = (bf16[8,8,16,384]{3,2,1,0:T(8,128)(2,1)S(1)}, bf16[8,8,16,384]{3,2,1,0:T(8,128)(2,1)S(1)}, u32[]{:S(2)}, u32[]{:S(2)}) collective-permute-start(bf16[8,8,16,384]{3,2,1,0:T(8,128)(2,1)S(1)} %bitcast.22), channel_id=1, source_target_pairs={{0,1},{1,0},{2,3},{3,2},{4,5},{5,4},{6,7},{7,6},{8,9},{9,8},{10,11... | collective-permute-start | bytes 2359304 | tf_op jit(solution)/shard_map/ppermute | solution.py:351

commit v3 on v2

--- a/solution.py
+++ b/solution.py
@@ -38,55 +38,130 @@
     return lax.dot_general(a, b, NT, preferred_element_type=jnp.float32)
 
 
-def pack_kernel(hidden, wq_down, wv_down, fq, fk, fv, grad, wq_up, wv_up, out, low):
-    width = fq.shape[1]
-
-    @pl.when(pl.program_id(0) == 0)
-    def _():
-        low[:, :RANK] = dot_nt(hidden[...], wq_down[...]).astype(jnp.bfloat16)
-        low[:, RANK:] = dot_nt(hidden[...], wv_down[...]).astype(jnp.bfloat16)
-
-    q_add = ADAPTER_SCALE * dot(low[:, :RANK], wq_up[...])
-    v_add = ADAPTER_SCALE * dot(low[:, RANK:], wv_up[...])
-    out[0, :, 0:width] = (fq[...].astype(jnp.float32) + q_add).astype(jnp.bfloat16)
-    out[0, :, width : 2 * width] = fk[...]
-    out[0, :, 2 * width : 3 * width] = (fv[...].astype(jnp.float32) + v_add).astype(jnp.bfloat16)
-    out[0, :, 3 * width : 4 * width] = grad[...]
-    out[0, :, 4 * width :] = low[...]
+HIDDEN_PARTS = 4
+
+
+def pack_kernel(
+    hidden, wq_down, wv_down, fq, fk, fv, grad, wq_up, wv_up, out, low,
+    hidden_v, wq_down_v, wv_down_v, fq_v, fv_v, wq_up_v, wv_up_v, q_v, v_v, low_v,
+    down_sems, hidden_sems, row_sems, through_sems, out_sems, low_sem,
+):
+    devices, rows, packed = out.shape
+    width = packed // 4
+    model = hidden.shape[1]
+    step = model // HIDDEN_PARTS
+
+    def part(index):
+        return pl.ds(index * step, step)
+
+    def columns(index):
+        return pl.ds(index * width, width)
+
+    downs = [
+        pltpu.make_async_copy(wq_down, wq_down_v, down_sems.at[0]),
+        pltpu.make_async_copy(wv_down, wv_down_v, down_sems.at[1]),
+    ]
+    hiddens = [
+        pltpu.make_async_copy(
+            hidden.at[:, part(index)], hidden_v.at[:, part(index)], hidden_sems.at[index]
+        )
+        for index in range(HIDDEN_PARTS)
+    ]
+    whole = [
+        pltpu.make_async_copy(wq_up, wq_up_v, row_sems.at[0]),
+        pltpu.make_async_copy(fq, fq_v, row_sems.at[1]),
+        pltpu.make_async_copy(wv_up, wv_up_v, row_sems.at[2]),
+        pltpu.make_async_copy(fv, fv_v, row_sems.at[3]),
+    ]
+    through = []
+    for device in range(devices):
+        for which, source in ((1, fk), (3, grad)):
+            through.append(
+                pltpu.make_async_copy(
+                    source.at[:, columns(device)],
+                    out.at[device, :, columns(which)],
+                    through_sems.at[len(through)],
+                )
+            )
+    for copy in downs + hiddens + whole + through:
+        copy.start()
+
+    for copy in downs:
+        copy.wait()
+    low_q = jnp.zeros((rows, RANK), jnp.float32)
+    low_v_ = jnp.zeros((rows, RANK), jnp.float32)
+    for index in range(HIDDEN_PARTS):
+        hiddens[index].wait()
+        low_q += dot_nt(hidden_v[:, part(index)], wq_down_v[:, part(index)])
+        low_v_ += dot_nt(hidden_v[:, part(index)], wv_down_v[:, part(index)])
+    low_v[:, :RANK] = low_q.astype(jnp.bfloat16)
+    low_v[:, RANK:] = low_v_.astype(jnp.bfloat16)
+    low_copy = pltpu.make_async_copy(low_v, low, low_sem)
+    low_copy.start()
+
+    outs = []
+    for which, (frozen, weight, ready, begin) in enumerate(
+        ((fq_v, wq_up_v, q_v, 0), (fv_v, wv_up_v, v_v, RANK))
+    ):
+        whole[2 * which].wait()
+        whole[2 * which + 1].wait()
+        for device in range(devices):
+            at = slice(device * width, (device + 1) * width)
+            added = ADAPTER_SCALE * dot(low_v[:, begin : begin + RANK], weight[:, at])
+            ready[device] = (frozen[:, at].astype(jnp.float32) + added).astype(jnp.bfloat16)
+            copy = pltpu.make_async_copy(
+                ready.at[device],
+                out.at[device, :, columns(2 * which)],
+                out_sems.at[len(outs)],
+            )
+            copy.start()
+            outs.append(copy)
+    for copy in through + outs:
+        copy.wait()
+    low_copy.wait()
 
 
 def pack(hidden, wq_down_t, wv_down_t, fq, fk, fv, grad, wq_up, wv_up, seq_size):
     rows, model = hidden.shape
-    width = fq.shape[1] // seq_size
-    whole = lambda s: pl.BlockSpec(s, lambda d: (0, 0))
-    column = lambda r: pl.BlockSpec((r, width), lambda d: (0, d))
-    packed = 4 * width + 2 * RANK
+    columns = fq.shape[1]
+    width = columns // seq_size
+    bf16 = jnp.bfloat16
+    any_space = pl.BlockSpec(memory_space=pl.ANY)
     return pl.pallas_call(
         pack_kernel,
-        grid=(seq_size,),
-        in_specs=[
-            whole((rows, model)),
-            whole((RANK, model)),
-            whole((RANK, model)),
-            column(rows),
-            column(rows),
-            column(rows),
-            column(rows),
-            column(RANK),
-            column(RANK),
+        in_specs=[any_space] * 9,
+        out_specs=[any_space] * 2,
+        out_shape=[
+            jax.ShapeDtypeStruct((seq_size, rows, 4 * width), bf16),
+            jax.ShapeDtypeStruct((rows, 2 * RANK), bf16),
         ],
-        out_specs=pl.BlockSpec((1, rows, packed), lambda d: (d, 0, 0)),
-        out_shape=jax.ShapeDtypeStruct((seq_size, rows, packed), jnp.bfloat16),
-        scratch_shapes=[pltpu.VMEM((rows, 2 * RANK), jnp.bfloat16)],
+        scratch_shapes=[
+            pltpu.VMEM((rows, model), bf16),
+            pltpu.VMEM((RANK, model), bf16),
+            pltpu.VMEM((RANK, model), bf16),
+            pltpu.VMEM((rows, columns), bf16),
+            pltpu.VMEM((rows, columns), bf16),
+            pltpu.VMEM((RANK, columns), bf16),
+            pltpu.VMEM((RANK, columns), bf16),
+            pltpu.VMEM((seq_size, rows, width), bf16),
+            pltpu.VMEM((seq_size, rows, width), bf16),
+            pltpu.VMEM((rows, 2 * RANK), bf16),
+            pltpu.SemaphoreType.DMA((2,)),
+            pltpu.SemaphoreType.DMA((HIDDEN_PARTS,)),
+            pltpu.SemaphoreType.DMA((4,)),
+            pltpu.SemaphoreType.DMA((2 * seq_size,)),
+            pltpu.SemaphoreType.DMA((2 * seq_size,)),
+            pltpu.SemaphoreType.DMA,
+        ],
         compiler_params=pltpu.CompilerParams(vmem_limit_bytes=60 << 20),
         name="pack",
     )(hidden, wq_down_t, wv_down_t, fq, fk, fv, grad, wq_up, wv_up)
 
 
 def attention_kernel(
-    meta, packed, wq_up, wv_up, out, back_0, back_1, back_2, back_3, up,
-    q_t, k_t, v_t, g_t, dq_t, dv, dv_t, returned,
+    meta, packed, wq_up, wv_up, *refs
 ):
+    out, back_0, back_1, back_2, back_3, dq_t, dv_t, q_t, k_t, v_t, g_t, dv, returned = refs[-13:]
     length = packed.shape[0]
     heads = out.shape[1] // HEAD_SIZE
     width = heads * HEAD_SIZE
@@ -172,7 +247,50 @@
             begin = pl.multiple_of((target * 2 + core) * rows, rows)
             backs[step][core] = returned[:, pl.ds(begin, rows)]
 
-    low = packed[:, 4 * width :]
+
+VMEM = pl.BlockSpec(memory_space=pltpu.VMEM)
+SMEM = pl.BlockSpec(memory_space=pltpu.SMEM)
+ANY = pl.BlockSpec(memory_space=pl.ANY)
+
+
+def attention(meta, packed, wq_up, wv_up, seq_size, after):
+    length = packed.shape[0]
+    width = packed.shape[1] // 4
+    rows = length // seq_size
+    heads = width // HEAD_SIZE
+    chips = seq_size // 2
+    wide_t = pltpu.VMEM((width, length), jnp.bfloat16)
+    back = jax.ShapeDtypeStruct((2, 2 * RANK, rows), jnp.bfloat16)
+    grad_t = jax.ShapeDtypeStruct((width, length), jnp.bfloat16)
+    return pl.pallas_call(
+        attention_kernel,
+        in_specs=[SMEM, VMEM, VMEM, VMEM] + [ANY] * len(after),
+        out_specs=[VMEM] * (3 + chips),
+        scratch_shapes=[
+            wide_t,
+            wide_t,
+            wide_t,
+            wide_t,
+            pltpu.VMEM((heads, length, HEAD_SIZE), jnp.float32),
+            pltpu.VMEM((2 * RANK, length), jnp.bfloat16),
+        ],
+        out_shape=[jax.ShapeDtypeStruct((length, width), jnp.bfloat16)]
+        + [back] * chips
+        + [grad_t, grad_t],
+        compiler_params=pltpu.CompilerParams(vmem_limit_bytes=40 << 20),
+        cost_estimate=pl.CostEstimate(
+            flops=8 << 30, bytes_accessed=16 << 20, transcendentals=4 << 20
+        ),
+        name="attention",
+    )(meta, packed, wq_up, wv_up, *after)
+
+
+def up_kernel(where, *refs):
+    chip, core = where[0], where[1]
+    *lows, dq_t, dv_t, up = refs
+    steps = len(lows) // 2
+    rows = lows[0].shape[0]
+    width = dq_t.shape[0]
     lane = lax.broadcasted_iota(jnp.int32, (width, up.shape[1]), 1)
     source = lax.broadcasted_iota(jnp.int32, (width, up.shape[1]), 0)
     mine = (source == (lane // 128) * UP_COLS + lane % UP_COLS) & (
@@ -180,69 +298,107 @@
     )
     mine = jnp.where(mine, 1.0, 0.0).astype(jnp.bfloat16)
     for part, grads in enumerate((dq_t, dv_t)):
-        up_part = (dot(grads[...], low) * ADAPTER_SCALE).T[part * RANK : (part + 1) * RANK, :]
-        up[part * RANK : (part + 1) * RANK, :] = dot(up_part.astype(jnp.bfloat16), mine).astype(
+        total = jnp.zeros((width, 2 * RANK), jnp.float32)
+        for index, low in enumerate(lows):
+            origin = lax.rem(chip + steps - index % steps, steps)
+            holder = core if index < steps else 1 - core
+            begin = pl.multiple_of((origin * 2 + holder) * rows, rows)
+            total += dot(grads[:, pl.ds(begin, rows)], low[...])
+        share = (total * ADAPTER_SCALE).T[part * RANK : (part + 1) * RANK, :]
+        up[part * RANK : (part + 1) * RANK, :] = dot(share.astype(jnp.bfloat16), mine).astype(
             jnp.bfloat16
         )
 
 
-VMEM = pl.BlockSpec(memory_space=pltpu.VMEM)
-SMEM = pl.BlockSpec(memory_space=pltpu.SMEM)
-
-
-def attention(meta, packed, wq_up, wv_up, seq_size):
-    length = packed.shape[0]
-    width = (packed.shape[1] - 2 * RANK) // 4
-    rows = length // seq_size
-    heads = width // HEAD_SIZE
-    chips = seq_size // 2
-    wide_t = pltpu.VMEM((width, length), jnp.bfloat16)
-    back = jax.ShapeDtypeStruct((2, 2 * RANK, rows), jnp.bfloat16)
-    return pl.pallas_call(
-        attention_kernel,
-        in_specs=[SMEM, VMEM, VMEM, VMEM],
-        out_specs=[VMEM] * (2 + chips),
-        scratch_shapes=[
-            wide_t,
-            wide_t,
-            wide_t,
-            wide_t,
-            wide_t,
-            pltpu.VMEM((heads, length, HEAD_SIZE), jnp.float32),
-            wide_t,
-            pltpu.VMEM((2 * RANK, length), jnp.bfloat16),
-        ],
-        out_shape=[jax.ShapeDtypeStruct((length, width), jnp.bfloat16)]
-        + [back] * chips
-        + [jax.ShapeDtypeStruct((2 * RANK, width // UP_COLS * 128), jnp.bfloat16)],
-        compiler_params=pltpu.CompilerParams(vmem_limit_bytes=40 << 20),
-        name="attention",
-    )(meta, packed, wq_up, wv_up)
-
-
-def chips_kernel(part_0, part_1, part_2, part_3, out):
-    total = part_0[...].astype(jnp.float32)
-    for part in (part_1, part_2, part_3):
-        total += part[...].astype(jnp.float32)
-    out[...] = total.astype(out.dtype)
-
-
-def sum_chips(parts):
-    return pl.pallas_call(
-        chips_kernel,
-        in_specs=[VMEM] * len(parts),
+def up_gradient(where, lows, dq_t, dv_t):
+    width = dq_t.shape[0]
+    return pl.pallas_call(
+        up_kernel,
+        in_specs=[SMEM] + [VMEM] * (len(lows) + 2),
         out_specs=VMEM,
-        out_shape=jax.ShapeDtypeStruct(parts[0].shape, parts[0].dtype),
-        name="sum_chips",
-    )(*parts)
-
-
-def down_kernel(core, own, other, hidden, hidden_other, up, out):
-    total = (own[...].astype(jnp.float32) + other[...].astype(jnp.float32)).astype(jnp.bfloat16)
-    first = core[0] == 0
-    here = jnp.where(first, total[0], total[1])
-    there = jnp.where(first, total[1], total[0])
-    grad = (dot(here, hidden[...]) + dot(there, hidden_other[...])).astype(out.dtype)
+        out_shape=jax.ShapeDtypeStruct((2 * RANK, width // UP_COLS * 128), jnp.bfloat16),
+        compiler_params=pltpu.CompilerParams(vmem_limit_bytes=24 << 20),
+        name="up_gradient",
+    )(where, *lows, dq_t, dv_t)
+
+
+def leaving_kernel(where, result, out):
+    chip, core = where[0], where[1]
+    chips, rows, _ = out.shape
+    for step in range(chips):
+        target = lax.rem(chip + step, chips)
+        begin = pl.multiple_of((target * 2 + 1 - core) * rows, rows)
+        out[step] = result[pl.ds(begin, rows), :]
+
+
+def leaving(where, result, seq_size):
+    length, width = result.shape
+    shape = (seq_size // 2, length // seq_size, width)
+    return pl.pallas_call(
+        leaving_kernel,
+        in_specs=[SMEM, VMEM],
+        out_specs=VMEM,
+        out_shape=jax.ShapeDtypeStruct(shape, result.dtype),
+        name="leaving",
+    )(where, result)
+
+
+def join_kernel(where, result, other, *refs):
+    chip, core = where[0], where[1]
+    chips, rows, width = other.shape
+    outs = refs[-chips:]
+    here = pl.multiple_of(core * width, width)
+    there = pl.multiple_of((1 - core) * width, width)
+    for step in range(chips):
+        target = lax.rem(chip + step, chips)
+        begin = pl.multiple_of((target * 2 + core) * rows, rows)
+        outs[step][:, pl.ds(here, width)] = result[pl.ds(begin, rows), :]
+        outs[step][:, pl.ds(there, width)] = other[step]
+
+
+def join(where, result, other, after):
+    chips, rows, width = other.shape
+    return pl.pallas_call(
+        join_kernel,
+        in_specs=[SMEM, VMEM, VMEM] + [ANY] * len(after),
+        out_specs=[VMEM] * chips,
+        out_shape=[jax.ShapeDtypeStruct((rows, 2 * width), other.dtype)] * chips,
+        name="join",
+    )(where, result, other, *after)
+
+
+def arrive_kernel(where, part_0, part_1, part_2, part_3, out):
+    chip = where[0]
+    parts = (part_0, part_1, part_2, part_3)
+    width = part_0.shape[1]
+    for step in range(len(parts)):
+        origin = lax.rem(chip + len(parts) - step, len(parts))
+        out[0, :, pl.ds(pl.multiple_of(origin * width, width), width)] = parts[step][...]
+
+
+def arrive(where, parts):
+    rows, width = parts[0].shape
+    return pl.pallas_call(
+        arrive_kernel,
+        in_specs=[SMEM] + [VMEM] * len(parts),
+        out_specs=VMEM,
+        out_shape=jax.ShapeDtypeStruct((1, rows, len(parts) * width), parts[0].dtype),
+        name="arrive",
+    )(where, *parts)
+
+
+def down_kernel(core, *refs):
+    *parts, hidden, hidden_other, up, out, back = refs
+
+    @pl.when(pl.program_id(0) == 0)
+    def _():
+        total = parts[0][...].astype(jnp.float32)
+        for part in parts[1:]:
+            total += part[...].astype(jnp.float32)
+        back[...] = total.astype(jnp.bfloat16)
+
+    grad = dot(back[core[0]], hidden[...]) + dot(back[1 - core[0]], hidden_other[...])
+    grad = grad.astype(out.dtype)
     for row in range(out.shape[0]):
         across = slice(row * SHARE_ROWS, (row + 1) * SHARE_ROWS)
         for column in range(out.shape[1]):
@@ -252,20 +408,20 @@
             out[row, column, :, DOWN_COLS:] = up[across, column * 128 : (column + 1) * 128]
 
 
-def down_gradient(core, own, other, hidden, hidden_other, up):
+def down_gradient(core, parts, hidden, hidden_other, up):
     rows, half = hidden_other.shape
-    steps = 4
+    steps = 2
     step = half // steps
     columns = half // DOWN_COLS
     across = 2 * RANK // SHARE_ROWS
+    shape = parts[0].shape
     return pl.pallas_call(
         down_kernel,
         grid_spec=pltpu.PrefetchScalarGridSpec(
             num_scalar_prefetch=1,
             grid=(steps,),
-            in_specs=[
-                pl.BlockSpec(own.shape, lambda i, core: (0, 0, 0)),
-                pl.BlockSpec(own.shape, lambda i, core: (0, 0, 0)),
+            in_specs=[pl.BlockSpec(shape, lambda i, core: (0, 0, 0))] * len(parts)
+            + [
                 pl.BlockSpec((rows, step), lambda i, core: (0, core[0] * steps + i)),
                 pl.BlockSpec((rows, step), lambda i, core: (0, i)),
                 pl.BlockSpec((2 * RANK, columns // steps * 128), lambda i, core: (0, i)),
@@ -274,16 +430,18 @@
                 (across, columns // steps, SHARE_ROWS, DOWN_COLS + 128),
                 lambda i, core: (0, i, 0, 0),
             ),
+            scratch_shapes=[pltpu.VMEM(shape, jnp.bfloat16)],
         ),
         out_shape=jax.ShapeDtypeStruct(
             (across, columns, SHARE_ROWS, DOWN_COLS + 128), jnp.bfloat16
         ),
         compiler_params=pltpu.CompilerParams(vmem_limit_bytes=24 << 20),
         name="down_gradient",
-    )(core, own, other, hidden, hidden_other, up)
-
-
-def share_kernel(parts, out):
+    )(core, *parts, hidden, hidden_other, up)
+
+
+def share_kernel(parts, *refs):
+    out = refs[-1]
     total = parts[0].astype(jnp.float32)
     for part in range(1, parts.shape[0]):
         total += parts[part].astype(jnp.float32)
@@ -292,14 +450,14 @@
         out[part] = total
 
 
-def sum_share(parts):
+def sum_share(parts, after):
     return pl.pallas_call(
         share_kernel,
-        in_specs=[VMEM],
+        in_specs=[VMEM] + [ANY] * len(after),
         out_specs=VMEM,
         out_shape=jax.ShapeDtypeStruct(parts.shape, parts.dtype),
         name="sum_share",
-    )(parts)
+    )(parts, *after)
 
 
 def place_kernel(core, own, other, grad_a_q, up_q, grad_a_v, up_v, wide):
@@ -370,7 +528,12 @@
     half = model // 2
     chip = lax.axis_index("y").astype(jnp.int32)
     core = lax.axis_index("core").astype(jnp.int32)
-    packed = pack(
+    where = jnp.stack([chip, core])
+
+    def to_chip(x, step):
+        return lax.ppermute(x, "y", [(c, (c + step) % chips) for c in range(chips)])
+
+    packed, low = pack(
         hidden[0],
         query_down_weight.T,
         value_down_weight.T,
@@ -386,26 +549,25 @@
     hidden_other = to_other_core(
         lax.dynamic_slice(hidden[0], (0, (1 - core) * half), (rows, half))
     )
+    lows = [low] + [to_chip(low, step) for step in range(1, chips)]
+    lows = lows + [to_other_core(low) for low in lows]
     width = frozen_queries.shape[2] // seq_size
     own_columns = (0, (chip * 2 + core) * width)
     wq_up = lax.dynamic_slice(query_up_weight, own_columns, (RANK, width))
     wv_up = lax.dynamic_slice(value_up_weight, own_columns, (RANK, width))
     meta = jnp.concatenate([document_length_list[0], chip[None]])
-    result, *backs, up = attention(meta, received, wq_up, wv_up, seq_size)
-
-    arrived = [backs[0]] + [
-        lax.ppermute(backs[step], "y", [(c, (c + step) % chips) for c in range(chips)])
-        for step in range(1, chips)
-    ]
-    back = sum_chips(arrived)
-    back_other = to_other_core(back)
-    result, back_other = lax.optimization_barrier((result, back_other))
-    down = down_gradient(core[None], back, back_other, hidden[0], hidden_other, up)
-    attended = swap(result.reshape(seq_size, rows, width), SEQ)
-    attended = attended.transpose(1, 0, 2).reshape(1, rows, seq_size * width)
+    result, *backs, dq_t, dv_t = attention(meta, received, wq_up, wv_up, seq_size, after=lows)
+
+    backs = [backs[0]] + [to_chip(backs[step], step) for step in range(1, chips)]
+    backs_other = [to_other_core(back) for back in backs]
+    up = up_gradient(where, lows, dq_t, dv_t)
+    joined = join(where, result, to_other_core(leaving(where, result, seq_size)), after=backs)
+    parts = [joined[0]] + [to_chip(joined[step], step) for step in range(1, chips)]
+    attended = arrive(where, parts)
+    down = down_gradient(core[None], backs + backs_other, hidden[0], hidden_other, up)
 
     shares = swap(down.reshape((-1,) + down.shape[2:]), PLANE)
-    shares = swap(sum_share(shares), PLANE).reshape(down.shape)
+    shares = swap(sum_share(shares, after=parts[1:]), PLANE).reshape(down.shape)
     shares_other = to_other_core(shares)
     grad_a_q, up_q, grad_a_v, up_v = place(
         core[None], shares, shares_other, model, seq_size * width

time: 181 us -> 245 us (1.35)
  Pallas kernels: 35.5 us -> 96.1 us
  blocking collectives: 43.6 us -> 22.1 us
  starting transfers between devices: 17.7 us -> 38 us
  local copies, waits for them, and re-layouts: 7.96 us -> 22 us
  waiting for transfers between devices: 74.5 us -> 63.8 us
    all_to_all x2, waiting for transfers between devices: 67.4 us -> 0.01 us  [swap(): return lax.all_to_all(x, axes, 0, 0, tiled=True)]
    pallas_call x4 -> x7, Pallas kernels: 31.3 us -> 90.4 us  [the longest x1 65.1 us: pack(): pl.pallas_call(pack_kernel, in_specs=[any_space] * 9, out_specs=[any_spac...]
    ppermute x3 -> x9, waiting for transfers between devices: 5.83 us -> 63.8 us  [to_chip(): return lax.ppermute(x, 'y', [(c, (c + step) % chips) for c in range(chips)])]
    all_to_all x2 -> x1, blocking collectives: 43.6 us -> 22.1 us  [swap(): return lax.all_to_all(x, axes, 0, 0, tiled=True)]
    unnamed x14 -> x70, local copies, waits for them, and re-layouts: 2.22 us -> 19.5 us
    ppermute x3 -> x9, starting transfers between devices: 2.68 us -> 12.2 us  [to_chip(): return lax.ppermute(x, 'y', [(c, (c + step) % chips) for c in range(chips)])]
    ppermute x3 -> x11, starting transfers between devices: 2.36 us -> 8.22 us  [to_other_core(): return lax.ppermute(x, 'core', [(0, 1), (1, 0)])]
    all_to_all x2, starting transfers between devices: 12.6 us -> 17.6 us  [swap(): return lax.all_to_all(x, axes, 0, 0, tiled=True)]
  transfers between devices with their start and end apart: 8 -> 22, of which waited for: 6 -> 5; matrix products, arithmetic and copies ran while one was open for 3% -> 1% of each run, Pallas kernels for 11% -> 11%
where the time goes in v3:
time: 245 us; the launch traced here: 244 us
  Pallas kernels  96.1 us (39%)
  waiting for transfers between devices  63.8 us (26%)
  starting transfers between devices  38 us (16%)
  blocking collectives  22.1 us (9%)
  local copies, waits for them, and re-layouts  22 us (9%)
    pallas_call x1, Pallas kernels, pack(): pl.pallas_call(pack_kernel, in_specs=[any_space] * 9, out_specs=[any_spac...  65.1 us
    ppermute x9, waiting for transfers between devices, to_chip(): return lax.ppermute(x, 'y', [(c, (c + step) % chips) for c in range(chips)])  63.8 us
    all_to_all x1, blocking collectives, swap(): return lax.all_to_all(x, axes, 0, 0, tiled=True)  22.1 us
    unnamed x70, local copies, waits for them, and re-layouts  19.5 us
    all_to_all x2, starting transfers between devices, swap(): return lax.all_to_all(x, axes, 0, 0, tiled=True)  17.6 us
    pallas_call x1, Pallas kernels, attention(): pl.pallas_call(attention_kernel, in_specs=[SMEM, VMEM, VMEM, VMEM] + [ANY...  14.7 us
    ppermute x9, starting transfers between devices, to_chip(): return lax.ppermute(x, 'y', [(c, (c + step) % chips) for c in range(chips)])  12.2 us
    ppermute x11, starting transfers between devices, to_other_core(): return lax.ppermute(x, 'core', [(0, 1), (1, 0)])  8.22 us
  transfers between devices with their start and end apart: 22, of which 5 were waited for; matrix products, arithmetic and copies ran while one was open for 1% of the time, Pallas kernels for 11%

profile of v3, /device:TPU:1, one launch (start us, length us, event | category | flops | bytes accessed | tf_op | source)
XLA Modules:
  0.0 243.6 jit_solution(13833855540792878511)
XLA Ops:
  0.6 65.1 %pack.1 = (bf16[8,256,1024]{2,1,0:T(8,128)(2,1)}, bf16[256,128]{1,0:T(8,128)(2,1)}) custom-call(bf16[256,4096]{1,0:T(8,128)(2,1)} %bitcast.17, bf16[64,4096]{1,0:T(8,128)(2,1)} %bitcast.25, bf16[64,4096]{1,0:T(8,128)(2,1)} %bitcast.26, bf16[256,2048]{1,0:T(8,128)(2,1)} %bitcast.21, bf16[256,2048]{1,0:T(8,128)(2,1)} %bitcast.22, bf16[256,2048]{1,0:T(8,128)(2,1)} %bitcast.23, ...), custom_call_target="tpu_custom_call" | custom-call | tf_op jit(solution)/shard_map/pack/pallas_call | solution.py:130
  65.7 6.1 %all-to-all-start = ((bf16[8,256,1024]{2,1,0:T(8,128)(2,1)}), bf16[8,256,1024]{2,1,0:T(8,128)(2,1)}, u32[]{:S(2)}, u32[]{:S(2)}) async-start(bf16[8,256,1024]{2,1,0:T(8,128)(2,1)} %get-tuple-element.22), calls=%async_computation | async-start | bytes 8388608 | tf_op jit(solution)/shard_map/all_to_all | solution.py:505
  71.9 1.4 collective-permute-start
  73.2 2.4 collective-permute-start.1
  75.6 1.2 collective-permute-start.2
  76.8 1.2 collective-permute-start.3
  78.0 1.1 dynamic-slice_bitcast_fusion
  79.1 1.4 constant_dynamic-slice_fusion
  80.5 41.4 %collective-permute-done.refs_1_ = bf16[256,128]{1,0:T(8,128)(2,1)S(1)} collective-permute-done((bf16[256,128]{1,0:T(8,128)(2,1)S(1)}, bf16[256,128]{1,0:T(8,128)(2,1)S(1)}, u32[]{:S(2)}, u32[]{:S(2)}) %collective-permute-start) | collective-permute-done | bytes 65568 | tf_op jit(solution)/shard_map/ppermute | solution.py:534
  121.9 0.9 collective-permute-start.4
  123.5 0.9 collective-permute-start.5
  127.2 0.8 copy-done.16
  128.1 0.8 copy-done.19
  128.9 0.8 copy-done.22
  129.8 0.8 copy-done.25
  132.1 14.7 %attention.1 = (bf16[2048,256]{1,0:T(8,128)(2,1)S(1)}, bf16[2,128,256]{2,1,0:T(8,128)(2,1)S(1)}, bf16[2,128,256]{2,1,0:T(8,128)(2,1)S(1)}, bf16[2,128,256]{2,1,0...) custom-call(s32[9]{0:T(128)S(1)} %pad_add_fusion.1.meta, ...), custom_call_target="tpu_custom_call" | custom-call | flops 8589934592 | bytes 16777216 | tf_op jit(solution)/shard_map/attention/pallas_call | solution.py:265
  146.9 1.0 copy-done.1
  147.9 1.0 copy-done.2
  148.8 1.2 collective-permute-start.9
  150.0 1.5 collective-permute-start.10
  151.5 0.8 collective-permute-start.14
  152.4 5.4 %collective-permute-done.8.refs_1_ = bf16[2,128,256]{2,1,0:T(8,128)(2,1)S(1)} collective-permute-done((bf16[2,128,256]{2,1,0:T(8,128)(2,1)S(1)}, bf16[2,128,256]{2,1,0:T(8,128)(2,1)S(1)}, u32[]{:S(2)}, u32[]{:S(2)}) %collective-permute-start.8) | collective-permute-done | bytes 131104 | tf_op jit(solution)/shard_map/ppermute | solution.py:534
  157.7 1.0 collective-permute-start.15
  160.1 2.1 leaving.1
  162.2 1.2 copy-done.3
  163.4 0.8 copy-done.8
  164.2 0.8 copy-done.10
  165.1 0.8 copy-done.12
  165.9 0.8 copy-done.14
  166.7 0.8 copy-done.17
  167.6 0.8 copy-done.20
  168.4 0.8 copy-done.23
  169.3 0.8 copy-done.26
  170.7 1.8 up_gradient.1.refs_10_
  172.5 2.9 %down_gradient.1 = bf16[8,8,16,384]{3,2,1,0:T(8,128)(2,1)} custom-call(s32[1]{0:T(128)} %bitcast.1.core, bf16[2,128,256]{2,1,0:T(8,128)(2,1)S(1)} %get-tuple-element.25.refs_0_, bf16[2,128,256]{2,1,0:T(8,128)(2,1)S(1)} %collective-permute-done.8.refs_1_, bf16[2,128,256]{2,1,0:T(8,128)(2,1)S(1)} %collective-permute-done.9.refs_2_, ...), custom_call_target="tpu_custom_call" | custom-call | tf_op jit(solution)/shard_map/down_gradient/pallas_call | solution.py:418
  175.4 11.4 %all-to-all-start.1 = ((bf16[64,16,384]{2,1,0:T(8,128)(2,1)}), bf16[64,16,384]{2,1,0:T(8,128)(2,1)S(1)}, u32[]{:S(2)}, u32[]{:S(2)}) async-start(bf16[64,16,384]{2,1,0:T(8,128)(2,1)} %bitcast.12), calls=%async_computation.1 | async-start | bytes 1572864 | tf_op jit(solution)/shard_map/all_to_all | solution.py:505
  186.9 2.4 join.1
  189.3 1.0 collective-permute-start.11
  190.3 2.4 collective-permute-start.12
  192.7 1.2 collective-permute-start.13
  193.8 10.4 %collective-permute-done.11.part_1.refs_0_ = bf16[256,512]{1,0:T(8,128)(2,1)S(1)} collective-permute-done((bf16[256,512]{1,0:T(8,128)(2,1)}, bf16[256,512]{1,0:T(8,128)(2,1)S(1)}, u32[]{:S(2)}, u32[]{:S(2)}) %collective-permute-start.11) | collective-permute-done | bytes 262176 | tf_op jit(solution)/shard_map/ppermute | solution.py:534
  204.3 5.9 %collective-permute-done.12.part_2.refs_1_ = bf16[256,512]{1,0:T(8,128)(2,1)S(1)} collective-permute-done((bf16[256,512]{1,0:T(8,128)(2,1)}, bf16[256,512]{1,0:T(8,128)(2,1)S(1)}, u32[]{:S(2)}, u32[]{:S(2)}) %collective-permute-start.12) | collective-permute-done | bytes 262176 | tf_op jit(solution)/shard_map/ppermute | solution.py:534
  210.9 0.9 copy-done.30
  211.8 2.2 sum_share.1
  214.0 22.1 %all_to_all.15 = bf16[64,16,384]{2,1,0:T(8,128)(2,1)S(1)} all-to-all(bf16[64,16,384]{2,1,0:T(8,128)(2,1)} %sum_share.1), channel_id=1, replica_groups=mesh['x'=4,'z'=4,'y'=4,'core'=2] {'x','z','y'}, dimensions={0} | all-to-all | bytes 1572864 | tf_op jit(solution)/shard_map/all_to_all | solution.py:505
  236.1 2.4 collective-permute-start.19
  238.6 2.2 arrive.1
  240.8 2.8 %place.1 = (f32[64,4096]{1,0:T(8,128)}, f32[64,2048]{1,0:T(8,128)}, f32[64,4096]{1,0:T(8,128)}, f32[64,2048]{1,0:T(8,128)}) custom-call(s32[1]{0:T(128)} %bitcast.1.core, bf16[8,8,16,384]{3,2,1,0:T(8,128)(2,1)S(1)} %bitcast.20, bf16[8,8,16,384]{3,2,1,0:T(8,128)(2,1)S(1)} %collective-permute-done.19.other), custom_call_target="tpu_custom_call" | custom-call | tf_op jit(solution)/shard_map/place/pallas_call | solution.py:493
  (80 shorter events, 7.9 us)
Async XLA Ops:
  65.7 6.2 %copy-start.7 = (bf16[256,128]{1,0:T(8,128)(2,1)S(1)}, bf16[256,128]{1,0:T(8,128)(2,1)}, u32[]{:S(2)}) copy-start(bf16[256,128]{1,0:T(8,128)(2,1)} %get-tuple-element.23.refs_0_) | copy-start | bytes 196612
  65.7 12.3 %copy-start = (bf16[1,256,4096]{2,1,0:T(8,128)(2,1)S(1)}, bf16[1,256,4096]{2,1,0:T(8,128)(2,1)}, u32[]{:S(2)}) copy-start(bf16[1,256,4096]{2,1,0:T(8,128)(2,1)} %param.10) | copy-start | bytes 6291460
  65.7 58.9 %copy-start.34 = (s32[1,8]{1,0:T(1,128)S(1)}, s32[1,8]{1,0:T(1,128)}, u32[]{:S(2)}) copy-start(s32[1,8]{1,0:T(1,128)} %param.14) | copy-start | bytes 100
  65.7 61.5 %all-to-all-start = ((bf16[8,256,1024]{2,1,0:T(8,128)(2,1)}), bf16[8,256,1024]{2,1,0:T(8,128)(2,1)}, u32[]{:S(2)}, u32[]{:S(2)}) async-start(bf16[8,256,1024]{2,1,0:T(8,128)(2,1)} %get-tuple-element.22), calls=%async_computation | async-start | bytes 8388608 | tf_op jit(solution)/shard_map/all_to_all | solution.py:505
  71.9 50.1 %collective-permute-start = (bf16[256,128]{1,0:T(8,128)(2,1)S(1)}, bf16[256,128]{1,0:T(8,128)(2,1)S(1)}, u32[]{:S(2)}, u32[]{:S(2)}) collective-permute-start(bf16[256,128]{1,0:T(8,128)(2,1)S(1)} %copy-done.7), channel_id=1, source_target_pairs={{0,2},{2,4},{4,6},{6,0},{1,3},{3,5},{5,7},{7,1},{8,10},{10,12},{12... | collective-permute-start | bytes 196616 | tf_op jit(solution)/shard_map/ppermute | solution.py:534
  73.2 50.3 %collective-permute-start.1 = (bf16[256,128]{1,0:T(8,128)(2,1)S(1)}, bf16[256,128]{1,0:T(8,128)(2,1)S(1)}, u32[]{:S(2)}, u32[]{:S(2)}) collective-permute-start(bf16[256,128]{1,0:T(8,128)(2,1)S(1)} %copy-done.7), channel_id=1, source_target_pairs={{0,4},{2,6},{4,0},{6,2},{1,5},{3,7},{5,1},{7,3},{8,12},{10,14},{12... | collective-permute-start | bytes 196616 | tf_op jit(solution)/shard_map/ppermute | solution.py:534
  75.6 48.8 %collective-permute-start.2 = (bf16[256,128]{1,0:T(8,128)(2,1)S(1)}, bf16[256,128]{1,0:T(8,128)(2,1)S(1)}, u32[]{:S(2)}, u32[]{:S(2)}) collective-permute-start(bf16[256,128]{1,0:T(8,128)(2,1)S(1)} %copy-done.7), channel_id=1, source_target_pairs={{0,6},{2,0},{4,2},{6,4},{1,7},{3,1},{5,3},{7,5},{8,14},{10,8},{12,... | collective-permute-start | bytes 196616 | tf_op jit(solution)/shard_map/ppermute | solution.py:534
  76.8 47.9 %collective-permute-start.3 = (bf16[256,128]{1,0:T(8,128)(2,1)S(1)}, bf16[256,128]{1,0:T(8,128)(2,1)S(1)}, u32[]{:S(2)}, u32[]{:S(2)}) collective-permute-start(bf16[256,128]{1,0:T(8,128)(2,1)S(1)} %copy-done.7), channel_id=1, source_target_pairs={{0,1},{1,0},{2,3},{3,2},{4,5},{5,4},{6,7},{7,6},{8,9},{9,8},{10,11... | collective-permute-start | bytes 196616 | tf_op jit(solution)/shard_map/ppermute | solution.py:509
  79.1 83.1 %collective-permute-start.18 = (bf16[256,2048]{1,0:T(8,128)(2,1)}, bf16[256,2048]{1,0:T(8,128)(2,1)}, u32[]{:S(2)}, u32[]{:S(2)}) collective-permute-start(bf16[256,2048]{1,0:T(8,128)(2,1)} %dynamic-slice_bitcast_fusion), channel_id=1, source_target_pairs={{0,1},{1,0},{2,3},{3,2},{4,5},{5,4},{6,7},{7,6},{8,9},{9,8},{10,11... | collective-permute-start | bytes 3145736 | tf_op jit(solution)/shard_map/ppermute | solution.py:509
  121.9 24.9 %copy-start.9 = (bf16[256,128]{1,0:T(8,128)(2,1)}, bf16[256,128]{1,0:T(8,128)(2,1)S(1)}, u32[]{:S(2)}) copy-start(bf16[256,128]{1,0:T(8,128)(2,1)S(1)} %collective-permute-done.refs_1_) | copy-start | bytes 196612
  121.9 3.4 %collective-permute-start.4 = (bf16[256,128]{1,0:T(8,128)(2,1)S(1)}, bf16[256,128]{1,0:T(8,128)(2,1)S(1)}, u32[]{:S(2)}, u32[]{:S(2)}) collective-permute-start(bf16[256,128]{1,0:T(8,128)(2,1)S(1)} %collective-permute-done.refs_1_), channel_id=1, source_target_pairs={{0,1},{1,0},{2,3},{3,2},{4,5},{5,4},{6,7},{7,6},{8,9},{9,8},{10,11... | collective-permute-start | bytes 196616 | tf_op jit(solution)/shard_map/ppermute | solution.py:509
  123.5 23.4 %copy-start.11 = (bf16[256,128]{1,0:T(8,128)(2,1)}, bf16[256,128]{1,0:T(8,128)(2,1)S(1)}, u32[]{:S(2)}) copy-start(bf16[256,128]{1,0:T(8,128)(2,1)S(1)} %collective-permute-done.1.refs_2_) | copy-start | bytes 196612
  123.5 2.5 %collective-permute-start.5 = (bf16[256,128]{1,0:T(8,128)(2,1)S(1)}, bf16[256,128]{1,0:T(8,128)(2,1)S(1)}, u32[]{:S(2)}, u32[]{:S(2)}) collective-permute-start(bf16[256,128]{1,0:T(8,128)(2,1)S(1)} %collective-permute-done.1.refs_2_), channel_id=1, source_target_pairs={{0,1},{1,0},{2,3},{3,2},{4,5},{5,4},{6,7},{7,6},{8,9},{9,8},{10,11... | collective-permute-start | bytes 196616 | tf_op jit(solution)/shard_map/ppermute | solution.py:509
  124.4 22.5 %copy-start.13 = (bf16[256,128]{1,0:T(8,128)(2,1)}, bf16[256,128]{1,0:T(8,128)(2,1)S(1)}, u32[]{:S(2)}) copy-start(bf16[256,128]{1,0:T(8,128)(2,1)S(1)} %collective-permute-done.2.refs_3_) | copy-start | bytes 196612
  124.4 2.2 collective-permute-start.6
  127.2 0.8 copy-start.16
  128.1 0.8 copy-start.19
  128.9 0.8 copy-start.22
  129.8 0.8 copy-start.25
  146.9 1.0 copy-start.1
  147.9 1.0 copy-start.2
  148.8 26.6 %copy-start.4 = (bf16[2,128,256]{2,1,0:T(8,128)(2,1)}, bf16[2,128,256]{2,1,0:T(8,128)(2,1)S(1)}, u32[]{:S(2)}) copy-start(bf16[2,128,256]{2,1,0:T(8,128)(2,1)S(1)} %get-tuple-element.25.refs_0_) | copy-start | bytes 393220
  148.8 8.9 %collective-permute-start.8 = (bf16[2,128,256]{2,1,0:T(8,128)(2,1)S(1)}, bf16[2,128,256]{2,1,0:T(8,128)(2,1)S(1)}, u32[]{:S(2)}, u32[]{:S(2)}) collective-permute-start(bf16[2,128,256]{2,1,0:T(8,128)(2,1)S(1)} %get-tuple-element.26), channel_id=1, source_target_pairs={{0,2},{2,4},{4,6},{6,0},{1,3},{3,5},{5,7},{7,1},{8,10},{10,12},{12... | collective-permute-start | bytes 393224 | tf_op jit(solution)/shard_map/ppermute | solution.py:534
  148.8 9.9 %collective-permute-start.9 = (bf16[2,128,256]{2,1,0:T(8,128)(2,1)S(1)}, bf16[2,128,256]{2,1,0:T(8,128)(2,1)S(1)}, u32[]{:S(2)}, u32[]{:S(2)}) collective-permute-start(bf16[2,128,256]{2,1,0:T(8,128)(2,1)S(1)} %get-tuple-element.27), channel_id=1, source_target_pairs={{0,4},{2,6},{4,0},{6,2},{1,5},{3,7},{5,1},{7,3},{8,12},{10,14},{12... | collective-permute-start | bytes 393224 | tf_op jit(solution)/shard_map/ppermute | solution.py:534
  150.0 8.9 %collective-permute-start.10 = (bf16[2,128,256]{2,1,0:T(8,128)(2,1)S(1)}, bf16[2,128,256]{2,1,0:T(8,128)(2,1)}, u32[]{:S(2)}, u32[]{:S(2)}) collective-permute-start(bf16[2,128,256]{2,1,0:T(8,128)(2,1)S(1)} %get-tuple-element.28), channel_id=1, source_target_pairs={{0,6},{2,0},{4,2},{6,4},{1,7},{3,1},{5,3},{7,5},{8,14},{10,8},{12,... | collective-permute-start | bytes 393224 | tf_op jit(solution)/shard_map/ppermute | solution.py:534
  151.5 21.0 %collective-permute-start.14 = (bf16[2,128,256]{2,1,0:T(8,128)(2,1)S(1)}, bf16[2,128,256]{2,1,0:T(8,128)(2,1)}, u32[]{:S(2)}, u32[]{:S(2)}) collective-permute-start(bf16[2,128,256]{2,1,0:T(8,128)(2,1)S(1)} %get-tuple-element.25.refs_0_), channel_id=1, source_target_pairs={{0,1},{1,0},{2,3},{3,2},{4,5},{5,4},{6,7},{7,6},{8,9},{9,8},{10,11... | collective-permute-start | bytes 393224 | tf_op jit(solution)/shard_map/ppermute | solution.py:509
  157.7 17.7 %copy-start.5 = (bf16[2,128,256]{2,1,0:T(8,128)(2,1)}, bf16[2,128,256]{2,1,0:T(8,128)(2,1)S(1)}, u32[]{:S(2)}) copy-start(bf16[2,128,256]{2,1,0:T(8,128)(2,1)S(1)} %collective-permute-done.8.refs_1_) | copy-start | bytes 393220
  157.7 14.8 %collective-permute-start.15 = (bf16[2,128,256]{2,1,0:T(8,128)(2,1)S(1)}, bf16[2,128,256]{2,1,0:T(8,128)(2,1)}, u32[]{:S(2)}, u32[]{:S(2)}) collective-permute-start(bf16[2,128,256]{2,1,0:T(8,128)(2,1)S(1)} %collective-permute-done.8.refs_1_), channel_id=1, source_target_pairs={{0,1},{1,0},{2,3},{3,2},{4,5},{5,4},{6,7},{7,6},{8,9},{9,8},{10,11... | collective-permute-start | bytes 393224 | tf_op jit(solution)/shard_map/ppermute | solution.py:509
  158.8 16.6 %copy-start.6 = (bf16[2,128,256]{2,1,0:T(8,128)(2,1)}, bf16[2,128,256]{2,1,0:T(8,128)(2,1)S(1)}, u32[]{:S(2)}) copy-start(bf16[2,128,256]{2,1,0:T(8,128)(2,1)S(1)} %collective-permute-done.9.refs_2_) | copy-start | bytes 393220
  158.8 13.7 %collective-permute-start.16 = (bf16[2,128,256]{2,1,0:T(8,128)(2,1)S(1)}, bf16[2,128,256]{2,1,0:T(8,128)(2,1)}, u32[]{:S(2)}, u32[]{:S(2)}) collective-permute-start(bf16[2,128,256]{2,1,0:T(8,128)(2,1)S(1)} %collective-permute-done.9.refs_2_), channel_id=1, source_target_pairs={{0,1},{1,0},{2,3},{3,2},{4,5},{5,4},{6,7},{7,6},{8,9},{9,8},{10,11... | collective-permute-start | bytes 393224 | tf_op jit(solution)/shard_map/ppermute | solution.py:509
  158.9 13.6 %collective-permute-start.17 = (bf16[2,128,256]{2,1,0:T(8,128)(2,1)}, bf16[2,128,256]{2,1,0:T(8,128)(2,1)}, u32[]{:S(2)}, u32[]{:S(2)}) collective-permute-start(bf16[2,128,256]{2,1,0:T(8,128)(2,1)} %collective-permute-done.10.refs_3_), channel_id=1, source_target_pairs={{0,1},{1,0},{2,3},{3,2},{4,5},{5,4},{6,7},{7,6},{8,9},{9,8},{10,11... | collective-permute-start | bytes 393224 | tf_op jit(solution)/shard_map/ppermute | solution.py:509
  162.2 24.7 %collective-permute-start.7 = (bf16[4,256,256]{2,1,0:T(8,128)(2,1)}, bf16[4,256,256]{2,1,0:T(8,128)(2,1)}, u32[]{:S(2)}, u32[]{:S(2)}) collective-permute-start(bf16[4,256,256]{2,1,0:T(8,128)(2,1)} %leaving.1), channel_id=1, source_target_pairs={{0,1},{1,0},{2,3},{3,2},{4,5},{5,4},{6,7},{7,6},{8,9},{9,8},{10,11... | collective-permute-start | bytes 1572872 | tf_op jit(solution)/shard_map/ppermute | solution.py:509
  162.2 1.2 copy-start.3
  163.4 0.8 copy-start.8
  164.2 0.8 copy-start.10
  165.1 0.8 copy-start.12
  165.9 0.8 copy-start.14
  166.7 0.8 copy-start.17
  167.6 0.8 copy-start.20
  168.4 0.8 copy-start.23
  169.3 0.8 copy-start.26
  175.4 34.7 %all-to-all-start.1 = ((bf16[64,16,384]{2,1,0:T(8,128)(2,1)}), bf16[64,16,384]{2,1,0:T(8,128)(2,1)S(1)}, u32[]{:S(2)}, u32[]{:S(2)}) async-start(bf16[64,16,384]{2,1,0:T(8,128)(2,1)} %bitcast.12), calls=%async_computation.1 | async-start | bytes 1572864 | tf_op jit(solution)/shard_map/all_to_all | solution.py:505
  189.3 15.0 %collective-permute-start.11 = (bf16[256,512]{1,0:T(8,128)(2,1)}, bf16[256,512]{1,0:T(8,128)(2,1)S(1)}, u32[]{:S(2)}, u32[]{:S(2)}) collective-permute-start(bf16[256,512]{1,0:T(8,128)(2,1)} %get-tuple-element.30), channel_id=1, source_target_pairs={{0,2},{2,4},{4,6},{6,0},{1,3},{3,5},{5,7},{7,1},{8,10},{10,12},{12... | collective-permute-start | bytes 786440 | tf_op jit(solution)/shard_map/ppermute | solution.py:534
  190.3 19.9 %collective-permute-start.12 = (bf16[256,512]{1,0:T(8,128)(2,1)}, bf16[256,512]{1,0:T(8,128)(2,1)S(1)}, u32[]{:S(2)}, u32[]{:S(2)}) collective-permute-start(bf16[256,512]{1,0:T(8,128)(2,1)} %get-tuple-element.31), channel_id=1, source_target_pairs={{0,4},{2,6},{4,0},{6,2},{1,5},{3,7},{5,1},{7,3},{8,12},{10,14},{12... | collective-permute-start | bytes 786440 | tf_op jit(solution)/shard_map/ppermute | solution.py:534
  192.7 17.5 %collective-permute-start.13 = (bf16[256,512]{1,0:T(8,128)(2,1)}, bf16[256,512]{1,0:T(8,128)(2,1)S(1)}, u32[]{:S(2)}, u32[]{:S(2)}) collective-permute-start(bf16[256,512]{1,0:T(8,128)(2,1)} %get-tuple-element.32), channel_id=1, source_target_pairs={{0,6},{2,0},{4,2},{6,4},{1,7},{3,1},{5,3},{7,5},{8,14},{10,8},{12,... | collective-permute-start | bytes 786440 | tf_op jit(solution)/shard_map/ppermute | solution.py:534
  204.3 5.9 %copy-start.31 = (bf16[256,512]{1,0:T(8,128)(2,1)}, bf16[256,512]{1,0:T(8,128)(2,1)S(1)}, u32[]{:S(2)}) copy-start(bf16[256,512]{1,0:T(8,128)(2,1)S(1)} %collective-permute-done.11.part_1.refs_0_) | copy-start | bytes 786436
  210.9 0.9 copy-start.30
  236.1 4.7 %collective-permute-start.19 = (bf16[8,8,16,384]{3,2,1,0:T(8,128)(2,1)S(1)}, bf16[8,8,16,384]{3,2,1,0:T(8,128)(2,1)S(1)}, u32[]{:S(2)}, u32[]{:S(2)}) collective-permute-start(bf16[8,8,16,384]{3,2,1,0:T(8,128)(2,1)S(1)} %bitcast.19), channel_id=1, source_target_pairs={{0,1},{1,0},{2,3},{3,2},{4,5},{5,4},{6,7},{7,6},{8,9},{9,8},{10,11... | collective-permute-start | bytes 2359304 | tf_op jit(solution)/shard_map/ppermute | solution.py:509
  (9 other events, 6.1 us)

commit v4 on v3

--- a/solution.py
+++ b/solution.py
@@ -39,12 +39,17 @@
 
 
 HIDDEN_PARTS = 4
+PACK_VMEM = 56 << 20
+SMALL_VMEM = 8 << 20
+VMEM = pl.BlockSpec(memory_space=pltpu.VMEM)
+SMEM = pl.BlockSpec(memory_space=pltpu.SMEM)
+ANY = pl.BlockSpec(memory_space=pl.ANY)
 
 
 def pack_kernel(
     hidden, wq_down, wv_down, fq, fk, fv, grad, wq_up, wv_up, out, low,
-    hidden_v, wq_down_v, wv_down_v, fq_v, fv_v, wq_up_v, wv_up_v, q_v, v_v, low_v,
-    down_sems, hidden_sems, row_sems, through_sems, out_sems, low_sem,
+    hidden_v, wq_down_v, wv_down_v, fq_v, fv_v, wq_up_v, wv_up_v, out_v,
+    down_sems, hidden_sems, row_sems, through_sems, out_sems,
 ):
     devices, rows, packed = out.shape
     width = packed // 4
@@ -79,7 +84,7 @@
             through.append(
                 pltpu.make_async_copy(
                     source.at[:, columns(device)],
-                    out.at[device, :, columns(which)],
+                    out_v.at[device, :, columns(which)],
                     through_sems.at[len(through)],
                 )
             )
@@ -89,36 +94,32 @@
     for copy in downs:
         copy.wait()
     low_q = jnp.zeros((rows, RANK), jnp.float32)
-    low_v_ = jnp.zeros((rows, RANK), jnp.float32)
+    low_v = jnp.zeros((rows, RANK), jnp.float32)
     for index in range(HIDDEN_PARTS):
         hiddens[index].wait()
         low_q += dot_nt(hidden_v[:, part(index)], wq_down_v[:, part(index)])
-        low_v_ += dot_nt(hidden_v[:, part(index)], wv_down_v[:, part(index)])
-    low_v[:, :RANK] = low_q.astype(jnp.bfloat16)
-    low_v[:, RANK:] = low_v_.astype(jnp.bfloat16)
-    low_copy = pltpu.make_async_copy(low_v, low, low_sem)
-    low_copy.start()
-
+        low_v += dot_nt(hidden_v[:, part(index)], wv_down_v[:, part(index)])
+    low[:, :RANK] = low_q.astype(jnp.bfloat16)
+    low[:, RANK:] = low_v.astype(jnp.bfloat16)
+
+    for copy in whole:
+        copy.wait()
     outs = []
-    for which, (frozen, weight, ready, begin) in enumerate(
-        ((fq_v, wq_up_v, q_v, 0), (fv_v, wv_up_v, v_v, RANK))
-    ):
-        whole[2 * which].wait()
-        whole[2 * which + 1].wait()
-        for device in range(devices):
-            at = slice(device * width, (device + 1) * width)
-            added = ADAPTER_SCALE * dot(low_v[:, begin : begin + RANK], weight[:, at])
-            ready[device] = (frozen[:, at].astype(jnp.float32) + added).astype(jnp.bfloat16)
-            copy = pltpu.make_async_copy(
-                ready.at[device],
-                out.at[device, :, columns(2 * which)],
-                out_sems.at[len(outs)],
-            )
-            copy.start()
-            outs.append(copy)
-    for copy in through + outs:
+    for device in range(devices):
+        at = slice(device * width, (device + 1) * width)
+        for which, (frozen, weight, begin) in enumerate(
+            ((fq_v, wq_up_v, 0), (fv_v, wv_up_v, RANK))
+        ):
+            added = ADAPTER_SCALE * dot(low[:, begin : begin + RANK], weight[:, at])
+            out_v[device, :, 2 * which * width : (2 * which + 1) * width] = (
+                frozen[:, at].astype(jnp.float32) + added
+            ).astype(jnp.bfloat16)
+        through[2 * device].wait()
+        through[2 * device + 1].wait()
+        outs.append(pltpu.make_async_copy(out_v.at[device], out.at[device], out_sems.at[device]))
+        outs[-1].start()
+    for copy in outs:
         copy.wait()
-    low_copy.wait()
 
 
 def pack(hidden, wq_down_t, wv_down_t, fq, fk, fv, grad, wq_up, wv_up, seq_size):
@@ -126,11 +127,10 @@
     columns = fq.shape[1]
     width = columns // seq_size
     bf16 = jnp.bfloat16
-    any_space = pl.BlockSpec(memory_space=pl.ANY)
     return pl.pallas_call(
         pack_kernel,
-        in_specs=[any_space] * 9,
-        out_specs=[any_space] * 2,
+        in_specs=[ANY] * 9,
+        out_specs=[ANY, VMEM],
         out_shape=[
             jax.ShapeDtypeStruct((seq_size, rows, 4 * width), bf16),
             jax.ShapeDtypeStruct((rows, 2 * RANK), bf16),
@@ -143,17 +143,14 @@
             pltpu.VMEM((rows, columns), bf16),
             pltpu.VMEM((RANK, columns), bf16),
             pltpu.VMEM((RANK, columns), bf16),
-            pltpu.VMEM((seq_size, rows, width), bf16),
-            pltpu.VMEM((seq_size, rows, width), bf16),
-            pltpu.VMEM((rows, 2 * RANK), bf16),
+            pltpu.VMEM((seq_size, rows, 4 * width), bf16),
             pltpu.SemaphoreType.DMA((2,)),
             pltpu.SemaphoreType.DMA((HIDDEN_PARTS,)),
             pltpu.SemaphoreType.DMA((4,)),
             pltpu.SemaphoreType.DMA((2 * seq_size,)),
-            pltpu.SemaphoreType.DMA((2 * seq_size,)),
-            pltpu.SemaphoreType.DMA,
+            pltpu.SemaphoreType.DMA((seq_size,)),
         ],
-        compiler_params=pltpu.CompilerParams(vmem_limit_bytes=60 << 20),
+        compiler_params=pltpu.CompilerParams(vmem_limit_bytes=PACK_VMEM),
         name="pack",
     )(hidden, wq_down_t, wv_down_t, fq, fk, fv, grad, wq_up, wv_up)
 
@@ -161,12 +158,14 @@
 def attention_kernel(
     meta, packed, wq_up, wv_up, *refs
 ):
-    out, back_0, back_1, back_2, back_3, dq_t, dv_t, q_t, k_t, v_t, g_t, dv, returned = refs[-13:]
+    out, leaving, back_0, back_1, back_2, back_3, dq_t, dv_t, q_t, k_t, v_t, g_t, dv, returned = (
+        refs[-14:]
+    )
     length = packed.shape[0]
     heads = out.shape[1] // HEAD_SIZE
     width = heads * HEAD_SIZE
     blocks = length // TILE
-    chip = meta[NDOC]
+    chip, core = meta[NDOC], meta[NDOC + 1]
     span = [slice(head * HEAD_SIZE, (head + 1) * HEAD_SIZE) for head in range(heads)]
 
     def columns(which, head):
@@ -243,14 +242,11 @@
     rows = back_0.shape[2]
     for step in range(len(backs)):
         target = lax.rem(chip + step, len(backs))
-        for core in range(2):
-            begin = pl.multiple_of((target * 2 + core) * rows, rows)
-            backs[step][core] = returned[:, pl.ds(begin, rows)]
-
-
-VMEM = pl.BlockSpec(memory_space=pltpu.VMEM)
-SMEM = pl.BlockSpec(memory_space=pltpu.SMEM)
-ANY = pl.BlockSpec(memory_space=pl.ANY)
+        for holder in range(2):
+            begin = pl.multiple_of((target * 2 + holder) * rows, rows)
+            backs[step][holder] = returned[:, pl.ds(begin, rows)]
+        begin = pl.multiple_of((target * 2 + 1 - core) * rows, rows)
+        leaving[step] = out[pl.ds(begin, rows), :]
 
 
 def attention(meta, packed, wq_up, wv_up, seq_size, after):
@@ -264,8 +260,8 @@
     grad_t = jax.ShapeDtypeStruct((width, length), jnp.bfloat16)
     return pl.pallas_call(
         attention_kernel,
-        in_specs=[SMEM, VMEM, VMEM, VMEM] + [ANY] * len(after),
-        out_specs=[VMEM] * (3 + chips),
+        in_specs=[SMEM, VMEM, VMEM, VMEM] + [VMEM] * len(after),
+        out_specs=[VMEM] * (4 + chips),
         scratch_shapes=[
             wide_t,
             wide_t,
@@ -274,7 +270,10 @@
             pltpu.VMEM((heads, length, HEAD_SIZE), jnp.float32),
             pltpu.VMEM((2 * RANK, length), jnp.bfloat16),
         ],
-        out_shape=[jax.ShapeDtypeStruct((length, width), jnp.bfloat16)]
+        out_shape=[
+            jax.ShapeDtypeStruct((length, width), jnp.bfloat16),
+            jax.ShapeDtypeStruct((chips, rows, width), jnp.bfloat16),
+        ]
         + [back] * chips
         + [grad_t, grad_t],
         compiler_params=pltpu.CompilerParams(vmem_limit_bytes=40 << 20),
@@ -322,31 +321,9 @@
     )(where, *lows, dq_t, dv_t)
 
 
-def leaving_kernel(where, result, out):
-    chip, core = where[0], where[1]
-    chips, rows, _ = out.shape
-    for step in range(chips):
-        target = lax.rem(chip + step, chips)
-        begin = pl.multiple_of((target * 2 + 1 - core) * rows, rows)
-        out[step] = result[pl.ds(begin, rows), :]
-
-
-def leaving(where, result, seq_size):
-    length, width = result.shape
-    shape = (seq_size // 2, length // seq_size, width)
-    return pl.pallas_call(
-        leaving_kernel,
-        in_specs=[SMEM, VMEM],
-        out_specs=VMEM,
-        out_shape=jax.ShapeDtypeStruct(shape, result.dtype),
-        name="leaving",
-    )(where, result)
-
-
-def join_kernel(where, result, other, *refs):
+def join_kernel(where, result, other, *outs):
     chip, core = where[0], where[1]
     chips, rows, width = other.shape
-    outs = refs[-chips:]
     here = pl.multiple_of(core * width, width)
     there = pl.multiple_of((1 - core) * width, width)
     for step in range(chips):
@@ -356,15 +333,16 @@
         outs[step][:, pl.ds(there, width)] = other[step]
 
 
-def join(where, result, other, after):
+def join(where, result, other):
     chips, rows, width = other.shape
     return pl.pallas_call(
         join_kernel,
-        in_specs=[SMEM, VMEM, VMEM] + [ANY] * len(after),
+        in_specs=[SMEM, VMEM, VMEM],
         out_specs=[VMEM] * chips,
         out_shape=[jax.ShapeDtypeStruct((rows, 2 * width), other.dtype)] * chips,
+        compiler_params=pltpu.CompilerParams(vmem_limit_bytes=SMALL_VMEM),
         name="join",
-    )(where, result, other, *after)
+    )(where, result, other)
 
 
 def arrive_kernel(where, part_0, part_1, part_2, part_3, out):
@@ -383,12 +361,14 @@
         in_specs=[SMEM] + [VMEM] * len(parts),
         out_specs=VMEM,
         out_shape=jax.ShapeDtypeStruct((1, rows, len(parts) * width), parts[0].dtype),
+        compiler_params=pltpu.CompilerParams(vmem_limit_bytes=SMALL_VMEM),
         name="arrive",
     )(where, *parts)
 
 
 def down_kernel(core, *refs):
-    *parts, hidden, hidden_other, up, out, back = refs
+    parts, (hidden, hidden_other, up) = refs[:8], refs[8:11]
+    out, back = refs[-2:]
 
     @pl.when(pl.program_id(0) == 0)
     def _():
@@ -408,7 +388,7 @@
             out[row, column, :, DOWN_COLS:] = up[across, column * 128 : (column + 1) * 128]
 
 
-def down_gradient(core, parts, hidden, hidden_other, up):
+def down_gradient(core, parts, hidden, hidden_other, up, after):
     rows, half = hidden_other.shape
     steps = 2
     step = half // steps
@@ -425,7 +405,8 @@
                 pl.BlockSpec((rows, step), lambda i, core: (0, core[0] * steps + i)),
                 pl.BlockSpec((rows, step), lambda i, core: (0, i)),
                 pl.BlockSpec((2 * RANK, columns // steps * 128), lambda i, core: (0, i)),
-            ],
+            ]
+            + [VMEM] * len(after),
             out_specs=pl.BlockSpec(
                 (across, columns // steps, SHARE_ROWS, DOWN_COLS + 128),
                 lambda i, core: (0, i, 0, 0),
@@ -437,7 +418,7 @@
         ),
         compiler_params=pltpu.CompilerParams(vmem_limit_bytes=24 << 20),
         name="down_gradient",
-    )(core, *parts, hidden, hidden_other, up)
+    )(core, *parts, hidden, hidden_other, up, *after)
 
 
 def share_kernel(parts, *refs):
@@ -453,9 +434,10 @@
 def sum_share(parts, after):
     return pl.pallas_call(
         share_kernel,
-        in_specs=[VMEM] + [ANY] * len(after),
+        in_specs=[VMEM] + [VMEM] * len(after),
         out_specs=VMEM,
         out_shape=jax.ShapeDtypeStruct(parts.shape, parts.dtype),
+        compiler_params=pltpu.CompilerParams(vmem_limit_bytes=SMALL_VMEM),
         name="sum_share",
     )(parts, *after)
 
@@ -555,16 +537,18 @@
     own_columns = (0, (chip * 2 + core) * width)
     wq_up = lax.dynamic_slice(query_up_weight, own_columns, (RANK, width))
     wv_up = lax.dynamic_slice(value_up_weight, own_columns, (RANK, width))
-    meta = jnp.concatenate([document_length_list[0], chip[None]])
-    result, *backs, dq_t, dv_t = attention(meta, received, wq_up, wv_up, seq_size, after=lows)
+    meta = jnp.concatenate([document_length_list[0], where])
+    result, leaving, *backs, dq_t, dv_t = attention(
+        meta, received, wq_up, wv_up, seq_size, after=lows[1:chips]
+    )
 
     backs = [backs[0]] + [to_chip(backs[step], step) for step in range(1, chips)]
     backs_other = [to_other_core(back) for back in backs]
     up = up_gradient(where, lows, dq_t, dv_t)
-    joined = join(where, result, to_other_core(leaving(where, result, seq_size)), after=backs)
+    joined = join(where, result, to_other_core(leaving))
     parts = [joined[0]] + [to_chip(joined[step], step) for step in range(1, chips)]
     attended = arrive(where, parts)
-    down = down_gradient(core[None], backs + backs_other, hidden[0], hidden_other, up)
+    down = down_gradient(core[None], backs + backs_other, hidden[0], hidden_other, up, after=joined)
 
     shares = swap(down.reshape((-1,) + down.shape[2:]), PLANE)
     shares = swap(sum_share(shares, after=parts[1:]), PLANE).reshape(down.shape)

time: 245 us -> 164 us (0.67)
  Pallas kernels: 96.1 us -> 32.8 us
  local copies, waits for them, and re-layouts: 22 us -> 1.85 us
  waiting for transfers between devices: 63.8 us -> 68.7 us
    pallas_call x5 -> x4, Pallas kernels: 86.4 us -> 24.9 us  [the longest x1 16 us: attention(): pl.pallas_call(attention_kernel, in_specs=[SMEM, VMEM, VMEM, VMEM] + [VME...]
    unnamed x70 -> x12, local copies, waits for them, and re-layouts: 19.5 us -> 0.04 us
    ppermute x9, waiting for transfers between devices: 63.8 us -> 67.3 us  [to_chip(): return lax.ppermute(x, 'y', [(c, (c + step) % chips) for c in range(chips)])]
  transfers between devices with their start and end apart: 22 -> 22, of which waited for: 5 -> 7; matrix products, arithmetic and copies ran while one was open for 1% -> 1% of each run, Pallas kernels for 11% -> 12%
where the time goes in v4:
time: 164 us; the launch traced here: 163 us
  waiting for transfers between devices  68.7 us (42%)
  starting transfers between devices  36.7 us (22%)
  Pallas kernels  32.8 us (20%)
  blocking collectives  22.5 us (14%)
  local copies, waits for them, and re-layouts  1.85 us (1%)
    ppermute x9, waiting for transfers between devices, to_chip(): return lax.ppermute(x, 'y', [(c, (c + step) % chips) for c in range(chips)])  67.3 us
    all_to_all x1, blocking collectives, swap(): return lax.all_to_all(x, axes, 0, 0, tiled=True)  22.5 us
    all_to_all x2, starting transfers between devices, swap(): return lax.all_to_all(x, axes, 0, 0, tiled=True)  16.4 us
    pallas_call x1, Pallas kernels, attention(): pl.pallas_call(attention_kernel, in_specs=[SMEM, VMEM, VMEM, VMEM] + [VME...  16 us
    ppermute x9, starting transfers between devices, to_chip(): return lax.ppermute(x, 'y', [(c, (c + step) % chips) for c in range(chips)])  12.6 us
    pallas_call x1, Pallas kernels, pack(): pl.pallas_call(pack_kernel, in_specs=[ANY] * 9, out_specs=[ANY, VMEM], ou...  8.1 us
    ppermute x11, starting transfers between devices, to_other_core(): return lax.ppermute(x, 'core', [(0, 1), (1, 0)])  7.7 us
  transfers between devices with their start and end apart: 22, of which 7 were waited for; matrix products, arithmetic and copies ran while one was open for 1% of the time, Pallas kernels for 12%

profile of v4, /device:TPU:1, one launch (start us, length us, event | category | flops | bytes accessed | tf_op | source)
XLA Modules:
  0.0 163.4 jit_solution(1434463460206099825)
XLA Ops:
  0.6 8.1 %pack.1 = (bf16[8,256,1024]{2,1,0:T(8,128)(2,1)}, bf16[256,128]{1,0:T(8,128)(2,1)}) custom-call(bf16[256,4096]{1,0:T(8,128)(2,1)} %bitcast.17, bf16[64,4096]{1,0:T(8,128)(2,1)} %bitcast.25, bf16[64,4096]{1,0:T(8,128)(2,1)} %bitcast.26, bf16[256,2048]{1,0:T(8,128)(2,1)} %bitcast.21, bf16[256,2048]{1,0:T(8,128)(2,1)} %bitcast.22, bf16[256,2048]{1,0:T(8,128)(2,1)} %bitcast.23, ...), custom_call_target="tpu_custom_call" | custom-call | tf_op jit(solution)/shard_map/pack/pallas_call | solution.py:130
  8.7 0.0 copy-start.4
  8.8 0.0 copy-start
  8.8 0.0 copy-start.5
  8.8 6.1 %all-to-all-start = ((bf16[8,256,1024]{2,1,0:T(8,128)(2,1)}), bf16[8,256,1024]{2,1,0:T(8,128)(2,1)}, u32[]{:S(2)}, u32[]{:S(2)}) async-start(bf16[8,256,1024]{2,1,0:T(8,128)(2,1)} %get-tuple-element.23), calls=%async_computation | async-start | bytes 8388608 | tf_op jit(solution)/shard_map/all_to_all | solution.py:487
  14.9 1.4 collective-permute-start
  16.3 2.4 %collective-permute-start.1 = (bf16[256,128]{1,0:T(8,128)(2,1)S(1)}, bf16[256,128]{1,0:T(8,128)(2,1)S(1)}, u32[]{:S(2)}, u32[]{:S(2)}) collective-permute-start(bf16[256,128]{1,0:T(8,128)(2,1)S(1)} %copy-done.4), channel_id=1, source_target_pairs={{0,4},{2,6},{4,0},{6,2},{1,5},{3,7},{5,1},{7,3},{8,12},{10,14},{12... | collective-permute-start | bytes 196616 | tf_op jit(solution)/shard_map/ppermute | solution.py:516
  18.7 1.2 collective-permute-start.2
  19.9 1.0 dynamic-slice_bitcast_fusion
  20.9 1.2 collective-permute-start.14
  22.1 0.8 constant_dynamic-slice_fusion
  22.9 0.1 pad_add_fusion.1.meta
  23.0 42.0 %collective-permute-done.refs_0_.refs_1_ = bf16[256,128]{1,0:T(8,128)(2,1)S(1)} collective-permute-done((bf16[256,128]{1,0:T(8,128)(2,1)S(1)}, bf16[256,128]{1,0:T(8,128)(2,1)S(1)}, u32[]{:S(2)}, u32[]{:S(2)}) %collective-permute-start) | collective-permute-done | bytes 65568 | tf_op jit(solution)/shard_map/ppermute | solution.py:516
  65.0 1.6 collective-permute-done.1.refs_1_.refs_2_
  66.6 0.0 collective-permute-done.2.refs_2_.refs_3_
  66.6 16.0 %attention.1 = (bf16[2048,256]{1,0:T(8,128)(2,1)S(1)}, bf16[4,256,256]{2,1,0:T(8,128)(2,1)S(1)}, bf16[2,128,256]{2,1,0:T(8,128)(2,1)S(1)}, bf16[2,128,256]{2,1,0...) custom-call(s32[10]{0:T(128)S(1)} %pad_add_fusion.1.meta, ...), custom_call_target="tpu_custom_call" | custom-call | flops 8589934592 | bytes 16777216 | tf_op jit(solution)/shard_map/attention/pallas_call | solution.py:261
  82.5 1.0 collective-permute-start.3
  83.5 0.1 collective-permute-start.15
  83.6 0.4 collective-permute-start.16
  84.0 0.1 collective-permute-start.17
  84.1 1.0 collective-permute-done.15.refs_4_
  85.1 0.4 collective-permute-start.18
  85.5 1.1 collective-permute-start.8
  86.6 1.8 %collective-permute-start.9 = (bf16[2,128,256]{2,1,0:T(8,128)(2,1)S(1)}, bf16[2,128,256]{2,1,0:T(8,128)(2,1)S(1)}, u32[]{:S(2)}, u32[]{:S(2)}) collective-permute-start(bf16[2,128,256]{2,1,0:T(8,128)(2,1)S(1)} %get-tuple-element.34), channel_id=1, source_target_pairs={{0,6},{2,0},{4,2},{6,4},{1,7},{3,1},{5,3},{7,5},{8,14},{10,8},{12,... | collective-permute-start | bytes 393224 | tf_op jit(solution)/shard_map/ppermute | solution.py:516
  88.5 6.0 %collective-permute-done.7.refs_1_ = bf16[2,128,256]{2,1,0:T(8,128)(2,1)S(1)} collective-permute-done((bf16[2,128,256]{2,1,0:T(8,128)(2,1)S(1)}, bf16[2,128,256]{2,1,0:T(8,128)(2,1)S(1)}, u32[]{:S(2)}, u32[]{:S(2)}) %collective-permute-start.7) | collective-permute-done | bytes 131104 | tf_op jit(solution)/shard_map/ppermute | solution.py:516
  94.5 1.0 collective-permute-start.10
  95.4 0.0 collective-permute-start.11
  95.4 0.6 collective-permute-start.12
  96.1 0.2 collective-permute-start.13
  96.3 0.1 pad_add_fusion.where
  96.4 1.8 %up_gradient.1.refs_10_ = bf16[128,1024]{1,0:T(8,128)(2,1)S(1)} custom-call(s32[2]{0:T(128)S(1)} %pad_add_fusion.where, bf16[256,128]{1,0:T(8,128)(2,1)S(1)} %copy-done.4, bf16[256,128]{1,0:T(8,128)(2,1)S(1)} %collective-permute-done.refs_0_.refs_1_, bf16[256,128]{1,0:T(8,128)(2,1)S(1)} %collective-permute-done.1.refs_1_.refs_2_, ...), custom_call_target="tpu_custom_call" | custom-call | tf_op jit(solution)/shard_map/up_gradient/pallas_call | solution.py:314
  98.1 0.6 join.1
  98.8 0.0 copy-start.1
  98.8 0.0 copy-start.2
  98.8 0.0 copy-start.3
  98.9 1.8 %down_gradient.1 = bf16[8,8,16,384]{3,2,1,0:T(8,128)(2,1)} custom-call(s32[1]{0:T(128)} %bitcast.1.core, bf16[2,128,256]{2,1,0:T(8,128)(2,1)S(1)} %get-tuple-element.31.refs_0_, bf16[2,128,256]{2,1,0:T(8,128)(2,1)S(1)} %collective-permute-done.7.refs_1_, bf16[2,128,256]{2,1,0:T(8,128)(2,1)S(1)} %collective-permute-done.8.refs_2_, ...), custom_call_target="tpu_custom_call" | custom-call | tf_op jit(solution)/shard_map/down_gradient/pallas_call | solution.py:398
  100.7 10.3 %all-to-all-start.1 = ((bf16[64,16,384]{2,1,0:T(8,128)(2,1)}), bf16[64,16,384]{2,1,0:T(8,128)(2,1)S(1)}, u32[]{:S(2)}, u32[]{:S(2)}) async-start(bf16[64,16,384]{2,1,0:T(8,128)(2,1)} %bitcast.12), calls=%async_computation.1 | async-start | bytes 1572864 | tf_op jit(solution)/shard_map/all_to_all | solution.py:487
  111.0 1.1 collective-permute-start.4
  112.1 2.4 %collective-permute-start.5 = (bf16[256,512]{1,0:T(8,128)(2,1)}, bf16[256,512]{1,0:T(8,128)(2,1)S(1)}, u32[]{:S(2)}, u32[]{:S(2)}) collective-permute-start(bf16[256,512]{1,0:T(8,128)(2,1)} %copy-done.2), channel_id=1, source_target_pairs={{0,4},{2,6},{4,0},{6,2},{1,5},{3,7},{5,1},{7,3},{8,12},{10,14},{12... | collective-permute-start | bytes 786440 | tf_op jit(solution)/shard_map/ppermute | solution.py:516
  114.5 1.2 collective-permute-start.6
  115.6 12.3 %collective-permute-done.4.part_1.refs_0_ = bf16[256,512]{1,0:T(8,128)(2,1)S(1)} collective-permute-done((bf16[256,512]{1,0:T(8,128)(2,1)}, bf16[256,512]{1,0:T(8,128)(2,1)S(1)}, u32[]{:S(2)}, u32[]{:S(2)}) %collective-permute-start.4) | collective-permute-done | bytes 262176 | tf_op jit(solution)/shard_map/ppermute | solution.py:516
  128.0 5.3 %collective-permute-done.5.part_2.refs_1_ = bf16[256,512]{1,0:T(8,128)(2,1)S(1)} collective-permute-done((bf16[256,512]{1,0:T(8,128)(2,1)}, bf16[256,512]{1,0:T(8,128)(2,1)S(1)}, u32[]{:S(2)}, u32[]{:S(2)}) %collective-permute-start.5) | collective-permute-done | bytes 262176 | tf_op jit(solution)/shard_map/ppermute | solution.py:516
  133.3 0.2 sum_share.1
  133.5 22.5 %all_to_all.15 = bf16[64,16,384]{2,1,0:T(8,128)(2,1)S(1)} all-to-all(bf16[64,16,384]{2,1,0:T(8,128)(2,1)S(1)} %sum_share.1), channel_id=1, replica_groups=mesh['x'=4,'z'=4,'y'=4,'core'=2] {'x','z','y'}, dimensions={0} | all-to-all | bytes 1572864 | tf_op jit(solution)/shard_map/all_to_all | solution.py:487
  156.0 2.7 %collective-permute-start.19 = (bf16[8,8,16,384]{3,2,1,0:T(8,128)(2,1)S(1)}, bf16[8,8,16,384]{3,2,1,0:T(8,128)(2,1)S(1)}, u32[]{:S(2)}, u32[]{:S(2)}) collective-permute-start(bf16[8,8,16,384]{3,2,1,0:T(8,128)(2,1)S(1)} %bitcast.19), channel_id=1, source_target_pairs={{0,1},{1,0},{2,3},{3,2},{4,5},{5,4},{6,7},{7,6},{8,9},{9,8},{10,11... | collective-permute-start | bytes 2359304 | tf_op jit(solution)/shard_map/ppermute | solution.py:491
  158.7 1.6 arrive.1
  160.3 0.3 collective-permute-done.19.other
  160.6 2.8 %place.1 = (f32[64,4096]{1,0:T(8,128)}, f32[64,2048]{1,0:T(8,128)}, f32[64,4096]{1,0:T(8,128)}, f32[64,2048]{1,0:T(8,128)}) custom-call(s32[1]{0:T(128)} %bitcast.1.core, bf16[8,8,16,384]{3,2,1,0:T(8,128)(2,1)S(1)} %bitcast.20, bf16[8,8,16,384]{3,2,1,0:T(8,128)(2,1)S(1)} %collective-permute-done.19.other), custom_call_target="tpu_custom_call" | custom-call | tf_op jit(solution)/shard_map/place/pallas_call | solution.py:475
  (21 shorter events, 0.1 us)
Async XLA Ops:
  8.7 6.2 %copy-start.4 = (bf16[256,128]{1,0:T(8,128)(2,1)S(1)}, bf16[256,128]{1,0:T(8,128)(2,1)}, u32[]{:S(2)}) copy-start(bf16[256,128]{1,0:T(8,128)(2,1)} %get-tuple-element.24.refs_0_) | copy-start | bytes 196612
  8.8 11.1 %copy-start = (bf16[1,256,4096]{2,1,0:T(8,128)(2,1)S(1)}, bf16[1,256,4096]{2,1,0:T(8,128)(2,1)}, u32[]{:S(2)}) copy-start(bf16[1,256,4096]{2,1,0:T(8,128)(2,1)} %param.10) | copy-start | bytes 6291460
  8.8 14.1 %copy-start.5 = (s32[1,8]{1,0:T(1,128)S(1)}, s32[1,8]{1,0:T(1,128)}, u32[]{:S(2)}) copy-start(s32[1,8]{1,0:T(1,128)} %param.14) | copy-start | bytes 100
  8.8 57.8 %all-to-all-start = ((bf16[8,256,1024]{2,1,0:T(8,128)(2,1)}), bf16[8,256,1024]{2,1,0:T(8,128)(2,1)}, u32[]{:S(2)}, u32[]{:S(2)}) async-start(bf16[8,256,1024]{2,1,0:T(8,128)(2,1)} %get-tuple-element.23), calls=%async_computation | async-start | bytes 8388608 | tf_op jit(solution)/shard_map/all_to_all | solution.py:487
  14.9 50.1 %collective-permute-start = (bf16[256,128]{1,0:T(8,128)(2,1)S(1)}, bf16[256,128]{1,0:T(8,128)(2,1)S(1)}, u32[]{:S(2)}, u32[]{:S(2)}) collective-permute-start(bf16[256,128]{1,0:T(8,128)(2,1)S(1)} %copy-done.4), channel_id=1, source_target_pairs={{0,2},{2,4},{4,6},{6,0},{1,3},{3,5},{5,7},{7,1},{8,10},{10,12},{12... | collective-permute-start | bytes 196616 | tf_op jit(solution)/shard_map/ppermute | solution.py:516
  16.3 50.3 %collective-permute-start.1 = (bf16[256,128]{1,0:T(8,128)(2,1)S(1)}, bf16[256,128]{1,0:T(8,128)(2,1)S(1)}, u32[]{:S(2)}, u32[]{:S(2)}) collective-permute-start(bf16[256,128]{1,0:T(8,128)(2,1)S(1)} %copy-done.4), channel_id=1, source_target_pairs={{0,4},{2,6},{4,0},{6,2},{1,5},{3,7},{5,1},{7,3},{8,12},{10,14},{12... | collective-permute-start | bytes 196616 | tf_op jit(solution)/shard_map/ppermute | solution.py:516
  18.7 47.9 %collective-permute-start.2 = (bf16[256,128]{1,0:T(8,128)(2,1)S(1)}, bf16[256,128]{1,0:T(8,128)(2,1)S(1)}, u32[]{:S(2)}, u32[]{:S(2)}) collective-permute-start(bf16[256,128]{1,0:T(8,128)(2,1)S(1)} %copy-done.4), channel_id=1, source_target_pairs={{0,6},{2,0},{4,2},{6,4},{1,7},{3,1},{5,3},{7,5},{8,14},{10,8},{12,... | collective-permute-start | bytes 196616 | tf_op jit(solution)/shard_map/ppermute | solution.py:516
  20.9 77.9 %collective-permute-start.14 = (bf16[256,2048]{1,0:T(8,128)(2,1)}, bf16[256,2048]{1,0:T(8,128)(2,1)S(1)}, u32[]{:S(2)}, u32[]{:S(2)}) collective-permute-start(bf16[256,2048]{1,0:T(8,128)(2,1)} %dynamic-slice_bitcast_fusion), channel_id=1, source_target_pairs={{0,1},{1,0},{2,3},{3,2},{4,5},{5,4},{6,7},{7,6},{8,9},{9,8},{10,11... | collective-permute-start | bytes 3145736 | tf_op jit(solution)/shard_map/ppermute | solution.py:491
  82.5 13.5 %collective-permute-start.3 = (bf16[4,256,256]{2,1,0:T(8,128)(2,1)S(1)}, bf16[4,256,256]{2,1,0:T(8,128)(2,1)S(1)}, u32[]{:S(2)}, u32[]{:S(2)}) collective-permute-start(bf16[4,256,256]{2,1,0:T(8,128)(2,1)S(1)} %get-tuple-element.26), channel_id=1, source_target_pairs={{0,1},{1,0},{2,3},{3,2},{4,5},{5,4},{6,7},{7,6},{8,9},{9,8},{10,11... | collective-permute-start | bytes 1572872 | tf_op jit(solution)/shard_map/ppermute | solution.py:491
  83.5 1.6 collective-permute-start.15
  83.6 1.9 %collective-permute-start.16 = (bf16[256,128]{1,0:T(8,128)(2,1)S(1)}, bf16[256,128]{1,0:T(8,128)(2,1)S(1)}, u32[]{:S(2)}, u32[]{:S(2)}) collective-permute-start(bf16[256,128]{1,0:T(8,128)(2,1)S(1)} %collective-permute-done.refs_0_.refs_1_), channel_id=1, source_target_pairs={{0,1},{1,0},{2,3},{3,2},{4,5},{5,4},{6,7},{7,6},{8,9},{9,8},{10,11... | collective-permute-start | bytes 196616 | tf_op jit(solution)/shard_map/ppermute | solution.py:491
  84.0 1.5 collective-permute-start.17
  85.1 1.5 collective-permute-start.18
  85.5 9.0 %collective-permute-start.7 = (bf16[2,128,256]{2,1,0:T(8,128)(2,1)S(1)}, bf16[2,128,256]{2,1,0:T(8,128)(2,1)S(1)}, u32[]{:S(2)}, u32[]{:S(2)}) collective-permute-start(bf16[2,128,256]{2,1,0:T(8,128)(2,1)S(1)} %get-tuple-element.32), channel_id=1, source_target_pairs={{0,2},{2,4},{4,6},{6,0},{1,3},{3,5},{5,7},{7,1},{8,10},{10,12},{12... | collective-permute-start | bytes 393224 | tf_op jit(solution)/shard_map/ppermute | solution.py:516
  85.5 9.9 %collective-permute-start.8 = (bf16[2,128,256]{2,1,0:T(8,128)(2,1)S(1)}, bf16[2,128,256]{2,1,0:T(8,128)(2,1)S(1)}, u32[]{:S(2)}, u32[]{:S(2)}) collective-permute-start(bf16[2,128,256]{2,1,0:T(8,128)(2,1)S(1)} %get-tuple-element.33), channel_id=1, source_target_pairs={{0,4},{2,6},{4,0},{6,2},{1,5},{3,7},{5,1},{7,3},{8,12},{10,14},{12... | collective-permute-start | bytes 393224 | tf_op jit(solution)/shard_map/ppermute | solution.py:516
  86.6 8.8 %collective-permute-start.9 = (bf16[2,128,256]{2,1,0:T(8,128)(2,1)S(1)}, bf16[2,128,256]{2,1,0:T(8,128)(2,1)S(1)}, u32[]{:S(2)}, u32[]{:S(2)}) collective-permute-start(bf16[2,128,256]{2,1,0:T(8,128)(2,1)S(1)} %get-tuple-element.34), channel_id=1, source_target_pairs={{0,6},{2,0},{4,2},{6,4},{1,7},{3,1},{5,3},{7,5},{8,14},{10,8},{12,... | collective-permute-start | bytes 393224 | tf_op jit(solution)/shard_map/ppermute | solution.py:516
  94.5 4.4 %collective-permute-start.10 = (bf16[2,128,256]{2,1,0:T(8,128)(2,1)S(1)}, bf16[2,128,256]{2,1,0:T(8,128)(2,1)S(1)}, u32[]{:S(2)}, u32[]{:S(2)}) collective-permute-start(bf16[2,128,256]{2,1,0:T(8,128)(2,1)S(1)} %get-tuple-element.31.refs_0_), channel_id=1, source_target_pairs={{0,1},{1,0},{2,3},{3,2},{4,5},{5,4},{6,7},{7,6},{8,9},{9,8},{10,11... | collective-permute-start | bytes 393224 | tf_op jit(solution)/shard_map/ppermute | solution.py:491
  95.4 3.4 %collective-permute-start.11 = (bf16[2,128,256]{2,1,0:T(8,128)(2,1)S(1)}, bf16[2,128,256]{2,1,0:T(8,128)(2,1)S(1)}, u32[]{:S(2)}, u32[]{:S(2)}) collective-permute-start(bf16[2,128,256]{2,1,0:T(8,128)(2,1)S(1)} %collective-permute-done.7.refs_1_), channel_id=1, source_target_pairs={{0,1},{1,0},{2,3},{3,2},{4,5},{5,4},{6,7},{7,6},{8,9},{9,8},{10,11... | collective-permute-start | bytes 393224 | tf_op jit(solution)/shard_map/ppermute | solution.py:491
  95.4 3.4 %collective-permute-start.12 = (bf16[2,128,256]{2,1,0:T(8,128)(2,1)S(1)}, bf16[2,128,256]{2,1,0:T(8,128)(2,1)S(1)}, u32[]{:S(2)}, u32[]{:S(2)}) collective-permute-start(bf16[2,128,256]{2,1,0:T(8,128)(2,1)S(1)} %collective-permute-done.8.refs_2_), channel_id=1, source_target_pairs={{0,1},{1,0},{2,3},{3,2},{4,5},{5,4},{6,7},{7,6},{8,9},{9,8},{10,11... | collective-permute-start | bytes 393224 | tf_op jit(solution)/shard_map/ppermute | solution.py:491
  96.1 2.8 %collective-permute-start.13 = (bf16[2,128,256]{2,1,0:T(8,128)(2,1)S(1)}, bf16[2,128,256]{2,1,0:T(8,128)(2,1)S(1)}, u32[]{:S(2)}, u32[]{:S(2)}) collective-permute-start(bf16[2,128,256]{2,1,0:T(8,128)(2,1)S(1)} %collective-permute-done.9.refs_3_), channel_id=1, source_target_pairs={{0,1},{1,0},{2,3},{3,2},{4,5},{5,4},{6,7},{7,6},{8,9},{9,8},{10,11... | collective-permute-start | bytes 393224 | tf_op jit(solution)/shard_map/ppermute | solution.py:491
  98.8 1.9 %copy-start.1 = (bf16[256,512]{1,0:T(8,128)(2,1)}, bf16[256,512]{1,0:T(8,128)(2,1)S(1)}, u32[]{:S(2)}) copy-start(bf16[256,512]{1,0:T(8,128)(2,1)S(1)} %get-tuple-element.30.refs_14_) | copy-start | bytes 786436
  98.8 1.9 %copy-start.2 = (bf16[256,512]{1,0:T(8,128)(2,1)}, bf16[256,512]{1,0:T(8,128)(2,1)S(1)}, u32[]{:S(2)}) copy-start(bf16[256,512]{1,0:T(8,128)(2,1)S(1)} %get-tuple-element.29.refs_13_) | copy-start | bytes 786436
  98.8 1.8 %copy-start.3 = (bf16[256,512]{1,0:T(8,128)(2,1)}, bf16[256,512]{1,0:T(8,128)(2,1)S(1)}, u32[]{:S(2)}) copy-start(bf16[256,512]{1,0:T(8,128)(2,1)S(1)} %get-tuple-element.28.refs_12_) | copy-start | bytes 786436
  100.7 32.7 %all-to-all-start.1 = ((bf16[64,16,384]{2,1,0:T(8,128)(2,1)}), bf16[64,16,384]{2,1,0:T(8,128)(2,1)S(1)}, u32[]{:S(2)}, u32[]{:S(2)}) async-start(bf16[64,16,384]{2,1,0:T(8,128)(2,1)} %bitcast.12), calls=%async_computation.1 | async-start | bytes 1572864 | tf_op jit(solution)/shard_map/all_to_all | solution.py:487
  111.0 17.0 %collective-permute-start.4 = (bf16[256,512]{1,0:T(8,128)(2,1)}, bf16[256,512]{1,0:T(8,128)(2,1)S(1)}, u32[]{:S(2)}, u32[]{:S(2)}) collective-permute-start(bf16[256,512]{1,0:T(8,128)(2,1)} %copy-done.3), channel_id=1, source_target_pairs={{0,2},{2,4},{4,6},{6,0},{1,3},{3,5},{5,7},{7,1},{8,10},{10,12},{12... | collective-permute-start | bytes 786440 | tf_op jit(solution)/shard_map/ppermute | solution.py:516
  112.1 21.2 %collective-permute-start.5 = (bf16[256,512]{1,0:T(8,128)(2,1)}, bf16[256,512]{1,0:T(8,128)(2,1)S(1)}, u32[]{:S(2)}, u32[]{:S(2)}) collective-permute-start(bf16[256,512]{1,0:T(8,128)(2,1)} %copy-done.2), channel_id=1, source_target_pairs={{0,4},{2,6},{4,0},{6,2},{1,5},{3,7},{5,1},{7,3},{8,12},{10,14},{12... | collective-permute-start | bytes 786440 | tf_op jit(solution)/shard_map/ppermute | solution.py:516
  114.5 18.9 %collective-permute-start.6 = (bf16[256,512]{1,0:T(8,128)(2,1)}, bf16[256,512]{1,0:T(8,128)(2,1)S(1)}, u32[]{:S(2)}, u32[]{:S(2)}) collective-permute-start(bf16[256,512]{1,0:T(8,128)(2,1)} %copy-done.1), channel_id=1, source_target_pairs={{0,6},{2,0},{4,2},{6,4},{1,7},{3,1},{5,3},{7,5},{8,14},{10,8},{12,... | collective-permute-start | bytes 786440 | tf_op jit(solution)/shard_map/ppermute | solution.py:516
  156.0 4.7 %collective-permute-start.19 = (bf16[8,8,16,384]{3,2,1,0:T(8,128)(2,1)S(1)}, bf16[8,8,16,384]{3,2,1,0:T(8,128)(2,1)S(1)}, u32[]{:S(2)}, u32[]{:S(2)}) collective-permute-start(bf16[8,8,16,384]{3,2,1,0:T(8,128)(2,1)S(1)} %bitcast.19), channel_id=1, source_target_pairs={{0,1},{1,0},{2,3},{3,2},{4,5},{5,4},{6,7},{7,6},{8,9},{9,8},{10,11... | collective-permute-start | bytes 2359304 | tf_op jit(solution)/shard_map/ppermute | solution.py:491

commit v5 on v4

--- a/solution.py
+++ b/solution.py
@@ -47,12 +47,12 @@
 
 
 def pack_kernel(
-    hidden, wq_down, wv_down, fq, fk, fv, grad, wq_up, wv_up, out, low,
-    hidden_v, wq_down_v, wv_down_v, fq_v, fv_v, wq_up_v, wv_up_v, out_v,
+    hidden, wq_down, wv_down, fq, fk, fv, grad, wq_up, wv_up, out,
+    hidden_v, wq_down_v, wv_down_v, fq_v, fv_v, wq_up_v, wv_up_v, out_v, low,
     down_sems, hidden_sems, row_sems, through_sems, out_sems,
 ):
     devices, rows, packed = out.shape
-    width = packed // 4
+    width = (packed - 2 * RANK) // 4
     model = hidden.shape[1]
     step = model // HIDDEN_PARTS
 
@@ -114,6 +114,7 @@
             out_v[device, :, 2 * which * width : (2 * which + 1) * width] = (
                 frozen[:, at].astype(jnp.float32) + added
             ).astype(jnp.bfloat16)
+        out_v[device, :, 4 * width :] = low[...]
         through[2 * device].wait()
         through[2 * device + 1].wait()
         outs.append(pltpu.make_async_copy(out_v.at[device], out.at[device], out_sems.at[device]))
@@ -130,11 +131,8 @@
     return pl.pallas_call(
         pack_kernel,
         in_specs=[ANY] * 9,
-        out_specs=[ANY, VMEM],
-        out_shape=[
-            jax.ShapeDtypeStruct((seq_size, rows, 4 * width), bf16),
-            jax.ShapeDtypeStruct((rows, 2 * RANK), bf16),
-        ],
+        out_specs=ANY,
+        out_shape=jax.ShapeDtypeStruct((seq_size, rows, 4 * width + 2 * RANK), bf16),
         scratch_shapes=[
             pltpu.VMEM((rows, model), bf16),
             pltpu.VMEM((RANK, model), bf16),
@@ -143,7 +141,8 @@
             pltpu.VMEM((rows, columns), bf16),
             pltpu.VMEM((RANK, columns), bf16),
             pltpu.VMEM((RANK, columns), bf16),
-            pltpu.VMEM((seq_size, rows, 4 * width), bf16),
+            pltpu.VMEM((seq_size, rows, 4 * width + 2 * RANK), bf16),
+            pltpu.VMEM((rows, 2 * RANK), bf16),
             pltpu.SemaphoreType.DMA((2,)),
             pltpu.SemaphoreType.DMA((HIDDEN_PARTS,)),
             pltpu.SemaphoreType.DMA((4,)),
@@ -158,14 +157,13 @@
 def attention_kernel(
     meta, packed, wq_up, wv_up, *refs
 ):
-    out, leaving, back_0, back_1, back_2, back_3, dq_t, dv_t, q_t, k_t, v_t, g_t, dv, returned = (
-        refs[-14:]
-    )
+    *outs, dq_t, dv_t, low, q_t, k_t, v_t, g_t, dv, returned, out = refs
+    outs, backs = outs[: len(outs) // 2], outs[len(outs) // 2 :]
     length = packed.shape[0]
     heads = out.shape[1] // HEAD_SIZE
     width = heads * HEAD_SIZE
     blocks = length // TILE
-    chip, core = meta[NDOC], meta[NDOC + 1]
+    chip = meta[NDOC]
     span = [slice(head * HEAD_SIZE, (head + 1) * HEAD_SIZE) for head in range(heads)]
 
     def columns(which, head):
@@ -238,20 +236,19 @@
         returned[part * RANK : (part + 1) * RANK, :] = (
             ADAPTER_SCALE * dot(weight[...], grads[...])
         ).astype(jnp.bfloat16)
-    backs = (back_0, back_1, back_2, back_3)
-    rows = back_0.shape[2]
+    low[...] = packed[:, 4 * width :]
+    rows = backs[0].shape[2]
     for step in range(len(backs)):
         target = lax.rem(chip + step, len(backs))
         for holder in range(2):
             begin = pl.multiple_of((target * 2 + holder) * rows, rows)
             backs[step][holder] = returned[:, pl.ds(begin, rows)]
-        begin = pl.multiple_of((target * 2 + 1 - core) * rows, rows)
-        leaving[step] = out[pl.ds(begin, rows), :]
-
-
-def attention(meta, packed, wq_up, wv_up, seq_size, after):
+            outs[step][holder] = out[pl.ds(begin, rows), :]
+
+
+def attention(meta, packed, wq_up, wv_up, seq_size):
     length = packed.shape[0]
-    width = packed.shape[1] // 4
+    width = (packed.shape[1] - 2 * RANK) // 4
     rows = length // seq_size
     heads = width // HEAD_SIZE
     chips = seq_size // 2
@@ -260,8 +257,8 @@
     grad_t = jax.ShapeDtypeStruct((width, length), jnp.bfloat16)
     return pl.pallas_call(
         attention_kernel,
-        in_specs=[SMEM, VMEM, VMEM, VMEM] + [VMEM] * len(after),
-        out_specs=[VMEM] * (4 + chips),
+        in_specs=[SMEM, VMEM, VMEM, VMEM],
+        out_specs=[VMEM] * (3 + 2 * chips),
         scratch_shapes=[
             wide_t,
             wide_t,
@@ -269,106 +266,89 @@
             wide_t,
             pltpu.VMEM((heads, length, HEAD_SIZE), jnp.float32),
             pltpu.VMEM((2 * RANK, length), jnp.bfloat16),
+            pltpu.VMEM((length, width), jnp.bfloat16),
         ],
-        out_shape=[
-            jax.ShapeDtypeStruct((length, width), jnp.bfloat16),
-            jax.ShapeDtypeStruct((chips, rows, width), jnp.bfloat16),
-        ]
+        out_shape=[jax.ShapeDtypeStruct((2, rows, width), jnp.bfloat16)] * chips
         + [back] * chips
-        + [grad_t, grad_t],
+        + [grad_t, grad_t, jax.ShapeDtypeStruct((length, 2 * RANK), jnp.bfloat16)],
         compiler_params=pltpu.CompilerParams(vmem_limit_bytes=40 << 20),
         cost_estimate=pl.CostEstimate(
             flops=8 << 30, bytes_accessed=16 << 20, transcendentals=4 << 20
         ),
         name="attention",
-    )(meta, packed, wq_up, wv_up, *after)
-
-
-def up_kernel(where, *refs):
-    chip, core = where[0], where[1]
-    *lows, dq_t, dv_t, up = refs
-    steps = len(lows) // 2
-    rows = lows[0].shape[0]
+    )(meta, packed, wq_up, wv_up)
+
+
+def up_kernel(where, low, dq_t, dv_t, up):
     width = dq_t.shape[0]
     lane = lax.broadcasted_iota(jnp.int32, (width, up.shape[1]), 1)
     source = lax.broadcasted_iota(jnp.int32, (width, up.shape[1]), 0)
     mine = (source == (lane // 128) * UP_COLS + lane % UP_COLS) & (
-        (lane % 128) // UP_COLS == chip
+        (lane % 128) // UP_COLS == where[0]
     )
     mine = jnp.where(mine, 1.0, 0.0).astype(jnp.bfloat16)
     for part, grads in enumerate((dq_t, dv_t)):
-        total = jnp.zeros((width, 2 * RANK), jnp.float32)
-        for index, low in enumerate(lows):
-            origin = lax.rem(chip + steps - index % steps, steps)
-            holder = core if index < steps else 1 - core
-            begin = pl.multiple_of((origin * 2 + holder) * rows, rows)
-            total += dot(grads[:, pl.ds(begin, rows)], low[...])
-        share = (total * ADAPTER_SCALE).T[part * RANK : (part + 1) * RANK, :]
+        share = (dot(grads[...], low[...]) * ADAPTER_SCALE).T[part * RANK : (part + 1) * RANK, :]
         up[part * RANK : (part + 1) * RANK, :] = dot(share.astype(jnp.bfloat16), mine).astype(
             jnp.bfloat16
         )
 
 
-def up_gradient(where, lows, dq_t, dv_t):
+def up_gradient(where, low, dq_t, dv_t):
     width = dq_t.shape[0]
     return pl.pallas_call(
         up_kernel,
-        in_specs=[SMEM] + [VMEM] * (len(lows) + 2),
+        in_specs=[SMEM] + [VMEM] * 3,
         out_specs=VMEM,
         out_shape=jax.ShapeDtypeStruct((2 * RANK, width // UP_COLS * 128), jnp.bfloat16),
-        compiler_params=pltpu.CompilerParams(vmem_limit_bytes=24 << 20),
+        compiler_params=pltpu.CompilerParams(vmem_limit_bytes=16 << 20),
         name="up_gradient",
-    )(where, *lows, dq_t, dv_t)
-
-
-def join_kernel(where, result, other, *outs):
+    )(where, low, dq_t, dv_t)
+
+
+def pick_kernel(where, part_0, part_1, part_2, part_3, out):
+    core = where[1]
+    for step, part in enumerate((part_0, part_1, part_2, part_3)):
+        out[step] = part[1 - core]
+
+
+def pick(where, parts):
+    return pl.pallas_call(
+        pick_kernel,
+        in_specs=[SMEM] + [VMEM] * len(parts),
+        out_specs=VMEM,
+        out_shape=jax.ShapeDtypeStruct((len(parts),) + parts[0].shape[1:], parts[0].dtype),
+        compiler_params=pltpu.CompilerParams(vmem_limit_bytes=SMALL_VMEM),
+        name="pick",
+    )(where, *parts)
+
+
+def arrive_kernel(where, part_0, part_1, part_2, part_3, other, out):
     chip, core = where[0], where[1]
-    chips, rows, width = other.shape
-    here = pl.multiple_of(core * width, width)
-    there = pl.multiple_of((1 - core) * width, width)
-    for step in range(chips):
-        target = lax.rem(chip + step, chips)
-        begin = pl.multiple_of((target * 2 + core) * rows, rows)
-        outs[step][:, pl.ds(here, width)] = result[pl.ds(begin, rows), :]
-        outs[step][:, pl.ds(there, width)] = other[step]
-
-
-def join(where, result, other):
-    chips, rows, width = other.shape
-    return pl.pallas_call(
-        join_kernel,
-        in_specs=[SMEM, VMEM, VMEM],
-        out_specs=[VMEM] * chips,
-        out_shape=[jax.ShapeDtypeStruct((rows, 2 * width), other.dtype)] * chips,
-        compiler_params=pltpu.CompilerParams(vmem_limit_bytes=SMALL_VMEM),
-        name="join",
-    )(where, result, other)
-
-
-def arrive_kernel(where, part_0, part_1, part_2, part_3, out):
-    chip = where[0]
     parts = (part_0, part_1, part_2, part_3)
-    width = part_0.shape[1]
+    width = part_0.shape[2]
     for step in range(len(parts)):
         origin = lax.rem(chip + len(parts) - step, len(parts))
-        out[0, :, pl.ds(pl.multiple_of(origin * width, width), width)] = parts[step][...]
-
-
-def arrive(where, parts):
-    rows, width = parts[0].shape
+        here = pl.multiple_of((origin * 2 + core) * width, width)
+        there = pl.multiple_of((origin * 2 + 1 - core) * width, width)
+        out[0, :, pl.ds(here, width)] = parts[step][core]
+        out[0, :, pl.ds(there, width)] = other[step]
+
+
+def arrive(where, parts, other):
+    _, rows, width = parts[0].shape
     return pl.pallas_call(
         arrive_kernel,
-        in_specs=[SMEM] + [VMEM] * len(parts),
+        in_specs=[SMEM] + [VMEM] * (len(parts) + 1),
         out_specs=VMEM,
-        out_shape=jax.ShapeDtypeStruct((1, rows, len(parts) * width), parts[0].dtype),
+        out_shape=jax.ShapeDtypeStruct((1, rows, 2 * len(parts) * width), parts[0].dtype),
         compiler_params=pltpu.CompilerParams(vmem_limit_bytes=SMALL_VMEM),
         name="arrive",
-    )(where, *parts)
+    )(where, *parts, other)
 
 
 def down_kernel(core, *refs):
-    parts, (hidden, hidden_other, up) = refs[:8], refs[8:11]
-    out, back = refs[-2:]
+    *parts, hidden, hidden_other, up, out, back = refs
 
     @pl.when(pl.program_id(0) == 0)
     def _():
@@ -388,7 +368,7 @@
             out[row, column, :, DOWN_COLS:] = up[across, column * 128 : (column + 1) * 128]
 
 
-def down_gradient(core, parts, hidden, hidden_other, up, after):
+def down_gradient(core, parts, hidden, hidden_other, up):
     rows, half = hidden_other.shape
     steps = 2
     step = half // steps
@@ -405,8 +385,7 @@
                 pl.BlockSpec((rows, step), lambda i, core: (0, core[0] * steps + i)),
                 pl.BlockSpec((rows, step), lambda i, core: (0, i)),
                 pl.BlockSpec((2 * RANK, columns // steps * 128), lambda i, core: (0, i)),
-            ]
-            + [VMEM] * len(after),
+            ],
             out_specs=pl.BlockSpec(
                 (across, columns // steps, SHARE_ROWS, DOWN_COLS + 128),
                 lambda i, core: (0, i, 0, 0),
@@ -418,7 +397,7 @@
         ),
         compiler_params=pltpu.CompilerParams(vmem_limit_bytes=24 << 20),
         name="down_gradient",
-    )(core, *parts, hidden, hidden_other, up, *after)
+    )(core, *parts, hidden, hidden_other, up)
 
 
 def share_kernel(parts, *refs):
@@ -442,45 +421,71 @@
     )(parts, *after)
 
 
-def place_kernel(core, own, other, grad_a_q, up_q, grad_a_v, up_v, wide):
-    half = own.shape[0] // 2
-    columns = own.shape[1]
-    for part, shares in enumerate((own, other)):
-        which = core[0] if part == 0 else 1 - core[0]
-        for row in range(own.shape[0]):
-            across = slice(row % half * SHARE_ROWS, (row % half + 1) * SHARE_ROWS)
-            target = (grad_a_q, grad_a_v)[row // half]
+def place_kernel(which, shares, *refs):
+    *outs, downs, ups, wide, sems = refs[-8:]
+    which = which[0]
+    half = shares.shape[0] // 2
+    columns = shares.shape[1]
+    copies = []
+
+    def send(source, target, begin, size):
+        begin = pl.multiple_of(begin, size)
+        copies.append(
+            pltpu.make_async_copy(source, target.at[:, pl.ds(begin, size)], sems.at[len(copies)])
+        )
+        copies[-1].start()
+
+    for part in range(2):
+        for row in range(half):
+            across = slice(row * SHARE_ROWS, (row + 1) * SHARE_ROWS)
             for column in range(columns):
-                begin = pl.multiple_of((which * columns + column) * DOWN_COLS, DOWN_COLS)
-                target[across, pl.ds(begin, DOWN_COLS)] = shares[
-                    row, column, :, :DOWN_COLS
+                share = shares[part * half + row, column]
+                downs[part, across, column * DOWN_COLS : (column + 1) * DOWN_COLS] = share[
+                    :, :DOWN_COLS
                 ].astype(jnp.float32)
                 wide[
-                    row * SHARE_ROWS : (row + 1) * SHARE_ROWS, column * 128 : (column + 1) * 128
-                ] = shares[row, column, :, DOWN_COLS:]
-        width = columns * UP_COLS
-        source = lax.broadcasted_iota(jnp.int32, (columns * 128, width), 0)
-        lane = lax.broadcasted_iota(jnp.int32, (columns * 128, width), 1)
-        lane = (lane // UP_COLS) * 128 + lane % UP_COLS
-        for chip in range(128 // UP_COLS):
-            pick = jnp.where(source == lane + chip * UP_COLS, 1.0, 0.0).astype(jnp.bfloat16)
-            picked = dot(wide[...], pick)
-            begin = pl.multiple_of((2 * chip + which) * width, width)
-            up_q[:, pl.ds(begin, width)] = picked[:RANK]
-            up_v[:, pl.ds(begin, width)] = picked[RANK:]
-
-
-def place(core, own, other, model, width):
+                    part * RANK + row * SHARE_ROWS : part * RANK + (row + 1) * SHARE_ROWS,
+                    column * 128 : (column + 1) * 128,
+                ] = share[:, DOWN_COLS:]
+        width = columns * DOWN_COLS
+        send(downs.at[part], outs[2 * part], which * width, width)
+    width = columns * UP_COLS
+    source = lax.broadcasted_iota(jnp.int32, (columns * 128, width), 0)
+    lane = lax.broadcasted_iota(jnp.int32, (columns * 128, width), 1)
+    lane = (lane // UP_COLS) * 128 + lane % UP_COLS
+    for chip in range(128 // UP_COLS):
+        chosen = jnp.where(source == lane + chip * UP_COLS, 1.0, 0.0).astype(jnp.bfloat16)
+        ups[chip] = dot(wide[...], chosen)
+        for part in range(2):
+            send(
+                ups.at[chip, part * RANK : (part + 1) * RANK, :],
+                outs[2 * part + 1],
+                (2 * chip + which) * width,
+                width,
+            )
+    for copy in copies:
+        copy.wait()
+
+
+def place(which, shares, model, width, earlier=(), after=()):
     shapes = [(RANK, model), (RANK, width), (RANK, model), (RANK, width)]
+    columns = shares.shape[1]
+    chips = 128 // UP_COLS
     return pl.pallas_call(
         place_kernel,
-        in_specs=[SMEM, VMEM, VMEM],
-        out_specs=[VMEM] * 4,
+        in_specs=[SMEM, VMEM] + [ANY] * len(earlier) + [VMEM] * len(after),
+        out_specs=[ANY] * 4,
         out_shape=[jax.ShapeDtypeStruct(shape, jnp.float32) for shape in shapes],
-        scratch_shapes=[pltpu.VMEM((2 * RANK, own.shape[1] * 128), jnp.bfloat16)],
-        compiler_params=pltpu.CompilerParams(vmem_limit_bytes=30 << 20),
+        scratch_shapes=[
+            pltpu.VMEM((2, RANK, columns * DOWN_COLS), jnp.float32),
+            pltpu.VMEM((chips, 2 * RANK, columns * UP_COLS), jnp.float32),
+            pltpu.VMEM((2 * RANK, columns * 128), jnp.bfloat16),
+            pltpu.SemaphoreType.DMA((2 + 2 * chips,)),
+        ],
+        input_output_aliases={2 + index: index for index in range(len(earlier))},
+        compiler_params=pltpu.CompilerParams(vmem_limit_bytes=16 << 20),
         name="place",
-    )(core, own, other)
+    )(which[None], shares, *earlier, *after)
 
 
 def swap(x, axes):
@@ -515,7 +520,7 @@
     def to_chip(x, step):
         return lax.ppermute(x, "y", [(c, (c + step) % chips) for c in range(chips)])
 
-    packed, low = pack(
+    packed = pack(
         hidden[0],
         query_down_weight.T,
         value_down_weight.T,
@@ -531,30 +536,27 @@
     hidden_other = to_other_core(
         lax.dynamic_slice(hidden[0], (0, (1 - core) * half), (rows, half))
     )
-    lows = [low] + [to_chip(low, step) for step in range(1, chips)]
-    lows = lows + [to_other_core(low) for low in lows]
     width = frozen_queries.shape[2] // seq_size
     own_columns = (0, (chip * 2 + core) * width)
     wq_up = lax.dynamic_slice(query_up_weight, own_columns, (RANK, width))
     wv_up = lax.dynamic_slice(value_up_weight, own_columns, (RANK, width))
     meta = jnp.concatenate([document_length_list[0], where])
-    result, leaving, *backs, dq_t, dv_t = attention(
-        meta, received, wq_up, wv_up, seq_size, after=lows[1:chips]
-    )
+    *outs, dq_t, dv_t, low = attention(meta, received, wq_up, wv_up, seq_size)
+    parts, backs = outs[:chips], outs[chips:]
 
     backs = [backs[0]] + [to_chip(backs[step], step) for step in range(1, chips)]
     backs_other = [to_other_core(back) for back in backs]
-    up = up_gradient(where, lows, dq_t, dv_t)
-    joined = join(where, result, to_other_core(leaving))
-    parts = [joined[0]] + [to_chip(joined[step], step) for step in range(1, chips)]
-    attended = arrive(where, parts)
-    down = down_gradient(core[None], backs + backs_other, hidden[0], hidden_other, up, after=joined)
+    parts = [parts[0]] + [to_chip(parts[step], step) for step in range(1, chips)]
+    up = up_gradient(where, low, dq_t, dv_t)
+    down = down_gradient(core[None], backs + backs_other, hidden[0], hidden_other, up)
 
     shares = swap(down.reshape((-1,) + down.shape[2:]), PLANE)
-    shares = swap(sum_share(shares, after=parts[1:]), PLANE).reshape(down.shape)
+    shares = swap(sum_share(shares, after=[parts[1], parts[3]]), PLANE).reshape(down.shape)
+    attended = arrive(where, parts, to_other_core(pick(where, parts)))
     shares_other = to_other_core(shares)
+    grads = place(core, shares, model, seq_size * width, after=[parts[2]])
     grad_a_q, up_q, grad_a_v, up_v = place(
-        core[None], shares, shares_other, model, seq_size * width
+        1 - core, shares_other, model, seq_size * width, earlier=grads
     )
     return attended, grad_a_q.T, up_q, grad_a_v.T, up_v
 

time: 164 us -> 162 us (0.988)
  blocking collectives: 22.5 us -> 0 us
  waiting for transfers between devices: 68.7 us -> 81.9 us
  starting transfers between devices: 36.7 us -> 43 us
    all_to_all x2 -> x3, waiting for transfers between devices: 0.01 us -> 63.9 us  [swap(): return lax.all_to_all(x, axes, 0, 0, tiled=True)]
    ppermute x9 -> x6, waiting for transfers between devices: 67.3 us -> 16.4 us  [to_chip(): return lax.ppermute(x, 'y', [(c, (c + step) % chips) for c in range(chips)])]
    all_to_all x1 -> x0, blocking collectives: 22.5 us -> none  [swap(): return lax.all_to_all(x, axes, 0, 0, tiled=True)]
    all_to_all x2 -> x3, starting transfers between devices: 16.4 us -> 24.9 us  [swap(): return lax.all_to_all(x, axes, 0, 0, tiled=True)]
    ppermute x9 -> x6, starting transfers between devices: 12.6 us -> 8.36 us  [to_chip(): return lax.ppermute(x, 'y', [(c, (c + step) % chips) for c in range(chips)])]
    ppermute x11 -> x7, starting transfers between devices: 7.7 us -> 9.78 us  [to_other_core(): return lax.ppermute(x, 'core', [(0, 1), (1, 0)])]
    pallas_call x6 -> x7, Pallas kernels: 30.8 us -> 30.6 us  [the longest x1 16.1 us: attention(): pl.pallas_call(attention_kernel, in_specs=[SMEM, VMEM, VMEM, VMEM], out_s...]
  transfers between devices with their start and end apart: 22 -> 16, of which waited for: 7 -> 5; matrix products, arithmetic and copies ran while one was open for 1% -> 1% of each run, Pallas kernels for 12% -> 13%
where the time goes in v5:
time: 162 us; the launch traced here: 161 us
  waiting for transfers between devices  81.9 us (51%)
  starting transfers between devices  43 us (27%)
  Pallas kernels  33.4 us (21%)
  local copies, waits for them, and re-layouts  1.86 us (1%)
    all_to_all x3, waiting for transfers between devices, swap(): return lax.all_to_all(x, axes, 0, 0, tiled=True)  63.9 us
    all_to_all x3, starting transfers between devices, swap(): return lax.all_to_all(x, axes, 0, 0, tiled=True)  24.9 us
    ppermute x6, waiting for transfers between devices, to_chip(): return lax.ppermute(x, 'y', [(c, (c + step) % chips) for c in range(chips)])  16.4 us
    pallas_call x1, Pallas kernels, attention(): pl.pallas_call(attention_kernel, in_specs=[SMEM, VMEM, VMEM, VMEM], out_s...  16.1 us
    ppermute x7, starting transfers between devices, to_other_core(): return lax.ppermute(x, 'core', [(0, 1), (1, 0)])  9.78 us
    ppermute x6, starting transfers between devices, to_chip(): return lax.ppermute(x, 'y', [(c, (c + step) % chips) for c in range(chips)])  8.36 us
    pallas_call x1, Pallas kernels, pack(): pl.pallas_call(pack_kernel, in_specs=[ANY] * 9, out_specs=ANY, out_shape=...  7.52 us
  transfers between devices with their start and end apart: 16, of which 5 were waited for; matrix products, arithmetic and copies ran while one was open for 1% of the time, Pallas kernels for 13%

profile of v5, /device:TPU:1, one launch (start us, length us, event | category | flops | bytes accessed | tf_op | source)
XLA Modules:
  0.0 161.3 jit_solution(4784831602341250450)
XLA Ops:
  0.6 7.5 %pack.1 = bf16[8,256,1152]{2,1,0:T(8,128)(2,1)} custom-call(bf16[256,4096]{1,0:T(8,128)(2,1)} %bitcast.18, bf16[64,4096]{1,0:T(8,128)(2,1)} %bitcast.28, bf16[64,4096]{1,0:T(8,128)(2,1)} %bitcast.29, bf16[256,2048]{1,0:T(8,128)(2,1)} %bitcast.22, bf16[256,2048]{1,0:T(8,128)(2,1)} %bitcast.23, bf16[256,2048]{1,0:T(8,128)(2,1)} %bitcast.24, ...), custom_call_target="tpu_custom_call" | custom-call | tf_op jit(solution)/shard_map/pack/pallas_call | solution.py:131
  8.2 0.0 copy-start
  8.2 0.0 copy-start.5
  8.2 6.1 %all-to-all-start = ((bf16[8,256,1152]{2,1,0:T(8,128)(2,1)}), bf16[8,256,1152]{2,1,0:T(8,128)(2,1)}, u32[]{:S(2)}, u32[]{:S(2)}) async-start(bf16[8,256,1152]{2,1,0:T(8,128)(2,1)} %pack.1), calls=%async_computation | async-start | bytes 9437184 | tf_op jit(solution)/shard_map/all_to_all | solution.py:492
  14.3 1.0 dynamic-slice_bitcast_fusion
  15.3 0.1 collective-permute-start.11
  15.4 0.1 pad_add_fusion.1.meta
  15.5 0.8 constant_dynamic-slice_fusion
  16.3 52.5 %all-to-all-done = bf16[8,256,1152]{2,1,0:T(8,128)(2,1)} async-done(((bf16[8,256,1152]{2,1,0:T(8,128)(2,1)}), bf16[8,256,1152]{2,1,0:T(8,128)(2,1)}, u32[]{:S(2)}, u32[]{:S(2)}) %all-to-all-start) | async-done | bytes 4718624 | tf_op jit(solution)/shard_map/all_to_all | solution.py:492
  68.8 16.1 %attention.1 = (bf16[2,256,256]{2,1,0:T(8,128)(2,1)S(1)}, bf16[2,256,256]{2,1,0:T(8,128)(2,1)S(1)}, bf16[2,256,256]{2,1,0:T(8,128)(2,1)S(1)}, bf16[2,256,256]{2,...) custom-call(s32[10]{0:T(128)S(1)} %pad_add_fusion.1.meta, ...), custom_call_target="tpu_custom_call" | custom-call | flops 8589934592 | bytes 16777216 | tf_op jit(solution)/shard_map/attention/pallas_call | solution.py:258
  84.9 0.0 copy-start.1
  84.9 0.0 copy-start.3
  84.9 0.0 copy-start.4
  84.9 0.5 collective-permute-start.4
  85.5 1.8 %collective-permute-start.5 = (bf16[2,128,256]{2,1,0:T(8,128)(2,1)S(1)}, bf16[2,128,256]{2,1,0:T(8,128)(2,1)S(1)}, u32[]{:S(2)}, u32[]{:S(2)}) collective-permute-start(bf16[2,128,256]{2,1,0:T(8,128)(2,1)S(1)} %get-tuple-element.30), channel_id=1, source_target_pairs={{0,4},{2,6},{4,0},{6,2},{1,5},{3,7},{5,1},{7,3},{8,12},{10,14},{12... | collective-permute-start | bytes 393224 | tf_op jit(solution)/shard_map/ppermute | solution.py:521
  87.2 0.7 collective-permute-start.6
  87.9 1.4 collective-permute-start.7
  89.4 2.2 %collective-permute-done.4.refs_1_ = bf16[2,128,256]{2,1,0:T(8,128)(2,1)S(1)} collective-permute-done((bf16[2,128,256]{2,1,0:T(8,128)(2,1)S(1)}, bf16[2,128,256]{2,1,0:T(8,128)(2,1)S(1)}, u32[]{:S(2)}, u32[]{:S(2)}) %collective-permute-start.4) | collective-permute-done | bytes 131104 | tf_op jit(solution)/shard_map/ppermute | solution.py:521
  91.6 3.5 %collective-permute-start.8 = (bf16[2,128,256]{2,1,0:T(8,128)(2,1)S(1)}, bf16[2,128,256]{2,1,0:T(8,128)(2,1)S(1)}, u32[]{:S(2)}, u32[]{:S(2)}) collective-permute-start(bf16[2,128,256]{2,1,0:T(8,128)(2,1)S(1)} %collective-permute-done.4.refs_1_), channel_id=1, source_target_pairs={{0,1},{1,0},{2,3},{3,2},{4,5},{5,4},{6,7},{7,6},{8,9},{9,8},{10,11... | collective-permute-start | bytes 393224 | tf_op jit(solution)/shard_map/ppermute | solution.py:496
  95.1 0.0 collective-permute-done.5.refs_2_
  95.1 0.0 collective-permute-start.9
  95.1 0.0 collective-permute-done.6.refs_3_
  95.1 0.6 collective-permute-start.10
  95.7 0.1 pad_add_fusion.where
  95.8 1.8 %up_gradient.1.refs_10_ = bf16[128,1024]{1,0:T(8,128)(2,1)S(1)} custom-call(s32[2]{0:T(128)S(1)} %pad_add_fusion.where, bf16[2048,128]{1,0:T(8,128)(2,1)S(1)} %get-tuple-element.32.low, bf16[256,2048]{1,0:T(8,128)(2,1)S(1)} %get-tuple-element.33.dq_t, bf16[256,2048]{1,0:T(8,128)(2,1)S(1)} %get-tuple-element.34.dv_t), custom_call_target="tpu_custom_call" | custom-call | tf_op jit(solution)/shard_map/up_gradient/pallas_call | solution.py:299
  97.6 0.0 collective-permute-done.11.refs_9_
  97.6 0.0 collective-permute-done.7.refs_4_
  97.6 0.0 collective-permute-done.8.refs_5_
  97.6 0.0 collective-permute-done.9.refs_6_
  97.6 1.8 %down_gradient.1 = bf16[8,8,16,384]{3,2,1,0:T(8,128)(2,1)} custom-call(s32[1]{0:T(128)} %bitcast.1.core.which, bf16[2,128,256]{2,1,0:T(8,128)(2,1)S(1)} %get-tuple-element.28.refs_0_, bf16[2,128,256]{2,1,0:T(8,128)(2,1)S(1)} %collective-permute-done.4.refs_1_, bf16[2,128,256]{2,1,0:T(8,128)(2,1)S(1)} %collective-permute-done.5.refs_2_, ...), custom_call_target="tpu_custom_call" | custom-call | tf_op jit(solution)/shard_map/down_gradient/pallas_call | solution.py:378
  99.4 0.0 copy-start.2
  99.4 10.5 %all-to-all-start.1 = ((bf16[64,16,384]{2,1,0:T(8,128)(2,1)}), bf16[64,16,384]{2,1,0:T(8,128)(2,1)S(1)}, u32[]{:S(2)}, u32[]{:S(2)}) async-start(bf16[64,16,384]{2,1,0:T(8,128)(2,1)} %bitcast.13), calls=%async_computation.1 | async-start | bytes 1572864 | tf_op jit(solution)/shard_map/all_to_all | solution.py:492
  109.9 1.1 collective-permute-start
  111.0 1.7 %collective-permute-start.2 = (bf16[2,256,256]{2,1,0:T(8,128)(2,1)}, bf16[2,256,256]{2,1,0:T(8,128)(2,1)S(1)}, u32[]{:S(2)}, u32[]{:S(2)}) collective-permute-start(bf16[2,256,256]{2,1,0:T(8,128)(2,1)} %copy-done.3), channel_id=1, source_target_pairs={{0,6},{2,0},{4,2},{6,4},{1,7},{3,1},{5,3},{7,5},{8,14},{10,8},{12,... | collective-permute-start | bytes 786440 | tf_op jit(solution)/shard_map/ppermute | solution.py:521
  112.7 14.2 %collective-permute-done.part_1.refs_0_ = bf16[2,256,256]{2,1,0:T(8,128)(2,1)S(1)} collective-permute-done((bf16[2,256,256]{2,1,0:T(8,128)(2,1)}, bf16[2,256,256]{2,1,0:T(8,128)(2,1)S(1)}, u32[]{:S(2)}, u32[]{:S(2)}) %collective-permute-start) | collective-permute-done | bytes 262176 | tf_op jit(solution)/shard_map/ppermute | solution.py:521
  126.9 1.1 sum_share.1
  127.9 8.2 %all-to-all-start.2 = ((bf16[64,16,384]{2,1,0:T(8,128)(2,1)}), bf16[64,16,384]{2,1,0:T(8,128)(2,1)S(1)}, u32[]{:S(2)}, u32[]{:S(2)}) async-start(bf16[64,16,384]{2,1,0:T(8,128)(2,1)} %sum_share.1), calls=%async_computation.2 | async-start | bytes 1572864 | tf_op jit(solution)/shard_map/all_to_all | solution.py:492
  136.2 2.6 %collective-permute-start.1 = (bf16[2,256,256]{2,1,0:T(8,128)(2,1)S(1)}, bf16[2,256,256]{2,1,0:T(8,128)(2,1)S(1)}, u32[]{:S(2)}, u32[]{:S(2)}) collective-permute-start(bf16[2,256,256]{2,1,0:T(8,128)(2,1)S(1)} %copy-done.2), channel_id=1, source_target_pairs={{0,4},{2,6},{4,0},{6,2},{1,5},{3,7},{5,1},{7,3},{8,12},{10,14},{12... | collective-permute-start | bytes 786440 | tf_op jit(solution)/shard_map/ppermute | solution.py:521
  138.8 11.4 %all-to-all-done.2 = bf16[64,16,384]{2,1,0:T(8,128)(2,1)S(1)} async-done(((bf16[64,16,384]{2,1,0:T(8,128)(2,1)}), bf16[64,16,384]{2,1,0:T(8,128)(2,1)S(1)}, u32[]{:S(2)}, u32[]{:S(2)}) %all-to-all-start.2) | async-done | bytes 786464 | tf_op jit(solution)/shard_map/all_to_all | solution.py:492
  150.2 3.0 %collective-permute-start.12 = (bf16[8,8,16,384]{3,2,1,0:T(8,128)(2,1)S(1)}, bf16[8,8,16,384]{3,2,1,0:T(8,128)(2,1)S(1)}, u32[]{:S(2)}, u32[]{:S(2)}) collective-permute-start(bf16[8,8,16,384]{3,2,1,0:T(8,128)(2,1)S(1)} %bitcast.20), channel_id=1, source_target_pairs={{0,1},{1,0},{2,3},{3,2},{4,5},{5,4},{6,7},{7,6},{8,9},{9,8},{10,11... | collective-permute-start | bytes 2359304 | tf_op jit(solution)/shard_map/ppermute | solution.py:496
  153.1 0.0 collective-permute-done.1.part_2.refs_0_
  153.1 0.6 pick.1
  153.7 1.2 collective-permute-start.3
  154.9 1.5 collective-permute-done.3.other
  156.4 1.6 %arrive.1 = bf16[1,256,2048]{2,1,0:T(8,128)(2,1)} custom-call(s32[2]{0:T(128)S(1)} %pad_add_fusion.where, bf16[2,256,256]{2,1,0:T(8,128)(2,1)S(1)} %get-tuple-element.24.part_0, bf16[2,256,256]{2,1,0:T(8,128)(2,1)S(1)} %collective-permute-done.part_1.refs_0_, bf16[2,256,256]{2,1,0:T(8,128)(2,1)S(1)} %collective-permute-done.1.part_2.refs_0_, ...), custom_call_target="tpu_custom_call" | custom-call | tf_op jit(solution)/shard_map/arrive/pallas_call | solution.py:340
  158.0 1.5 place.2
  159.6 0.0 collective-permute-done.12.shares
  159.6 1.5 place.3
  (9 shorter events, 0.0 us)
Async XLA Ops:
  8.2 6.1 %copy-start = (bf16[1,256,4096]{2,1,0:T(8,128)(2,1)S(1)}, bf16[1,256,4096]{2,1,0:T(8,128)(2,1)}, u32[]{:S(2)}) copy-start(bf16[1,256,4096]{2,1,0:T(8,128)(2,1)} %param.10) | copy-start | bytes 6291460
  8.2 7.3 %copy-start.5 = (s32[1,8]{1,0:T(1,128)S(1)}, s32[1,8]{1,0:T(1,128)}, u32[]{:S(2)}) copy-start(s32[1,8]{1,0:T(1,128)} %param.14) | copy-start | bytes 100
  8.2 60.6 %all-to-all-start = ((bf16[8,256,1152]{2,1,0:T(8,128)(2,1)}), bf16[8,256,1152]{2,1,0:T(8,128)(2,1)}, u32[]{:S(2)}, u32[]{:S(2)}) async-start(bf16[8,256,1152]{2,1,0:T(8,128)(2,1)} %pack.1), calls=%async_computation | async-start | bytes 9437184 | tf_op jit(solution)/shard_map/all_to_all | solution.py:492
  15.3 82.2 %collective-permute-start.11 = (bf16[256,2048]{1,0:T(8,128)(2,1)}, bf16[256,2048]{1,0:T(8,128)(2,1)S(1)}, u32[]{:S(2)}, u32[]{:S(2)}) collective-permute-start(bf16[256,2048]{1,0:T(8,128)(2,1)} %dynamic-slice_bitcast_fusion), channel_id=1, source_target_pairs={{0,1},{1,0},{2,3},{3,2},{4,5},{5,4},{6,7},{7,6},{8,9},{9,8},{10,11... | collective-permute-start | bytes 3145736 | tf_op jit(solution)/shard_map/ppermute | solution.py:496
  84.9 14.5 %copy-start.1 = (bf16[2,256,256]{2,1,0:T(8,128)(2,1)}, bf16[2,256,256]{2,1,0:T(8,128)(2,1)S(1)}, u32[]{:S(2)}) copy-start(bf16[2,256,256]{2,1,0:T(8,128)(2,1)S(1)} %get-tuple-element.26) | copy-start | bytes 786436
  84.9 14.5 %copy-start.3 = (bf16[2,256,256]{2,1,0:T(8,128)(2,1)}, bf16[2,256,256]{2,1,0:T(8,128)(2,1)S(1)}, u32[]{:S(2)}) copy-start(bf16[2,256,256]{2,1,0:T(8,128)(2,1)S(1)} %get-tuple-element.27) | copy-start | bytes 786436
  84.9 14.5 %copy-start.4 = (bf16[2,256,256]{2,1,0:T(8,128)(2,1)}, bf16[2,256,256]{2,1,0:T(8,128)(2,1)S(1)}, u32[]{:S(2)}) copy-start(bf16[2,256,256]{2,1,0:T(8,128)(2,1)S(1)} %get-tuple-element.25) | copy-start | bytes 786436
  84.9 6.7 %collective-permute-start.4 = (bf16[2,128,256]{2,1,0:T(8,128)(2,1)S(1)}, bf16[2,128,256]{2,1,0:T(8,128)(2,1)S(1)}, u32[]{:S(2)}, u32[]{:S(2)}) collective-permute-start(bf16[2,128,256]{2,1,0:T(8,128)(2,1)S(1)} %get-tuple-element.29), channel_id=1, source_target_pairs={{0,2},{2,4},{4,6},{6,0},{1,3},{3,5},{5,7},{7,1},{8,10},{10,12},{12... | collective-permute-start | bytes 393224 | tf_op jit(solution)/shard_map/ppermute | solution.py:521
  85.5 9.6 %collective-permute-start.5 = (bf16[2,128,256]{2,1,0:T(8,128)(2,1)S(1)}, bf16[2,128,256]{2,1,0:T(8,128)(2,1)S(1)}, u32[]{:S(2)}, u32[]{:S(2)}) collective-permute-start(bf16[2,128,256]{2,1,0:T(8,128)(2,1)S(1)} %get-tuple-element.30), channel_id=1, source_target_pairs={{0,4},{2,6},{4,0},{6,2},{1,5},{3,7},{5,1},{7,3},{8,12},{10,14},{12... | collective-permute-start | bytes 393224 | tf_op jit(solution)/shard_map/ppermute | solution.py:521
  87.2 7.9 %collective-permute-start.6 = (bf16[2,128,256]{2,1,0:T(8,128)(2,1)S(1)}, bf16[2,128,256]{2,1,0:T(8,128)(2,1)S(1)}, u32[]{:S(2)}, u32[]{:S(2)}) collective-permute-start(bf16[2,128,256]{2,1,0:T(8,128)(2,1)S(1)} %get-tuple-element.31), channel_id=1, source_target_pairs={{0,6},{2,0},{4,2},{6,4},{1,7},{3,1},{5,3},{7,5},{8,14},{10,8},{12,... | collective-permute-start | bytes 393224 | tf_op jit(solution)/shard_map/ppermute | solution.py:521
  87.9 9.6 %collective-permute-start.7 = (bf16[2,128,256]{2,1,0:T(8,128)(2,1)S(1)}, bf16[2,128,256]{2,1,0:T(8,128)(2,1)S(1)}, u32[]{:S(2)}, u32[]{:S(2)}) collective-permute-start(bf16[2,128,256]{2,1,0:T(8,128)(2,1)S(1)} %get-tuple-element.28.refs_0_), channel_id=1, source_target_pairs={{0,1},{1,0},{2,3},{3,2},{4,5},{5,4},{6,7},{7,6},{8,9},{9,8},{10,11... | collective-permute-start | bytes 393224 | tf_op jit(solution)/shard_map/ppermute | solution.py:496
  91.6 6.0 %collective-permute-start.8 = (bf16[2,128,256]{2,1,0:T(8,128)(2,1)S(1)}, bf16[2,128,256]{2,1,0:T(8,128)(2,1)S(1)}, u32[]{:S(2)}, u32[]{:S(2)}) collective-permute-start(bf16[2,128,256]{2,1,0:T(8,128)(2,1)S(1)} %collective-permute-done.4.refs_1_), channel_id=1, source_target_pairs={{0,1},{1,0},{2,3},{3,2},{4,5},{5,4},{6,7},{7,6},{8,9},{9,8},{10,11... | collective-permute-start | bytes 393224 | tf_op jit(solution)/shard_map/ppermute | solution.py:496
  95.1 2.5 %collective-permute-start.9 = (bf16[2,128,256]{2,1,0:T(8,128)(2,1)S(1)}, bf16[2,128,256]{2,1,0:T(8,128)(2,1)S(1)}, u32[]{:S(2)}, u32[]{:S(2)}) collective-permute-start(bf16[2,128,256]{2,1,0:T(8,128)(2,1)S(1)} %collective-permute-done.5.refs_2_), channel_id=1, source_target_pairs={{0,1},{1,0},{2,3},{3,2},{4,5},{5,4},{6,7},{7,6},{8,9},{9,8},{10,11... | collective-permute-start | bytes 393224 | tf_op jit(solution)/shard_map/ppermute | solution.py:496
  95.1 2.5 %collective-permute-start.10 = (bf16[2,128,256]{2,1,0:T(8,128)(2,1)S(1)}, bf16[2,128,256]{2,1,0:T(8,128)(2,1)S(1)}, u32[]{:S(2)}, u32[]{:S(2)}) collective-permute-start(bf16[2,128,256]{2,1,0:T(8,128)(2,1)S(1)} %collective-permute-done.6.refs_3_), channel_id=1, source_target_pairs={{0,1},{1,0},{2,3},{3,2},{4,5},{5,4},{6,7},{7,6},{8,9},{9,8},{10,11... | collective-permute-start | bytes 393224 | tf_op jit(solution)/shard_map/ppermute | solution.py:496
  99.4 36.8 %copy-start.2 = (bf16[2,256,256]{2,1,0:T(8,128)(2,1)S(1)}, bf16[2,256,256]{2,1,0:T(8,128)(2,1)}, u32[]{:S(2)}) copy-start(bf16[2,256,256]{2,1,0:T(8,128)(2,1)} %copy-done.1) | copy-start | bytes 786436
  99.4 27.4 %all-to-all-start.1 = ((bf16[64,16,384]{2,1,0:T(8,128)(2,1)}), bf16[64,16,384]{2,1,0:T(8,128)(2,1)S(1)}, u32[]{:S(2)}, u32[]{:S(2)}) async-start(bf16[64,16,384]{2,1,0:T(8,128)(2,1)} %bitcast.13), calls=%async_computation.1 | async-start | bytes 1572864 | tf_op jit(solution)/shard_map/all_to_all | solution.py:492
  109.9 16.9 %collective-permute-start = (bf16[2,256,256]{2,1,0:T(8,128)(2,1)}, bf16[2,256,256]{2,1,0:T(8,128)(2,1)S(1)}, u32[]{:S(2)}, u32[]{:S(2)}) collective-permute-start(bf16[2,256,256]{2,1,0:T(8,128)(2,1)} %copy-done.4), channel_id=1, source_target_pairs={{0,2},{2,4},{4,6},{6,0},{1,3},{3,5},{5,7},{7,1},{8,10},{10,12},{12... | collective-permute-start | bytes 786440 | tf_op jit(solution)/shard_map/ppermute | solution.py:521
  111.0 15.8 %collective-permute-start.2 = (bf16[2,256,256]{2,1,0:T(8,128)(2,1)}, bf16[2,256,256]{2,1,0:T(8,128)(2,1)S(1)}, u32[]{:S(2)}, u32[]{:S(2)}) collective-permute-start(bf16[2,256,256]{2,1,0:T(8,128)(2,1)} %copy-done.3), channel_id=1, source_target_pairs={{0,6},{2,0},{4,2},{6,4},{1,7},{3,1},{5,3},{7,5},{8,14},{10,8},{12,... | collective-permute-start | bytes 786440 | tf_op jit(solution)/shard_map/ppermute | solution.py:521
  127.9 22.3 %all-to-all-start.2 = ((bf16[64,16,384]{2,1,0:T(8,128)(2,1)}), bf16[64,16,384]{2,1,0:T(8,128)(2,1)S(1)}, u32[]{:S(2)}, u32[]{:S(2)}) async-start(bf16[64,16,384]{2,1,0:T(8,128)(2,1)} %sum_share.1), calls=%async_computation.2 | async-start | bytes 1572864 | tf_op jit(solution)/shard_map/all_to_all | solution.py:492
  136.2 16.9 %collective-permute-start.1 = (bf16[2,256,256]{2,1,0:T(8,128)(2,1)S(1)}, bf16[2,256,256]{2,1,0:T(8,128)(2,1)S(1)}, u32[]{:S(2)}, u32[]{:S(2)}) collective-permute-start(bf16[2,256,256]{2,1,0:T(8,128)(2,1)S(1)} %copy-done.2), channel_id=1, source_target_pairs={{0,4},{2,6},{4,0},{6,2},{1,5},{3,7},{5,1},{7,3},{8,12},{10,14},{12... | collective-permute-start | bytes 786440 | tf_op jit(solution)/shard_map/ppermute | solution.py:521
  150.2 9.4 %collective-permute-start.12 = (bf16[8,8,16,384]{3,2,1,0:T(8,128)(2,1)S(1)}, bf16[8,8,16,384]{3,2,1,0:T(8,128)(2,1)S(1)}, u32[]{:S(2)}, u32[]{:S(2)}) collective-permute-start(bf16[8,8,16,384]{3,2,1,0:T(8,128)(2,1)S(1)} %bitcast.20), channel_id=1, source_target_pairs={{0,1},{1,0},{2,3},{3,2},{4,5},{5,4},{6,7},{7,6},{8,9},{9,8},{10,11... | collective-permute-start | bytes 2359304 | tf_op jit(solution)/shard_map/ppermute | solution.py:496
  153.7 2.7 %collective-permute-start.3 = (bf16[4,256,256]{2,1,0:T(8,128)(2,1)S(1)}, bf16[4,256,256]{2,1,0:T(8,128)(2,1)S(1)}, u32[]{:S(2)}, u32[]{:S(2)}) collective-permute-start(bf16[4,256,256]{2,1,0:T(8,128)(2,1)S(1)} %pick.1), channel_id=1, source_target_pairs={{0,1},{1,0},{2,3},{3,2},{4,5},{5,4},{6,7},{7,6},{8,9},{9,8},{10,11... | collective-permute-start | bytes 1572872 | tf_op jit(solution)/shard_map/ppermute | solution.py:496

commit v6 on v5

--- a/solution.py
+++ b/solution.py
@@ -157,7 +157,7 @@
 def attention_kernel(
     meta, packed, wq_up, wv_up, *refs
 ):
-    *outs, dq_t, dv_t, low, q_t, k_t, v_t, g_t, dv, returned, out = refs
+    *outs, dq_t, dv_t, low, q_t, k_t, v_t, g_t, dv, returned, out = refs[1:]
     outs, backs = outs[: len(outs) // 2], outs[len(outs) // 2 :]
     length = packed.shape[0]
     heads = out.shape[1] // HEAD_SIZE
@@ -246,7 +246,7 @@
             outs[step][holder] = out[pl.ds(begin, rows), :]
 
 
-def attention(meta, packed, wq_up, wv_up, seq_size):
+def attention(meta, packed, wq_up, wv_up, seq_size, after):
     length = packed.shape[0]
     width = (packed.shape[1] - 2 * RANK) // 4
     rows = length // seq_size
@@ -257,7 +257,7 @@
     grad_t = jax.ShapeDtypeStruct((width, length), jnp.bfloat16)
     return pl.pallas_call(
         attention_kernel,
-        in_specs=[SMEM, VMEM, VMEM, VMEM],
+        in_specs=[SMEM, VMEM, VMEM, VMEM, VMEM],
         out_specs=[VMEM] * (3 + 2 * chips),
         scratch_shapes=[
             wide_t,
@@ -276,10 +276,11 @@
             flops=8 << 30, bytes_accessed=16 << 20, transcendentals=4 << 20
         ),
         name="attention",
-    )(meta, packed, wq_up, wv_up)
-
-
-def up_kernel(where, low, dq_t, dv_t, up):
+    )(meta, packed, wq_up, wv_up, after)
+
+
+def up_kernel(where, low, dq_t, dv_t, *refs):
+    up = refs[len(refs) // 2]
     width = dq_t.shape[0]
     lane = lax.broadcasted_iota(jnp.int32, (width, up.shape[1]), 1)
     source = lax.broadcasted_iota(jnp.int32, (width, up.shape[1]), 0)
@@ -294,16 +295,18 @@
         )
 
 
-def up_gradient(where, low, dq_t, dv_t):
+def up_gradient(where, low, dq_t, dv_t, held):
     width = dq_t.shape[0]
     return pl.pallas_call(
         up_kernel,
-        in_specs=[SMEM] + [VMEM] * 3,
-        out_specs=VMEM,
-        out_shape=jax.ShapeDtypeStruct((2 * RANK, width // UP_COLS * 128), jnp.bfloat16),
+        in_specs=[SMEM] + [VMEM] * (3 + len(held)),
+        out_specs=[VMEM] * (1 + len(held)),
+        out_shape=[jax.ShapeDtypeStruct((2 * RANK, width // UP_COLS * 128), jnp.bfloat16)]
+        + [jax.ShapeDtypeStruct(part.shape, part.dtype) for part in held],
+        input_output_aliases={4 + index: 1 + index for index in range(len(held))},
         compiler_params=pltpu.CompilerParams(vmem_limit_bytes=16 << 20),
         name="up_gradient",
-    )(where, low, dq_t, dv_t)
+    )(where, low, dq_t, dv_t, *held)
 
 
 def pick_kernel(where, part_0, part_1, part_2, part_3, out):
@@ -348,7 +351,8 @@
 
 
 def down_kernel(core, *refs):
-    *parts, hidden, hidden_other, up, out, back = refs
+    parts, (hidden, hidden_other, up) = refs[:8], refs[8:11]
+    out, back = refs[-2:]
 
     @pl.when(pl.program_id(0) == 0)
     def _():
@@ -368,7 +372,7 @@
             out[row, column, :, DOWN_COLS:] = up[across, column * 128 : (column + 1) * 128]
 
 
-def down_gradient(core, parts, hidden, hidden_other, up):
+def down_gradient(core, parts, hidden, hidden_other, up, after):
     rows, half = hidden_other.shape
     steps = 2
     step = half // steps
@@ -385,7 +389,8 @@
                 pl.BlockSpec((rows, step), lambda i, core: (0, core[0] * steps + i)),
                 pl.BlockSpec((rows, step), lambda i, core: (0, i)),
                 pl.BlockSpec((2 * RANK, columns // steps * 128), lambda i, core: (0, i)),
-            ],
+            ]
+            + [VMEM] * len(after),
             out_specs=pl.BlockSpec(
                 (across, columns // steps, SHARE_ROWS, DOWN_COLS + 128),
                 lambda i, core: (0, i, 0, 0),
@@ -397,7 +402,7 @@
         ),
         compiler_params=pltpu.CompilerParams(vmem_limit_bytes=24 << 20),
         name="down_gradient",
-    )(core, *parts, hidden, hidden_other, up)
+    )(core, *parts, hidden, hidden_other, up, *after)
 
 
 def share_kernel(parts, *refs):
@@ -467,13 +472,13 @@
         copy.wait()
 
 
-def place(which, shares, model, width, earlier=(), after=()):
+def place(which, shares, model, width, earlier=()):
     shapes = [(RANK, model), (RANK, width), (RANK, model), (RANK, width)]
     columns = shares.shape[1]
     chips = 128 // UP_COLS
     return pl.pallas_call(
         place_kernel,
-        in_specs=[SMEM, VMEM] + [ANY] * len(earlier) + [VMEM] * len(after),
+        in_specs=[SMEM, VMEM] + [ANY] * len(earlier),
         out_specs=[ANY] * 4,
         out_shape=[jax.ShapeDtypeStruct(shape, jnp.float32) for shape in shapes],
         scratch_shapes=[
@@ -485,7 +490,7 @@
         input_output_aliases={2 + index: index for index in range(len(earlier))},
         compiler_params=pltpu.CompilerParams(vmem_limit_bytes=16 << 20),
         name="place",
-    )(which[None], shares, *earlier, *after)
+    )(which[None], shares, *earlier)
 
 
 def swap(x, axes):
@@ -541,20 +546,29 @@
     wq_up = lax.dynamic_slice(query_up_weight, own_columns, (RANK, width))
     wv_up = lax.dynamic_slice(value_up_weight, own_columns, (RANK, width))
     meta = jnp.concatenate([document_length_list[0], where])
-    *outs, dq_t, dv_t, low = attention(meta, received, wq_up, wv_up, seq_size)
+    *outs, dq_t, dv_t, low = attention(
+        meta, received, wq_up, wv_up, seq_size, after=hidden_other
+    )
     parts, backs = outs[:chips], outs[chips:]
 
     backs = [backs[0]] + [to_chip(backs[step], step) for step in range(1, chips)]
     backs_other = [to_other_core(back) for back in backs]
-    parts = [parts[0]] + [to_chip(parts[step], step) for step in range(1, chips)]
-    up = up_gradient(where, low, dq_t, dv_t)
-    down = down_gradient(core[None], backs + backs_other, hidden[0], hidden_other, up)
+    up, *held = up_gradient(where, low, dq_t, dv_t, parts[1:])
+    parts = [parts[0]] + [to_chip(held[step - 1], step) for step in range(1, chips)]
+    down = down_gradient(
+        core[None],
+        backs + backs_other,
+        hidden[0],
+        hidden_other,
+        up,
+        after=[parts[1], parts[3]],
+    )
 
     shares = swap(down.reshape((-1,) + down.shape[2:]), PLANE)
-    shares = swap(sum_share(shares, after=[parts[1], parts[3]]), PLANE).reshape(down.shape)
+    shares = swap(sum_share(shares, after=[parts[2]]), PLANE).reshape(down.shape)
     attended = arrive(where, parts, to_other_core(pick(where, parts)))
     shares_other = to_other_core(shares)
-    grads = place(core, shares, model, seq_size * width, after=[parts[2]])
+    grads = place(core, shares, model, seq_size * width)
     grad_a_q, up_q, grad_a_v, up_v = place(
         1 - core, shares_other, model, seq_size * width, earlier=grads
     )

time: 162 us -> 168 us (1.037)
  blocking collectives: 0 us -> 22.2 us
  starting transfers between devices: 43 us -> 33.5 us
  waiting for transfers between devices: 81.9 us -> 75.3 us
    all_to_all x0 -> x1, blocking collectives: none -> 22.2 us  [swap(): return lax.all_to_all(x, axes, 0, 0, tiled=True)]
    all_to_all x3 -> x2, waiting for transfers between devices: 63.9 us -> 50.6 us  [swap(): return lax.all_to_all(x, axes, 0, 0, tiled=True)]
    all_to_all x3 -> x2, starting transfers between devices: 24.9 us -> 17.8 us  [swap(): return lax.all_to_all(x, axes, 0, 0, tiled=True)]
    ppermute x7, waiting for transfers between devices: 1.55 us -> 5.21 us  [to_other_core(): return lax.ppermute(x, 'core', [(0, 1), (1, 0)])]
    ppermute x6, waiting for transfers between devices: 16.4 us -> 19.5 us  [to_chip(): return lax.ppermute(x, 'y', [(c, (c + step) % chips) for c in range(chips)])]
  transfers between devices with their start and end apart: 16 -> 15, of which waited for: 5 -> 7; matrix products, arithmetic and copies ran while one was open for 1% -> 1% of each run, Pallas kernels for 13% -> 3%
where the time goes in v6:
time: 168 us
  waiting for transfers between devices  75.3 us (45%)
  starting transfers between devices  33.5 us (20%)
  Pallas kernels  32.5 us (19%)
  blocking collectives  22.2 us (13%)
  local copies, waits for them, and re-layouts  3.07 us (2%)
    all_to_all x2, waiting for transfers between devices, swap(): return lax.all_to_all(x, axes, 0, 0, tiled=True)  50.6 us
    all_to_all x1, blocking collectives, swap(): return lax.all_to_all(x, axes, 0, 0, tiled=True)  22.2 us
    ppermute x6, waiting for transfers between devices, to_chip(): return lax.ppermute(x, 'y', [(c, (c + step) % chips) for c in range(chips)])  19.5 us
    all_to_all x2, starting transfers between devices, swap(): return lax.all_to_all(x, axes, 0, 0, tiled=True)  17.8 us
    pallas_call x1, Pallas kernels, attention(): pl.pallas_call(attention_kernel, in_specs=[SMEM, VMEM, VMEM, VMEM, VMEM],...  16 us
    ppermute x7, starting transfers between devices, to_other_core(): return lax.ppermute(x, 'core', [(0, 1), (1, 0)])  8.56 us
    pallas_call x1, Pallas kernels, pack(): pl.pallas_call(pack_kernel, in_specs=[ANY] * 9, out_specs=ANY, out_shape=...  7.52 us
    ppermute x6, starting transfers between devices, to_chip(): return lax.ppermute(x, 'y', [(c, (c + step) % chips) for c in range(chips)])  7.14 us
  transfers between devices with their start and end apart: 15, of which 7 were waited for; matrix products, arithmetic and copies ran while one was open for 1% of the time, Pallas kernels for 3%

profile of v6, /device:TPU:1, one launch (start us, length us, event | category | flops | bytes accessed | tf_op | source)
XLA Modules:
  0.0 167.7 jit_solution(15027023053419398940)
XLA Ops:
  0.6 7.5 %pack.1 = bf16[8,256,1152]{2,1,0:T(8,128)(2,1)} custom-call(bf16[256,4096]{1,0:T(8,128)(2,1)} %bitcast.18, bf16[64,4096]{1,0:T(8,128)(2,1)} %bitcast.28, bf16[64,4096]{1,0:T(8,128)(2,1)} %bitcast.29, bf16[256,2048]{1,0:T(8,128)(2,1)} %bitcast.22, bf16[256,2048]{1,0:T(8,128)(2,1)} %bitcast.23, bf16[256,2048]{1,0:T(8,128)(2,1)} %bitcast.24, ...), custom_call_target="tpu_custom_call" | custom-call | tf_op jit(solution)/shard_map/pack/pallas_call | solution.py:131
  8.2 0.0 copy-start
  8.2 0.0 copy-start.4
  8.2 6.1 %all-to-all-start = ((bf16[8,256,1152]{2,1,0:T(8,128)(2,1)}), bf16[8,256,1152]{2,1,0:T(8,128)(2,1)}, u32[]{:S(2)}, u32[]{:S(2)}) async-start(bf16[8,256,1152]{2,1,0:T(8,128)(2,1)} %pack.1), calls=%async_computation | async-start | bytes 9437184 | tf_op jit(solution)/shard_map/all_to_all | solution.py:497
  14.3 1.0 dynamic-slice_bitcast_fusion
  15.3 0.1 collective-permute-start
  15.5 0.1 pad_add_fusion.1.meta
  15.5 0.8 constant_dynamic-slice_fusion
  16.3 1.9 %collective-permute-done.refs_0_.refs_9_ = bf16[256,2048]{1,0:T(8,128)(2,1)S(1)} collective-permute-done((bf16[256,2048]{1,0:T(8,128)(2,1)}, bf16[256,2048]{1,0:T(8,128)(2,1)S(1)}, u32[]{:S(2)}, u32[]{:S(2)}) %collective-permute-start) | collective-permute-done | bytes 1048608 | tf_op jit(solution)/shard_map/ppermute | solution.py:501
  18.2 50.6 %all-to-all-done = bf16[8,256,1152]{2,1,0:T(8,128)(2,1)} async-done(((bf16[8,256,1152]{2,1,0:T(8,128)(2,1)}), bf16[8,256,1152]{2,1,0:T(8,128)(2,1)}, u32[]{:S(2)}, u32[]{:S(2)}) %all-to-all-start) | async-done | bytes 4718624 | tf_op jit(solution)/shard_map/all_to_all | solution.py:497
  68.8 16.0 %attention.1 = (bf16[2,256,256]{2,1,0:T(8,128)(2,1)S(1)}, bf16[2,256,256]{2,1,0:T(8,128)(2,1)S(1)}, bf16[2,256,256]{2,1,0:T(8,128)(2,1)S(1)}, bf16[2,256,256]{2,...) custom-call(s32[10]{0:T(128)S(1)} %pad_add_fusion.1.meta, ...), custom_call_target="tpu_custom_call" | custom-call | flops 8589934592 | bytes 16777216 | tf_op jit(solution)/shard_map/attention/pallas_call | solution.py:258
  84.9 0.5 collective-permute-start.5
  85.4 0.1 pad_add_fusion.where
  85.5 1.8 %up_gradient.1 = (bf16[128,1024]{1,0:T(8,128)(2,1)S(1)}, bf16[2,256,256]{2,1,0:T(8,128)(2,1)S(1)}, bf16[2,256,256]{2,1,0:T(8,128)(2,1)S(1)}, bf16[2,256,256]{2,1,0:T(8,128)(2,1)S(1)}) custom-call(s32[2]{0:T(128)S(1)} %pad_add_fusion.where, bf16[2048,128]{1,0:T(8,128)(2,1)S(1)} %get-tuple-element.29.low, ...), custom_call_target="tpu_custom_call", output_to_operand_aliasing={{1}: (4, {}), {2}: (5, {}), {3}: (6, {})} | custom-call | tf_op jit(solution)/shard_map/up_gradient/pallas_call | solution.py:300
  87.3 0.0 copy-start.3
  87.3 0.1 collective-permute-start.1
  87.4 2.7 %collective-permute-start.3 = (bf16[2,256,256]{2,1,0:T(8,128)(2,1)S(1)}, bf16[2,256,256]{2,1,0:T(8,128)(2,1)S(1)}, u32[]{:S(2)}, u32[]{:S(2)}) collective-permute-start(bf16[2,256,256]{2,1,0:T(8,128)(2,1)S(1)} %get-tuple-element.37), channel_id=1, source_target_pairs={{0,6},{2,0},{4,2},{6,4},{1,7},{3,1},{5,3},{7,5},{8,14},{10,8},{12,... | collective-permute-start | bytes 786440 | tf_op jit(solution)/shard_map/ppermute | solution.py:526
  90.0 0.9 collective-permute-start.6
  90.9 0.4 collective-permute-start.7
  91.3 0.0 collective-permute-done.5.refs_1_
  91.3 2.0 %collective-permute-start.8 = (bf16[2,128,256]{2,1,0:T(8,128)(2,1)S(1)}, bf16[2,128,256]{2,1,0:T(8,128)(2,1)S(1)}, u32[]{:S(2)}, u32[]{:S(2)}) collective-permute-start(bf16[2,128,256]{2,1,0:T(8,128)(2,1)S(1)} %get-tuple-element.38.refs_0_), channel_id=1, source_target_pairs={{0,1},{1,0},{2,3},{3,2},{4,5},{5,4},{6,7},{7,6},{8,9},{9,8},{10,11... | collective-permute-start | bytes 393224 | tf_op jit(solution)/shard_map/ppermute | solution.py:501
  93.3 5.3 %collective-permute-done.6.refs_2_ = bf16[2,128,256]{2,1,0:T(8,128)(2,1)S(1)} collective-permute-done((bf16[2,128,256]{2,1,0:T(8,128)(2,1)S(1)}, bf16[2,128,256]{2,1,0:T(8,128)(2,1)S(1)}, u32[]{:S(2)}, u32[]{:S(2)}) %collective-permute-start.6) | collective-permute-done | bytes 131104 | tf_op jit(solution)/shard_map/ppermute | solution.py:526
  98.6 2.4 %collective-permute-start.9 = (bf16[2,128,256]{2,1,0:T(8,128)(2,1)S(1)}, bf16[2,128,256]{2,1,0:T(8,128)(2,1)S(1)}, u32[]{:S(2)}, u32[]{:S(2)}) collective-permute-start(bf16[2,128,256]{2,1,0:T(8,128)(2,1)S(1)} %collective-permute-done.5.refs_1_), channel_id=1, source_target_pairs={{0,1},{1,0},{2,3},{3,2},{4,5},{5,4},{6,7},{7,6},{8,9},{9,8},{10,11... | collective-permute-start | bytes 393224 | tf_op jit(solution)/shard_map/ppermute | solution.py:501
  101.0 0.0 collective-permute-done.7.refs_3_
  101.0 1.2 collective-permute-start.10
  102.2 0.0 collective-permute-done.8.refs_4_
  102.2 0.0 collective-permute-start.11
  102.2 0.0 collective-permute-done.1.part_1.refs_11_
  102.2 0.0 collective-permute-done.3.part_3.refs_12_
  102.2 0.0 collective-permute-done.9.refs_5_
  102.2 1.0 collective-permute-done.10.refs_6_
  103.2 0.4 collective-permute-done.11.refs_7_
  103.5 1.2 copy-done.2
  104.8 1.7 %down_gradient.1 = bf16[8,8,16,384]{3,2,1,0:T(8,128)(2,1)} custom-call(s32[1]{0:T(128)} %bitcast.1.core.which, bf16[2,128,256]{2,1,0:T(8,128)(2,1)S(1)} %get-tuple-element.38.refs_0_, bf16[2,128,256]{2,1,0:T(8,128)(2,1)S(1)} %collective-permute-done.5.refs_1_, bf16[2,128,256]{2,1,0:T(8,128)(2,1)S(1)} %collective-permute-done.6.refs_2_, ...), custom_call_target="tpu_custom_call" | custom-call | tf_op jit(solution)/shard_map/down_gradient/pallas_call | solution.py:382
  106.5 11.7 %all-to-all-start.1 = ((bf16[64,16,384]{2,1,0:T(8,128)(2,1)}), bf16[64,16,384]{2,1,0:T(8,128)(2,1)S(1)}, u32[]{:S(2)}, u32[]{:S(2)}) async-start(bf16[64,16,384]{2,1,0:T(8,128)(2,1)} %bitcast.13), calls=%async_computation.1 | async-start | bytes 1572864 | tf_op jit(solution)/shard_map/all_to_all | solution.py:497
  118.2 2.6 %collective-permute-start.2 = (bf16[2,256,256]{2,1,0:T(8,128)(2,1)}, bf16[2,256,256]{2,1,0:T(8,128)(2,1)S(1)}, u32[]{:S(2)}, u32[]{:S(2)}) collective-permute-start(bf16[2,256,256]{2,1,0:T(8,128)(2,1)} %copy-done.3), channel_id=1, source_target_pairs={{0,4},{2,6},{4,0},{6,2},{1,5},{3,7},{5,1},{7,3},{8,12},{10,14},{12... | collective-permute-start | bytes 786440 | tf_op jit(solution)/shard_map/ppermute | solution.py:526
  120.8 14.1 %collective-permute-done.2.part_2.refs_0_ = bf16[2,256,256]{2,1,0:T(8,128)(2,1)S(1)} collective-permute-done((bf16[2,256,256]{2,1,0:T(8,128)(2,1)}, bf16[2,256,256]{2,1,0:T(8,128)(2,1)S(1)}, u32[]{:S(2)}, u32[]{:S(2)}) %collective-permute-start.2) | collective-permute-done | bytes 262176 | tf_op jit(solution)/shard_map/ppermute | solution.py:526
  135.0 0.0 all-to-all-done.1.parts
  135.0 0.2 sum_share.1
  135.1 22.2 %all_to_all.15 = bf16[64,16,384]{2,1,0:T(8,128)(2,1)S(1)} all-to-all(bf16[64,16,384]{2,1,0:T(8,128)(2,1)S(1)} %sum_share.1), channel_id=1, replica_groups=mesh['x'=4,'z'=4,'y'=4,'core'=2] {'x','z','y'}, dimensions={0} | all-to-all | bytes 1572864 | tf_op jit(solution)/shard_map/all_to_all | solution.py:497
  157.4 2.8 %collective-permute-start.12 = (bf16[8,8,16,384]{3,2,1,0:T(8,128)(2,1)S(1)}, bf16[8,8,16,384]{3,2,1,0:T(8,128)(2,1)S(1)}, u32[]{:S(2)}, u32[]{:S(2)}) collective-permute-start(bf16[8,8,16,384]{3,2,1,0:T(8,128)(2,1)S(1)} %bitcast.20), channel_id=1, source_target_pairs={{0,1},{1,0},{2,3},{3,2},{4,5},{5,4},{6,7},{7,6},{8,9},{9,8},{10,11... | collective-permute-start | bytes 2359304 | tf_op jit(solution)/shard_map/ppermute | solution.py:501
  160.2 0.6 pick.1
  160.8 0.1 collective-permute-start.4
  160.9 2.0 %collective-permute-done.4.other = bf16[4,256,256]{2,1,0:T(8,128)(2,1)S(1)} collective-permute-done((bf16[4,256,256]{2,1,0:T(8,128)(2,1)S(1)}, bf16[4,256,256]{2,1,0:T(8,128)(2,1)S(1)}, u32[]{:S(2)}, u32[]{:S(2)}) %collective-permute-start.4) | collective-permute-done | bytes 524320 | tf_op jit(solution)/shard_map/ppermute | solution.py:501
  162.9 1.6 arrive.1
  164.5 1.5 place.2
  166.0 0.0 collective-permute-done.12.shares
  166.0 1.5 place.3
  (6 shorter events, 0.0 us)
Async XLA Ops:
  8.2 6.1 %copy-start = (bf16[1,256,4096]{2,1,0:T(8,128)(2,1)S(1)}, bf16[1,256,4096]{2,1,0:T(8,128)(2,1)}, u32[]{:S(2)}) copy-start(bf16[1,256,4096]{2,1,0:T(8,128)(2,1)} %param.10) | copy-start | bytes 6291460
  8.2 7.3 %copy-start.4 = (s32[1,8]{1,0:T(1,128)S(1)}, s32[1,8]{1,0:T(1,128)}, u32[]{:S(2)}) copy-start(s32[1,8]{1,0:T(1,128)} %param.14) | copy-start | bytes 100
  8.2 60.6 %all-to-all-start = ((bf16[8,256,1152]{2,1,0:T(8,128)(2,1)}), bf16[8,256,1152]{2,1,0:T(8,128)(2,1)}, u32[]{:S(2)}, u32[]{:S(2)}) async-start(bf16[8,256,1152]{2,1,0:T(8,128)(2,1)} %pack.1), calls=%async_computation | async-start | bytes 9437184 | tf_op jit(solution)/shard_map/all_to_all | solution.py:497
  15.3 2.9 %collective-permute-start = (bf16[256,2048]{1,0:T(8,128)(2,1)}, bf16[256,2048]{1,0:T(8,128)(2,1)S(1)}, u32[]{:S(2)}, u32[]{:S(2)}) collective-permute-start(bf16[256,2048]{1,0:T(8,128)(2,1)} %dynamic-slice_bitcast_fusion), channel_id=1, source_target_pairs={{0,1},{1,0},{2,3},{3,2},{4,5},{5,4},{6,7},{7,6},{8,9},{9,8},{10,11... | collective-permute-start | bytes 3145736 | tf_op jit(solution)/shard_map/ppermute | solution.py:501
  18.2 66.7 %copy-start.1 = (bf16[256,2048]{1,0:T(8,128)(2,1)}, bf16[256,2048]{1,0:T(8,128)(2,1)S(1)}, u32[]{:S(2)}) copy-start(bf16[256,2048]{1,0:T(8,128)(2,1)S(1)} %collective-permute-done.refs_0_.refs_9_) | copy-start | bytes 3145732
  84.9 6.4 %collective-permute-start.5 = (bf16[2,128,256]{2,1,0:T(8,128)(2,1)S(1)}, bf16[2,128,256]{2,1,0:T(8,128)(2,1)S(1)}, u32[]{:S(2)}, u32[]{:S(2)}) collective-permute-start(bf16[2,128,256]{2,1,0:T(8,128)(2,1)S(1)} %get-tuple-element.39), channel_id=1, source_target_pairs={{0,2},{2,4},{4,6},{6,0},{1,3},{3,5},{5,7},{7,1},{8,10},{10,12},{12... | collective-permute-start | bytes 393224 | tf_op jit(solution)/shard_map/ppermute | solution.py:526
  87.3 19.2 %copy-start.3 = (bf16[2,256,256]{2,1,0:T(8,128)(2,1)}, bf16[2,256,256]{2,1,0:T(8,128)(2,1)S(1)}, u32[]{:S(2)}) copy-start(bf16[2,256,256]{2,1,0:T(8,128)(2,1)S(1)} %get-tuple-element.36) | copy-start | bytes 786436
  87.3 14.9 %collective-permute-start.1 = (bf16[2,256,256]{2,1,0:T(8,128)(2,1)S(1)}, bf16[2,256,256]{2,1,0:T(8,128)(2,1)S(1)}, u32[]{:S(2)}, u32[]{:S(2)}) collective-permute-start(bf16[2,256,256]{2,1,0:T(8,128)(2,1)S(1)} %get-tuple-element.35), channel_id=1, source_target_pairs={{0,2},{2,4},{4,6},{6,0},{1,3},{3,5},{5,7},{7,1},{8,10},{10,12},{12... | collective-permute-start | bytes 786440 | tf_op jit(solution)/shard_map/ppermute | solution.py:526
  87.4 14.8 %collective-permute-start.3 = (bf16[2,256,256]{2,1,0:T(8,128)(2,1)S(1)}, bf16[2,256,256]{2,1,0:T(8,128)(2,1)S(1)}, u32[]{:S(2)}, u32[]{:S(2)}) collective-permute-start(bf16[2,256,256]{2,1,0:T(8,128)(2,1)S(1)} %get-tuple-element.37), channel_id=1, source_target_pairs={{0,6},{2,0},{4,2},{6,4},{1,7},{3,1},{5,3},{7,5},{8,14},{10,8},{12,... | collective-permute-start | bytes 786440 | tf_op jit(solution)/shard_map/ppermute | solution.py:526
  90.0 8.6 %collective-permute-start.6 = (bf16[2,128,256]{2,1,0:T(8,128)(2,1)S(1)}, bf16[2,128,256]{2,1,0:T(8,128)(2,1)S(1)}, u32[]{:S(2)}, u32[]{:S(2)}) collective-permute-start(bf16[2,128,256]{2,1,0:T(8,128)(2,1)S(1)} %get-tuple-element.40), channel_id=1, source_target_pairs={{0,4},{2,6},{4,0},{6,2},{1,5},{3,7},{5,1},{7,3},{8,12},{10,14},{12... | collective-permute-start | bytes 393224 | tf_op jit(solution)/shard_map/ppermute | solution.py:526
  90.9 10.1 %collective-permute-start.7 = (bf16[2,128,256]{2,1,0:T(8,128)(2,1)S(1)}, bf16[2,128,256]{2,1,0:T(8,128)(2,1)S(1)}, u32[]{:S(2)}, u32[]{:S(2)}) collective-permute-start(bf16[2,128,256]{2,1,0:T(8,128)(2,1)S(1)} %get-tuple-element.41), channel_id=1, source_target_pairs={{0,6},{2,0},{4,2},{6,4},{1,7},{3,1},{5,3},{7,5},{8,14},{10,8},{12,... | collective-permute-start | bytes 393224 | tf_op jit(solution)/shard_map/ppermute | solution.py:526
  91.3 10.9 %collective-permute-start.8 = (bf16[2,128,256]{2,1,0:T(8,128)(2,1)S(1)}, bf16[2,128,256]{2,1,0:T(8,128)(2,1)S(1)}, u32[]{:S(2)}, u32[]{:S(2)}) collective-permute-start(bf16[2,128,256]{2,1,0:T(8,128)(2,1)S(1)} %get-tuple-element.38.refs_0_), channel_id=1, source_target_pairs={{0,1},{1,0},{2,3},{3,2},{4,5},{5,4},{6,7},{7,6},{8,9},{9,8},{10,11... | collective-permute-start | bytes 393224 | tf_op jit(solution)/shard_map/ppermute | solution.py:501
  98.6 3.6 %collective-permute-start.9 = (bf16[2,128,256]{2,1,0:T(8,128)(2,1)S(1)}, bf16[2,128,256]{2,1,0:T(8,128)(2,1)S(1)}, u32[]{:S(2)}, u32[]{:S(2)}) collective-permute-start(bf16[2,128,256]{2,1,0:T(8,128)(2,1)S(1)} %collective-permute-done.5.refs_1_), channel_id=1, source_target_pairs={{0,1},{1,0},{2,3},{3,2},{4,5},{5,4},{6,7},{7,6},{8,9},{9,8},{10,11... | collective-permute-start | bytes 393224 | tf_op jit(solution)/shard_map/ppermute | solution.py:501
  101.0 2.2 %collective-permute-start.10 = (bf16[2,128,256]{2,1,0:T(8,128)(2,1)S(1)}, bf16[2,128,256]{2,1,0:T(8,128)(2,1)S(1)}, u32[]{:S(2)}, u32[]{:S(2)}) collective-permute-start(bf16[2,128,256]{2,1,0:T(8,128)(2,1)S(1)} %collective-permute-done.6.refs_2_), channel_id=1, source_target_pairs={{0,1},{1,0},{2,3},{3,2},{4,5},{5,4},{6,7},{7,6},{8,9},{9,8},{10,11... | collective-permute-start | bytes 393224 | tf_op jit(solution)/shard_map/ppermute | solution.py:501
  102.2 1.3 collective-permute-start.11
  103.5 1.2 copy-start.2
  106.5 28.4 %all-to-all-start.1 = ((bf16[64,16,384]{2,1,0:T(8,128)(2,1)}), bf16[64,16,384]{2,1,0:T(8,128)(2,1)S(1)}, u32[]{:S(2)}, u32[]{:S(2)}) async-start(bf16[64,16,384]{2,1,0:T(8,128)(2,1)} %bitcast.13), calls=%async_computation.1 | async-start | bytes 1572864 | tf_op jit(solution)/shard_map/all_to_all | solution.py:497
  118.2 16.7 %collective-permute-start.2 = (bf16[2,256,256]{2,1,0:T(8,128)(2,1)}, bf16[2,256,256]{2,1,0:T(8,128)(2,1)S(1)}, u32[]{:S(2)}, u32[]{:S(2)}) collective-permute-start(bf16[2,256,256]{2,1,0:T(8,128)(2,1)} %copy-done.3), channel_id=1, source_target_pairs={{0,4},{2,6},{4,0},{6,2},{1,5},{3,7},{5,1},{7,3},{8,12},{10,14},{12... | collective-permute-start | bytes 786440 | tf_op jit(solution)/shard_map/ppermute | solution.py:526
  157.4 8.7 %collective-permute-start.12 = (bf16[8,8,16,384]{3,2,1,0:T(8,128)(2,1)S(1)}, bf16[8,8,16,384]{3,2,1,0:T(8,128)(2,1)S(1)}, u32[]{:S(2)}, u32[]{:S(2)}) collective-permute-start(bf16[8,8,16,384]{3,2,1,0:T(8,128)(2,1)S(1)} %bitcast.20), channel_id=1, source_target_pairs={{0,1},{1,0},{2,3},{3,2},{4,5},{5,4},{6,7},{7,6},{8,9},{9,8},{10,11... | collective-permute-start | bytes 2359304 | tf_op jit(solution)/shard_map/ppermute | solution.py:501
  160.8 2.1 %collective-permute-start.4 = (bf16[4,256,256]{2,1,0:T(8,128)(2,1)S(1)}, bf16[4,256,256]{2,1,0:T(8,128)(2,1)S(1)}, u32[]{:S(2)}, u32[]{:S(2)}) collective-permute-start(bf16[4,256,256]{2,1,0:T(8,128)(2,1)S(1)} %pick.1), channel_id=1, source_target_pairs={{0,1},{1,0},{2,3},{3,2},{4,5},{5,4},{6,7},{7,6},{8,9},{9,8},{10,11... | collective-permute-start | bytes 1572872 | tf_op jit(solution)/shard_map/ppermute | solution.py:501

commit v7 on v5

--- a/solution.py
+++ b/solution.py
@@ -20,12 +20,11 @@
 LOG2_E = 1.4426950408889634
 
 SHARE_ROWS = 16
-DOWN_COLS = 256
-UP_COLS = 32
+DOWN_COLS = 1024
+UP_COLS = 128
 
 DP = ("x", "z")
 SEQ = ("y", "core")
-PLANE = ("x", "z", "y")
 ALL = ("x", "z", "y", "core")
 NT = (((1,), (1,)), ((), ()))
 
@@ -279,31 +278,21 @@
     )(meta, packed, wq_up, wv_up)
 
 
-def up_kernel(where, low, dq_t, dv_t, up):
-    width = dq_t.shape[0]
-    lane = lax.broadcasted_iota(jnp.int32, (width, up.shape[1]), 1)
-    source = lax.broadcasted_iota(jnp.int32, (width, up.shape[1]), 0)
-    mine = (source == (lane // 128) * UP_COLS + lane % UP_COLS) & (
-        (lane % 128) // UP_COLS == where[0]
-    )
-    mine = jnp.where(mine, 1.0, 0.0).astype(jnp.bfloat16)
+def up_kernel(low, dq_t, dv_t, up):
     for part, grads in enumerate((dq_t, dv_t)):
         share = (dot(grads[...], low[...]) * ADAPTER_SCALE).T[part * RANK : (part + 1) * RANK, :]
-        up[part * RANK : (part + 1) * RANK, :] = dot(share.astype(jnp.bfloat16), mine).astype(
-            jnp.bfloat16
-        )
-
-
-def up_gradient(where, low, dq_t, dv_t):
-    width = dq_t.shape[0]
+        up[part * RANK : (part + 1) * RANK, :] = share.astype(jnp.bfloat16)
+
+
+def up_gradient(low, dq_t, dv_t):
     return pl.pallas_call(
         up_kernel,
-        in_specs=[SMEM] + [VMEM] * 3,
+        in_specs=[VMEM] * 3,
         out_specs=VMEM,
-        out_shape=jax.ShapeDtypeStruct((2 * RANK, width // UP_COLS * 128), jnp.bfloat16),
+        out_shape=jax.ShapeDtypeStruct((2 * RANK, dq_t.shape[0]), jnp.bfloat16),
         compiler_params=pltpu.CompilerParams(vmem_limit_bytes=16 << 20),
         name="up_gradient",
-    )(where, low, dq_t, dv_t)
+    )(low, dq_t, dv_t)
 
 
 def pick_kernel(where, part_0, part_1, part_2, part_3, out):
@@ -361,18 +350,13 @@
     grad = grad.astype(out.dtype)
     for row in range(out.shape[0]):
         across = slice(row * SHARE_ROWS, (row + 1) * SHARE_ROWS)
-        for column in range(out.shape[1]):
-            out[row, column, :, :DOWN_COLS] = grad[
-                across, column * DOWN_COLS : (column + 1) * DOWN_COLS
-            ]
-            out[row, column, :, DOWN_COLS:] = up[across, column * 128 : (column + 1) * 128]
+        out[row, 0, :, :DOWN_COLS] = grad[across, :]
+        out[row, 0, :, DOWN_COLS:] = up[across, :]
 
 
 def down_gradient(core, parts, hidden, hidden_other, up):
     rows, half = hidden_other.shape
-    steps = 2
-    step = half // steps
-    columns = half // DOWN_COLS
+    steps = half // DOWN_COLS
     across = 2 * RANK // SHARE_ROWS
     shape = parts[0].shape
     return pl.pallas_call(
@@ -382,18 +366,17 @@
             grid=(steps,),
             in_specs=[pl.BlockSpec(shape, lambda i, core: (0, 0, 0))] * len(parts)
             + [
-                pl.BlockSpec((rows, step), lambda i, core: (0, core[0] * steps + i)),
-                pl.BlockSpec((rows, step), lambda i, core: (0, i)),
-                pl.BlockSpec((2 * RANK, columns // steps * 128), lambda i, core: (0, i)),
+                pl.BlockSpec((rows, DOWN_COLS), lambda i, core: (0, core[0] * steps + i)),
+                pl.BlockSpec((rows, DOWN_COLS), lambda i, core: (0, i)),
+                pl.BlockSpec((2 * RANK, UP_COLS), lambda i, core: (0, i)),
             ],
             out_specs=pl.BlockSpec(
-                (across, columns // steps, SHARE_ROWS, DOWN_COLS + 128),
-                lambda i, core: (0, i, 0, 0),
+                (across, 1, SHARE_ROWS, DOWN_COLS + UP_COLS), lambda i, core: (0, i, 0, 0)
             ),
             scratch_shapes=[pltpu.VMEM(shape, jnp.bfloat16)],
         ),
         out_shape=jax.ShapeDtypeStruct(
-            (across, columns, SHARE_ROWS, DOWN_COLS + 128), jnp.bfloat16
+            (across, steps, SHARE_ROWS, DOWN_COLS + UP_COLS), jnp.bfloat16
         ),
         compiler_params=pltpu.CompilerParams(vmem_limit_bytes=24 << 20),
         name="down_gradient",
@@ -405,9 +388,7 @@
     total = parts[0].astype(jnp.float32)
     for part in range(1, parts.shape[0]):
         total += parts[part].astype(jnp.float32)
-    total = total.astype(out.dtype)
-    for part in range(out.shape[0]):
-        out[part] = total
+    out[...] = total.astype(out.dtype)
 
 
 def sum_share(parts, after):
@@ -415,14 +396,42 @@
         share_kernel,
         in_specs=[VMEM] + [VMEM] * len(after),
         out_specs=VMEM,
-        out_shape=jax.ShapeDtypeStruct(parts.shape, parts.dtype),
+        out_shape=jax.ShapeDtypeStruct(parts.shape[1:], parts.dtype),
         compiler_params=pltpu.CompilerParams(vmem_limit_bytes=SMALL_VMEM),
         name="sum_share",
     )(parts, *after)
 
 
+def chips_kernel(where, *refs):
+    *parts, _, out = refs
+    chip = where[0]
+    total = parts[0][:, :DOWN_COLS].astype(jnp.float32)
+    for part in parts[1:]:
+        total += part[:, :DOWN_COLS].astype(jnp.float32)
+    total = total.astype(out.dtype)
+    for device in range(out.shape[0]):
+        out[device, :, :DOWN_COLS] = total
+    for step, part in enumerate(parts):
+        origin = lax.rem(chip + len(parts) - step, len(parts))
+        begin = pl.multiple_of(DOWN_COLS + origin * UP_COLS, UP_COLS)
+        for device in range(out.shape[0]):
+            out[device, :, pl.ds(begin, UP_COLS)] = part[:, DOWN_COLS:]
+
+
+def sum_chips(where, parts, devices, after):
+    shape = (devices, SHARE_ROWS, DOWN_COLS + len(parts) * UP_COLS)
+    return pl.pallas_call(
+        chips_kernel,
+        in_specs=[SMEM] + [VMEM] * (len(parts) + 1),
+        out_specs=VMEM,
+        out_shape=jax.ShapeDtypeStruct(shape, parts[0].dtype),
+        compiler_params=pltpu.CompilerParams(vmem_limit_bytes=SMALL_VMEM),
+        name="sum_chips",
+    )(where, *parts, after)
+
+
 def place_kernel(which, shares, *refs):
-    *outs, downs, ups, wide, sems = refs[-8:]
+    *outs, downs, ups, sems = refs[-7:]
     which = which[0]
     half = shares.shape[0] // 2
     columns = shares.shape[1]
@@ -435,57 +444,52 @@
         )
         copies[-1].start()
 
-    for part in range(2):
-        for row in range(half):
-            across = slice(row * SHARE_ROWS, (row + 1) * SHARE_ROWS)
-            for column in range(columns):
-                share = shares[part * half + row, column]
-                downs[part, across, column * DOWN_COLS : (column + 1) * DOWN_COLS] = share[
-                    :, :DOWN_COLS
-                ].astype(jnp.float32)
-                wide[
-                    part * RANK + row * SHARE_ROWS : part * RANK + (row + 1) * SHARE_ROWS,
-                    column * 128 : (column + 1) * 128,
-                ] = share[:, DOWN_COLS:]
-        width = columns * DOWN_COLS
-        send(downs.at[part], outs[2 * part], which * width, width)
-    width = columns * UP_COLS
-    source = lax.broadcasted_iota(jnp.int32, (columns * 128, width), 0)
-    lane = lax.broadcasted_iota(jnp.int32, (columns * 128, width), 1)
-    lane = (lane // UP_COLS) * 128 + lane % UP_COLS
-    for chip in range(128 // UP_COLS):
-        chosen = jnp.where(source == lane + chip * UP_COLS, 1.0, 0.0).astype(jnp.bfloat16)
-        ups[chip] = dot(wide[...], chosen)
-        for part in range(2):
-            send(
-                ups.at[chip, part * RANK : (part + 1) * RANK, :],
-                outs[2 * part + 1],
-                (2 * chip + which) * width,
-                width,
-            )
+    chips, _, width = ups.shape
+    for row in range(2 * half):
+        part, across = row // half, slice(row % half * SHARE_ROWS, (row % half + 1) * SHARE_ROWS)
+        for column in range(columns):
+            share = shares[row, column]
+            downs[part, across, column * DOWN_COLS : (column + 1) * DOWN_COLS] = share[
+                :, :DOWN_COLS
+            ].astype(jnp.float32)
+            for chip in range(chips):
+                begin = DOWN_COLS + chip * UP_COLS
+                ups[
+                    chip,
+                    row * SHARE_ROWS : (row + 1) * SHARE_ROWS,
+                    column * UP_COLS : (column + 1) * UP_COLS,
+                ] = share[:, begin : begin + UP_COLS].astype(jnp.float32)
+        if row % half == half - 1:
+            send(downs.at[part], outs[2 * part], which * downs.shape[2], downs.shape[2])
+            for chip in range(chips):
+                send(
+                    ups.at[chip, part * RANK : (part + 1) * RANK, :],
+                    outs[2 * part + 1],
+                    (2 * chip + which) * width,
+                    width,
+                )
     for copy in copies:
         copy.wait()
 
 
-def place(which, shares, model, width, earlier=(), after=()):
+def place(which, shares, model, width, earlier=()):
     shapes = [(RANK, model), (RANK, width), (RANK, model), (RANK, width)]
     columns = shares.shape[1]
-    chips = 128 // UP_COLS
+    chips = (shares.shape[3] - DOWN_COLS) // UP_COLS
     return pl.pallas_call(
         place_kernel,
-        in_specs=[SMEM, VMEM] + [ANY] * len(earlier) + [VMEM] * len(after),
+        in_specs=[SMEM, VMEM] + [ANY] * len(earlier),
         out_specs=[ANY] * 4,
         out_shape=[jax.ShapeDtypeStruct(shape, jnp.float32) for shape in shapes],
         scratch_shapes=[
             pltpu.VMEM((2, RANK, columns * DOWN_COLS), jnp.float32),
             pltpu.VMEM((chips, 2 * RANK, columns * UP_COLS), jnp.float32),
-            pltpu.VMEM((2 * RANK, columns * 128), jnp.bfloat16),
             pltpu.SemaphoreType.DMA((2 + 2 * chips,)),
         ],
         input_output_aliases={2 + index: index for index in range(len(earlier))},
         compiler_params=pltpu.CompilerParams(vmem_limit_bytes=16 << 20),
         name="place",
-    )(which[None], shares, *earlier, *after)
+    )(which[None], shares, *earlier)
 
 
 def swap(x, axes):
@@ -547,14 +551,19 @@
     backs = [backs[0]] + [to_chip(backs[step], step) for step in range(1, chips)]
     backs_other = [to_other_core(back) for back in backs]
     parts = [parts[0]] + [to_chip(parts[step], step) for step in range(1, chips)]
-    up = up_gradient(where, low, dq_t, dv_t)
+    up = up_gradient(low, dq_t, dv_t)
     down = down_gradient(core[None], backs + backs_other, hidden[0], hidden_other, up)
 
-    shares = swap(down.reshape((-1,) + down.shape[2:]), PLANE)
-    shares = swap(sum_share(shares, after=[parts[1], parts[3]]), PLANE).reshape(down.shape)
-    attended = arrive(where, parts, to_other_core(pick(where, parts)))
+    other = to_other_core(pick(where, parts))
+    attended = arrive(where, parts, other)
+
+    shares = swap(down.reshape((-1,) + down.shape[2:]), DP)
+    share = sum_share(shares, after=parts[1:])
+    share = [share] + [to_chip(share, step) for step in range(1, chips)]
+    shares = swap(sum_chips(where, share, shares.shape[0], after=other), DP)
+    shares = shares.reshape(down.shape[:2] + shares.shape[1:])
     shares_other = to_other_core(shares)
-    grads = place(core, shares, model, seq_size * width, after=[parts[2]])
+    grads = place(core, shares, model, seq_size * width)
     grad_a_q, up_q, grad_a_v, up_v = place(
         1 - core, shares_other, model, seq_size * width, earlier=grads
     )

time: 162 us -> 153 us (0.944)
  waiting for transfers between devices: 81.9 us -> 65.4 us
  blocking collectives: 0 us -> 14.8 us
  starting transfers between devices: 43 us -> 35 us
  local copies, waits for them, and re-layouts: 1.86 us -> 4.02 us
    all_to_all x0 -> x1, blocking collectives: none -> 14.8 us  [swap(): return lax.all_to_all(x, axes, 0, 0, tiled=True)]
    ppermute x6 -> x9, waiting for transfers between devices: 16.4 us -> 3.43 us  [to_chip(): return lax.ppermute(x, 'y', [(c, (c + step) % chips) for c in range(chips)])]
    all_to_all x3 -> x2, starting transfers between devices: 24.9 us -> 13.8 us  [swap(): return lax.all_to_all(x, axes, 0, 0, tiled=True)]
    all_to_all x3 -> x2, waiting for transfers between devices: 63.9 us -> 61.5 us  [swap(): return lax.all_to_all(x, axes, 0, 0, tiled=True)]
    unnamed x12 -> x8, local copies, waits for them, and re-layouts: 0.04 us -> 2.21 us
    ppermute x6 -> x9, starting transfers between devices: 8.36 us -> 10.1 us  [to_chip(): return lax.ppermute(x, 'y', [(c, (c + step) % chips) for c in range(chips)])]
  transfers between devices with their start and end apart: 16 -> 18, of which waited for: 5 -> 7; matrix products, arithmetic and copies ran while one was open for 1% -> 1% of each run, Pallas kernels for 13% -> 15%
where the time goes in v7:
time: 153 us
  waiting for transfers between devices  65.4 us (43%)
  starting transfers between devices  35 us (23%)
  Pallas kernels  32.3 us (21%)
  blocking collectives  14.8 us (10%)
  local copies, waits for them, and re-layouts  4.02 us (3%)
    all_to_all x2, waiting for transfers between devices, swap(): return lax.all_to_all(x, axes, 0, 0, tiled=True)  61.5 us
    pallas_call x1, Pallas kernels, attention(): pl.pallas_call(attention_kernel, in_specs=[SMEM, VMEM, VMEM, VMEM], out_s...  16.9 us
    all_to_all x1, blocking collectives, swap(): return lax.all_to_all(x, axes, 0, 0, tiled=True)  14.8 us
    all_to_all x2, starting transfers between devices, swap(): return lax.all_to_all(x, axes, 0, 0, tiled=True)  13.8 us
    ppermute x7, starting transfers between devices, to_other_core(): return lax.ppermute(x, 'core', [(0, 1), (1, 0)])  11.1 us
    ppermute x9, starting transfers between devices, to_chip(): return lax.ppermute(x, 'y', [(c, (c + step) % chips) for c in range(chips)])  10.1 us
    pallas_call x1, Pallas kernels, pack(): pl.pallas_call(pack_kernel, in_specs=[ANY] * 9, out_specs=ANY, out_shape=...  7.52 us
    ppermute x9, waiting for transfers between devices, to_chip(): return lax.ppermute(x, 'y', [(c, (c + step) % chips) for c in range(chips)])  3.43 us
  transfers between devices with their start and end apart: 18, of which 7 were waited for; matrix products, arithmetic and copies ran while one was open for 1% of the time, Pallas kernels for 15%

profile of v7, /device:TPU:1, one launch (start us, length us, event | category | flops | bytes accessed | tf_op | source)
XLA Modules:
  0.0 152.6 jit_solution(17820135279611849055)
XLA Ops:
  0.6 7.5 %pack.1 = bf16[8,256,1152]{2,1,0:T(8,128)(2,1)} custom-call(bf16[256,4096]{1,0:T(8,128)(2,1)} %bitcast.18, bf16[64,4096]{1,0:T(8,128)(2,1)} %bitcast.28, bf16[64,4096]{1,0:T(8,128)(2,1)} %bitcast.29, bf16[256,2048]{1,0:T(8,128)(2,1)} %bitcast.22, bf16[256,2048]{1,0:T(8,128)(2,1)} %bitcast.23, bf16[256,2048]{1,0:T(8,128)(2,1)} %bitcast.24, ...), custom_call_target="tpu_custom_call" | custom-call | tf_op jit(solution)/shard_map/pack/pallas_call | solution.py:130
  8.2 0.0 copy-start
  8.2 0.0 copy-start.3
  8.2 6.1 %all-to-all-start = ((bf16[8,256,1152]{2,1,0:T(8,128)(2,1)}), bf16[8,256,1152]{2,1,0:T(8,128)(2,1)}, u32[]{:S(2)}, u32[]{:S(2)}) async-start(bf16[8,256,1152]{2,1,0:T(8,128)(2,1)} %pack.1), calls=%async_computation | async-start | bytes 9437184 | tf_op jit(solution)/shard_map/all_to_all | solution.py:496
  14.3 1.0 dynamic-slice_bitcast_fusion
  15.3 0.1 collective-permute-start.11
  15.4 0.8 constant_dynamic-slice_fusion
  16.2 0.1 pad_add_fusion.1.meta
  16.3 52.5 %all-to-all-done = bf16[8,256,1152]{2,1,0:T(8,128)(2,1)} async-done(((bf16[8,256,1152]{2,1,0:T(8,128)(2,1)}), bf16[8,256,1152]{2,1,0:T(8,128)(2,1)}, u32[]{:S(2)}, u32[]{:S(2)}) %all-to-all-start) | async-done | bytes 4718624 | tf_op jit(solution)/shard_map/all_to_all | solution.py:496
  68.8 16.9 %attention.1 = (bf16[2,256,256]{2,1,0:T(8,128)(2,1)S(1)}, bf16[2,256,256]{2,1,0:T(8,128)(2,1)}, bf16[2,256,256]{2,1,0:T(8,128)(2,1)}, bf16[2,256,256]{2,1,0:T(8,...) custom-call(s32[10]{0:T(128)S(1)} %pad_add_fusion.1.meta, ...), custom_call_target="tpu_custom_call" | custom-call | flops 8589934592 | bytes 16777216 | tf_op jit(solution)/shard_map/attention/pallas_call | solution.py:257
  85.7 0.3 collective-permute-start.4
  86.0 1.8 %collective-permute-start.5 = (bf16[2,128,256]{2,1,0:T(8,128)(2,1)S(1)}, bf16[2,128,256]{2,1,0:T(8,128)(2,1)S(1)}, u32[]{:S(2)}, u32[]{:S(2)}) collective-permute-start(bf16[2,128,256]{2,1,0:T(8,128)(2,1)S(1)} %get-tuple-element.30), channel_id=1, source_target_pairs={{0,4},{2,6},{4,0},{6,2},{1,5},{3,7},{5,1},{7,3},{8,12},{10,14},{12... | collective-permute-start | bytes 393224 | tf_op jit(solution)/shard_map/ppermute | solution.py:525
  87.8 0.6 collective-permute-start.6
  88.4 1.4 collective-permute-start.7
  89.8 2.4 %collective-permute-done.4.refs_1_ = bf16[2,128,256]{2,1,0:T(8,128)(2,1)S(1)} collective-permute-done((bf16[2,128,256]{2,1,0:T(8,128)(2,1)S(1)}, bf16[2,128,256]{2,1,0:T(8,128)(2,1)S(1)}, u32[]{:S(2)}, u32[]{:S(2)}) %collective-permute-start.4) | collective-permute-done | bytes 131104 | tf_op jit(solution)/shard_map/ppermute | solution.py:525
  92.1 3.5 %collective-permute-start.8 = (bf16[2,128,256]{2,1,0:T(8,128)(2,1)S(1)}, bf16[2,128,256]{2,1,0:T(8,128)(2,1)S(1)}, u32[]{:S(2)}, u32[]{:S(2)}) collective-permute-start(bf16[2,128,256]{2,1,0:T(8,128)(2,1)S(1)} %collective-permute-done.4.refs_1_), channel_id=1, source_target_pairs={{0,1},{1,0},{2,3},{3,2},{4,5},{5,4},{6,7},{7,6},{8,9},{9,8},{10,11... | collective-permute-start | bytes 393224 | tf_op jit(solution)/shard_map/ppermute | solution.py:500
  95.6 0.0 collective-permute-done.11.refs_9_
  95.6 1.0 copy-done.1
  96.6 0.0 collective-permute-start
  96.6 0.0 collective-permute-done.5.refs_2_
  96.6 0.5 collective-permute-start.1
  97.1 2.3 %collective-permute-start.2 = (bf16[2,256,256]{2,1,0:T(8,128)(2,1)}, bf16[2,256,256]{2,1,0:T(8,128)(2,1)S(1)}, u32[]{:S(2)}, u32[]{:S(2)}) collective-permute-start(bf16[2,256,256]{2,1,0:T(8,128)(2,1)} %get-tuple-element.27), channel_id=1, source_target_pairs={{0,6},{2,0},{4,2},{6,4},{1,7},{3,1},{5,3},{7,5},{8,14},{10,8},{12,... | collective-permute-start | bytes 786440 | tf_op jit(solution)/shard_map/ppermute | solution.py:525
  99.3 0.6 collective-permute-start.9
  99.9 0.1 collective-permute-start.10
  100.0 0.8 up_gradient.1.refs_10_
  100.8 0.1 collective-permute-done.9.refs_6_
  100.9 0.4 collective-permute-done.10.refs_7_
  101.3 1.2 copy-done.2
  102.5 1.7 %down_gradient.1 = bf16[8,2,16,1152]{3,2,1,0:T(8,128)(2,1)} custom-call(s32[1]{0:T(128)} %bitcast.1.core.which, bf16[2,128,256]{2,1,0:T(8,128)(2,1)S(1)} %get-tuple-element.28.refs_0_, bf16[2,128,256]{2,1,0:T(8,128)(2,1)S(1)} %collective-permute-done.4.refs_1_, bf16[2,128,256]{2,1,0:T(8,128)(2,1)S(1)} %collective-permute-done.5.refs_2_, ...), custom_call_target="tpu_custom_call" | custom-call | tf_op jit(solution)/shard_map/down_gradient/pallas_call | solution.py:362
  104.2 7.7 %all-to-all-start.1 = ((bf16[16,16,1152]{2,1,0:T(8,128)(2,1)}), bf16[16,16,1152]{2,1,0:T(8,128)(2,1)S(1)}, u32[]{:S(2)}, u32[]{:S(2)}) async-start(bf16[16,16,1152]{2,1,0:T(8,128)(2,1)} %bitcast.13), calls=%async_computation.1 | async-start | bytes 1179648 | tf_op jit(solution)/shard_map/all_to_all | solution.py:496
  111.8 0.1 pad_add_fusion.where
  111.9 0.6 pick.1
  112.5 1.1 collective-permute-start.3
  113.6 9.0 %all-to-all-done.1.parts = bf16[16,16,1152]{2,1,0:T(8,128)(2,1)S(1)} async-done(((bf16[16,16,1152]{2,1,0:T(8,128)(2,1)}), bf16[16,16,1152]{2,1,0:T(8,128)(2,1)S(1)}, u32[]{:S(2)}, u32[]{:S(2)}) %all-to-all-start.1) | async-done | bytes 589856 | tf_op jit(solution)/shard_map/all_to_all | solution.py:496
  122.6 0.1 sum_share.1.refs_0_
  122.7 0.7 collective-permute-start.12
  123.3 2.1 %collective-permute-start.13 = (bf16[16,1152]{1,0:T(8,128)(2,1)S(1)}, bf16[16,1152]{1,0:T(8,128)(2,1)S(1)}, u32[]{:S(2)}, u32[]{:S(2)}) collective-permute-start(bf16[16,1152]{1,0:T(8,128)(2,1)S(1)} %sum_share.1.refs_0_), channel_id=1, source_target_pairs={{0,4},{2,6},{4,0},{6,2},{1,5},{3,7},{5,1},{7,3},{8,12},{10,14},{12... | collective-permute-start | bytes 110600 | tf_op jit(solution)/shard_map/ppermute | solution.py:525
  125.4 2.0 %collective-permute-start.14 = (bf16[16,1152]{1,0:T(8,128)(2,1)S(1)}, bf16[16,1152]{1,0:T(8,128)(2,1)S(1)}, u32[]{:S(2)}, u32[]{:S(2)}) collective-permute-start(bf16[16,1152]{1,0:T(8,128)(2,1)S(1)} %sum_share.1.refs_0_), channel_id=1, source_target_pairs={{0,6},{2,0},{4,2},{6,4},{1,7},{3,1},{5,3},{7,5},{8,14},{10,8},{12,... | collective-permute-start | bytes 110600 | tf_op jit(solution)/shard_map/ppermute | solution.py:525
  127.4 0.0 collective-permute-done.12.refs_1_
  127.4 0.3 collective-permute-done.13.refs_2_
  127.7 0.8 collective-permute-done.14.refs_3_
  128.5 0.6 sum_chips.1
  129.1 14.8 %all_to_all.15 = bf16[16,16,1536]{2,1,0:T(8,128)(2,1)S(1)} all-to-all(bf16[16,16,1536]{2,1,0:T(8,128)(2,1)S(1)} %sum_chips.1), channel_id=1, replica_groups=mesh['x'=4,'z'=4,'y'=4,'core'=2] {'x','z'}, dimensions={0} | all-to-all | bytes 1572864 | tf_op jit(solution)/shard_map/all_to_all | solution.py:496
  143.9 4.4 %collective-permute-start.15 = (bf16[8,2,16,1536]{3,2,1,0:T(8,128)(2,1)S(1)}, bf16[8,2,16,1536]{3,2,1,0:T(8,128)(2,1)S(1)}, u32[]{:S(2)}, u32[]{:S(2)}) collective-permute-start(bf16[8,2,16,1536]{3,2,1,0:T(8,128)(2,1)S(1)} %bitcast.20), channel_id=1, source_target_pairs={{0,1},{1,0},{2,3},{3,2},{4,5},{5,4},{6,7},{7,6},{8,9},{9,8},{10,11... | collective-permute-start | bytes 2359304 | tf_op jit(solution)/shard_map/ppermute | solution.py:500
  148.3 1.6 %arrive.1 = bf16[1,256,2048]{2,1,0:T(8,128)(2,1)} custom-call(s32[2]{0:T(128)S(1)} %pad_add_fusion.where, bf16[2,256,256]{2,1,0:T(8,128)(2,1)S(1)} %get-tuple-element.24.part_0, bf16[2,256,256]{2,1,0:T(8,128)(2,1)S(1)} %collective-permute-done.part_1.refs_0_, bf16[2,256,256]{2,1,0:T(8,128)(2,1)S(1)} %collective-permute-done.1.part_2.refs_1_, ...), custom_call_target="tpu_custom_call" | custom-call | tf_op jit(solution)/shard_map/arrive/pallas_call | solution.py:329
  149.9 1.2 place.2
  151.2 0.0 collective-permute-done.15.shares
  151.2 1.2 place.3
  (11 shorter events, 0.0 us)
Async XLA Ops:
  8.2 6.1 %copy-start = (bf16[1,256,4096]{2,1,0:T(8,128)(2,1)S(1)}, bf16[1,256,4096]{2,1,0:T(8,128)(2,1)}, u32[]{:S(2)}) copy-start(bf16[1,256,4096]{2,1,0:T(8,128)(2,1)} %param.10) | copy-start | bytes 6291460
  8.2 8.1 %copy-start.3 = (s32[1,8]{1,0:T(1,128)S(1)}, s32[1,8]{1,0:T(1,128)}, u32[]{:S(2)}) copy-start(s32[1,8]{1,0:T(1,128)} %param.14) | copy-start | bytes 100
  8.2 60.6 %all-to-all-start = ((bf16[8,256,1152]{2,1,0:T(8,128)(2,1)}), bf16[8,256,1152]{2,1,0:T(8,128)(2,1)}, u32[]{:S(2)}, u32[]{:S(2)}) async-start(bf16[8,256,1152]{2,1,0:T(8,128)(2,1)} %pack.1), calls=%async_computation | async-start | bytes 9437184 | tf_op jit(solution)/shard_map/all_to_all | solution.py:496
  15.3 80.3 %collective-permute-start.11 = (bf16[256,2048]{1,0:T(8,128)(2,1)}, bf16[256,2048]{1,0:T(8,128)(2,1)S(1)}, u32[]{:S(2)}, u32[]{:S(2)}) collective-permute-start(bf16[256,2048]{1,0:T(8,128)(2,1)} %dynamic-slice_bitcast_fusion), channel_id=1, source_target_pairs={{0,1},{1,0},{2,3},{3,2},{4,5},{5,4},{6,7},{7,6},{8,9},{9,8},{10,11... | collective-permute-start | bytes 3145736 | tf_op jit(solution)/shard_map/ppermute | solution.py:500
  85.7 6.5 %collective-permute-start.4 = (bf16[2,128,256]{2,1,0:T(8,128)(2,1)S(1)}, bf16[2,128,256]{2,1,0:T(8,128)(2,1)S(1)}, u32[]{:S(2)}, u32[]{:S(2)}) collective-permute-start(bf16[2,128,256]{2,1,0:T(8,128)(2,1)S(1)} %get-tuple-element.29), channel_id=1, source_target_pairs={{0,2},{2,4},{4,6},{6,0},{1,3},{3,5},{5,7},{7,1},{8,10},{10,12},{12... | collective-permute-start | bytes 393224 | tf_op jit(solution)/shard_map/ppermute | solution.py:525
  86.0 10.6 %collective-permute-start.5 = (bf16[2,128,256]{2,1,0:T(8,128)(2,1)S(1)}, bf16[2,128,256]{2,1,0:T(8,128)(2,1)S(1)}, u32[]{:S(2)}, u32[]{:S(2)}) collective-permute-start(bf16[2,128,256]{2,1,0:T(8,128)(2,1)S(1)} %get-tuple-element.30), channel_id=1, source_target_pairs={{0,4},{2,6},{4,0},{6,2},{1,5},{3,7},{5,1},{7,3},{8,12},{10,14},{12... | collective-permute-start | bytes 393224 | tf_op jit(solution)/shard_map/ppermute | solution.py:525
  87.8 9.3 %collective-permute-start.6 = (bf16[2,128,256]{2,1,0:T(8,128)(2,1)S(1)}, bf16[2,128,256]{2,1,0:T(8,128)(2,1)S(1)}, u32[]{:S(2)}, u32[]{:S(2)}) collective-permute-start(bf16[2,128,256]{2,1,0:T(8,128)(2,1)S(1)} %get-tuple-element.31), channel_id=1, source_target_pairs={{0,6},{2,0},{4,2},{6,4},{1,7},{3,1},{5,3},{7,5},{8,14},{10,8},{12,... | collective-permute-start | bytes 393224 | tf_op jit(solution)/shard_map/ppermute | solution.py:525
  88.4 11.0 %collective-permute-start.7 = (bf16[2,128,256]{2,1,0:T(8,128)(2,1)S(1)}, bf16[2,128,256]{2,1,0:T(8,128)(2,1)S(1)}, u32[]{:S(2)}, u32[]{:S(2)}) collective-permute-start(bf16[2,128,256]{2,1,0:T(8,128)(2,1)S(1)} %get-tuple-element.28.refs_0_), channel_id=1, source_target_pairs={{0,1},{1,0},{2,3},{3,2},{4,5},{5,4},{6,7},{7,6},{8,9},{9,8},{10,11... | collective-permute-start | bytes 393224 | tf_op jit(solution)/shard_map/ppermute | solution.py:500
  92.1 7.8 %collective-permute-start.8 = (bf16[2,128,256]{2,1,0:T(8,128)(2,1)S(1)}, bf16[2,128,256]{2,1,0:T(8,128)(2,1)S(1)}, u32[]{:S(2)}, u32[]{:S(2)}) collective-permute-start(bf16[2,128,256]{2,1,0:T(8,128)(2,1)S(1)} %collective-permute-done.4.refs_1_), channel_id=1, source_target_pairs={{0,1},{1,0},{2,3},{3,2},{4,5},{5,4},{6,7},{7,6},{8,9},{9,8},{10,11... | collective-permute-start | bytes 393224 | tf_op jit(solution)/shard_map/ppermute | solution.py:500
  95.6 1.0 copy-start.1
  96.6 15.3 %collective-permute-start = (bf16[2,256,256]{2,1,0:T(8,128)(2,1)}, bf16[2,256,256]{2,1,0:T(8,128)(2,1)S(1)}, u32[]{:S(2)}, u32[]{:S(2)}) collective-permute-start(bf16[2,256,256]{2,1,0:T(8,128)(2,1)} %get-tuple-element.25), channel_id=1, source_target_pairs={{0,2},{2,4},{4,6},{6,0},{1,3},{3,5},{5,7},{7,1},{8,10},{10,12},{12... | collective-permute-start | bytes 786440 | tf_op jit(solution)/shard_map/ppermute | solution.py:525
  96.6 15.3 %collective-permute-start.1 = (bf16[2,256,256]{2,1,0:T(8,128)(2,1)}, bf16[2,256,256]{2,1,0:T(8,128)(2,1)S(1)}, u32[]{:S(2)}, u32[]{:S(2)}) collective-permute-start(bf16[2,256,256]{2,1,0:T(8,128)(2,1)} %get-tuple-element.26), channel_id=1, source_target_pairs={{0,4},{2,6},{4,0},{6,2},{1,5},{3,7},{5,1},{7,3},{8,12},{10,14},{12... | collective-permute-start | bytes 786440 | tf_op jit(solution)/shard_map/ppermute | solution.py:525
  97.1 14.9 %collective-permute-start.2 = (bf16[2,256,256]{2,1,0:T(8,128)(2,1)}, bf16[2,256,256]{2,1,0:T(8,128)(2,1)S(1)}, u32[]{:S(2)}, u32[]{:S(2)}) collective-permute-start(bf16[2,256,256]{2,1,0:T(8,128)(2,1)} %get-tuple-element.27), channel_id=1, source_target_pairs={{0,6},{2,0},{4,2},{6,4},{1,7},{3,1},{5,3},{7,5},{8,14},{10,8},{12,... | collective-permute-start | bytes 786440 | tf_op jit(solution)/shard_map/ppermute | solution.py:525
  99.3 1.6 %collective-permute-start.9 = (bf16[2,128,256]{2,1,0:T(8,128)(2,1)S(1)}, bf16[2,128,256]{2,1,0:T(8,128)(2,1)S(1)}, u32[]{:S(2)}, u32[]{:S(2)}) collective-permute-start(bf16[2,128,256]{2,1,0:T(8,128)(2,1)S(1)} %collective-permute-done.5.refs_2_), channel_id=1, source_target_pairs={{0,1},{1,0},{2,3},{3,2},{4,5},{5,4},{6,7},{7,6},{8,9},{9,8},{10,11... | collective-permute-start | bytes 393224 | tf_op jit(solution)/shard_map/ppermute | solution.py:500
  99.9 1.3 collective-permute-start.10
  101.3 1.2 copy-start.2
  104.2 18.4 %all-to-all-start.1 = ((bf16[16,16,1152]{2,1,0:T(8,128)(2,1)}), bf16[16,16,1152]{2,1,0:T(8,128)(2,1)S(1)}, u32[]{:S(2)}, u32[]{:S(2)}) async-start(bf16[16,16,1152]{2,1,0:T(8,128)(2,1)} %bitcast.13), calls=%async_computation.1 | async-start | bytes 1179648 | tf_op jit(solution)/shard_map/all_to_all | solution.py:496
  112.5 14.9 %collective-permute-start.3 = (bf16[4,256,256]{2,1,0:T(8,128)(2,1)S(1)}, bf16[4,256,256]{2,1,0:T(8,128)(2,1)S(1)}, u32[]{:S(2)}, u32[]{:S(2)}) collective-permute-start(bf16[4,256,256]{2,1,0:T(8,128)(2,1)S(1)} %pick.1), channel_id=1, source_target_pairs={{0,1},{1,0},{2,3},{3,2},{4,5},{5,4},{6,7},{7,6},{8,9},{9,8},{10,11... | collective-permute-start | bytes 1572872 | tf_op jit(solution)/shard_map/ppermute | solution.py:500
  122.7 4.7 %collective-permute-start.12 = (bf16[16,1152]{1,0:T(8,128)(2,1)S(1)}, bf16[16,1152]{1,0:T(8,128)(2,1)S(1)}, u32[]{:S(2)}, u32[]{:S(2)}) collective-permute-start(bf16[16,1152]{1,0:T(8,128)(2,1)S(1)} %sum_share.1.refs_0_), channel_id=1, source_target_pairs={{0,2},{2,4},{4,6},{6,0},{1,3},{3,5},{5,7},{7,1},{8,10},{10,12},{12... | collective-permute-start | bytes 110600 | tf_op jit(solution)/shard_map/ppermute | solution.py:525
  123.3 4.3 %collective-permute-start.13 = (bf16[16,1152]{1,0:T(8,128)(2,1)S(1)}, bf16[16,1152]{1,0:T(8,128)(2,1)S(1)}, u32[]{:S(2)}, u32[]{:S(2)}) collective-permute-start(bf16[16,1152]{1,0:T(8,128)(2,1)S(1)} %sum_share.1.refs_0_), channel_id=1, source_target_pairs={{0,4},{2,6},{4,0},{6,2},{1,5},{3,7},{5,1},{7,3},{8,12},{10,14},{12... | collective-permute-start | bytes 110600 | tf_op jit(solution)/shard_map/ppermute | solution.py:525
  125.4 3.0 %collective-permute-start.14 = (bf16[16,1152]{1,0:T(8,128)(2,1)S(1)}, bf16[16,1152]{1,0:T(8,128)(2,1)S(1)}, u32[]{:S(2)}, u32[]{:S(2)}) collective-permute-start(bf16[16,1152]{1,0:T(8,128)(2,1)S(1)} %sum_share.1.refs_0_), channel_id=1, source_target_pairs={{0,6},{2,0},{4,2},{6,4},{1,7},{3,1},{5,3},{7,5},{8,14},{10,8},{12,... | collective-permute-start | bytes 110600 | tf_op jit(solution)/shard_map/ppermute | solution.py:525
  143.9 7.3 %collective-permute-start.15 = (bf16[8,2,16,1536]{3,2,1,0:T(8,128)(2,1)S(1)}, bf16[8,2,16,1536]{3,2,1,0:T(8,128)(2,1)S(1)}, u32[]{:S(2)}, u32[]{:S(2)}) collective-permute-start(bf16[8,2,16,1536]{3,2,1,0:T(8,128)(2,1)S(1)} %bitcast.20), channel_id=1, source_target_pairs={{0,1},{1,0},{2,3},{3,2},{4,5},{5,4},{6,7},{7,6},{8,9},{9,8},{10,11... | collective-permute-start | bytes 2359304 | tf_op jit(solution)/shard_map/ppermute | solution.py:500

commit v8 on v7

--- a/solution.py
+++ b/solution.py
@@ -47,7 +47,7 @@
 
 def pack_kernel(
     hidden, wq_down, wv_down, fq, fk, fv, grad, wq_up, wv_up, out,
-    hidden_v, wq_down_v, wv_down_v, fq_v, fv_v, wq_up_v, wv_up_v, out_v, low,
+    hidden_v, down_v, fq_v, fv_v, wq_up_v, wv_up_v, out_v, low,
     down_sems, hidden_sems, row_sems, through_sems, out_sems,
 ):
     devices, rows, packed = out.shape
@@ -62,8 +62,8 @@
         return pl.ds(index * width, width)
 
     downs = [
-        pltpu.make_async_copy(wq_down, wq_down_v, down_sems.at[0]),
-        pltpu.make_async_copy(wv_down, wv_down_v, down_sems.at[1]),
+        pltpu.make_async_copy(wq_down, down_v.at[pl.ds(0, RANK)], down_sems.at[0]),
+        pltpu.make_async_copy(wv_down, down_v.at[pl.ds(RANK, RANK)], down_sems.at[1]),
     ]
     hiddens = [
         pltpu.make_async_copy(
@@ -71,53 +71,53 @@
         )
         for index in range(HIDDEN_PARTS)
     ]
+    through = [
+        pltpu.make_async_copy(
+            source.at[:, columns(device)],
+            out_v.at[device, :, columns(which)],
+            through_sems.at[which - 2, device],
+        )
+        for device in range(devices)
+        for which, source in ((2, fk), (3, grad))
+    ]
     whole = [
         pltpu.make_async_copy(wq_up, wq_up_v, row_sems.at[0]),
         pltpu.make_async_copy(fq, fq_v, row_sems.at[1]),
         pltpu.make_async_copy(wv_up, wv_up_v, row_sems.at[2]),
         pltpu.make_async_copy(fv, fv_v, row_sems.at[3]),
     ]
-    through = []
-    for device in range(devices):
-        for which, source in ((1, fk), (3, grad)):
-            through.append(
-                pltpu.make_async_copy(
-                    source.at[:, columns(device)],
-                    out_v.at[device, :, columns(which)],
-                    through_sems.at[len(through)],
-                )
-            )
-    for copy in downs + hiddens + whole + through:
+    for copy in downs + hiddens + through + whole:
         copy.start()
+
+    def leave(device, begin, size, number):
+        at = (device, slice(None), pl.ds(begin, size))
+        copy = pltpu.make_async_copy(out_v.at[at], out.at[at], out_sems.at[number, device])
+        copy.start()
+        return copy
 
     for copy in downs:
         copy.wait()
-    low_q = jnp.zeros((rows, RANK), jnp.float32)
-    low_v = jnp.zeros((rows, RANK), jnp.float32)
+    total = jnp.zeros((rows, 2 * RANK), jnp.float32)
     for index in range(HIDDEN_PARTS):
         hiddens[index].wait()
-        low_q += dot_nt(hidden_v[:, part(index)], wq_down_v[:, part(index)])
-        low_v += dot_nt(hidden_v[:, part(index)], wv_down_v[:, part(index)])
-    low[:, :RANK] = low_q.astype(jnp.bfloat16)
-    low[:, RANK:] = low_v.astype(jnp.bfloat16)
-
+        total += dot_nt(hidden_v[:, part(index)], down_v[:, part(index)])
+    low[...] = total.astype(jnp.bfloat16)
+    outs = []
+    for device in range(devices):
+        through[2 * device].wait()
+        through[2 * device + 1].wait()
+        out_v[device, :, 4 * width :] = low[...]
+        outs.append(leave(device, 2 * width, 2 * width + 2 * RANK, 0))
     for copy in whole:
         copy.wait()
-    outs = []
     for device in range(devices):
         at = slice(device * width, (device + 1) * width)
-        for which, (frozen, weight, begin) in enumerate(
-            ((fq_v, wq_up_v, 0), (fv_v, wv_up_v, RANK))
-        ):
-            added = ADAPTER_SCALE * dot(low[:, begin : begin + RANK], weight[:, at])
-            out_v[device, :, 2 * which * width : (2 * which + 1) * width] = (
+        for which, (frozen, weight) in enumerate(((fq_v, wq_up_v), (fv_v, wv_up_v))):
+            added = ADAPTER_SCALE * dot(low[:, which * RANK : (which + 1) * RANK], weight[:, at])
+            out_v[device, :, which * width : (which + 1) * width] = (
                 frozen[:, at].astype(jnp.float32) + added
             ).astype(jnp.bfloat16)
-        out_v[device, :, 4 * width :] = low[...]
-        through[2 * device].wait()
-        through[2 * device + 1].wait()
-        outs.append(pltpu.make_async_copy(out_v.at[device], out.at[device], out_sems.at[device]))
-        outs[-1].start()
+        outs.append(leave(device, 0, 2 * width, 1))
     for copy in outs:
         copy.wait()
 
@@ -134,8 +134,7 @@
         out_shape=jax.ShapeDtypeStruct((seq_size, rows, 4 * width + 2 * RANK), bf16),
         scratch_shapes=[
             pltpu.VMEM((rows, model), bf16),
-            pltpu.VMEM((RANK, model), bf16),
-            pltpu.VMEM((RANK, model), bf16),
+            pltpu.VMEM((2 * RANK, model), bf16),
             pltpu.VMEM((rows, columns), bf16),
             pltpu.VMEM((rows, columns), bf16),
             pltpu.VMEM((RANK, columns), bf16),
@@ -145,8 +144,8 @@
             pltpu.SemaphoreType.DMA((2,)),
             pltpu.SemaphoreType.DMA((HIDDEN_PARTS,)),
             pltpu.SemaphoreType.DMA((4,)),
-            pltpu.SemaphoreType.DMA((2 * seq_size,)),
-            pltpu.SemaphoreType.DMA((seq_size,)),
+            pltpu.SemaphoreType.DMA((2, seq_size)),
+            pltpu.SemaphoreType.DMA((2, seq_size)),
         ],
         compiler_params=pltpu.CompilerParams(vmem_limit_bytes=PACK_VMEM),
         name="pack",
@@ -156,7 +155,7 @@
 def attention_kernel(
     meta, packed, wq_up, wv_up, *refs
 ):
-    *outs, dq_t, dv_t, low, q_t, k_t, v_t, g_t, dv, returned, out = refs
+    *outs, dq_t, dv_t, low, q_t, k_t, v_t, g_t, dv, returned, out = refs[1:]
     outs, backs = outs[: len(outs) // 2], outs[len(outs) // 2 :]
     length = packed.shape[0]
     heads = out.shape[1] // HEAD_SIZE
@@ -171,8 +170,8 @@
 
     for head in range(heads):
         q_t[span[head], :] = packed[:, columns(0, head)].T
-        k_t[span[head], :] = packed[:, columns(1, head)].T
-        v_t[span[head], :] = packed[:, columns(2, head)].T
+        v_t[span[head], :] = packed[:, columns(1, head)].T
+        k_t[span[head], :] = packed[:, columns(2, head)].T
         g_t[span[head], :] = packed[:, columns(3, head)].T
     dv[...] = jnp.zeros_like(dv)
 
@@ -199,8 +198,8 @@
             )
             held = []
             for head in range(heads):
-                scores = dot(packed[k_rows, columns(1, head)], q_t[span[head], q_rows])
-                prob_grad = dot(packed[k_rows, columns(2, head)], g_t[span[head], q_rows])
+                scores = dot(packed[k_rows, columns(2, head)], q_t[span[head], q_rows])
+                prob_grad = dot(packed[k_rows, columns(1, head)], g_t[span[head], q_rows])
                 scores = jnp.where(in_document, scores, NEG_FILL)
                 last = jnp.where(causal, scores[(count - 1) * TILE :], NEG_FILL)
                 if count > 1:
@@ -245,7 +244,7 @@
             outs[step][holder] = out[pl.ds(begin, rows), :]
 
 
-def attention(meta, packed, wq_up, wv_up, seq_size):
+def attention(meta, packed, wq_up, wv_up, seq_size, after):
     length = packed.shape[0]
     width = (packed.shape[1] - 2 * RANK) // 4
     rows = length // seq_size
@@ -256,7 +255,7 @@
     grad_t = jax.ShapeDtypeStruct((width, length), jnp.bfloat16)
     return pl.pallas_call(
         attention_kernel,
-        in_specs=[SMEM, VMEM, VMEM, VMEM],
+        in_specs=[SMEM, VMEM, VMEM, VMEM, VMEM],
         out_specs=[VMEM] * (3 + 2 * chips),
         scratch_shapes=[
             wide_t,
@@ -270,12 +269,12 @@
         out_shape=[jax.ShapeDtypeStruct((2, rows, width), jnp.bfloat16)] * chips
         + [back] * chips
         + [grad_t, grad_t, jax.ShapeDtypeStruct((length, 2 * RANK), jnp.bfloat16)],
-        compiler_params=pltpu.CompilerParams(vmem_limit_bytes=40 << 20),
+        compiler_params=pltpu.CompilerParams(vmem_limit_bytes=32 << 20),
         cost_estimate=pl.CostEstimate(
             flops=8 << 30, bytes_accessed=16 << 20, transcendentals=4 << 20
         ),
         name="attention",
-    )(meta, packed, wq_up, wv_up)
+    )(meta, packed, wq_up, wv_up, after)
 
 
 def up_kernel(low, dq_t, dv_t, up):
@@ -312,7 +311,7 @@
     )(where, *parts)
 
 
-def arrive_kernel(where, part_0, part_1, part_2, part_3, other, out):
+def arrive_kernel(where, part_0, part_1, part_2, part_3, other, out, done):
     chip, core = where[0], where[1]
     parts = (part_0, part_1, part_2, part_3)
     width = part_0.shape[2]
@@ -322,6 +321,7 @@
         there = pl.multiple_of((origin * 2 + 1 - core) * width, width)
         out[0, :, pl.ds(here, width)] = parts[step][core]
         out[0, :, pl.ds(there, width)] = other[step]
+    done[...] = jnp.zeros_like(done)
 
 
 def arrive(where, parts, other):
@@ -329,15 +329,37 @@
     return pl.pallas_call(
         arrive_kernel,
         in_specs=[SMEM] + [VMEM] * (len(parts) + 1),
-        out_specs=VMEM,
-        out_shape=jax.ShapeDtypeStruct((1, rows, 2 * len(parts) * width), parts[0].dtype),
+        out_specs=[VMEM] * 2,
+        out_shape=[
+            jax.ShapeDtypeStruct((1, rows, 2 * len(parts) * width), parts[0].dtype),
+            jax.ShapeDtypeStruct((8, 128), jnp.float32),
+        ],
         compiler_params=pltpu.CompilerParams(vmem_limit_bytes=SMALL_VMEM),
         name="arrive",
     )(where, *parts, other)
 
 
+def halves_kernel(core, hidden, other, out):
+    rows, half = other.shape
+    out[:rows] = hidden[:, pl.ds(pl.multiple_of(core[0] * half, half), half)]
+    out[rows:] = other[...]
+
+
+def halves(core, hidden, other):
+    rows, half = other.shape
+    return pl.pallas_call(
+        halves_kernel,
+        in_specs=[SMEM, VMEM, VMEM],
+        out_specs=VMEM,
+        out_shape=jax.ShapeDtypeStruct((2 * rows, half), hidden.dtype),
+        compiler_params=pltpu.CompilerParams(vmem_limit_bytes=SMALL_VMEM),
+        name="halves",
+    )(core, hidden, other)
+
+
 def down_kernel(core, *refs):
-    *parts, hidden, hidden_other, up, out, back = refs
+    *parts, hidden, up, out, back = refs
+    rows = parts[0].shape[2]
 
     @pl.when(pl.program_id(0) == 0)
     def _():
@@ -346,7 +368,7 @@
             total += part[...].astype(jnp.float32)
         back[...] = total.astype(jnp.bfloat16)
 
-    grad = dot(back[core[0]], hidden[...]) + dot(back[1 - core[0]], hidden_other[...])
+    grad = dot(back[core[0]], hidden[:rows]) + dot(back[1 - core[0]], hidden[rows:])
     grad = grad.astype(out.dtype)
     for row in range(out.shape[0]):
         across = slice(row * SHARE_ROWS, (row + 1) * SHARE_ROWS)
@@ -354,8 +376,8 @@
         out[row, 0, :, DOWN_COLS:] = up[across, :]
 
 
-def down_gradient(core, parts, hidden, hidden_other, up):
-    rows, half = hidden_other.shape
+def down_gradient(core, parts, hidden, up):
+    rows, half = hidden.shape
     steps = half // DOWN_COLS
     across = 2 * RANK // SHARE_ROWS
     shape = parts[0].shape
@@ -366,7 +388,6 @@
             grid=(steps,),
             in_specs=[pl.BlockSpec(shape, lambda i, core: (0, 0, 0))] * len(parts)
             + [
-                pl.BlockSpec((rows, DOWN_COLS), lambda i, core: (0, core[0] * steps + i)),
                 pl.BlockSpec((rows, DOWN_COLS), lambda i, core: (0, i)),
                 pl.BlockSpec((2 * RANK, UP_COLS), lambda i, core: (0, i)),
             ],
@@ -380,7 +401,7 @@
         ),
         compiler_params=pltpu.CompilerParams(vmem_limit_bytes=24 << 20),
         name="down_gradient",
-    )(core, *parts, hidden, hidden_other, up)
+    )(core, *parts, hidden, up)
 
 
 def share_kernel(parts, *refs):
@@ -403,7 +424,7 @@
 
 
 def chips_kernel(where, *refs):
-    *parts, _, out = refs
+    *parts, out = refs
     chip = where[0]
     total = parts[0][:, :DOWN_COLS].astype(jnp.float32)
     for part in parts[1:]:
@@ -418,16 +439,16 @@
             out[device, :, pl.ds(begin, UP_COLS)] = part[:, DOWN_COLS:]
 
 
-def sum_chips(where, parts, devices, after):
+def sum_chips(where, parts, devices):
     shape = (devices, SHARE_ROWS, DOWN_COLS + len(parts) * UP_COLS)
     return pl.pallas_call(
         chips_kernel,
-        in_specs=[SMEM] + [VMEM] * (len(parts) + 1),
+        in_specs=[SMEM] + [VMEM] * len(parts),
         out_specs=VMEM,
         out_shape=jax.ShapeDtypeStruct(shape, parts[0].dtype),
         compiler_params=pltpu.CompilerParams(vmem_limit_bytes=SMALL_VMEM),
         name="sum_chips",
-    )(where, *parts, after)
+    )(where, *parts)
 
 
 def place_kernel(which, shares, *refs):
@@ -540,27 +561,30 @@
     hidden_other = to_other_core(
         lax.dynamic_slice(hidden[0], (0, (1 - core) * half), (rows, half))
     )
+    hidden_half = halves(core[None], hidden[0], hidden_other)
     width = frozen_queries.shape[2] // seq_size
     own_columns = (0, (chip * 2 + core) * width)
     wq_up = lax.dynamic_slice(query_up_weight, own_columns, (RANK, width))
     wv_up = lax.dynamic_slice(value_up_weight, own_columns, (RANK, width))
     meta = jnp.concatenate([document_length_list[0], where])
-    *outs, dq_t, dv_t, low = attention(meta, received, wq_up, wv_up, seq_size)
+    *outs, dq_t, dv_t, low = attention(
+        meta, received, wq_up, wv_up, seq_size, after=hidden_half
+    )
     parts, backs = outs[:chips], outs[chips:]
 
     backs = [backs[0]] + [to_chip(backs[step], step) for step in range(1, chips)]
     backs_other = [to_other_core(back) for back in backs]
     parts = [parts[0]] + [to_chip(parts[step], step) for step in range(1, chips)]
     up = up_gradient(low, dq_t, dv_t)
-    down = down_gradient(core[None], backs + backs_other, hidden[0], hidden_other, up)
+    down = down_gradient(core[None], backs + backs_other, hidden_half, up)
 
     other = to_other_core(pick(where, parts))
-    attended = arrive(where, parts, other)
+    attended, attended_done = arrive(where, parts, other)
 
     shares = swap(down.reshape((-1,) + down.shape[2:]), DP)
-    share = sum_share(shares, after=parts[1:])
+    share = sum_share(shares, after=[attended_done])
     share = [share] + [to_chip(share, step) for step in range(1, chips)]
-    shares = swap(sum_chips(where, share, shares.shape[0], after=other), DP)
+    shares = swap(sum_chips(where, share, shares.shape[0]), DP)
     shares = shares.reshape(down.shape[:2] + shares.shape[1:])
     shares_other = to_other_core(shares)
     grads = place(core, shares, model, seq_size * width)

time: 153 us -> 150 us (0.980)
  Pallas kernels: 32.3 us -> 29.4 us
  waiting for transfers between devices: 65.4 us -> 63.1 us
    all_to_all x2, waiting for transfers between devices: 61.5 us -> 55.3 us  [swap(): return lax.all_to_all(x, axes, 0, 0, tiled=True)]
    ppermute x7, waiting for transfers between devices: 0.51 us -> 4.59 us  [to_other_core(): return lax.ppermute(x, 'core', [(0, 1), (1, 0)])]
    pallas_call x2 -> x3, Pallas kernels: 17.5 us -> 15.3 us  [the longest x1 14.5 us: attention(): pl.pallas_call(attention_kernel, in_specs=[SMEM, VMEM, VMEM, VMEM, VMEM],...]
  transfers between devices with their start and end apart: 18 -> 18, of which waited for: 7 -> 10; matrix products, arithmetic and copies ran while one was open for 1% -> 1% of each run, Pallas kernels for 15% -> 4%
where the time goes in v8:
time: 150 us; the launch traced here: 149 us
  waiting for transfers between devices  63.1 us (42%)
  starting transfers between devices  36.4 us (24%)
  Pallas kernels  29.4 us (20%)
  blocking collectives  14.8 us (10%)
  local copies, waits for them, and re-layouts  4.72 us (3%)
    all_to_all x2, waiting for transfers between devices, swap(): return lax.all_to_all(x, axes, 0, 0, tiled=True)  55.3 us
    all_to_all x2, starting transfers between devices, swap(): return lax.all_to_all(x, axes, 0, 0, tiled=True)  15.2 us
    all_to_all x1, blocking collectives, swap(): return lax.all_to_all(x, axes, 0, 0, tiled=True)  14.8 us
    pallas_call x1, Pallas kernels, attention(): pl.pallas_call(attention_kernel, in_specs=[SMEM, VMEM, VMEM, VMEM, VMEM],...  14.5 us
    ppermute x7, starting transfers between devices, to_other_core(): return lax.ppermute(x, 'core', [(0, 1), (1, 0)])  10.8 us
    ppermute x9, starting transfers between devices, to_chip(): return lax.ppermute(x, 'y', [(c, (c + step) % chips) for c in range(chips)])  10.5 us
    pallas_call x1, Pallas kernels, pack(): pl.pallas_call(pack_kernel, in_specs=[ANY] * 9, out_specs=ANY, out_shape=...  6.85 us
    ppermute x7, waiting for transfers between devices, to_other_core(): return lax.ppermute(x, 'core', [(0, 1), (1, 0)])  4.59 us
  transfers between devices with their start and end apart: 18, of which 10 were waited for; matrix products, arithmetic and copies ran while one was open for 1% of the time, Pallas kernels for 4%

profile of v8, /device:TPU:1, one launch (start us, length us, event | category | flops | bytes accessed | tf_op | source)
XLA Modules:
  0.0 149.5 jit_solution(4656622840635007413)
XLA Ops:
  0.6 6.9 %pack.1 = bf16[8,256,1152]{2,1,0:T(8,128)(2,1)} custom-call(bf16[256,4096]{1,0:T(8,128)(2,1)} %bitcast.18, bf16[64,4096]{1,0:T(8,128)(2,1)} %bitcast.28, bf16[64,4096]{1,0:T(8,128)(2,1)} %bitcast.29, bf16[256,2048]{1,0:T(8,128)(2,1)} %bitcast.22, bf16[256,2048]{1,0:T(8,128)(2,1)} %bitcast.23, bf16[256,2048]{1,0:T(8,128)(2,1)} %bitcast.24, ...), custom_call_target="tpu_custom_call" | custom-call | tf_op jit(solution)/shard_map/pack/pallas_call | solution.py:130
  7.5 0.0 copy-start
  7.5 6.1 %all-to-all-start = ((bf16[8,256,1152]{2,1,0:T(8,128)(2,1)}), bf16[8,256,1152]{2,1,0:T(8,128)(2,1)}, u32[]{:S(2)}, u32[]{:S(2)}) async-start(bf16[8,256,1152]{2,1,0:T(8,128)(2,1)} %pack.1), calls=%async_computation | async-start | bytes 9437184 | tf_op jit(solution)/shard_map/all_to_all | solution.py:517
  13.6 1.0 dynamic-slice_bitcast_fusion
  14.7 0.1 collective-permute-start
  14.8 0.1 pad_add_fusion.1.meta
  14.9 0.8 constant_dynamic-slice_fusion
  15.6 1.9 %collective-permute-done.other = bf16[256,2048]{1,0:T(8,128)(2,1)S(1)} collective-permute-done((bf16[256,2048]{1,0:T(8,128)(2,1)}, bf16[256,2048]{1,0:T(8,128)(2,1)S(1)}, u32[]{:S(2)}, u32[]{:S(2)}) %collective-permute-start) | collective-permute-done | bytes 1048608 | tf_op jit(solution)/shard_map/ppermute | solution.py:521
  17.5 0.1 halves.1.refs_0_.refs_8_
  17.7 1.3 copy-done.1
  19.0 49.2 %all-to-all-done = bf16[8,256,1152]{2,1,0:T(8,128)(2,1)} async-done(((bf16[8,256,1152]{2,1,0:T(8,128)(2,1)}), bf16[8,256,1152]{2,1,0:T(8,128)(2,1)}, u32[]{:S(2)}, u32[]{:S(2)}) %all-to-all-start) | async-done | bytes 4718624 | tf_op jit(solution)/shard_map/all_to_all | solution.py:517
  68.1 1.6 %copy-done.2 = bf16[512,2048]{1,0:T(8,128)(2,1)S(1)} copy-done((bf16[512,2048]{1,0:T(8,128)(2,1)S(1)}, bf16[512,2048]{1,0:T(8,128)(2,1)}, u32[]{:S(2)}) %copy-start.2) | copy-done | bytes 2097176
  69.7 14.5 %attention.1 = (bf16[2,256,256]{2,1,0:T(8,128)(2,1)S(1)}, bf16[2,256,256]{2,1,0:T(8,128)(2,1)S(1)}, bf16[2,256,256]{2,1,0:T(8,128)(2,1)S(1)}, bf16[2,256,256]{2,...) custom-call(s32[10]{0:T(128)S(1)} %pad_add_fusion.1.meta, ...), custom_call_target="tpu_custom_call" | custom-call | flops 8589934592 | bytes 16777216 | tf_op jit(solution)/shard_map/attention/pallas_call | solution.py:256
  84.2 0.3 collective-permute-start.5
  84.6 1.8 %collective-permute-start.6 = (bf16[2,128,256]{2,1,0:T(8,128)(2,1)S(1)}, bf16[2,128,256]{2,1,0:T(8,128)(2,1)S(1)}, u32[]{:S(2)}, u32[]{:S(2)}) collective-permute-start(bf16[2,128,256]{2,1,0:T(8,128)(2,1)S(1)} %get-tuple-element.33), channel_id=1, source_target_pairs={{0,4},{2,6},{4,0},{6,2},{1,5},{3,7},{5,1},{7,3},{8,12},{10,14},{12... | collective-permute-start | bytes 393224 | tf_op jit(solution)/shard_map/ppermute | solution.py:546
  86.4 0.9 collective-permute-start.7
  87.3 1.4 collective-permute-start.8
  88.7 2.1 %collective-permute-done.5.refs_1_ = bf16[2,128,256]{2,1,0:T(8,128)(2,1)S(1)} collective-permute-done((bf16[2,128,256]{2,1,0:T(8,128)(2,1)S(1)}, bf16[2,128,256]{2,1,0:T(8,128)(2,1)S(1)}, u32[]{:S(2)}, u32[]{:S(2)}) %collective-permute-start.5) | collective-permute-done | bytes 131104 | tf_op jit(solution)/shard_map/ppermute | solution.py:546
  90.8 3.5 %collective-permute-start.9 = (bf16[2,128,256]{2,1,0:T(8,128)(2,1)S(1)}, bf16[2,128,256]{2,1,0:T(8,128)(2,1)S(1)}, u32[]{:S(2)}, u32[]{:S(2)}) collective-permute-start(bf16[2,128,256]{2,1,0:T(8,128)(2,1)S(1)} %collective-permute-done.5.refs_1_), channel_id=1, source_target_pairs={{0,1},{1,0},{2,3},{3,2},{4,5},{5,4},{6,7},{7,6},{8,9},{9,8},{10,11... | collective-permute-start | bytes 393224 | tf_op jit(solution)/shard_map/ppermute | solution.py:521
  94.2 0.0 collective-permute-start.1
  94.3 0.0 collective-permute-done.6.refs_2_
  94.3 0.5 collective-permute-start.2
  94.7 2.3 %collective-permute-start.3 = (bf16[2,256,256]{2,1,0:T(8,128)(2,1)S(1)}, bf16[2,256,256]{2,1,0:T(8,128)(2,1)S(1)}, u32[]{:S(2)}, u32[]{:S(2)}) collective-permute-start(bf16[2,256,256]{2,1,0:T(8,128)(2,1)S(1)} %get-tuple-element.29), channel_id=1, source_target_pairs={{0,6},{2,0},{4,2},{6,4},{1,7},{3,1},{5,3},{7,5},{8,14},{10,8},{12,... | collective-permute-start | bytes 786440 | tf_op jit(solution)/shard_map/ppermute | solution.py:546
  97.0 0.6 collective-permute-start.10
  97.6 0.1 collective-permute-start.11
  97.7 0.8 up_gradient.1.refs_9_
  98.4 0.1 collective-permute-done.10.refs_6_
  98.6 0.4 collective-permute-done.11.refs_7_
  98.9 1.7 %down_gradient.1 = bf16[8,2,16,1152]{3,2,1,0:T(8,128)(2,1)} custom-call(s32[1]{0:T(128)} %bitcast.1.core.which, bf16[2,128,256]{2,1,0:T(8,128)(2,1)S(1)} %get-tuple-element.31.refs_0_, bf16[2,128,256]{2,1,0:T(8,128)(2,1)S(1)} %collective-permute-done.5.refs_1_, bf16[2,128,256]{2,1,0:T(8,128)(2,1)S(1)} %collective-permute-done.6.refs_2_, ...), custom_call_target="tpu_custom_call" | custom-call | tf_op jit(solution)/shard_map/down_gradient/pallas_call | solution.py:384
  100.6 9.1 %all-to-all-start.1 = ((bf16[16,16,1152]{2,1,0:T(8,128)(2,1)}), bf16[16,16,1152]{2,1,0:T(8,128)(2,1)S(1)}, u32[]{:S(2)}, u32[]{:S(2)}) async-start(bf16[16,16,1152]{2,1,0:T(8,128)(2,1)} %bitcast.13), calls=%async_computation.1 | async-start | bytes 1179648 | tf_op jit(solution)/shard_map/all_to_all | solution.py:517
  109.7 0.1 pad_add_fusion.where
  109.8 0.6 pick.1
  110.4 0.7 collective-permute-start.4
  111.1 1.5 %collective-permute-done.4.other = bf16[4,256,256]{2,1,0:T(8,128)(2,1)S(1)} collective-permute-done((bf16[4,256,256]{2,1,0:T(8,128)(2,1)S(1)}, bf16[4,256,256]{2,1,0:T(8,128)(2,1)S(1)}, u32[]{:S(2)}, u32[]{:S(2)}) %collective-permute-start.4) | collective-permute-done | bytes 524320 | tf_op jit(solution)/shard_map/ppermute | solution.py:521
  112.6 1.6 %arrive.1 = (bf16[1,256,2048]{2,1,0:T(8,128)(2,1)}, f32[8,128]{1,0:T(8,128)S(1)}) custom-call(s32[2]{0:T(128)S(1)} %pad_add_fusion.where, bf16[2,256,256]{2,1,0:T(8,128)(2,1)S(1)} %get-tuple-element.26.part_0, bf16[2,256,256]{2,1,0:T(8,128)(2,1)S(1)} %collective-permute-done.1.part_1, bf16[2,256,256]{2,1,0:T(8,128)(2,1)S(1)} %collective-permute-done.2.part_2, ...), custom_call_target="tpu_custom_call" | custom-call | tf_op jit(solution)/shard_map/arrive/pallas_call | solution.py:329
  114.3 6.2 %all-to-all-done.1.parts = bf16[16,16,1152]{2,1,0:T(8,128)(2,1)S(1)} async-done(((bf16[16,16,1152]{2,1,0:T(8,128)(2,1)}), bf16[16,16,1152]{2,1,0:T(8,128)(2,1)S(1)}, u32[]{:S(2)}, u32[]{:S(2)}) %all-to-all-start.1) | async-done | bytes 589856 | tf_op jit(solution)/shard_map/all_to_all | solution.py:517
  120.5 0.1 sum_share.1.refs_0_
  120.5 0.7 collective-permute-start.12
  121.2 2.1 %collective-permute-start.13 = (bf16[16,1152]{1,0:T(8,128)(2,1)S(1)}, bf16[16,1152]{1,0:T(8,128)(2,1)S(1)}, u32[]{:S(2)}, u32[]{:S(2)}) collective-permute-start(bf16[16,1152]{1,0:T(8,128)(2,1)S(1)} %sum_share.1.refs_0_), channel_id=1, source_target_pairs={{0,4},{2,6},{4,0},{6,2},{1,5},{3,7},{5,1},{7,3},{8,12},{10,14},{12... | collective-permute-start | bytes 110600 | tf_op jit(solution)/shard_map/ppermute | solution.py:546
  123.3 2.0 %collective-permute-start.14 = (bf16[16,1152]{1,0:T(8,128)(2,1)S(1)}, bf16[16,1152]{1,0:T(8,128)(2,1)S(1)}, u32[]{:S(2)}, u32[]{:S(2)}) collective-permute-start(bf16[16,1152]{1,0:T(8,128)(2,1)S(1)} %sum_share.1.refs_0_), channel_id=1, source_target_pairs={{0,6},{2,0},{4,2},{6,4},{1,7},{3,1},{5,3},{7,5},{8,14},{10,8},{12,... | collective-permute-start | bytes 110600 | tf_op jit(solution)/shard_map/ppermute | solution.py:546
  125.3 0.3 collective-permute-done.13.refs_2_
  125.5 0.8 collective-permute-done.14.refs_3_
  126.3 0.6 sum_chips.1
  127.0 14.8 %all_to_all.15 = bf16[16,16,1536]{2,1,0:T(8,128)(2,1)S(1)} all-to-all(bf16[16,16,1536]{2,1,0:T(8,128)(2,1)S(1)} %sum_chips.1), channel_id=1, replica_groups=mesh['x'=4,'z'=4,'y'=4,'core'=2] {'x','z'}, dimensions={0} | all-to-all | bytes 1572864 | tf_op jit(solution)/shard_map/all_to_all | solution.py:517
  141.8 4.4 %collective-permute-start.15 = (bf16[8,2,16,1536]{3,2,1,0:T(8,128)(2,1)S(1)}, bf16[8,2,16,1536]{3,2,1,0:T(8,128)(2,1)S(1)}, u32[]{:S(2)}, u32[]{:S(2)}) collective-permute-start(bf16[8,2,16,1536]{3,2,1,0:T(8,128)(2,1)S(1)} %bitcast.20), channel_id=1, source_target_pairs={{0,1},{1,0},{2,3},{3,2},{4,5},{5,4},{6,7},{7,6},{8,9},{9,8},{10,11... | collective-permute-start | bytes 2359304 | tf_op jit(solution)/shard_map/ppermute | solution.py:521
  146.2 1.2 place.2
  147.4 0.7 collective-permute-done.15.shares
  148.1 1.2 place.3
  (12 shorter events, 0.0 us)
Async XLA Ops:
  7.5 6.1 %copy-start = (bf16[1,256,4096]{2,1,0:T(8,128)(2,1)S(1)}, bf16[1,256,4096]{2,1,0:T(8,128)(2,1)}, u32[]{:S(2)}) copy-start(bf16[1,256,4096]{2,1,0:T(8,128)(2,1)} %param.10) | copy-start | bytes 6291460
  7.5 60.6 %all-to-all-start = ((bf16[8,256,1152]{2,1,0:T(8,128)(2,1)}), bf16[8,256,1152]{2,1,0:T(8,128)(2,1)}, u32[]{:S(2)}, u32[]{:S(2)}) async-start(bf16[8,256,1152]{2,1,0:T(8,128)(2,1)} %pack.1), calls=%async_computation | async-start | bytes 9437184 | tf_op jit(solution)/shard_map/all_to_all | solution.py:517
  13.6 1.2 copy-start.3
  14.7 2.9 %collective-permute-start = (bf16[256,2048]{1,0:T(8,128)(2,1)}, bf16[256,2048]{1,0:T(8,128)(2,1)S(1)}, u32[]{:S(2)}, u32[]{:S(2)}) collective-permute-start(bf16[256,2048]{1,0:T(8,128)(2,1)} %dynamic-slice_bitcast_fusion), channel_id=1, source_target_pairs={{0,1},{1,0},{2,3},{3,2},{4,5},{5,4},{6,7},{7,6},{8,9},{9,8},{10,11... | collective-permute-start | bytes 3145736 | tf_op jit(solution)/shard_map/ppermute | solution.py:521
  17.7 1.3 copy-start.1
  68.1 1.6 %copy-start.2 = (bf16[512,2048]{1,0:T(8,128)(2,1)S(1)}, bf16[512,2048]{1,0:T(8,128)(2,1)}, u32[]{:S(2)}) copy-start(bf16[512,2048]{1,0:T(8,128)(2,1)} %copy-done.1) | copy-start | bytes 6291460
  84.2 6.5 %collective-permute-start.5 = (bf16[2,128,256]{2,1,0:T(8,128)(2,1)S(1)}, bf16[2,128,256]{2,1,0:T(8,128)(2,1)S(1)}, u32[]{:S(2)}, u32[]{:S(2)}) collective-permute-start(bf16[2,128,256]{2,1,0:T(8,128)(2,1)S(1)} %get-tuple-element.32), channel_id=1, source_target_pairs={{0,2},{2,4},{4,6},{6,0},{1,3},{3,5},{5,7},{7,1},{8,10},{10,12},{12... | collective-permute-start | bytes 393224 | tf_op jit(solution)/shard_map/ppermute | solution.py:546
  84.6 9.7 %collective-permute-start.6 = (bf16[2,128,256]{2,1,0:T(8,128)(2,1)S(1)}, bf16[2,128,256]{2,1,0:T(8,128)(2,1)S(1)}, u32[]{:S(2)}, u32[]{:S(2)}) collective-permute-start(bf16[2,128,256]{2,1,0:T(8,128)(2,1)S(1)} %get-tuple-element.33), channel_id=1, source_target_pairs={{0,4},{2,6},{4,0},{6,2},{1,5},{3,7},{5,1},{7,3},{8,12},{10,14},{12... | collective-permute-start | bytes 393224 | tf_op jit(solution)/shard_map/ppermute | solution.py:546
  86.4 8.4 %collective-permute-start.7 = (bf16[2,128,256]{2,1,0:T(8,128)(2,1)S(1)}, bf16[2,128,256]{2,1,0:T(8,128)(2,1)S(1)}, u32[]{:S(2)}, u32[]{:S(2)}) collective-permute-start(bf16[2,128,256]{2,1,0:T(8,128)(2,1)S(1)} %get-tuple-element.34), channel_id=1, source_target_pairs={{0,6},{2,0},{4,2},{6,4},{1,7},{3,1},{5,3},{7,5},{8,14},{10,8},{12,... | collective-permute-start | bytes 393224 | tf_op jit(solution)/shard_map/ppermute | solution.py:546
  87.3 9.7 %collective-permute-start.8 = (bf16[2,128,256]{2,1,0:T(8,128)(2,1)S(1)}, bf16[2,128,256]{2,1,0:T(8,128)(2,1)S(1)}, u32[]{:S(2)}, u32[]{:S(2)}) collective-permute-start(bf16[2,128,256]{2,1,0:T(8,128)(2,1)S(1)} %get-tuple-element.31.refs_0_), channel_id=1, source_target_pairs={{0,1},{1,0},{2,3},{3,2},{4,5},{5,4},{6,7},{7,6},{8,9},{9,8},{10,11... | collective-permute-start | bytes 393224 | tf_op jit(solution)/shard_map/ppermute | solution.py:521
  90.8 6.8 %collective-permute-start.9 = (bf16[2,128,256]{2,1,0:T(8,128)(2,1)S(1)}, bf16[2,128,256]{2,1,0:T(8,128)(2,1)S(1)}, u32[]{:S(2)}, u32[]{:S(2)}) collective-permute-start(bf16[2,128,256]{2,1,0:T(8,128)(2,1)S(1)} %collective-permute-done.5.refs_1_), channel_id=1, source_target_pairs={{0,1},{1,0},{2,3},{3,2},{4,5},{5,4},{6,7},{7,6},{8,9},{9,8},{10,11... | collective-permute-start | bytes 393224 | tf_op jit(solution)/shard_map/ppermute | solution.py:521
  94.2 15.5 %collective-permute-start.1 = (bf16[2,256,256]{2,1,0:T(8,128)(2,1)S(1)}, bf16[2,256,256]{2,1,0:T(8,128)(2,1)S(1)}, u32[]{:S(2)}, u32[]{:S(2)}) collective-permute-start(bf16[2,256,256]{2,1,0:T(8,128)(2,1)S(1)} %get-tuple-element.27), channel_id=1, source_target_pairs={{0,2},{2,4},{4,6},{6,0},{1,3},{3,5},{5,7},{7,1},{8,10},{10,12},{12... | collective-permute-start | bytes 786440 | tf_op jit(solution)/shard_map/ppermute | solution.py:546
  94.3 15.5 %collective-permute-start.2 = (bf16[2,256,256]{2,1,0:T(8,128)(2,1)S(1)}, bf16[2,256,256]{2,1,0:T(8,128)(2,1)S(1)}, u32[]{:S(2)}, u32[]{:S(2)}) collective-permute-start(bf16[2,256,256]{2,1,0:T(8,128)(2,1)S(1)} %get-tuple-element.28), channel_id=1, source_target_pairs={{0,4},{2,6},{4,0},{6,2},{1,5},{3,7},{5,1},{7,3},{8,12},{10,14},{12... | collective-permute-start | bytes 786440 | tf_op jit(solution)/shard_map/ppermute | solution.py:546
  94.7 15.1 %collective-permute-start.3 = (bf16[2,256,256]{2,1,0:T(8,128)(2,1)S(1)}, bf16[2,256,256]{2,1,0:T(8,128)(2,1)S(1)}, u32[]{:S(2)}, u32[]{:S(2)}) collective-permute-start(bf16[2,256,256]{2,1,0:T(8,128)(2,1)S(1)} %get-tuple-element.29), channel_id=1, source_target_pairs={{0,6},{2,0},{4,2},{6,4},{1,7},{3,1},{5,3},{7,5},{8,14},{10,8},{12,... | collective-permute-start | bytes 786440 | tf_op jit(solution)/shard_map/ppermute | solution.py:546
  97.0 1.6 %collective-permute-start.10 = (bf16[2,128,256]{2,1,0:T(8,128)(2,1)S(1)}, bf16[2,128,256]{2,1,0:T(8,128)(2,1)S(1)}, u32[]{:S(2)}, u32[]{:S(2)}) collective-permute-start(bf16[2,128,256]{2,1,0:T(8,128)(2,1)S(1)} %collective-permute-done.6.refs_2_), channel_id=1, source_target_pairs={{0,1},{1,0},{2,3},{3,2},{4,5},{5,4},{6,7},{7,6},{8,9},{9,8},{10,11... | collective-permute-start | bytes 393224 | tf_op jit(solution)/shard_map/ppermute | solution.py:521
  97.6 1.3 collective-permute-start.11
  100.6 19.9 %all-to-all-start.1 = ((bf16[16,16,1152]{2,1,0:T(8,128)(2,1)}), bf16[16,16,1152]{2,1,0:T(8,128)(2,1)S(1)}, u32[]{:S(2)}, u32[]{:S(2)}) async-start(bf16[16,16,1152]{2,1,0:T(8,128)(2,1)} %bitcast.13), calls=%async_computation.1 | async-start | bytes 1179648 | tf_op jit(solution)/shard_map/all_to_all | solution.py:517
  110.4 2.2 %collective-permute-start.4 = (bf16[4,256,256]{2,1,0:T(8,128)(2,1)S(1)}, bf16[4,256,256]{2,1,0:T(8,128)(2,1)S(1)}, u32[]{:S(2)}, u32[]{:S(2)}) collective-permute-start(bf16[4,256,256]{2,1,0:T(8,128)(2,1)S(1)} %pick.1), channel_id=1, source_target_pairs={{0,1},{1,0},{2,3},{3,2},{4,5},{5,4},{6,7},{7,6},{8,9},{9,8},{10,11... | collective-permute-start | bytes 1572872 | tf_op jit(solution)/shard_map/ppermute | solution.py:521
  120.5 4.7 %collective-permute-start.12 = (bf16[16,1152]{1,0:T(8,128)(2,1)S(1)}, bf16[16,1152]{1,0:T(8,128)(2,1)S(1)}, u32[]{:S(2)}, u32[]{:S(2)}) collective-permute-start(bf16[16,1152]{1,0:T(8,128)(2,1)S(1)} %sum_share.1.refs_0_), channel_id=1, source_target_pairs={{0,2},{2,4},{4,6},{6,0},{1,3},{3,5},{5,7},{7,1},{8,10},{10,12},{12... | collective-permute-start | bytes 110600 | tf_op jit(solution)/shard_map/ppermute | solution.py:546
  121.2 4.3 %collective-permute-start.13 = (bf16[16,1152]{1,0:T(8,128)(2,1)S(1)}, bf16[16,1152]{1,0:T(8,128)(2,1)S(1)}, u32[]{:S(2)}, u32[]{:S(2)}) collective-permute-start(bf16[16,1152]{1,0:T(8,128)(2,1)S(1)} %sum_share.1.refs_0_), channel_id=1, source_target_pairs={{0,4},{2,6},{4,0},{6,2},{1,5},{3,7},{5,1},{7,3},{8,12},{10,14},{12... | collective-permute-start | bytes 110600 | tf_op jit(solution)/shard_map/ppermute | solution.py:546
  123.3 3.0 %collective-permute-start.14 = (bf16[16,1152]{1,0:T(8,128)(2,1)S(1)}, bf16[16,1152]{1,0:T(8,128)(2,1)S(1)}, u32[]{:S(2)}, u32[]{:S(2)}) collective-permute-start(bf16[16,1152]{1,0:T(8,128)(2,1)S(1)} %sum_share.1.refs_0_), channel_id=1, source_target_pairs={{0,6},{2,0},{4,2},{6,4},{1,7},{3,1},{5,3},{7,5},{8,14},{10,8},{12,... | collective-permute-start | bytes 110600 | tf_op jit(solution)/shard_map/ppermute | solution.py:546
  141.8 6.3 %collective-permute-start.15 = (bf16[8,2,16,1536]{3,2,1,0:T(8,128)(2,1)S(1)}, bf16[8,2,16,1536]{3,2,1,0:T(8,128)(2,1)S(1)}, u32[]{:S(2)}, u32[]{:S(2)}) collective-permute-start(bf16[8,2,16,1536]{3,2,1,0:T(8,128)(2,1)S(1)} %bitcast.20), channel_id=1, source_target_pairs={{0,1},{1,0},{2,3},{3,2},{4,5},{5,4},{6,7},{7,6},{8,9},{9,8},{10,11... | collective-permute-start | bytes 2359304 | tf_op jit(solution)/shard_map/ppermute | solution.py:521

commit v9 on v8

--- a/solution.py
+++ b/solution.py
@@ -43,6 +43,7 @@
 VMEM = pl.BlockSpec(memory_space=pltpu.VMEM)
 SMEM = pl.BlockSpec(memory_space=pltpu.SMEM)
 ANY = pl.BlockSpec(memory_space=pl.ANY)
+DONE = jax.ShapeDtypeStruct((8, 128), jnp.float32)
 
 
 def pack_kernel(
@@ -332,17 +333,36 @@
         out_specs=[VMEM] * 2,
         out_shape=[
             jax.ShapeDtypeStruct((1, rows, 2 * len(parts) * width), parts[0].dtype),
-            jax.ShapeDtypeStruct((8, 128), jnp.float32),
+            DONE,
         ],
         compiler_params=pltpu.CompilerParams(vmem_limit_bytes=SMALL_VMEM),
         name="arrive",
     )(where, *parts, other)
 
 
-def halves_kernel(core, hidden, other, out):
+def backs_kernel(part_0, part_1, part_2, part_3, out):
+    total = part_0[...].astype(jnp.float32)
+    for part in (part_1, part_2, part_3):
+        total += part[...].astype(jnp.float32)
+    out[...] = total.astype(out.dtype)
+
+
+def sum_backs(parts):
+    return pl.pallas_call(
+        backs_kernel,
+        in_specs=[VMEM] * len(parts),
+        out_specs=VMEM,
+        out_shape=jax.ShapeDtypeStruct(parts[0].shape, parts[0].dtype),
+        compiler_params=pltpu.CompilerParams(vmem_limit_bytes=SMALL_VMEM),
+        name="sum_backs",
+    )(*parts)
+
+
+def halves_kernel(core, hidden, other, out, done):
     rows, half = other.shape
     out[:rows] = hidden[:, pl.ds(pl.multiple_of(core[0] * half, half), half)]
     out[rows:] = other[...]
+    done[...] = jnp.zeros_like(done)
 
 
 def halves(core, hidden, other):
@@ -350,8 +370,8 @@
     return pl.pallas_call(
         halves_kernel,
         in_specs=[SMEM, VMEM, VMEM],
-        out_specs=VMEM,
-        out_shape=jax.ShapeDtypeStruct((2 * rows, half), hidden.dtype),
+        out_specs=[VMEM] * 2,
+        out_shape=[jax.ShapeDtypeStruct((2 * rows, half), hidden.dtype), DONE],
         compiler_params=pltpu.CompilerParams(vmem_limit_bytes=SMALL_VMEM),
         name="halves",
     )(core, hidden, other)
@@ -561,22 +581,23 @@
     hidden_other = to_other_core(
         lax.dynamic_slice(hidden[0], (0, (1 - core) * half), (rows, half))
     )
-    hidden_half = halves(core[None], hidden[0], hidden_other)
+    hidden_half, halves_done = halves(core[None], hidden[0], hidden_other)
     width = frozen_queries.shape[2] // seq_size
     own_columns = (0, (chip * 2 + core) * width)
     wq_up = lax.dynamic_slice(query_up_weight, own_columns, (RANK, width))
     wv_up = lax.dynamic_slice(value_up_weight, own_columns, (RANK, width))
     meta = jnp.concatenate([document_length_list[0], where])
     *outs, dq_t, dv_t, low = attention(
-        meta, received, wq_up, wv_up, seq_size, after=hidden_half
+        meta, received, wq_up, wv_up, seq_size, after=halves_done
     )
     parts, backs = outs[:chips], outs[chips:]
 
     backs = [backs[0]] + [to_chip(backs[step], step) for step in range(1, chips)]
-    backs_other = [to_other_core(back) for back in backs]
+    back = sum_backs(backs)
+    back_other = to_other_core(back)
     parts = [parts[0]] + [to_chip(parts[step], step) for step in range(1, chips)]
     up = up_gradient(low, dq_t, dv_t)
-    down = down_gradient(core[None], backs + backs_other, hidden_half, up)
+    down = down_gradient(core[None], [back, back_other], hidden_half, up)
 
     other = to_other_core(pick(where, parts))
     attended, attended_done = arrive(where, parts, other)

time: 150 us -> 151 us (level)
  waiting for transfers between devices: 63.1 us -> 66 us
  starting transfers between devices: 36.4 us -> 34.5 us
  local copies, waits for them, and re-layouts: 4.72 us -> 3.14 us
    ppermute x9, waiting for transfers between devices: 3.15 us -> 6.22 us  [to_chip(): return lax.ppermute(x, 'y', [(c, (c + step) % chips) for c in range(chips)])]
    ppermute x7 -> x4, starting transfers between devices: 10.8 us -> 7.93 us  [to_other_core(): return lax.ppermute(x, 'core', [(0, 1), (1, 0)])]
    ppermute x9, starting transfers between devices: 10.5 us -> 13 us  [to_chip(): return lax.ppermute(x, 'y', [(c, (c + step) % chips) for c in range(chips)])]
    all_to_all x2, starting transfers between devices: 15.2 us -> 13.6 us  [swap(): return lax.all_to_all(x, axes, 0, 0, tiled=True)]
    unnamed x8, local copies, waits for them, and re-layouts: 2.9 us -> 1.32 us
    pallas_call x1, Pallas kernels: 14.5 us -> 16 us  [attention(): pl.pallas_call(attention_kernel, in_specs=[SMEM, VMEM, VMEM, VMEM, VMEM],...]
    ppermute x7 -> x4, waiting for transfers between devices: 4.59 us -> 4.3 us  [to_other_core(): return lax.ppermute(x, 'core', [(0, 1), (1, 0)])]
  transfers between devices with their start and end apart: 18 -> 15, of which waited for: 10 -> 11; matrix products, arithmetic and copies ran while one was open for 1% -> 1% of each run, Pallas kernels for 4% -> 4%
where the time goes in v9:
time: 151 us; the launch traced here: 150 us
  waiting for transfers between devices  66 us (44%)
  starting transfers between devices  34.5 us (23%)
  Pallas kernels  30.9 us (20%)
  blocking collectives  14.4 us (10%)
  local copies, waits for them, and re-layouts  3.14 us (2%)
    all_to_all x2, waiting for transfers between devices, swap(): return lax.all_to_all(x, axes, 0, 0, tiled=True)  55.5 us
    pallas_call x1, Pallas kernels, attention(): pl.pallas_call(attention_kernel, in_specs=[SMEM, VMEM, VMEM, VMEM, VMEM],...  16 us
    all_to_all x1, blocking collectives, swap(): return lax.all_to_all(x, axes, 0, 0, tiled=True)  14.4 us
    all_to_all x2, starting transfers between devices, swap(): return lax.all_to_all(x, axes, 0, 0, tiled=True)  13.6 us
    ppermute x9, starting transfers between devices, to_chip(): return lax.ppermute(x, 'y', [(c, (c + step) % chips) for c in range(chips)])  13 us
    ppermute x4, starting transfers between devices, to_other_core(): return lax.ppermute(x, 'core', [(0, 1), (1, 0)])  7.93 us
    pallas_call x1, Pallas kernels, pack(): pl.pallas_call(pack_kernel, in_specs=[ANY] * 9, out_specs=ANY, out_shape=...  6.87 us
    ppermute x9, waiting for transfers between devices, to_chip(): return lax.ppermute(x, 'y', [(c, (c + step) % chips) for c in range(chips)])  6.22 us
  transfers between devices with their start and end apart: 15, of which 11 were waited for; matrix products, arithmetic and copies ran while one was open for 1% of the time, Pallas kernels for 4%

profile of v9, /device:TPU:1, one launch (start us, length us, event | category | flops | bytes accessed | tf_op | source)
XLA Modules:
  0.0 149.9 jit_solution(10197750401671652048)
XLA Ops:
  0.6 6.9 %pack.1 = bf16[8,256,1152]{2,1,0:T(8,128)(2,1)} custom-call(bf16[256,4096]{1,0:T(8,128)(2,1)} %bitcast.18, bf16[64,4096]{1,0:T(8,128)(2,1)} %bitcast.28, bf16[64,4096]{1,0:T(8,128)(2,1)} %bitcast.29, bf16[256,2048]{1,0:T(8,128)(2,1)} %bitcast.22, bf16[256,2048]{1,0:T(8,128)(2,1)} %bitcast.23, bf16[256,2048]{1,0:T(8,128)(2,1)} %bitcast.24, ...), custom_call_target="tpu_custom_call" | custom-call | tf_op jit(solution)/shard_map/pack/pallas_call | solution.py:131
  7.5 0.0 copy-start
  7.5 6.1 %all-to-all-start = ((bf16[8,256,1152]{2,1,0:T(8,128)(2,1)}), bf16[8,256,1152]{2,1,0:T(8,128)(2,1)}, u32[]{:S(2)}, u32[]{:S(2)}) async-start(bf16[8,256,1152]{2,1,0:T(8,128)(2,1)} %pack.1), calls=%async_computation | async-start | bytes 9437184 | tf_op jit(solution)/shard_map/all_to_all | solution.py:537
  13.6 1.0 dynamic-slice_bitcast_fusion
  14.7 0.1 collective-permute-start
  14.8 0.1 pad_add_fusion.1.meta
  14.9 0.8 constant_dynamic-slice_fusion
  15.7 1.9 %collective-permute-done.other = bf16[256,2048]{1,0:T(8,128)(2,1)S(1)} collective-permute-done((bf16[256,2048]{1,0:T(8,128)(2,1)}, bf16[256,2048]{1,0:T(8,128)(2,1)S(1)}, u32[]{:S(2)}, u32[]{:S(2)}) %collective-permute-start) | collective-permute-done | bytes 1048608 | tf_op jit(solution)/shard_map/ppermute | solution.py:541
  17.5 0.1 halves.1
  17.7 1.3 copy-done.1
  19.0 49.2 %all-to-all-done = bf16[8,256,1152]{2,1,0:T(8,128)(2,1)} async-done(((bf16[8,256,1152]{2,1,0:T(8,128)(2,1)}), bf16[8,256,1152]{2,1,0:T(8,128)(2,1)}, u32[]{:S(2)}, u32[]{:S(2)}) %all-to-all-start) | async-done | bytes 4718624 | tf_op jit(solution)/shard_map/all_to_all | solution.py:537
  68.2 16.0 %attention.1 = (bf16[2,256,256]{2,1,0:T(8,128)(2,1)S(1)}, bf16[2,256,256]{2,1,0:T(8,128)(2,1)S(1)}, bf16[2,256,256]{2,1,0:T(8,128)(2,1)S(1)}, bf16[2,256,256]{2,...) custom-call(s32[10]{0:T(128)S(1)} %pad_add_fusion.1.meta, ...), custom_call_target="tpu_custom_call" | custom-call | flops 8589934592 | bytes 16777216 | tf_op jit(solution)/shard_map/attention/pallas_call | solution.py:257
  84.2 0.4 collective-permute-start.5
  84.6 1.8 %collective-permute-start.6 = (bf16[2,128,256]{2,1,0:T(8,128)(2,1)S(1)}, bf16[2,128,256]{2,1,0:T(8,128)(2,1)S(1)}, u32[]{:S(2)}, u32[]{:S(2)}) collective-permute-start(bf16[2,128,256]{2,1,0:T(8,128)(2,1)S(1)} %get-tuple-element.36), channel_id=1, source_target_pairs={{0,4},{2,6},{4,0},{6,2},{1,5},{3,7},{5,1},{7,3},{8,12},{10,14},{12... | collective-permute-start | bytes 393224 | tf_op jit(solution)/shard_map/ppermute | solution.py:566
  86.4 0.9 collective-permute-start.7
  87.2 0.6 collective-permute-start.1
  87.8 1.5 %collective-permute-start.2 = (bf16[2,256,256]{2,1,0:T(8,128)(2,1)S(1)}, bf16[2,256,256]{2,1,0:T(8,128)(2,1)S(1)}, u32[]{:S(2)}, u32[]{:S(2)}) collective-permute-start(bf16[2,256,256]{2,1,0:T(8,128)(2,1)S(1)} %get-tuple-element.31), channel_id=1, source_target_pairs={{0,4},{2,6},{4,0},{6,2},{1,5},{3,7},{5,1},{7,3},{8,12},{10,14},{12... | collective-permute-start | bytes 786440 | tf_op jit(solution)/shard_map/ppermute | solution.py:566
  89.3 1.4 collective-permute-done.5.part_1
  90.7 0.7 collective-permute-start.3
  91.4 0.4 collective-permute-done.6.part_2
  91.8 2.2 %collective-permute-done.7.part_3 = bf16[2,128,256]{2,1,0:T(8,128)(2,1)S(1)} collective-permute-done((bf16[2,128,256]{2,1,0:T(8,128)(2,1)S(1)}, bf16[2,128,256]{2,1,0:T(8,128)(2,1)S(1)}, u32[]{:S(2)}, u32[]{:S(2)}) %collective-permute-start.7) | collective-permute-done | bytes 131104 | tf_op jit(solution)/shard_map/ppermute | solution.py:566
  94.0 0.1 sum_backs.1.refs_0_
  94.1 2.5 %collective-permute-start.8 = (bf16[2,128,256]{2,1,0:T(8,128)(2,1)S(1)}, bf16[2,128,256]{2,1,0:T(8,128)(2,1)S(1)}, u32[]{:S(2)}, u32[]{:S(2)}) collective-permute-start(bf16[2,128,256]{2,1,0:T(8,128)(2,1)S(1)} %sum_backs.1.refs_0_), channel_id=1, source_target_pairs={{0,1},{1,0},{2,3},{3,2},{4,5},{5,4},{6,7},{7,6},{8,9},{9,8},{10,11... | collective-permute-start | bytes 393224 | tf_op jit(solution)/shard_map/ppermute | solution.py:541
  96.6 0.8 up_gradient.1.refs_3_
  97.4 0.2 collective-permute-done.8.refs_1_
  97.6 1.6 %down_gradient.1 = bf16[8,2,16,1152]{3,2,1,0:T(8,128)(2,1)} custom-call(s32[1]{0:T(128)} %bitcast.1.core.which, bf16[2,128,256]{2,1,0:T(8,128)(2,1)S(1)} %sum_backs.1.refs_0_, bf16[2,128,256]{2,1,0:T(8,128)(2,1)S(1)} %collective-permute-done.8.refs_1_, bf16[512,2048]{1,0:T(8,128)(2,1)S(1)} %copy-done.2, bf16[128,256]{1,0:T(8,128)(2,1)S(1)} %up_gradient.1.refs_3_), custom_call_target="tpu_custom_call" | custom-call | tf_op jit(solution)/shard_map/down_gradient/pallas_call | solution.py:404
  99.2 7.5 %all-to-all-start.1 = ((bf16[16,16,1152]{2,1,0:T(8,128)(2,1)}), bf16[16,16,1152]{2,1,0:T(8,128)(2,1)S(1)}, u32[]{:S(2)}, u32[]{:S(2)}) async-start(bf16[16,16,1152]{2,1,0:T(8,128)(2,1)} %bitcast.13), calls=%async_computation.1 | async-start | bytes 1179648 | tf_op jit(solution)/shard_map/all_to_all | solution.py:537
  106.7 0.1 pad_add_fusion.where
  106.8 0.0 collective-permute-done.1.part_1
  106.8 0.0 collective-permute-done.2.part_2
  106.8 0.0 collective-permute-done.3.part_3
  106.8 0.6 pick.1
  107.4 0.7 collective-permute-start.4
  108.1 1.5 %collective-permute-done.4.other = bf16[4,256,256]{2,1,0:T(8,128)(2,1)S(1)} collective-permute-done((bf16[4,256,256]{2,1,0:T(8,128)(2,1)S(1)}, bf16[4,256,256]{2,1,0:T(8,128)(2,1)S(1)}, u32[]{:S(2)}, u32[]{:S(2)}) %collective-permute-start.4) | collective-permute-done | bytes 524320 | tf_op jit(solution)/shard_map/ppermute | solution.py:541
  109.6 1.6 %arrive.1 = (bf16[1,256,2048]{2,1,0:T(8,128)(2,1)}, f32[8,128]{1,0:T(8,128)S(1)}) custom-call(s32[2]{0:T(128)S(1)} %pad_add_fusion.where, bf16[2,256,256]{2,1,0:T(8,128)(2,1)S(1)} %get-tuple-element.29.part_0, bf16[2,256,256]{2,1,0:T(8,128)(2,1)S(1)} %collective-permute-done.1.part_1, bf16[2,256,256]{2,1,0:T(8,128)(2,1)S(1)} %collective-permute-done.2.part_2, ...), custom_call_target="tpu_custom_call" | custom-call | tf_op jit(solution)/shard_map/arrive/pallas_call | solution.py:330
  111.3 6.3 %all-to-all-done.1.parts = bf16[16,16,1152]{2,1,0:T(8,128)(2,1)S(1)} async-done(((bf16[16,16,1152]{2,1,0:T(8,128)(2,1)}), bf16[16,16,1152]{2,1,0:T(8,128)(2,1)S(1)}, u32[]{:S(2)}, u32[]{:S(2)}) %all-to-all-start.1) | async-done | bytes 589856 | tf_op jit(solution)/shard_map/all_to_all | solution.py:537
  117.6 0.1 sum_share.1.refs_0_
  117.7 4.7 %collective-permute-start.9 = (bf16[16,1152]{1,0:T(8,128)(2,1)S(1)}, bf16[16,1152]{1,0:T(8,128)(2,1)S(1)}, u32[]{:S(2)}, u32[]{:S(2)}) collective-permute-start(bf16[16,1152]{1,0:T(8,128)(2,1)S(1)} %sum_share.1.refs_0_), channel_id=1, source_target_pairs={{0,2},{2,4},{4,6},{6,0},{1,3},{3,5},{5,7},{7,1},{8,10},{10,12},{12... | collective-permute-start | bytes 110600 | tf_op jit(solution)/shard_map/ppermute | solution.py:566
  122.3 1.6 %collective-permute-start.10 = (bf16[16,1152]{1,0:T(8,128)(2,1)S(1)}, bf16[16,1152]{1,0:T(8,128)(2,1)S(1)}, u32[]{:S(2)}, u32[]{:S(2)}) collective-permute-start(bf16[16,1152]{1,0:T(8,128)(2,1)S(1)} %sum_share.1.refs_0_), channel_id=1, source_target_pairs={{0,4},{2,6},{4,0},{6,2},{1,5},{3,7},{5,1},{7,3},{8,12},{10,14},{12... | collective-permute-start | bytes 110600 | tf_op jit(solution)/shard_map/ppermute | solution.py:566
  123.9 0.9 collective-permute-start.11
  124.8 1.9 %collective-permute-done.10.refs_2_ = bf16[16,1152]{1,0:T(8,128)(2,1)S(1)} collective-permute-done((bf16[16,1152]{1,0:T(8,128)(2,1)S(1)}, bf16[16,1152]{1,0:T(8,128)(2,1)S(1)}, u32[]{:S(2)}, u32[]{:S(2)}) %collective-permute-start.10) | collective-permute-done | bytes 36896 | tf_op jit(solution)/shard_map/ppermute | solution.py:566
  126.8 0.3 collective-permute-done.11.refs_3_
  127.1 0.6 sum_chips.1
  127.7 14.4 %all_to_all.15 = bf16[16,16,1536]{2,1,0:T(8,128)(2,1)S(1)} all-to-all(bf16[16,16,1536]{2,1,0:T(8,128)(2,1)S(1)} %sum_chips.1), channel_id=1, replica_groups=mesh['x'=4,'z'=4,'y'=4,'core'=2] {'x','z'}, dimensions={0} | all-to-all | bytes 1572864 | tf_op jit(solution)/shard_map/all_to_all | solution.py:537
  142.0 4.5 %collective-permute-start.12 = (bf16[8,2,16,1536]{3,2,1,0:T(8,128)(2,1)S(1)}, bf16[8,2,16,1536]{3,2,1,0:T(8,128)(2,1)S(1)}, u32[]{:S(2)}, u32[]{:S(2)}) collective-permute-start(bf16[8,2,16,1536]{3,2,1,0:T(8,128)(2,1)S(1)} %bitcast.20), channel_id=1, source_target_pairs={{0,1},{1,0},{2,3},{3,2},{4,5},{5,4},{6,7},{7,6},{8,9},{9,8},{10,11... | collective-permute-start | bytes 2359304 | tf_op jit(solution)/shard_map/ppermute | solution.py:541
  146.6 1.2 place.2
  147.8 0.7 collective-permute-done.12.shares
  148.5 1.2 place.3
  (7 shorter events, 0.0 us)
Async XLA Ops:
  7.5 6.1 %copy-start = (bf16[1,256,4096]{2,1,0:T(8,128)(2,1)S(1)}, bf16[1,256,4096]{2,1,0:T(8,128)(2,1)}, u32[]{:S(2)}) copy-start(bf16[1,256,4096]{2,1,0:T(8,128)(2,1)} %param.10) | copy-start | bytes 6291460
  7.5 60.6 %all-to-all-start = ((bf16[8,256,1152]{2,1,0:T(8,128)(2,1)}), bf16[8,256,1152]{2,1,0:T(8,128)(2,1)}, u32[]{:S(2)}, u32[]{:S(2)}) async-start(bf16[8,256,1152]{2,1,0:T(8,128)(2,1)} %pack.1), calls=%async_computation | async-start | bytes 9437184 | tf_op jit(solution)/shard_map/all_to_all | solution.py:537
  13.6 1.2 copy-start.3
  14.7 2.9 %collective-permute-start = (bf16[256,2048]{1,0:T(8,128)(2,1)}, bf16[256,2048]{1,0:T(8,128)(2,1)S(1)}, u32[]{:S(2)}, u32[]{:S(2)}) collective-permute-start(bf16[256,2048]{1,0:T(8,128)(2,1)} %dynamic-slice_bitcast_fusion), channel_id=1, source_target_pairs={{0,1},{1,0},{2,3},{3,2},{4,5},{5,4},{6,7},{7,6},{8,9},{9,8},{10,11... | collective-permute-start | bytes 3145736 | tf_op jit(solution)/shard_map/ppermute | solution.py:541
  17.7 1.3 copy-start.1
  84.2 13.4 %copy-start.2 = (bf16[512,2048]{1,0:T(8,128)(2,1)S(1)}, bf16[512,2048]{1,0:T(8,128)(2,1)}, u32[]{:S(2)}) copy-start(bf16[512,2048]{1,0:T(8,128)(2,1)} %copy-done.1) | copy-start | bytes 6291460
  84.2 6.5 %collective-permute-start.5 = (bf16[2,128,256]{2,1,0:T(8,128)(2,1)S(1)}, bf16[2,128,256]{2,1,0:T(8,128)(2,1)S(1)}, u32[]{:S(2)}, u32[]{:S(2)}) collective-permute-start(bf16[2,128,256]{2,1,0:T(8,128)(2,1)S(1)} %get-tuple-element.35), channel_id=1, source_target_pairs={{0,2},{2,4},{4,6},{6,0},{1,3},{3,5},{5,7},{7,1},{8,10},{10,12},{12... | collective-permute-start | bytes 393224 | tf_op jit(solution)/shard_map/ppermute | solution.py:566
  84.6 7.3 %collective-permute-start.6 = (bf16[2,128,256]{2,1,0:T(8,128)(2,1)S(1)}, bf16[2,128,256]{2,1,0:T(8,128)(2,1)S(1)}, u32[]{:S(2)}, u32[]{:S(2)}) collective-permute-start(bf16[2,128,256]{2,1,0:T(8,128)(2,1)S(1)} %get-tuple-element.36), channel_id=1, source_target_pairs={{0,4},{2,6},{4,0},{6,2},{1,5},{3,7},{5,1},{7,3},{8,12},{10,14},{12... | collective-permute-start | bytes 393224 | tf_op jit(solution)/shard_map/ppermute | solution.py:566
  86.4 7.7 %collective-permute-start.7 = (bf16[2,128,256]{2,1,0:T(8,128)(2,1)S(1)}, bf16[2,128,256]{2,1,0:T(8,128)(2,1)S(1)}, u32[]{:S(2)}, u32[]{:S(2)}) collective-permute-start(bf16[2,128,256]{2,1,0:T(8,128)(2,1)S(1)} %get-tuple-element.37), channel_id=1, source_target_pairs={{0,6},{2,0},{4,2},{6,4},{1,7},{3,1},{5,3},{7,5},{8,14},{10,8},{12,... | collective-permute-start | bytes 393224 | tf_op jit(solution)/shard_map/ppermute | solution.py:566
  87.2 19.5 %collective-permute-start.1 = (bf16[2,256,256]{2,1,0:T(8,128)(2,1)S(1)}, bf16[2,256,256]{2,1,0:T(8,128)(2,1)S(1)}, u32[]{:S(2)}, u32[]{:S(2)}) collective-permute-start(bf16[2,256,256]{2,1,0:T(8,128)(2,1)S(1)} %get-tuple-element.30), channel_id=1, source_target_pairs={{0,2},{2,4},{4,6},{6,0},{1,3},{3,5},{5,7},{7,1},{8,10},{10,12},{12... | collective-permute-start | bytes 786440 | tf_op jit(solution)/shard_map/ppermute | solution.py:566
  87.8 18.9 %collective-permute-start.2 = (bf16[2,256,256]{2,1,0:T(8,128)(2,1)S(1)}, bf16[2,256,256]{2,1,0:T(8,128)(2,1)S(1)}, u32[]{:S(2)}, u32[]{:S(2)}) collective-permute-start(bf16[2,256,256]{2,1,0:T(8,128)(2,1)S(1)} %get-tuple-element.31), channel_id=1, source_target_pairs={{0,4},{2,6},{4,0},{6,2},{1,5},{3,7},{5,1},{7,3},{8,12},{10,14},{12... | collective-permute-start | bytes 786440 | tf_op jit(solution)/shard_map/ppermute | solution.py:566
  90.7 16.1 %collective-permute-start.3 = (bf16[2,256,256]{2,1,0:T(8,128)(2,1)S(1)}, bf16[2,256,256]{2,1,0:T(8,128)(2,1)S(1)}, u32[]{:S(2)}, u32[]{:S(2)}) collective-permute-start(bf16[2,256,256]{2,1,0:T(8,128)(2,1)S(1)} %get-tuple-element.32), channel_id=1, source_target_pairs={{0,6},{2,0},{4,2},{6,4},{1,7},{3,1},{5,3},{7,5},{8,14},{10,8},{12,... | collective-permute-start | bytes 786440 | tf_op jit(solution)/shard_map/ppermute | solution.py:566
  94.1 3.5 %collective-permute-start.8 = (bf16[2,128,256]{2,1,0:T(8,128)(2,1)S(1)}, bf16[2,128,256]{2,1,0:T(8,128)(2,1)S(1)}, u32[]{:S(2)}, u32[]{:S(2)}) collective-permute-start(bf16[2,128,256]{2,1,0:T(8,128)(2,1)S(1)} %sum_backs.1.refs_0_), channel_id=1, source_target_pairs={{0,1},{1,0},{2,3},{3,2},{4,5},{5,4},{6,7},{7,6},{8,9},{9,8},{10,11... | collective-permute-start | bytes 393224 | tf_op jit(solution)/shard_map/ppermute | solution.py:541
  99.2 18.4 %all-to-all-start.1 = ((bf16[16,16,1152]{2,1,0:T(8,128)(2,1)}), bf16[16,16,1152]{2,1,0:T(8,128)(2,1)S(1)}, u32[]{:S(2)}, u32[]{:S(2)}) async-start(bf16[16,16,1152]{2,1,0:T(8,128)(2,1)} %bitcast.13), calls=%async_computation.1 | async-start | bytes 1179648 | tf_op jit(solution)/shard_map/all_to_all | solution.py:537
  107.4 2.3 %collective-permute-start.4 = (bf16[4,256,256]{2,1,0:T(8,128)(2,1)S(1)}, bf16[4,256,256]{2,1,0:T(8,128)(2,1)S(1)}, u32[]{:S(2)}, u32[]{:S(2)}) collective-permute-start(bf16[4,256,256]{2,1,0:T(8,128)(2,1)S(1)} %pick.1), channel_id=1, source_target_pairs={{0,1},{1,0},{2,3},{3,2},{4,5},{5,4},{6,7},{7,6},{8,9},{9,8},{10,11... | collective-permute-start | bytes 1572872 | tf_op jit(solution)/shard_map/ppermute | solution.py:541
  117.7 7.2 %collective-permute-start.9 = (bf16[16,1152]{1,0:T(8,128)(2,1)S(1)}, bf16[16,1152]{1,0:T(8,128)(2,1)S(1)}, u32[]{:S(2)}, u32[]{:S(2)}) collective-permute-start(bf16[16,1152]{1,0:T(8,128)(2,1)S(1)} %sum_share.1.refs_0_), channel_id=1, source_target_pairs={{0,2},{2,4},{4,6},{6,0},{1,3},{3,5},{5,7},{7,1},{8,10},{10,12},{12... | collective-permute-start | bytes 110600 | tf_op jit(solution)/shard_map/ppermute | solution.py:566
  122.3 4.4 %collective-permute-start.10 = (bf16[16,1152]{1,0:T(8,128)(2,1)S(1)}, bf16[16,1152]{1,0:T(8,128)(2,1)S(1)}, u32[]{:S(2)}, u32[]{:S(2)}) collective-permute-start(bf16[16,1152]{1,0:T(8,128)(2,1)S(1)} %sum_share.1.refs_0_), channel_id=1, source_target_pairs={{0,4},{2,6},{4,0},{6,2},{1,5},{3,7},{5,1},{7,3},{8,12},{10,14},{12... | collective-permute-start | bytes 110600 | tf_op jit(solution)/shard_map/ppermute | solution.py:566
  123.9 3.1 %collective-permute-start.11 = (bf16[16,1152]{1,0:T(8,128)(2,1)S(1)}, bf16[16,1152]{1,0:T(8,128)(2,1)S(1)}, u32[]{:S(2)}, u32[]{:S(2)}) collective-permute-start(bf16[16,1152]{1,0:T(8,128)(2,1)S(1)} %sum_share.1.refs_0_), channel_id=1, source_target_pairs={{0,6},{2,0},{4,2},{6,4},{1,7},{3,1},{5,3},{7,5},{8,14},{10,8},{12,... | collective-permute-start | bytes 110600 | tf_op jit(solution)/shard_map/ppermute | solution.py:566
  142.0 6.5 %collective-permute-start.12 = (bf16[8,2,16,1536]{3,2,1,0:T(8,128)(2,1)S(1)}, bf16[8,2,16,1536]{3,2,1,0:T(8,128)(2,1)S(1)}, u32[]{:S(2)}, u32[]{:S(2)}) collective-permute-start(bf16[8,2,16,1536]{3,2,1,0:T(8,128)(2,1)S(1)} %bitcast.20), channel_id=1, source_target_pairs={{0,1},{1,0},{2,3},{3,2},{4,5},{5,4},{6,7},{7,6},{8,9},{9,8},{10,11... | collective-permute-start | bytes 2359304 | tf_op jit(solution)/shard_map/ppermute | solution.py:541

commit v10 on v9

--- a/solution.py
+++ b/solution.py
@@ -37,6 +37,8 @@
     return lax.dot_general(a, b, NT, preferred_element_type=jnp.float32)
 
 
+LOW_ROWS = 16
+
 HIDDEN_PARTS = 4
 PACK_VMEM = 56 << 20
 SMALL_VMEM = 8 << 20
@@ -51,9 +53,9 @@
     hidden_v, down_v, fq_v, fv_v, wq_up_v, wv_up_v, out_v, low,
     down_sems, hidden_sems, row_sems, through_sems, out_sems,
 ):
-    devices, rows, packed = out.shape
-    width = (packed - 2 * RANK) // 4
-    model = hidden.shape[1]
+    devices, _, packed = out.shape
+    width = packed // 4
+    rows, model = hidden.shape
     step = model // HIDDEN_PARTS
 
     def part(index):
@@ -75,7 +77,7 @@
     through = [
         pltpu.make_async_copy(
             source.at[:, columns(device)],
-            out_v.at[device, :, columns(which)],
+            out_v.at[device, pl.ds(0, rows), columns(which)],
             through_sems.at[which - 2, device],
         )
         for device in range(devices)
@@ -103,19 +105,28 @@
         hiddens[index].wait()
         total += dot_nt(hidden_v[:, part(index)], down_v[:, part(index)])
     low[...] = total.astype(jnp.bfloat16)
+    upper, lower = total[: rows // 2], total[rows // 2 :]
+    left = lax.broadcasted_iota(jnp.int32, upper.shape, 1) < RANK
+    sides = (
+        jnp.where(left, upper, pltpu.roll(lower, RANK, 1)).astype(jnp.bfloat16),
+        jnp.where(left, pltpu.roll(upper, RANK, 1), lower).astype(jnp.bfloat16),
+    )
     outs = []
     for device in range(devices):
+        for piece in range(rows // 2 // LOW_ROWS):
+            out_v[device, rows:, piece * 2 * RANK : (piece + 1) * 2 * RANK] = sides[device % 2][
+                piece * LOW_ROWS : (piece + 1) * LOW_ROWS
+            ]
         through[2 * device].wait()
         through[2 * device + 1].wait()
-        out_v[device, :, 4 * width :] = low[...]
-        outs.append(leave(device, 2 * width, 2 * width + 2 * RANK, 0))
+        outs.append(leave(device, 2 * width, 2 * width, 0))
     for copy in whole:
         copy.wait()
     for device in range(devices):
         at = slice(device * width, (device + 1) * width)
         for which, (frozen, weight) in enumerate(((fq_v, wq_up_v), (fv_v, wv_up_v))):
             added = ADAPTER_SCALE * dot(low[:, which * RANK : (which + 1) * RANK], weight[:, at])
-            out_v[device, :, which * width : (which + 1) * width] = (
+            out_v[device, :rows, which * width : (which + 1) * width] = (
                 frozen[:, at].astype(jnp.float32) + added
             ).astype(jnp.bfloat16)
         outs.append(leave(device, 0, 2 * width, 1))
@@ -132,7 +143,7 @@
         pack_kernel,
         in_specs=[ANY] * 9,
         out_specs=ANY,
-        out_shape=jax.ShapeDtypeStruct((seq_size, rows, 4 * width + 2 * RANK), bf16),
+        out_shape=jax.ShapeDtypeStruct((seq_size, rows + LOW_ROWS, 4 * width), bf16),
         scratch_shapes=[
             pltpu.VMEM((rows, model), bf16),
             pltpu.VMEM((2 * RANK, model), bf16),
@@ -140,7 +151,7 @@
             pltpu.VMEM((rows, columns), bf16),
             pltpu.VMEM((RANK, columns), bf16),
             pltpu.VMEM((RANK, columns), bf16),
-            pltpu.VMEM((seq_size, rows, 4 * width + 2 * RANK), bf16),
+            pltpu.VMEM((seq_size, rows + LOW_ROWS, 4 * width), bf16),
             pltpu.VMEM((rows, 2 * RANK), bf16),
             pltpu.SemaphoreType.DMA((2,)),
             pltpu.SemaphoreType.DMA((HIDDEN_PARTS,)),
@@ -158,7 +169,7 @@
 ):
     *outs, dq_t, dv_t, low, q_t, k_t, v_t, g_t, dv, returned, out = refs[1:]
     outs, backs = outs[: len(outs) // 2], outs[len(outs) // 2 :]
-    length = packed.shape[0]
+    length = out.shape[0]
     heads = out.shape[1] // HEAD_SIZE
     width = heads * HEAD_SIZE
     blocks = length // TILE
@@ -169,11 +180,15 @@
         begin = which * width + head * HEAD_SIZE
         return slice(begin, begin + HEAD_SIZE)
 
+    def tiles_of(first, count, which, head):
+        rows = packed[pl.ds(first, count), :TILE, columns(which, head)]
+        return rows.reshape(count * TILE, HEAD_SIZE)
+
     for head in range(heads):
-        q_t[span[head], :] = packed[:, columns(0, head)].T
-        v_t[span[head], :] = packed[:, columns(1, head)].T
-        k_t[span[head], :] = packed[:, columns(2, head)].T
-        g_t[span[head], :] = packed[:, columns(3, head)].T
+        q_t[span[head], :] = tiles_of(0, blocks, 0, head).T
+        v_t[span[head], :] = tiles_of(0, blocks, 1, head).T
+        k_t[span[head], :] = tiles_of(0, blocks, 2, head).T
+        g_t[span[head], :] = tiles_of(0, blocks, 3, head).T
     dv[...] = jnp.zeros_like(dv)
 
     def block(index, _):
@@ -190,7 +205,8 @@
         tiles = index - lax.div(first, TILE) + 1
 
         def body(count):
-            key0 = pl.multiple_of((index + 1 - count) * TILE, TILE)
+            tile0 = index + 1 - count
+            key0 = pl.multiple_of(tile0 * TILE, TILE)
             k_rows = pl.ds(key0, count * TILE)
             key_index = lax.broadcasted_iota(jnp.int32, (count * TILE, TILE), 0)
             in_document = key_index >= begin - key0
@@ -199,8 +215,8 @@
             )
             held = []
             for head in range(heads):
-                scores = dot(packed[k_rows, columns(2, head)], q_t[span[head], q_rows])
-                prob_grad = dot(packed[k_rows, columns(1, head)], g_t[span[head], q_rows])
+                scores = dot(tiles_of(tile0, count, 2, head), q_t[span[head], q_rows])
+                prob_grad = dot(tiles_of(tile0, count, 1, head), g_t[span[head], q_rows])
                 scores = jnp.where(in_document, scores, NEG_FILL)
                 last = jnp.where(causal, scores[(count - 1) * TILE :], NEG_FILL)
                 if count > 1:
@@ -213,9 +229,10 @@
                 held.append((prob_grad, powers.astype(jnp.bfloat16), inverse))
             for head in range(heads):
                 prob_grad, rounded, inverse = held[head]
+                powers = rounded.astype(jnp.float32)
                 result = (dot(v_t[span[head], k_rows], rounded) * inverse).astype(jnp.bfloat16)
+                row_dot = jnp.sum(powers * prob_grad, axis=0, keepdims=True) * inverse
                 g_wide = g_t[span[head], q_rows].astype(jnp.float32)
-                row_dot = jnp.sum(g_wide * result.astype(jnp.float32), axis=0, keepdims=True)
                 score_grad = rounded * (prob_grad - row_dot).astype(jnp.bfloat16)
                 query_grad = dot(k_t[span[head], k_rows], score_grad) * (inverse * SCALING)
                 dq_t[span[head], q_rows] = query_grad.astype(jnp.bfloat16)
@@ -235,7 +252,10 @@
         returned[part * RANK : (part + 1) * RANK, :] = (
             ADAPTER_SCALE * dot(weight[...], grads[...])
         ).astype(jnp.bfloat16)
-    low[...] = packed[:, 4 * width :]
+    for piece in range(low.shape[1] // LOW_ROWS):
+        low[:, piece * LOW_ROWS : (piece + 1) * LOW_ROWS, :] = packed[
+            :, TILE:, piece * 2 * RANK : (piece + 1) * 2 * RANK
+        ]
     rows = backs[0].shape[2]
     for step in range(len(backs)):
         target = lax.rem(chip + step, len(backs))
@@ -246,9 +266,9 @@
 
 
 def attention(meta, packed, wq_up, wv_up, seq_size, after):
-    length = packed.shape[0]
-    width = (packed.shape[1] - 2 * RANK) // 4
-    rows = length // seq_size
+    rows = packed.shape[1] - LOW_ROWS
+    length = seq_size * rows
+    width = packed.shape[2] // 4
     heads = width // HEAD_SIZE
     chips = seq_size // 2
     wide_t = pltpu.VMEM((width, length), jnp.bfloat16)
@@ -269,7 +289,8 @@
         ],
         out_shape=[jax.ShapeDtypeStruct((2, rows, width), jnp.bfloat16)] * chips
         + [back] * chips
-        + [grad_t, grad_t, jax.ShapeDtypeStruct((length, 2 * RANK), jnp.bfloat16)],
+        + [grad_t, grad_t]
+        + [jax.ShapeDtypeStruct((seq_size, rows // 2, 2 * RANK), jnp.bfloat16)],
         compiler_params=pltpu.CompilerParams(vmem_limit_bytes=32 << 20),
         cost_estimate=pl.CostEstimate(
             flops=8 << 30, bytes_accessed=16 << 20, transcendentals=4 << 20
@@ -278,21 +299,30 @@
     )(meta, packed, wq_up, wv_up, after)
 
 
-def up_kernel(low, dq_t, dv_t, up):
+def up_kernel(where, low, low_other, dq_t, dv_t, up, lows):
+    lows[where[1]] = low[...]
+    lows[1 - where[1]] = low_other[...]
+    devices, half, _ = low.shape
     for part, grads in enumerate((dq_t, dv_t)):
-        share = (dot(grads[...], low[...]) * ADAPTER_SCALE).T[part * RANK : (part + 1) * RANK, :]
+        upper = lower = jnp.zeros((grads.shape[0], 2 * RANK), jnp.float32)
+        for device in range(devices):
+            begin = 2 * device * half
+            upper += dot(grads[:, begin : begin + half], lows[part, device])
+            lower += dot(grads[:, begin + half : begin + 2 * half], lows[part, device])
+        share = ADAPTER_SCALE * (upper.T[:RANK] + lower.T[RANK:])
         up[part * RANK : (part + 1) * RANK, :] = share.astype(jnp.bfloat16)
 
 
-def up_gradient(low, dq_t, dv_t):
+def up_gradient(where, low, low_other, dq_t, dv_t):
     return pl.pallas_call(
         up_kernel,
-        in_specs=[VMEM] * 3,
+        in_specs=[SMEM] + [VMEM] * 4,
         out_specs=VMEM,
         out_shape=jax.ShapeDtypeStruct((2 * RANK, dq_t.shape[0]), jnp.bfloat16),
+        scratch_shapes=[pltpu.VMEM((2,) + low.shape, jnp.bfloat16)],
         compiler_params=pltpu.CompilerParams(vmem_limit_bytes=16 << 20),
         name="up_gradient",
-    )(low, dq_t, dv_t)
+    )(where, low, low_other, dq_t, dv_t)
 
 
 def pick_kernel(where, part_0, part_1, part_2, part_3, out):
@@ -340,22 +370,27 @@
     )(where, *parts, other)
 
 
-def backs_kernel(part_0, part_1, part_2, part_3, out):
+def backs_kernel(part_0, part_1, part_2, part_3, *refs):
+    out = refs[len(refs) // 2]
     total = part_0[...].astype(jnp.float32)
     for part in (part_1, part_2, part_3):
         total += part[...].astype(jnp.float32)
     out[...] = total.astype(out.dtype)
 
 
-def sum_backs(parts):
+def sum_backs(parts, held):
+    count = len(parts)
     return pl.pallas_call(
         backs_kernel,
-        in_specs=[VMEM] * len(parts),
-        out_specs=VMEM,
-        out_shape=jax.ShapeDtypeStruct(parts[0].shape, parts[0].dtype),
+        in_specs=[VMEM] * (count + len(held)),
+        out_specs=[VMEM] * (1 + len(held)),
+        out_shape=[
+            jax.ShapeDtypeStruct(part.shape, part.dtype) for part in [parts[0]] + list(held)
+        ],
+        input_output_aliases={count + index: 1 + index for index in range(len(held))},
         compiler_params=pltpu.CompilerParams(vmem_limit_bytes=SMALL_VMEM),
         name="sum_backs",
-    )(*parts)
+    )(*parts, *held)
 
 
 def halves_kernel(core, hidden, other, out, done):
@@ -577,7 +612,7 @@
         value_up_weight,
         seq_size,
     )
-    received = swap(packed, SEQ).reshape(seq_size * rows, packed.shape[2])
+    received = swap(packed, SEQ)
     hidden_other = to_other_core(
         lax.dynamic_slice(hidden[0], (0, (1 - core) * half), (rows, half))
     )
@@ -593,10 +628,11 @@
     parts, backs = outs[:chips], outs[chips:]
 
     backs = [backs[0]] + [to_chip(backs[step], step) for step in range(1, chips)]
-    back = sum_backs(backs)
+    back, *held = sum_backs(backs, parts[-2:])
+    parts = parts[:-2] + held
     back_other = to_other_core(back)
     parts = [parts[0]] + [to_chip(parts[step], step) for step in range(1, chips)]
-    up = up_gradient(low, dq_t, dv_t)
+    up = up_gradient(where, low, to_other_core(low), dq_t, dv_t)
     down = down_gradient(core[None], [back, back_other], hidden_half, up)
 
     other = to_other_core(pick(where, parts))

time: 151 us -> 145 us (0.960)
  waiting for transfers between devices: 66 us -> 60.7 us
    all_to_all x2, waiting for transfers between devices: 55.5 us -> 52.1 us  [swap(): return lax.all_to_all(x, axes, 0, 0, tiled=True)]
    ppermute x9, waiting for transfers between devices: 6.22 us -> 4.53 us  [to_chip(): return lax.ppermute(x, 'y', [(c, (c + step) % chips) for c in range(chips)])]
    ppermute x4 -> x5, starting transfers between devices: 7.93 us -> 8.51 us  [to_other_core(): return lax.ppermute(x, 'core', [(0, 1), (1, 0)])]
    ppermute x4 -> x5, waiting for transfers between devices: 4.3 us -> 4.11 us  [to_other_core(): return lax.ppermute(x, 'core', [(0, 1), (1, 0)])]
  transfers between devices with their start and end apart: 15 -> 16, of which waited for: 11 -> 10; matrix products, arithmetic and copies ran while one was open for 1% -> 1% of each run, Pallas kernels for 4% -> 5%
where the time goes in v10:
time: 145 us; the launch traced here: 144 us
  waiting for transfers between devices  60.7 us (42%)
  starting transfers between devices  34.2 us (24%)
  Pallas kernels  30.1 us (21%)
  blocking collectives  15.1 us (10%)
  local copies, waits for them, and re-layouts  3.14 us (2%)
    all_to_all x2, waiting for transfers between devices, swap(): return lax.all_to_all(x, axes, 0, 0, tiled=True)  52.1 us
    all_to_all x1, blocking collectives, swap(): return lax.all_to_all(x, axes, 0, 0, tiled=True)  15.1 us
    pallas_call x1, Pallas kernels, attention(): pl.pallas_call(attention_kernel, in_specs=[SMEM, VMEM, VMEM, VMEM, VMEM],...  14.7 us
    all_to_all x2, starting transfers between devices, swap(): return lax.all_to_all(x, axes, 0, 0, tiled=True)  13.9 us
    ppermute x9, starting transfers between devices, to_chip(): return lax.ppermute(x, 'y', [(c, (c + step) % chips) for c in range(chips)])  11.8 us
    ppermute x5, starting transfers between devices, to_other_core(): return lax.ppermute(x, 'core', [(0, 1), (1, 0)])  8.51 us
    pallas_call x1, Pallas kernels, pack(): pl.pallas_call(pack_kernel, in_specs=[ANY] * 9, out_specs=ANY, out_shape=...  6.79 us
    ppermute x9, waiting for transfers between devices, to_chip(): return lax.ppermute(x, 'y', [(c, (c + step) % chips) for c in range(chips)])  4.53 us
  transfers between devices with their start and end apart: 16, of which 10 were waited for; matrix products, arithmetic and copies ran while one was open for 1% of the time, Pallas kernels for 5%

profile of v10, /device:TPU:1, one launch (start us, length us, event | category | flops | bytes accessed | tf_op | source)
XLA Modules:
  0.0 144.3 jit_solution(3638956735559222379)
XLA Ops:
  0.6 6.8 %pack.1 = bf16[8,272,1024]{2,1,0:T(8,128)(2,1)} custom-call(bf16[256,4096]{1,0:T(8,128)(2,1)} %bitcast.17, bf16[64,4096]{1,0:T(8,128)(2,1)} %bitcast.27, bf16[64,4096]{1,0:T(8,128)(2,1)} %bitcast.28, bf16[256,2048]{1,0:T(8,128)(2,1)} %bitcast.21, bf16[256,2048]{1,0:T(8,128)(2,1)} %bitcast.22, bf16[256,2048]{1,0:T(8,128)(2,1)} %bitcast.23, ...), custom_call_target="tpu_custom_call" | custom-call | tf_op jit(solution)/shard_map/pack/pallas_call | solution.py:142
  7.4 0.0 copy-start
  7.4 6.1 %all-to-all-start = ((bf16[8,272,1024]{2,1,0:T(8,128)(2,1)}), bf16[8,272,1024]{2,1,0:T(8,128)(2,1)}, u32[]{:S(2)}, u32[]{:S(2)}) async-start(bf16[8,272,1024]{2,1,0:T(8,128)(2,1)} %pack.1), calls=%async_computation | async-start | bytes 8912896 | tf_op jit(solution)/shard_map/all_to_all | solution.py:572
  13.6 1.0 dynamic-slice_bitcast_fusion
  14.6 0.1 collective-permute-start
  14.7 0.1 pad_add_fusion.1.meta
  14.8 0.8 constant_dynamic-slice_fusion
  15.6 1.9 %collective-permute-done.other = bf16[256,2048]{1,0:T(8,128)(2,1)S(1)} collective-permute-done((bf16[256,2048]{1,0:T(8,128)(2,1)}, bf16[256,2048]{1,0:T(8,128)(2,1)S(1)}, u32[]{:S(2)}, u32[]{:S(2)}) %collective-permute-start) | collective-permute-done | bytes 1048608 | tf_op jit(solution)/shard_map/ppermute | solution.py:576
  17.5 0.1 halves.1
  17.6 1.3 copy-done.1
  18.9 46.3 %all-to-all-done.packed = bf16[8,272,1024]{2,1,0:T(8,128)(2,1)} async-done(((bf16[8,272,1024]{2,1,0:T(8,128)(2,1)}), bf16[8,272,1024]{2,1,0:T(8,128)(2,1)}, u32[]{:S(2)}, u32[]{:S(2)}) %all-to-all-start) | async-done | bytes 4456480 | tf_op jit(solution)/shard_map/all_to_all | solution.py:572
  65.3 14.7 %attention.1 = (bf16[2,256,256]{2,1,0:T(8,128)(2,1)S(1)}, bf16[2,256,256]{2,1,0:T(8,128)(2,1)S(1)}, bf16[2,256,256]{2,1,0:T(8,128)(2,1)S(1)}, bf16[2,256,256]{2,...) custom-call(s32[10]{0:T(128)S(1)} %pad_add_fusion.1.meta, ...), custom_call_target="tpu_custom_call" | custom-call | flops 8589934592 | bytes 16777216 | tf_op jit(solution)/shard_map/attention/pallas_call | solution.py:277
  80.0 0.4 collective-permute-start.2
  80.4 1.8 %collective-permute-start.3 = (bf16[2,128,256]{2,1,0:T(8,128)(2,1)S(1)}, bf16[2,128,256]{2,1,0:T(8,128)(2,1)S(1)}, u32[]{:S(2)}, u32[]{:S(2)}) collective-permute-start(bf16[2,128,256]{2,1,0:T(8,128)(2,1)S(1)} %get-tuple-element.36), channel_id=1, source_target_pairs={{0,4},{2,6},{4,0},{6,2},{1,5},{3,7},{5,1},{7,3},{8,12},{10,14},{12... | collective-permute-start | bytes 393224 | tf_op jit(solution)/shard_map/ppermute | solution.py:601
  82.2 0.9 collective-permute-start.4
  83.0 1.4 %collective-permute-start.9 = (bf16[8,128,128]{2,1,0:T(8,128)(2,1)S(1)}, bf16[8,128,128]{2,1,0:T(8,128)(2,1)S(1)}, u32[]{:S(2)}, u32[]{:S(2)}) collective-permute-start(bf16[8,128,128]{2,1,0:T(8,128)(2,1)S(1)} %get-tuple-element.45.low), channel_id=1, source_target_pairs={{0,1},{1,0},{2,3},{3,2},{4,5},{5,4},{6,7},{7,6},{8,9},{9,8},{10,11... | collective-permute-start | bytes 786440 | tf_op jit(solution)/shard_map/ppermute | solution.py:576
  84.5 0.9 collective-permute-start.1
  85.3 1.2 collective-permute-done.2.part_1
  86.5 1.1 collective-permute-done.3.part_2
  87.7 1.1 collective-permute-done.4.part_3
  88.8 0.1 sum_backs.1
  88.9 1.0 collective-permute-start.5
  89.8 2.7 %collective-permute-start.6 = (bf16[2,256,256]{2,1,0:T(8,128)(2,1)S(1)}, bf16[2,256,256]{2,1,0:T(8,128)(2,1)S(1)}, u32[]{:S(2)}, u32[]{:S(2)}) collective-permute-start(bf16[2,256,256]{2,1,0:T(8,128)(2,1)S(1)} %get-tuple-element.41), channel_id=1, source_target_pairs={{0,6},{2,0},{4,2},{6,4},{1,7},{3,1},{5,3},{7,5},{8,14},{10,8},{12,... | collective-permute-start | bytes 786440 | tf_op jit(solution)/shard_map/ppermute | solution.py:601
  92.6 1.4 collective-permute-start.8
  94.0 0.1 pad_add_fusion.where
  94.1 0.0 collective-permute-done.9.low_other
  94.1 1.4 up_gradient.1.refs_3_
  95.5 1.6 %down_gradient.1 = bf16[8,2,16,1152]{3,2,1,0:T(8,128)(2,1)} custom-call(s32[1]{0:T(128)} %bitcast.1.core.which, bf16[2,128,256]{2,1,0:T(8,128)(2,1)S(1)} %get-tuple-element.43.refs_0_, bf16[2,128,256]{2,1,0:T(8,128)(2,1)S(1)} %collective-permute-done.8.refs_1_, bf16[512,2048]{1,0:T(8,128)(2,1)S(1)} %copy-done.2, bf16[128,256]{1,0:T(8,128)(2,1)S(1)} %up_gradient.1.refs_3_), custom_call_target="tpu_custom_call" | custom-call | tf_op jit(solution)/shard_map/down_gradient/pallas_call | solution.py:439
  97.1 7.8 %all-to-all-start.1 = ((bf16[16,16,1152]{2,1,0:T(8,128)(2,1)}), bf16[16,16,1152]{2,1,0:T(8,128)(2,1)S(1)}, u32[]{:S(2)}, u32[]{:S(2)}) async-start(bf16[16,16,1152]{2,1,0:T(8,128)(2,1)} %bitcast.12), calls=%async_computation.1 | async-start | bytes 1179648 | tf_op jit(solution)/shard_map/all_to_all | solution.py:572
  104.8 0.0 collective-permute-done.1.part_1
  104.8 0.0 collective-permute-done.5.part_2
  104.9 0.6 pick.1
  105.5 1.2 collective-permute-start.7
  106.7 1.5 %collective-permute-done.7.other = bf16[4,256,256]{2,1,0:T(8,128)(2,1)S(1)} collective-permute-done((bf16[4,256,256]{2,1,0:T(8,128)(2,1)S(1)}, bf16[4,256,256]{2,1,0:T(8,128)(2,1)S(1)}, u32[]{:S(2)}, u32[]{:S(2)}) %collective-permute-start.7) | collective-permute-done | bytes 524320 | tf_op jit(solution)/shard_map/ppermute | solution.py:576
  108.2 1.6 %arrive.1 = (bf16[1,256,2048]{2,1,0:T(8,128)(2,1)}, f32[8,128]{1,0:T(8,128)S(1)}) custom-call(s32[2]{0:T(128)S(1)} %pad_add_fusion.where, bf16[2,256,256]{2,1,0:T(8,128)(2,1)S(1)} %get-tuple-element.32.part_0, bf16[2,256,256]{2,1,0:T(8,128)(2,1)S(1)} %collective-permute-done.1.part_1, bf16[2,256,256]{2,1,0:T(8,128)(2,1)S(1)} %collective-permute-done.5.part_2, ...), custom_call_target="tpu_custom_call" | custom-call | tf_op jit(solution)/shard_map/arrive/pallas_call | solution.py:360
  109.9 5.7 %all-to-all-done.1.parts = bf16[16,16,1152]{2,1,0:T(8,128)(2,1)S(1)} async-done(((bf16[16,16,1152]{2,1,0:T(8,128)(2,1)}), bf16[16,16,1152]{2,1,0:T(8,128)(2,1)S(1)}, u32[]{:S(2)}, u32[]{:S(2)}) %all-to-all-start.1) | async-done | bytes 589856 | tf_op jit(solution)/shard_map/all_to_all | solution.py:572
  115.6 0.1 sum_share.1.refs_0_
  115.7 0.1 collective-permute-start.10
  115.8 2.2 %collective-permute-start.11 = (bf16[16,1152]{1,0:T(8,128)(2,1)S(1)}, bf16[16,1152]{1,0:T(8,128)(2,1)S(1)}, u32[]{:S(2)}, u32[]{:S(2)}) collective-permute-start(bf16[16,1152]{1,0:T(8,128)(2,1)S(1)} %sum_share.1.refs_0_), channel_id=1, source_target_pairs={{0,4},{2,6},{4,0},{6,2},{1,5},{3,7},{5,1},{7,3},{8,12},{10,14},{12... | collective-permute-start | bytes 110600 | tf_op jit(solution)/shard_map/ppermute | solution.py:601
  117.9 2.0 %collective-permute-start.12 = (bf16[16,1152]{1,0:T(8,128)(2,1)S(1)}, bf16[16,1152]{1,0:T(8,128)(2,1)S(1)}, u32[]{:S(2)}, u32[]{:S(2)}) collective-permute-start(bf16[16,1152]{1,0:T(8,128)(2,1)S(1)} %sum_share.1.refs_0_), channel_id=1, source_target_pairs={{0,6},{2,0},{4,2},{6,4},{1,7},{3,1},{5,3},{7,5},{8,14},{10,8},{12,... | collective-permute-start | bytes 110600 | tf_op jit(solution)/shard_map/ppermute | solution.py:601
  119.9 0.3 collective-permute-done.11.refs_2_
  120.2 0.8 collective-permute-done.12.refs_3_
  121.0 0.6 sum_chips.1
  121.6 15.1 %all_to_all.15 = bf16[16,16,1536]{2,1,0:T(8,128)(2,1)S(1)} all-to-all(bf16[16,16,1536]{2,1,0:T(8,128)(2,1)S(1)} %sum_chips.1), channel_id=1, replica_groups=mesh['x'=4,'z'=4,'y'=4,'core'=2] {'x','z'}, dimensions={0} | all-to-all | bytes 1572864 | tf_op jit(solution)/shard_map/all_to_all | solution.py:572
  136.7 4.4 %collective-permute-start.13 = (bf16[8,2,16,1536]{3,2,1,0:T(8,128)(2,1)S(1)}, bf16[8,2,16,1536]{3,2,1,0:T(8,128)(2,1)S(1)}, u32[]{:S(2)}, u32[]{:S(2)}) collective-permute-start(bf16[8,2,16,1536]{3,2,1,0:T(8,128)(2,1)S(1)} %bitcast.19), channel_id=1, source_target_pairs={{0,1},{1,0},{2,3},{3,2},{4,5},{5,4},{6,7},{7,6},{8,9},{9,8},{10,11... | collective-permute-start | bytes 2359304 | tf_op jit(solution)/shard_map/ppermute | solution.py:576
  141.0 1.2 place.2
  142.3 0.7 collective-permute-done.13.shares
  142.9 1.2 place.3
  (9 shorter events, 0.0 us)
Async XLA Ops:
  7.4 6.1 %copy-start = (bf16[1,256,4096]{2,1,0:T(8,128)(2,1)S(1)}, bf16[1,256,4096]{2,1,0:T(8,128)(2,1)}, u32[]{:S(2)}) copy-start(bf16[1,256,4096]{2,1,0:T(8,128)(2,1)} %param.10) | copy-start | bytes 6291460
  7.4 57.8 %all-to-all-start = ((bf16[8,272,1024]{2,1,0:T(8,128)(2,1)}), bf16[8,272,1024]{2,1,0:T(8,128)(2,1)}, u32[]{:S(2)}, u32[]{:S(2)}) async-start(bf16[8,272,1024]{2,1,0:T(8,128)(2,1)} %pack.1), calls=%async_computation | async-start | bytes 8912896 | tf_op jit(solution)/shard_map/all_to_all | solution.py:572
  13.6 1.2 copy-start.3
  14.6 2.9 %collective-permute-start = (bf16[256,2048]{1,0:T(8,128)(2,1)}, bf16[256,2048]{1,0:T(8,128)(2,1)S(1)}, u32[]{:S(2)}, u32[]{:S(2)}) collective-permute-start(bf16[256,2048]{1,0:T(8,128)(2,1)} %dynamic-slice_bitcast_fusion), channel_id=1, source_target_pairs={{0,1},{1,0},{2,3},{3,2},{4,5},{5,4},{6,7},{7,6},{8,9},{9,8},{10,11... | collective-permute-start | bytes 3145736 | tf_op jit(solution)/shard_map/ppermute | solution.py:576
  17.6 1.3 copy-start.1
  80.0 15.5 %copy-start.2 = (bf16[512,2048]{1,0:T(8,128)(2,1)S(1)}, bf16[512,2048]{1,0:T(8,128)(2,1)}, u32[]{:S(2)}) copy-start(bf16[512,2048]{1,0:T(8,128)(2,1)} %copy-done.1) | copy-start | bytes 6291460
  80.0 6.5 %collective-permute-start.2 = (bf16[2,128,256]{2,1,0:T(8,128)(2,1)S(1)}, bf16[2,128,256]{2,1,0:T(8,128)(2,1)S(1)}, u32[]{:S(2)}, u32[]{:S(2)}) collective-permute-start(bf16[2,128,256]{2,1,0:T(8,128)(2,1)S(1)} %get-tuple-element.35), channel_id=1, source_target_pairs={{0,2},{2,4},{4,6},{6,0},{1,3},{3,5},{5,7},{7,1},{8,10},{10,12},{12... | collective-permute-start | bytes 393224 | tf_op jit(solution)/shard_map/ppermute | solution.py:601
  80.4 7.3 %collective-permute-start.3 = (bf16[2,128,256]{2,1,0:T(8,128)(2,1)S(1)}, bf16[2,128,256]{2,1,0:T(8,128)(2,1)S(1)}, u32[]{:S(2)}, u32[]{:S(2)}) collective-permute-start(bf16[2,128,256]{2,1,0:T(8,128)(2,1)S(1)} %get-tuple-element.36), channel_id=1, source_target_pairs={{0,4},{2,6},{4,0},{6,2},{1,5},{3,7},{5,1},{7,3},{8,12},{10,14},{12... | collective-permute-start | bytes 393224 | tf_op jit(solution)/shard_map/ppermute | solution.py:601
  82.2 6.6 %collective-permute-start.4 = (bf16[2,128,256]{2,1,0:T(8,128)(2,1)S(1)}, bf16[2,128,256]{2,1,0:T(8,128)(2,1)S(1)}, u32[]{:S(2)}, u32[]{:S(2)}) collective-permute-start(bf16[2,128,256]{2,1,0:T(8,128)(2,1)S(1)} %get-tuple-element.37), channel_id=1, source_target_pairs={{0,6},{2,0},{4,2},{6,4},{1,7},{3,1},{5,3},{7,5},{8,14},{10,8},{12,... | collective-permute-start | bytes 393224 | tf_op jit(solution)/shard_map/ppermute | solution.py:601
  83.0 11.0 %collective-permute-start.9 = (bf16[8,128,128]{2,1,0:T(8,128)(2,1)S(1)}, bf16[8,128,128]{2,1,0:T(8,128)(2,1)S(1)}, u32[]{:S(2)}, u32[]{:S(2)}) collective-permute-start(bf16[8,128,128]{2,1,0:T(8,128)(2,1)S(1)} %get-tuple-element.45.low), channel_id=1, source_target_pairs={{0,1},{1,0},{2,3},{3,2},{4,5},{5,4},{6,7},{7,6},{8,9},{9,8},{10,11... | collective-permute-start | bytes 786440 | tf_op jit(solution)/shard_map/ppermute | solution.py:576
  84.5 20.4 %collective-permute-start.1 = (bf16[2,256,256]{2,1,0:T(8,128)(2,1)S(1)}, bf16[2,256,256]{2,1,0:T(8,128)(2,1)S(1)}, u32[]{:S(2)}, u32[]{:S(2)}) collective-permute-start(bf16[2,256,256]{2,1,0:T(8,128)(2,1)S(1)} %get-tuple-element.33), channel_id=1, source_target_pairs={{0,2},{2,4},{4,6},{6,0},{1,3},{3,5},{5,7},{7,1},{8,10},{10,12},{12... | collective-permute-start | bytes 786440 | tf_op jit(solution)/shard_map/ppermute | solution.py:601
  88.9 16.0 %collective-permute-start.5 = (bf16[2,256,256]{2,1,0:T(8,128)(2,1)S(1)}, bf16[2,256,256]{2,1,0:T(8,128)(2,1)S(1)}, u32[]{:S(2)}, u32[]{:S(2)}) collective-permute-start(bf16[2,256,256]{2,1,0:T(8,128)(2,1)S(1)} %get-tuple-element.40), channel_id=1, source_target_pairs={{0,4},{2,6},{4,0},{6,2},{1,5},{3,7},{5,1},{7,3},{8,12},{10,14},{12... | collective-permute-start | bytes 786440 | tf_op jit(solution)/shard_map/ppermute | solution.py:601
  89.8 15.0 %collective-permute-start.6 = (bf16[2,256,256]{2,1,0:T(8,128)(2,1)S(1)}, bf16[2,256,256]{2,1,0:T(8,128)(2,1)S(1)}, u32[]{:S(2)}, u32[]{:S(2)}) collective-permute-start(bf16[2,256,256]{2,1,0:T(8,128)(2,1)S(1)} %get-tuple-element.41), channel_id=1, source_target_pairs={{0,6},{2,0},{4,2},{6,4},{1,7},{3,1},{5,3},{7,5},{8,14},{10,8},{12,... | collective-permute-start | bytes 786440 | tf_op jit(solution)/shard_map/ppermute | solution.py:601
  92.6 2.9 %collective-permute-start.8 = (bf16[2,128,256]{2,1,0:T(8,128)(2,1)S(1)}, bf16[2,128,256]{2,1,0:T(8,128)(2,1)S(1)}, u32[]{:S(2)}, u32[]{:S(2)}) collective-permute-start(bf16[2,128,256]{2,1,0:T(8,128)(2,1)S(1)} %get-tuple-element.43.refs_0_), channel_id=1, source_target_pairs={{0,1},{1,0},{2,3},{3,2},{4,5},{5,4},{6,7},{7,6},{8,9},{9,8},{10,11... | collective-permute-start | bytes 393224 | tf_op jit(solution)/shard_map/ppermute | solution.py:576
  97.1 18.5 %all-to-all-start.1 = ((bf16[16,16,1152]{2,1,0:T(8,128)(2,1)}), bf16[16,16,1152]{2,1,0:T(8,128)(2,1)S(1)}, u32[]{:S(2)}, u32[]{:S(2)}) async-start(bf16[16,16,1152]{2,1,0:T(8,128)(2,1)} %bitcast.12), calls=%async_computation.1 | async-start | bytes 1179648 | tf_op jit(solution)/shard_map/all_to_all | solution.py:572
  105.5 2.7 %collective-permute-start.7 = (bf16[4,256,256]{2,1,0:T(8,128)(2,1)S(1)}, bf16[4,256,256]{2,1,0:T(8,128)(2,1)S(1)}, u32[]{:S(2)}, u32[]{:S(2)}) collective-permute-start(bf16[4,256,256]{2,1,0:T(8,128)(2,1)S(1)} %pick.1), channel_id=1, source_target_pairs={{0,1},{1,0},{2,3},{3,2},{4,5},{5,4},{6,7},{7,6},{8,9},{9,8},{10,11... | collective-permute-start | bytes 1572872 | tf_op jit(solution)/shard_map/ppermute | solution.py:576
  115.7 4.2 %collective-permute-start.10 = (bf16[16,1152]{1,0:T(8,128)(2,1)S(1)}, bf16[16,1152]{1,0:T(8,128)(2,1)S(1)}, u32[]{:S(2)}, u32[]{:S(2)}) collective-permute-start(bf16[16,1152]{1,0:T(8,128)(2,1)S(1)} %sum_share.1.refs_0_), channel_id=1, source_target_pairs={{0,2},{2,4},{4,6},{6,0},{1,3},{3,5},{5,7},{7,1},{8,10},{10,12},{12... | collective-permute-start | bytes 110600 | tf_op jit(solution)/shard_map/ppermute | solution.py:601
  115.8 4.4 %collective-permute-start.11 = (bf16[16,1152]{1,0:T(8,128)(2,1)S(1)}, bf16[16,1152]{1,0:T(8,128)(2,1)S(1)}, u32[]{:S(2)}, u32[]{:S(2)}) collective-permute-start(bf16[16,1152]{1,0:T(8,128)(2,1)S(1)} %sum_share.1.refs_0_), channel_id=1, source_target_pairs={{0,4},{2,6},{4,0},{6,2},{1,5},{3,7},{5,1},{7,3},{8,12},{10,14},{12... | collective-permute-start | bytes 110600 | tf_op jit(solution)/shard_map/ppermute | solution.py:601
  117.9 3.0 %collective-permute-start.12 = (bf16[16,1152]{1,0:T(8,128)(2,1)S(1)}, bf16[16,1152]{1,0:T(8,128)(2,1)S(1)}, u32[]{:S(2)}, u32[]{:S(2)}) collective-permute-start(bf16[16,1152]{1,0:T(8,128)(2,1)S(1)} %sum_share.1.refs_0_), channel_id=1, source_target_pairs={{0,6},{2,0},{4,2},{6,4},{1,7},{3,1},{5,3},{7,5},{8,14},{10,8},{12,... | collective-permute-start | bytes 110600 | tf_op jit(solution)/shard_map/ppermute | solution.py:601
  136.7 6.3 %collective-permute-start.13 = (bf16[8,2,16,1536]{3,2,1,0:T(8,128)(2,1)S(1)}, bf16[8,2,16,1536]{3,2,1,0:T(8,128)(2,1)S(1)}, u32[]{:S(2)}, u32[]{:S(2)}) collective-permute-start(bf16[8,2,16,1536]{3,2,1,0:T(8,128)(2,1)S(1)} %bitcast.19), channel_id=1, source_target_pairs={{0,1},{1,0},{2,3},{3,2},{4,5},{5,4},{6,7},{7,6},{8,9},{9,8},{10,11... | collective-permute-start | bytes 2359304 | tf_op jit(solution)/shard_map/ppermute | solution.py:576

commit v11 on v10

--- a/solution.py
+++ b/solution.py
@@ -49,9 +49,9 @@
 
 
 def pack_kernel(
-    hidden, wq_down, wv_down, fq, fk, fv, grad, wq_up, wv_up, out,
+    core, hidden, wq_down, wv_down, fq, fk, fv, grad, wq_up, wv_up, out, other,
     hidden_v, down_v, fq_v, fv_v, wq_up_v, wv_up_v, out_v, low,
-    down_sems, hidden_sems, row_sems, through_sems, out_sems,
+    down_sems, hidden_sems, row_sems, through_sems, out_sems, other_sem,
 ):
     devices, _, packed = out.shape
     width = packed // 4
@@ -105,6 +105,10 @@
         hiddens[index].wait()
         total += dot_nt(hidden_v[:, part(index)], down_v[:, part(index)])
     low[...] = total.astype(jnp.bfloat16)
+    half = other.shape[1]
+    begin = pl.multiple_of((1 - core[0]) * half, half)
+    other_copy = pltpu.make_async_copy(hidden_v.at[:, pl.ds(begin, half)], other, other_sem)
+    other_copy.start()
     upper, lower = total[: rows // 2], total[rows // 2 :]
     left = lax.broadcasted_iota(jnp.int32, upper.shape, 1) < RANK
     sides = (
@@ -132,18 +136,22 @@
         outs.append(leave(device, 0, 2 * width, 1))
     for copy in outs:
         copy.wait()
-
-
-def pack(hidden, wq_down_t, wv_down_t, fq, fk, fv, grad, wq_up, wv_up, seq_size):
+    other_copy.wait()
+
+
+def pack(core, hidden, wq_down_t, wv_down_t, fq, fk, fv, grad, wq_up, wv_up, seq_size):
     rows, model = hidden.shape
     columns = fq.shape[1]
     width = columns // seq_size
     bf16 = jnp.bfloat16
     return pl.pallas_call(
         pack_kernel,
-        in_specs=[ANY] * 9,
-        out_specs=ANY,
-        out_shape=jax.ShapeDtypeStruct((seq_size, rows + LOW_ROWS, 4 * width), bf16),
+        in_specs=[SMEM] + [ANY] * 9,
+        out_specs=[ANY] * 2,
+        out_shape=[
+            jax.ShapeDtypeStruct((seq_size, rows + LOW_ROWS, 4 * width), bf16),
+            jax.ShapeDtypeStruct((rows, model // 2), bf16),
+        ],
         scratch_shapes=[
             pltpu.VMEM((rows, model), bf16),
             pltpu.VMEM((2 * RANK, model), bf16),
@@ -158,14 +166,15 @@
             pltpu.SemaphoreType.DMA((4,)),
             pltpu.SemaphoreType.DMA((2, seq_size)),
             pltpu.SemaphoreType.DMA((2, seq_size)),
+            pltpu.SemaphoreType.DMA,
         ],
         compiler_params=pltpu.CompilerParams(vmem_limit_bytes=PACK_VMEM),
         name="pack",
-    )(hidden, wq_down_t, wv_down_t, fq, fk, fv, grad, wq_up, wv_up)
+    )(core, hidden, wq_down_t, wv_down_t, fq, fk, fv, grad, wq_up, wv_up)
 
 
 def attention_kernel(
-    meta, packed, wq_up, wv_up, *refs
+    lengths, chip, core, packed, wq_up, wv_up, *refs
 ):
     *outs, dq_t, dv_t, low, q_t, k_t, v_t, g_t, dv, returned, out = refs[1:]
     outs, backs = outs[: len(outs) // 2], outs[len(outs) // 2 :]
@@ -173,7 +182,8 @@
     heads = out.shape[1] // HEAD_SIZE
     width = heads * HEAD_SIZE
     blocks = length // TILE
-    chip = meta[NDOC]
+    chip, core = chip[0], core[0]
+    own_columns = pl.ds(pl.multiple_of((chip * 2 + core) * width, width), width)
     span = [slice(head * HEAD_SIZE, (head + 1) * HEAD_SIZE) for head in range(heads)]
 
     def columns(which, head):
@@ -199,7 +209,7 @@
         first = jnp.int32(0)
         end = jnp.int32(0)
         for doc in range(NDOC):
-            end = end + meta[doc]
+            end = end + lengths[0, doc]
             begin = jnp.where(position >= end, end, begin)
             first = jnp.where(row0 >= end, end, first)
         tiles = index - lax.div(first, TILE) + 1
@@ -250,7 +260,7 @@
 
     for part, (grads, weight) in enumerate(((dq_t, wq_up), (dv_t, wv_up))):
         returned[part * RANK : (part + 1) * RANK, :] = (
-            ADAPTER_SCALE * dot(weight[...], grads[...])
+            ADAPTER_SCALE * dot(weight[:, own_columns], grads[...])
         ).astype(jnp.bfloat16)
     for piece in range(low.shape[1] // LOW_ROWS):
         low[:, piece * LOW_ROWS : (piece + 1) * LOW_ROWS, :] = packed[
@@ -265,7 +275,8 @@
             outs[step][holder] = out[pl.ds(begin, rows), :]
 
 
-def attention(meta, packed, wq_up, wv_up, seq_size, after):
+def attention(lengths, chip, core, packed, wq_up, wv_up, after):
+    seq_size = packed.shape[0]
     rows = packed.shape[1] - LOW_ROWS
     length = seq_size * rows
     width = packed.shape[2] // 4
@@ -276,7 +287,7 @@
     grad_t = jax.ShapeDtypeStruct((width, length), jnp.bfloat16)
     return pl.pallas_call(
         attention_kernel,
-        in_specs=[SMEM, VMEM, VMEM, VMEM, VMEM],
+        in_specs=[SMEM] * 3 + [VMEM] * 4,
         out_specs=[VMEM] * (3 + 2 * chips),
         scratch_shapes=[
             wide_t,
@@ -296,12 +307,12 @@
             flops=8 << 30, bytes_accessed=16 << 20, transcendentals=4 << 20
         ),
         name="attention",
-    )(meta, packed, wq_up, wv_up, after)
-
-
-def up_kernel(where, low, low_other, dq_t, dv_t, up, lows):
-    lows[where[1]] = low[...]
-    lows[1 - where[1]] = low_other[...]
+    )(lengths, chip, core, packed, wq_up, wv_up, after)
+
+
+def up_kernel(core, low, low_other, dq_t, dv_t, up, lows):
+    lows[core[0]] = low[...]
+    lows[1 - core[0]] = low_other[...]
     devices, half, _ = low.shape
     for part, grads in enumerate((dq_t, dv_t)):
         upper = lower = jnp.zeros((grads.shape[0], 2 * RANK), jnp.float32)
@@ -313,7 +324,7 @@
         up[part * RANK : (part + 1) * RANK, :] = share.astype(jnp.bfloat16)
 
 
-def up_gradient(where, low, low_other, dq_t, dv_t):
+def up_gradient(core, low, low_other, dq_t, dv_t):
     return pl.pallas_call(
         up_kernel,
         in_specs=[SMEM] + [VMEM] * 4,
@@ -322,16 +333,16 @@
         scratch_shapes=[pltpu.VMEM((2,) + low.shape, jnp.bfloat16)],
         compiler_params=pltpu.CompilerParams(vmem_limit_bytes=16 << 20),
         name="up_gradient",
-    )(where, low, low_other, dq_t, dv_t)
-
-
-def pick_kernel(where, part_0, part_1, part_2, part_3, out):
-    core = where[1]
+    )(core, low, low_other, dq_t, dv_t)
+
+
+def pick_kernel(core, part_0, part_1, part_2, part_3, out):
+    core = core[0]
     for step, part in enumerate((part_0, part_1, part_2, part_3)):
         out[step] = part[1 - core]
 
 
-def pick(where, parts):
+def pick(core, parts):
     return pl.pallas_call(
         pick_kernel,
         in_specs=[SMEM] + [VMEM] * len(parts),
@@ -339,11 +350,11 @@
         out_shape=jax.ShapeDtypeStruct((len(parts),) + parts[0].shape[1:], parts[0].dtype),
         compiler_params=pltpu.CompilerParams(vmem_limit_bytes=SMALL_VMEM),
         name="pick",
-    )(where, *parts)
-
-
-def arrive_kernel(where, part_0, part_1, part_2, part_3, other, out, done):
-    chip, core = where[0], where[1]
+    )(core, *parts)
+
+
+def arrive_kernel(chip, core, part_0, part_1, part_2, part_3, other, out, done):
+    chip, core = chip[0], core[0]
     parts = (part_0, part_1, part_2, part_3)
     width = part_0.shape[2]
     for step in range(len(parts)):
@@ -355,11 +366,11 @@
     done[...] = jnp.zeros_like(done)
 
 
-def arrive(where, parts, other):
+def arrive(chip, core, parts, other):
     _, rows, width = parts[0].shape
     return pl.pallas_call(
         arrive_kernel,
-        in_specs=[SMEM] + [VMEM] * (len(parts) + 1),
+        in_specs=[SMEM] * 2 + [VMEM] * (len(parts) + 1),
         out_specs=[VMEM] * 2,
         out_shape=[
             jax.ShapeDtypeStruct((1, rows, 2 * len(parts) * width), parts[0].dtype),
@@ -367,7 +378,7 @@
         ],
         compiler_params=pltpu.CompilerParams(vmem_limit_bytes=SMALL_VMEM),
         name="arrive",
-    )(where, *parts, other)
+    )(chip, core, *parts, other)
 
 
 def backs_kernel(part_0, part_1, part_2, part_3, *refs):
@@ -478,9 +489,9 @@
     )(parts, *after)
 
 
-def chips_kernel(where, *refs):
+def chips_kernel(chip, *refs):
     *parts, out = refs
-    chip = where[0]
+    chip = chip[0]
     total = parts[0][:, :DOWN_COLS].astype(jnp.float32)
     for part in parts[1:]:
         total += part[:, :DOWN_COLS].astype(jnp.float32)
@@ -494,7 +505,7 @@
             out[device, :, pl.ds(begin, UP_COLS)] = part[:, DOWN_COLS:]
 
 
-def sum_chips(where, parts, devices):
+def sum_chips(chip, parts, devices):
     shape = (devices, SHARE_ROWS, DOWN_COLS + len(parts) * UP_COLS)
     return pl.pallas_call(
         chips_kernel,
@@ -503,7 +514,7 @@
         out_shape=jax.ShapeDtypeStruct(shape, parts[0].dtype),
         compiler_params=pltpu.CompilerParams(vmem_limit_bytes=SMALL_VMEM),
         name="sum_chips",
-    )(where, *parts)
+    )(chip, *parts)
 
 
 def place_kernel(which, shares, *refs):
@@ -565,7 +576,7 @@
         input_output_aliases={2 + index: index for index in range(len(earlier))},
         compiler_params=pltpu.CompilerParams(vmem_limit_bytes=16 << 20),
         name="place",
-    )(which[None], shares, *earlier)
+    )(which, shares, *earlier)
 
 
 def swap(x, axes):
@@ -593,14 +604,15 @@
     chips = seq_size // 2
     rows, model = hidden.shape[1:]
     half = model // 2
-    chip = lax.axis_index("y").astype(jnp.int32)
-    core = lax.axis_index("core").astype(jnp.int32)
-    where = jnp.stack([chip, core])
+    chip = lax.axis_index("y").astype(jnp.int32)[None]
+    core = lax.axis_index("core").astype(jnp.int32)[None]
+    width = frozen_queries.shape[2] // seq_size
 
     def to_chip(x, step):
         return lax.ppermute(x, "y", [(c, (c + step) % chips) for c in range(chips)])
 
-    packed = pack(
+    packed, hidden_leaving = pack(
+        core,
         hidden[0],
         query_down_weight.T,
         value_down_weight.T,
@@ -613,17 +625,16 @@
         seq_size,
     )
     received = swap(packed, SEQ)
-    hidden_other = to_other_core(
-        lax.dynamic_slice(hidden[0], (0, (1 - core) * half), (rows, half))
-    )
-    hidden_half, halves_done = halves(core[None], hidden[0], hidden_other)
-    width = frozen_queries.shape[2] // seq_size
-    own_columns = (0, (chip * 2 + core) * width)
-    wq_up = lax.dynamic_slice(query_up_weight, own_columns, (RANK, width))
-    wv_up = lax.dynamic_slice(value_up_weight, own_columns, (RANK, width))
-    meta = jnp.concatenate([document_length_list[0], where])
+    hidden_other = to_other_core(hidden_leaving)
+    hidden_half, halves_done = halves(core, hidden[0], hidden_other)
     *outs, dq_t, dv_t, low = attention(
-        meta, received, wq_up, wv_up, seq_size, after=halves_done
+        document_length_list,
+        chip,
+        core,
+        received,
+        query_up_weight,
+        value_up_weight,
+        after=halves_done,
     )
     parts, backs = outs[:chips], outs[chips:]
 
@@ -632,16 +643,16 @@
     parts = parts[:-2] + held
     back_other = to_other_core(back)
     parts = [parts[0]] + [to_chip(parts[step], step) for step in range(1, chips)]
-    up = up_gradient(where, low, to_other_core(low), dq_t, dv_t)
-    down = down_gradient(core[None], [back, back_other], hidden_half, up)
-
-    other = to_other_core(pick(where, parts))
-    attended, attended_done = arrive(where, parts, other)
+    up = up_gradient(core, low, to_other_core(low), dq_t, dv_t)
+    down = down_gradient(core, [back, back_other], hidden_half, up)
+
+    other = to_other_core(pick(core, parts))
+    attended, attended_done = arrive(chip, core, parts, other)
 
     shares = swap(down.reshape((-1,) + down.shape[2:]), DP)
     share = sum_share(shares, after=[attended_done])
     share = [share] + [to_chip(share, step) for step in range(1, chips)]
-    shares = swap(sum_chips(where, share, shares.shape[0]), DP)
+    shares = swap(sum_chips(chip, share, shares.shape[0]), DP)
     shares = shares.reshape(down.shape[:2] + shares.shape[1:])
     shares_other = to_other_core(shares)
     grads = place(core, shares, model, seq_size * width)

time: 145 us -> 144 us (level)
  waiting for transfers between devices: 60.7 us -> 63.6 us
  Pallas kernels: 30.1 us -> 28 us
    dynamic_slice x2 -> x0, local copies, waits for them, and re-layouts: 1.82 us -> none  [the longest x1 1.04 us: per_device(): lax.dynamic_slice(hidden[0], (0, (1 - core) * half), (rows, half))]
  transfers between devices with their start and end apart: 16 -> 16, of which waited for: 10 -> 12; matrix products, arithmetic and copies ran while one was open for 1% -> 0% of each run, Pallas kernels for 5% -> 3%
where the time goes in v11:
time: 144 us
  waiting for transfers between devices  63.6 us (44%)
  starting transfers between devices  34.7 us (24%)
  Pallas kernels  28 us (19%)
  blocking collectives  14.2 us (10%)
  local copies, waits for them, and re-layouts  2.29 us (2%)
    all_to_all x2, waiting for transfers between devices, swap(): return lax.all_to_all(x, axes, 0, 0, tiled=True)  53.4 us
    pallas_call x1, Pallas kernels, attention(): pl.pallas_call(attention_kernel, in_specs=[SMEM] * 3 + [VMEM] * 4, out_sp...  14.8 us
    all_to_all x1, blocking collectives, swap(): return lax.all_to_all(x, axes, 0, 0, tiled=True)  14.2 us
    all_to_all x2, starting transfers between devices, swap(): return lax.all_to_all(x, axes, 0, 0, tiled=True)  13.9 us
    ppermute x9, starting transfers between devices, to_chip(): return lax.ppermute(x, 'y', [(c, (c + step) % chips) for c in range(chips)])  11.8 us
    ppermute x5, starting transfers between devices, to_other_core(): return lax.ppermute(x, 'core', [(0, 1), (1, 0)])  9 us
    pallas_call x1, Pallas kernels, pack(): pl.pallas_call(pack_kernel, in_specs=[SMEM] + [ANY] * 9, out_specs=[ANY]...  6.78 us
    ppermute x5, waiting for transfers between devices, to_other_core(): return lax.ppermute(x, 'core', [(0, 1), (1, 0)])  5.49 us
  transfers between devices with their start and end apart: 16, of which 12 were waited for; matrix products, arithmetic and copies ran while one was open for 0% of the time, Pallas kernels for 3%

profile of v11, /device:TPU:1, one launch (start us, length us, event | category | flops | bytes accessed | tf_op | source)
XLA Modules:
  0.0 143.9 jit_solution(13244273867024051198)
XLA Ops:
  0.6 6.8 %pack.1 = (bf16[8,272,1024]{2,1,0:T(8,128)(2,1)}, bf16[256,2048]{1,0:T(8,128)(2,1)}) custom-call(s32[1]{0:T(128)} %bitcast.1.core.which, bf16[256,4096]{1,0:T(8,128)(2,1)} %bitcast.13, bf16[64,4096]{1,0:T(8,128)(2,1)} %bitcast.23, bf16[64,4096]{1,0:T(8,128)(2,1)} %bitcast.24, bf16[256,2048]{1,0:T(8,128)(2,1)} %bitcast.17, bf16[256,2048]{1,0:T(8,128)(2,1)} %bitcast.18, ...), custom_call_target="tpu_custom_call" | custom-call | tf_op jit(solution)/shard_map/pack/pallas_call | solution.py:147
  7.4 0.0 copy-start
  7.4 0.0 copy-start.3
  7.5 0.0 copy-start.5
  7.5 6.1 %all-to-all-start = ((bf16[8,272,1024]{2,1,0:T(8,128)(2,1)}), bf16[8,272,1024]{2,1,0:T(8,128)(2,1)}, u32[]{:S(2)}, u32[]{:S(2)}) async-start(bf16[8,272,1024]{2,1,0:T(8,128)(2,1)} %get-tuple-element.33), calls=%async_computation | async-start | bytes 8912896 | tf_op jit(solution)/shard_map/all_to_all | solution.py:583
  13.6 0.1 collective-permute-start
  13.7 3.2 %collective-permute-done.other = bf16[256,2048]{1,0:T(8,128)(2,1)S(1)} collective-permute-done((bf16[256,2048]{1,0:T(8,128)(2,1)}, bf16[256,2048]{1,0:T(8,128)(2,1)S(1)}, u32[]{:S(2)}, u32[]{:S(2)}) %collective-permute-start) | collective-permute-done | bytes 1048608 | tf_op jit(solution)/shard_map/ppermute | solution.py:587
  16.9 0.1 halves.1
  17.0 1.3 copy-done.1
  18.3 47.0 %all-to-all-done.packed = bf16[8,272,1024]{2,1,0:T(8,128)(2,1)} async-done(((bf16[8,272,1024]{2,1,0:T(8,128)(2,1)}), bf16[8,272,1024]{2,1,0:T(8,128)(2,1)}, u32[]{:S(2)}, u32[]{:S(2)}) %all-to-all-start) | async-done | bytes 4456480 | tf_op jit(solution)/shard_map/all_to_all | solution.py:583
  65.3 0.9 copy-done.4
  66.3 14.8 %attention.1 = (bf16[2,256,256]{2,1,0:T(8,128)(2,1)S(1)}, bf16[2,256,256]{2,1,0:T(8,128)(2,1)S(1)}, bf16[2,256,256]{2,1,0:T(8,128)(2,1)S(1)}, bf16[2,256,256]{2,...) custom-call(s32[1,8]{1,0:T(1,128)S(1)} %copy-done.5, ...), custom_call_target="tpu_custom_call" | custom-call | flops 8589934592 | bytes 16777216 | tf_op jit(solution)/shard_map/attention/pallas_call | solution.py:288
  81.1 0.3 collective-permute-start.2
  81.4 1.8 %collective-permute-start.3 = (bf16[2,128,256]{2,1,0:T(8,128)(2,1)S(1)}, bf16[2,128,256]{2,1,0:T(8,128)(2,1)S(1)}, u32[]{:S(2)}, u32[]{:S(2)}) collective-permute-start(bf16[2,128,256]{2,1,0:T(8,128)(2,1)S(1)} %get-tuple-element.40), channel_id=1, source_target_pairs={{0,4},{2,6},{4,0},{6,2},{1,5},{3,7},{5,1},{7,3},{8,12},{10,14},{12... | collective-permute-start | bytes 393224 | tf_op jit(solution)/shard_map/ppermute | solution.py:612
  83.3 0.9 collective-permute-start.4
  84.1 1.4 collective-permute-start.9
  85.6 0.9 collective-permute-start.1
  86.4 1.2 collective-permute-done.2.part_1
  87.6 1.1 collective-permute-done.3.part_2
  88.7 1.1 collective-permute-done.4.part_3
  89.9 0.1 sum_backs.1
  90.0 1.0 collective-permute-start.5
  90.9 2.7 %collective-permute-start.6 = (bf16[2,256,256]{2,1,0:T(8,128)(2,1)S(1)}, bf16[2,256,256]{2,1,0:T(8,128)(2,1)S(1)}, u32[]{:S(2)}, u32[]{:S(2)}) collective-permute-start(bf16[2,256,256]{2,1,0:T(8,128)(2,1)S(1)} %get-tuple-element.45), channel_id=1, source_target_pairs={{0,6},{2,0},{4,2},{6,4},{1,7},{3,1},{5,3},{7,5},{8,14},{10,8},{12,... | collective-permute-start | bytes 786440 | tf_op jit(solution)/shard_map/ppermute | solution.py:612
  93.7 1.4 collective-permute-start.8
  95.1 0.0 collective-permute-done.9.low_other
  95.1 0.9 up_gradient.1.refs_3_
  95.9 0.1 collective-permute-done.8.refs_1_
  96.0 1.6 %down_gradient.1 = bf16[8,2,16,1152]{3,2,1,0:T(8,128)(2,1)} custom-call(s32[1]{0:T(128)} %bitcast.1.core.which, bf16[2,128,256]{2,1,0:T(8,128)(2,1)S(1)} %get-tuple-element.47.refs_0_, bf16[2,128,256]{2,1,0:T(8,128)(2,1)S(1)} %collective-permute-done.8.refs_1_, bf16[512,2048]{1,0:T(8,128)(2,1)S(1)} %copy-done.2, bf16[128,256]{1,0:T(8,128)(2,1)S(1)} %up_gradient.1.refs_3_), custom_call_target="tpu_custom_call" | custom-call | tf_op jit(solution)/shard_map/down_gradient/pallas_call | solution.py:450
  97.6 7.8 %all-to-all-start.1 = ((bf16[16,16,1152]{2,1,0:T(8,128)(2,1)}), bf16[16,16,1152]{2,1,0:T(8,128)(2,1)S(1)}, u32[]{:S(2)}, u32[]{:S(2)}) async-start(bf16[16,16,1152]{2,1,0:T(8,128)(2,1)} %bitcast.9), calls=%async_computation.1 | async-start | bytes 1179648 | tf_op jit(solution)/shard_map/all_to_all | solution.py:583
  105.4 0.0 collective-permute-done.1.part_1
  105.4 0.0 collective-permute-done.5.part_2
  105.4 0.2 collective-permute-done.6.part_3
  105.7 1.5 %collective-permute-start.7 = (bf16[4,256,256]{2,1,0:T(8,128)(2,1)S(1)}, bf16[4,256,256]{2,1,0:T(8,128)(2,1)S(1)}, u32[]{:S(2)}, u32[]{:S(2)}) collective-permute-start(bf16[4,256,256]{2,1,0:T(8,128)(2,1)S(1)} %pick.1), channel_id=1, source_target_pairs={{0,1},{1,0},{2,3},{3,2},{4,5},{5,4},{6,7},{7,6},{8,9},{9,8},{10,11... | collective-permute-start | bytes 1572872 | tf_op jit(solution)/shard_map/ppermute | solution.py:587
  107.2 1.5 %collective-permute-done.7.other = bf16[4,256,256]{2,1,0:T(8,128)(2,1)S(1)} collective-permute-done((bf16[4,256,256]{2,1,0:T(8,128)(2,1)S(1)}, bf16[4,256,256]{2,1,0:T(8,128)(2,1)S(1)}, u32[]{:S(2)}, u32[]{:S(2)}) %collective-permute-start.7) | collective-permute-done | bytes 524320 | tf_op jit(solution)/shard_map/ppermute | solution.py:587
  108.7 1.1 arrive.1
  109.8 6.5 %all-to-all-done.1.parts = bf16[16,16,1152]{2,1,0:T(8,128)(2,1)S(1)} async-done(((bf16[16,16,1152]{2,1,0:T(8,128)(2,1)}), bf16[16,16,1152]{2,1,0:T(8,128)(2,1)S(1)}, u32[]{:S(2)}, u32[]{:S(2)}) %all-to-all-start.1) | async-done | bytes 589856 | tf_op jit(solution)/shard_map/all_to_all | solution.py:583
  116.3 0.1 sum_share.1.refs_0_
  116.4 0.1 collective-permute-start.10
  116.5 2.1 %collective-permute-start.11 = (bf16[16,1152]{1,0:T(8,128)(2,1)S(1)}, bf16[16,1152]{1,0:T(8,128)(2,1)S(1)}, u32[]{:S(2)}, u32[]{:S(2)}) collective-permute-start(bf16[16,1152]{1,0:T(8,128)(2,1)S(1)} %sum_share.1.refs_0_), channel_id=1, source_target_pairs={{0,4},{2,6},{4,0},{6,2},{1,5},{3,7},{5,1},{7,3},{8,12},{10,14},{12... | collective-permute-start | bytes 110600 | tf_op jit(solution)/shard_map/ppermute | solution.py:612
  118.6 2.0 %collective-permute-start.12 = (bf16[16,1152]{1,0:T(8,128)(2,1)S(1)}, bf16[16,1152]{1,0:T(8,128)(2,1)S(1)}, u32[]{:S(2)}, u32[]{:S(2)}) collective-permute-start(bf16[16,1152]{1,0:T(8,128)(2,1)S(1)} %sum_share.1.refs_0_), channel_id=1, source_target_pairs={{0,6},{2,0},{4,2},{6,4},{1,7},{3,1},{5,3},{7,5},{8,14},{10,8},{12,... | collective-permute-start | bytes 110600 | tf_op jit(solution)/shard_map/ppermute | solution.py:612
  120.6 0.3 collective-permute-done.11.refs_2_
  120.9 0.8 collective-permute-done.12.refs_3_
  121.6 0.1 sum_chips.1
  121.7 14.2 %all_to_all.15 = bf16[16,16,1536]{2,1,0:T(8,128)(2,1)S(1)} all-to-all(bf16[16,16,1536]{2,1,0:T(8,128)(2,1)S(1)} %sum_chips.1), channel_id=1, replica_groups=mesh['x'=4,'z'=4,'y'=4,'core'=2] {'x','z'}, dimensions={0} | all-to-all | bytes 1572864 | tf_op jit(solution)/shard_map/all_to_all | solution.py:583
  136.0 4.6 %collective-permute-start.13 = (bf16[8,2,16,1536]{3,2,1,0:T(8,128)(2,1)S(1)}, bf16[8,2,16,1536]{3,2,1,0:T(8,128)(2,1)S(1)}, u32[]{:S(2)}, u32[]{:S(2)}) collective-permute-start(bf16[8,2,16,1536]{3,2,1,0:T(8,128)(2,1)S(1)} %bitcast.15), channel_id=1, source_target_pairs={{0,1},{1,0},{2,3},{3,2},{4,5},{5,4},{6,7},{7,6},{8,9},{9,8},{10,11... | collective-permute-start | bytes 2359304 | tf_op jit(solution)/shard_map/ppermute | solution.py:587
  140.5 1.2 place.2
  141.8 0.7 collective-permute-done.13.shares
  142.5 1.2 place.3
  (9 shorter events, 0.1 us)
Async XLA Ops:
  7.4 9.4 %copy-start = (bf16[1,256,4096]{2,1,0:T(8,128)(2,1)S(1)}, bf16[1,256,4096]{2,1,0:T(8,128)(2,1)}, u32[]{:S(2)}) copy-start(bf16[1,256,4096]{2,1,0:T(8,128)(2,1)} %param.10) | copy-start | bytes 6291460
  7.4 57.9 %copy-start.3 = (bf16[64,2048]{1,0:T(8,128)(2,1)S(1)}, bf16[64,2048]{1,0:T(8,128)(2,1)}, u32[]{:S(2)}) copy-start(bf16[64,2048]{1,0:T(8,128)(2,1)} %wq_up.3) | copy-start | bytes 786436
  7.5 57.9 %copy-start.5 = (s32[1,8]{1,0:T(1,128)S(1)}, s32[1,8]{1,0:T(1,128)}, u32[]{:S(2)}) copy-start(s32[1,8]{1,0:T(1,128)} %lengths.1) | copy-start | bytes 100
  7.5 57.8 %all-to-all-start = ((bf16[8,272,1024]{2,1,0:T(8,128)(2,1)}), bf16[8,272,1024]{2,1,0:T(8,128)(2,1)}, u32[]{:S(2)}, u32[]{:S(2)}) async-start(bf16[8,272,1024]{2,1,0:T(8,128)(2,1)} %get-tuple-element.33), calls=%async_computation | async-start | bytes 8912896 | tf_op jit(solution)/shard_map/all_to_all | solution.py:583
  13.6 3.3 %collective-permute-start = (bf16[256,2048]{1,0:T(8,128)(2,1)}, bf16[256,2048]{1,0:T(8,128)(2,1)S(1)}, u32[]{:S(2)}, u32[]{:S(2)}) collective-permute-start(bf16[256,2048]{1,0:T(8,128)(2,1)} %get-tuple-element.34), channel_id=1, source_target_pairs={{0,1},{1,0},{2,3},{3,2},{4,5},{5,4},{6,7},{7,6},{8,9},{9,8},{10,11... | collective-permute-start | bytes 3145736 | tf_op jit(solution)/shard_map/ppermute | solution.py:587
  17.0 1.3 copy-start.1
  65.3 1.0 copy-start.4
  81.1 15.0 %copy-start.2 = (bf16[512,2048]{1,0:T(8,128)(2,1)S(1)}, bf16[512,2048]{1,0:T(8,128)(2,1)}, u32[]{:S(2)}) copy-start(bf16[512,2048]{1,0:T(8,128)(2,1)} %copy-done.1) | copy-start | bytes 6291460
  81.1 6.5 %collective-permute-start.2 = (bf16[2,128,256]{2,1,0:T(8,128)(2,1)S(1)}, bf16[2,128,256]{2,1,0:T(8,128)(2,1)S(1)}, u32[]{:S(2)}, u32[]{:S(2)}) collective-permute-start(bf16[2,128,256]{2,1,0:T(8,128)(2,1)S(1)} %get-tuple-element.39), channel_id=1, source_target_pairs={{0,2},{2,4},{4,6},{6,0},{1,3},{3,5},{5,7},{7,1},{8,10},{10,12},{12... | collective-permute-start | bytes 393224 | tf_op jit(solution)/shard_map/ppermute | solution.py:612
  81.4 7.3 %collective-permute-start.3 = (bf16[2,128,256]{2,1,0:T(8,128)(2,1)S(1)}, bf16[2,128,256]{2,1,0:T(8,128)(2,1)S(1)}, u32[]{:S(2)}, u32[]{:S(2)}) collective-permute-start(bf16[2,128,256]{2,1,0:T(8,128)(2,1)S(1)} %get-tuple-element.40), channel_id=1, source_target_pairs={{0,4},{2,6},{4,0},{6,2},{1,5},{3,7},{5,1},{7,3},{8,12},{10,14},{12... | collective-permute-start | bytes 393224 | tf_op jit(solution)/shard_map/ppermute | solution.py:612
  83.3 6.6 %collective-permute-start.4 = (bf16[2,128,256]{2,1,0:T(8,128)(2,1)S(1)}, bf16[2,128,256]{2,1,0:T(8,128)(2,1)S(1)}, u32[]{:S(2)}, u32[]{:S(2)}) collective-permute-start(bf16[2,128,256]{2,1,0:T(8,128)(2,1)S(1)} %get-tuple-element.41), channel_id=1, source_target_pairs={{0,6},{2,0},{4,2},{6,4},{1,7},{3,1},{5,3},{7,5},{8,14},{10,8},{12,... | collective-permute-start | bytes 393224 | tf_op jit(solution)/shard_map/ppermute | solution.py:612
  84.1 10.9 %collective-permute-start.9 = (bf16[8,128,128]{2,1,0:T(8,128)(2,1)S(1)}, bf16[8,128,128]{2,1,0:T(8,128)(2,1)S(1)}, u32[]{:S(2)}, u32[]{:S(2)}) collective-permute-start(bf16[8,128,128]{2,1,0:T(8,128)(2,1)S(1)} %get-tuple-element.49.low), channel_id=1, source_target_pairs={{0,1},{1,0},{2,3},{3,2},{4,5},{5,4},{6,7},{7,6},{8,9},{9,8},{10,11... | collective-permute-start | bytes 786440 | tf_op jit(solution)/shard_map/ppermute | solution.py:587
  85.6 19.9 %collective-permute-start.1 = (bf16[2,256,256]{2,1,0:T(8,128)(2,1)S(1)}, bf16[2,256,256]{2,1,0:T(8,128)(2,1)S(1)}, u32[]{:S(2)}, u32[]{:S(2)}) collective-permute-start(bf16[2,256,256]{2,1,0:T(8,128)(2,1)S(1)} %get-tuple-element.37), channel_id=1, source_target_pairs={{0,2},{2,4},{4,6},{6,0},{1,3},{3,5},{5,7},{7,1},{8,10},{10,12},{12... | collective-permute-start | bytes 786440 | tf_op jit(solution)/shard_map/ppermute | solution.py:612
  90.0 15.5 %collective-permute-start.5 = (bf16[2,256,256]{2,1,0:T(8,128)(2,1)S(1)}, bf16[2,256,256]{2,1,0:T(8,128)(2,1)S(1)}, u32[]{:S(2)}, u32[]{:S(2)}) collective-permute-start(bf16[2,256,256]{2,1,0:T(8,128)(2,1)S(1)} %get-tuple-element.44), channel_id=1, source_target_pairs={{0,4},{2,6},{4,0},{6,2},{1,5},{3,7},{5,1},{7,3},{8,12},{10,14},{12... | collective-permute-start | bytes 786440 | tf_op jit(solution)/shard_map/ppermute | solution.py:612
  90.9 14.7 %collective-permute-start.6 = (bf16[2,256,256]{2,1,0:T(8,128)(2,1)S(1)}, bf16[2,256,256]{2,1,0:T(8,128)(2,1)S(1)}, u32[]{:S(2)}, u32[]{:S(2)}) collective-permute-start(bf16[2,256,256]{2,1,0:T(8,128)(2,1)S(1)} %get-tuple-element.45), channel_id=1, source_target_pairs={{0,6},{2,0},{4,2},{6,4},{1,7},{3,1},{5,3},{7,5},{8,14},{10,8},{12,... | collective-permute-start | bytes 786440 | tf_op jit(solution)/shard_map/ppermute | solution.py:612
  93.7 2.4 %collective-permute-start.8 = (bf16[2,128,256]{2,1,0:T(8,128)(2,1)S(1)}, bf16[2,128,256]{2,1,0:T(8,128)(2,1)S(1)}, u32[]{:S(2)}, u32[]{:S(2)}) collective-permute-start(bf16[2,128,256]{2,1,0:T(8,128)(2,1)S(1)} %get-tuple-element.47.refs_0_), channel_id=1, source_target_pairs={{0,1},{1,0},{2,3},{3,2},{4,5},{5,4},{6,7},{7,6},{8,9},{9,8},{10,11... | collective-permute-start | bytes 393224 | tf_op jit(solution)/shard_map/ppermute | solution.py:587
  97.6 18.7 %all-to-all-start.1 = ((bf16[16,16,1152]{2,1,0:T(8,128)(2,1)}), bf16[16,16,1152]{2,1,0:T(8,128)(2,1)S(1)}, u32[]{:S(2)}, u32[]{:S(2)}) async-start(bf16[16,16,1152]{2,1,0:T(8,128)(2,1)} %bitcast.9), calls=%async_computation.1 | async-start | bytes 1179648 | tf_op jit(solution)/shard_map/all_to_all | solution.py:583
  105.7 3.0 %collective-permute-start.7 = (bf16[4,256,256]{2,1,0:T(8,128)(2,1)S(1)}, bf16[4,256,256]{2,1,0:T(8,128)(2,1)S(1)}, u32[]{:S(2)}, u32[]{:S(2)}) collective-permute-start(bf16[4,256,256]{2,1,0:T(8,128)(2,1)S(1)} %pick.1), channel_id=1, source_target_pairs={{0,1},{1,0},{2,3},{3,2},{4,5},{5,4},{6,7},{7,6},{8,9},{9,8},{10,11... | collective-permute-start | bytes 1572872 | tf_op jit(solution)/shard_map/ppermute | solution.py:587
  116.4 4.2 %collective-permute-start.10 = (bf16[16,1152]{1,0:T(8,128)(2,1)S(1)}, bf16[16,1152]{1,0:T(8,128)(2,1)S(1)}, u32[]{:S(2)}, u32[]{:S(2)}) collective-permute-start(bf16[16,1152]{1,0:T(8,128)(2,1)S(1)} %sum_share.1.refs_0_), channel_id=1, source_target_pairs={{0,2},{2,4},{4,6},{6,0},{1,3},{3,5},{5,7},{7,1},{8,10},{10,12},{12... | collective-permute-start | bytes 110600 | tf_op jit(solution)/shard_map/ppermute | solution.py:612
  116.5 4.4 %collective-permute-start.11 = (bf16[16,1152]{1,0:T(8,128)(2,1)S(1)}, bf16[16,1152]{1,0:T(8,128)(2,1)S(1)}, u32[]{:S(2)}, u32[]{:S(2)}) collective-permute-start(bf16[16,1152]{1,0:T(8,128)(2,1)S(1)} %sum_share.1.refs_0_), channel_id=1, source_target_pairs={{0,4},{2,6},{4,0},{6,2},{1,5},{3,7},{5,1},{7,3},{8,12},{10,14},{12... | collective-permute-start | bytes 110600 | tf_op jit(solution)/shard_map/ppermute | solution.py:612
  118.6 3.0 %collective-permute-start.12 = (bf16[16,1152]{1,0:T(8,128)(2,1)S(1)}, bf16[16,1152]{1,0:T(8,128)(2,1)S(1)}, u32[]{:S(2)}, u32[]{:S(2)}) collective-permute-start(bf16[16,1152]{1,0:T(8,128)(2,1)S(1)} %sum_share.1.refs_0_), channel_id=1, source_target_pairs={{0,6},{2,0},{4,2},{6,4},{1,7},{3,1},{5,3},{7,5},{8,14},{10,8},{12,... | collective-permute-start | bytes 110600 | tf_op jit(solution)/shard_map/ppermute | solution.py:612
  136.0 6.5 %collective-permute-start.13 = (bf16[8,2,16,1536]{3,2,1,0:T(8,128)(2,1)S(1)}, bf16[8,2,16,1536]{3,2,1,0:T(8,128)(2,1)S(1)}, u32[]{:S(2)}, u32[]{:S(2)}) collective-permute-start(bf16[8,2,16,1536]{3,2,1,0:T(8,128)(2,1)S(1)} %bitcast.15), channel_id=1, source_target_pairs={{0,1},{1,0},{2,3},{3,2},{4,5},{5,4},{6,7},{7,6},{8,9},{9,8},{10,11... | collective-permute-start | bytes 2359304 | tf_op jit(solution)/shard_map/ppermute | solution.py:587

commit v12 on v11

--- a/solution.py
+++ b/solution.py
@@ -174,9 +174,10 @@
 
 
 def attention_kernel(
-    lengths, chip, core, packed, wq_up, wv_up, *refs
+    lengths, chip, core, received, wq_up, wv_up, *refs
 ):
-    *outs, dq_t, dv_t, low, q_t, k_t, v_t, g_t, dv, returned, out = refs[1:]
+    *outs, dq_t, dv_t, low, q_t, k_t, v_t, g_t, dv, returned, out = refs[1:-5]
+    packed, wq_v, wv_v, sems, up_sems = refs[-5:]
     outs, backs = outs[: len(outs) // 2], outs[len(outs) // 2 :]
     length = out.shape[0]
     heads = out.shape[1] // HEAD_SIZE
@@ -194,12 +195,25 @@
         rows = packed[pl.ds(first, count), :TILE, columns(which, head)]
         return rows.reshape(count * TILE, HEAD_SIZE)
 
-    for head in range(heads):
-        q_t[span[head], :] = tiles_of(0, blocks, 0, head).T
-        v_t[span[head], :] = tiles_of(0, blocks, 1, head).T
-        k_t[span[head], :] = tiles_of(0, blocks, 2, head).T
-        g_t[span[head], :] = tiles_of(0, blocks, 3, head).T
+    sections = []
+    for which in range(4):
+        for device in range(blocks):
+            at = (device, slice(None), pl.ds(which * width, width))
+            sections.append(
+                pltpu.make_async_copy(received.at[at], packed.at[at], sems.at[which, device])
+            )
+    ups = [
+        pltpu.make_async_copy(wq_up.at[:, own_columns], wq_v, up_sems.at[0]),
+        pltpu.make_async_copy(wv_up.at[:, own_columns], wv_v, up_sems.at[1]),
+    ]
+    for copy in sections + ups:
+        copy.start()
     dv[...] = jnp.zeros_like(dv)
+    for which, turned in enumerate((q_t, v_t, k_t, g_t)):
+        for copy in sections[which * blocks : (which + 1) * blocks]:
+            copy.wait()
+        for head in range(heads):
+            turned[span[head], :] = tiles_of(0, blocks, which, head).T
 
     def block(index, _):
         row0 = pl.multiple_of(index * TILE, TILE)
@@ -258,9 +272,11 @@
     for head in range(heads):
         dv_t[span[head], :] = dv[head].astype(jnp.bfloat16).T
 
-    for part, (grads, weight) in enumerate(((dq_t, wq_up), (dv_t, wv_up))):
+    for copy in ups:
+        copy.wait()
+    for part, (grads, weight) in enumerate(((dq_t, wq_v), (dv_t, wv_v))):
         returned[part * RANK : (part + 1) * RANK, :] = (
-            ADAPTER_SCALE * dot(weight[:, own_columns], grads[...])
+            ADAPTER_SCALE * dot(weight[...], grads[...])
         ).astype(jnp.bfloat16)
     for piece in range(low.shape[1] // LOW_ROWS):
         low[:, piece * LOW_ROWS : (piece + 1) * LOW_ROWS, :] = packed[
@@ -287,7 +303,7 @@
     grad_t = jax.ShapeDtypeStruct((width, length), jnp.bfloat16)
     return pl.pallas_call(
         attention_kernel,
-        in_specs=[SMEM] * 3 + [VMEM] * 4,
+        in_specs=[SMEM] * 3 + [ANY] * 3 + [VMEM],
         out_specs=[VMEM] * (3 + 2 * chips),
         scratch_shapes=[
             wide_t,
@@ -297,6 +313,11 @@
             pltpu.VMEM((heads, length, HEAD_SIZE), jnp.float32),
             pltpu.VMEM((2 * RANK, length), jnp.bfloat16),
             pltpu.VMEM((length, width), jnp.bfloat16),
+            pltpu.VMEM(packed.shape, jnp.bfloat16),
+            pltpu.VMEM((RANK, width), jnp.bfloat16),
+            pltpu.VMEM((RANK, width), jnp.bfloat16),
+            pltpu.SemaphoreType.DMA((4, seq_size)),
+            pltpu.SemaphoreType.DMA((2,)),
         ],
         out_shape=[jax.ShapeDtypeStruct((2, rows, width), jnp.bfloat16)] * chips
         + [back] * chips

time: 144 us -> 144 us (level)
  no operation moved by 1% of the time
where the time goes in v12:
time: 144 us
  waiting for transfers between devices  63.2 us (44%)
  starting transfers between devices  34.8 us (24%)
  Pallas kernels  28.4 us (20%)
  blocking collectives  14.2 us (10%)
  local copies, waits for them, and re-layouts  2.29 us (2%)
    all_to_all x2, waiting for transfers between devices, swap(): return lax.all_to_all(x, axes, 0, 0, tiled=True)  53.2 us
    pallas_call x1, Pallas kernels, attention(): pl.pallas_call(attention_kernel, in_specs=[SMEM] * 3 + [ANY] * 3 + [VMEM]...  15.2 us
    all_to_all x1, blocking collectives, swap(): return lax.all_to_all(x, axes, 0, 0, tiled=True)  14.2 us
    all_to_all x2, starting transfers between devices, swap(): return lax.all_to_all(x, axes, 0, 0, tiled=True)  13.6 us
    ppermute x9, starting transfers between devices, to_chip(): return lax.ppermute(x, 'y', [(c, (c + step) % chips) for c in range(chips)])  11.7 us
    ppermute x5, starting transfers between devices, to_other_core(): return lax.ppermute(x, 'core', [(0, 1), (1, 0)])  9.36 us
    pallas_call x1, Pallas kernels, pack(): pl.pallas_call(pack_kernel, in_specs=[SMEM] + [ANY] * 9, out_specs=[ANY]...  6.78 us
    ppermute x5, waiting for transfers between devices, to_other_core(): return lax.ppermute(x, 'core', [(0, 1), (1, 0)])  5.32 us
  transfers between devices with their start and end apart: 16, of which 12 were waited for; matrix products, arithmetic and copies ran while one was open for 0% of the time, Pallas kernels for 3%

profile of v12, /device:TPU:1, one launch (start us, length us, event | category | flops | bytes accessed | tf_op | source)
XLA Modules:
  0.0 143.9 jit_solution(11807894319068368492)
XLA Ops:
  0.6 6.8 %pack.1 = (bf16[8,272,1024]{2,1,0:T(8,128)(2,1)}, bf16[256,2048]{1,0:T(8,128)(2,1)}) custom-call(s32[1]{0:T(128)} %bitcast.1.core.which, bf16[256,4096]{1,0:T(8,128)(2,1)} %bitcast.13, bf16[64,4096]{1,0:T(8,128)(2,1)} %bitcast.23, bf16[64,4096]{1,0:T(8,128)(2,1)} %bitcast.24, bf16[256,2048]{1,0:T(8,128)(2,1)} %bitcast.17, bf16[256,2048]{1,0:T(8,128)(2,1)} %bitcast.18, ...), custom_call_target="tpu_custom_call" | custom-call | tf_op jit(solution)/shard_map/pack/pallas_call | solution.py:147
  7.4 0.0 copy-start
  7.4 0.0 copy-start.3
  7.5 0.0 copy-start.5
  7.5 6.1 %all-to-all-start = ((bf16[8,272,1024]{2,1,0:T(8,128)(2,1)}), bf16[8,272,1024]{2,1,0:T(8,128)(2,1)}, u32[]{:S(2)}, u32[]{:S(2)}) async-start(bf16[8,272,1024]{2,1,0:T(8,128)(2,1)} %get-tuple-element.33), calls=%async_computation | async-start | bytes 8912896 | tf_op jit(solution)/shard_map/all_to_all | solution.py:604
  13.6 0.3 collective-permute-start
  13.9 3.0 %collective-permute-done.other = bf16[256,2048]{1,0:T(8,128)(2,1)S(1)} collective-permute-done((bf16[256,2048]{1,0:T(8,128)(2,1)}, bf16[256,2048]{1,0:T(8,128)(2,1)S(1)}, u32[]{:S(2)}, u32[]{:S(2)}) %collective-permute-start) | collective-permute-done | bytes 1048608 | tf_op jit(solution)/shard_map/ppermute | solution.py:608
  16.9 0.1 halves.1
  17.0 1.3 copy-done.1
  18.3 47.0 %all-to-all-done.received = bf16[8,272,1024]{2,1,0:T(8,128)(2,1)} async-done(((bf16[8,272,1024]{2,1,0:T(8,128)(2,1)}), bf16[8,272,1024]{2,1,0:T(8,128)(2,1)}, u32[]{:S(2)}, u32[]{:S(2)}) %all-to-all-start) | async-done | bytes 4456480 | tf_op jit(solution)/shard_map/all_to_all | solution.py:604
  65.3 0.9 copy-done.4
  66.3 15.2 %attention.1 = (bf16[2,256,256]{2,1,0:T(8,128)(2,1)S(1)}, bf16[2,256,256]{2,1,0:T(8,128)(2,1)S(1)}, bf16[2,256,256]{2,1,0:T(8,128)(2,1)S(1)}, bf16[2,256,256]{2,...) custom-call(s32[1,8]{1,0:T(1,128)S(1)} %copy-done.5, ...), custom_call_target="tpu_custom_call" | custom-call | flops 8589934592 | bytes 16777216 | tf_op jit(solution)/shard_map/attention/pallas_call | solution.py:304
  81.5 0.4 collective-permute-start.2
  81.8 1.8 %collective-permute-start.3 = (bf16[2,128,256]{2,1,0:T(8,128)(2,1)S(1)}, bf16[2,128,256]{2,1,0:T(8,128)(2,1)S(1)}, u32[]{:S(2)}, u32[]{:S(2)}) collective-permute-start(bf16[2,128,256]{2,1,0:T(8,128)(2,1)S(1)} %get-tuple-element.40), channel_id=1, source_target_pairs={{0,4},{2,6},{4,0},{6,2},{1,5},{3,7},{5,1},{7,3},{8,12},{10,14},{12... | collective-permute-start | bytes 393224 | tf_op jit(solution)/shard_map/ppermute | solution.py:633
  83.6 0.7 collective-permute-start.4
  84.3 1.4 collective-permute-start.9
  85.8 1.0 collective-permute-start.1
  86.8 1.2 collective-permute-done.2.part_1
  88.0 1.1 collective-permute-done.3.part_2
  89.1 1.0 collective-permute-done.4.part_3
  90.1 0.1 sum_backs.1
  90.2 1.0 collective-permute-start.5
  91.1 2.7 %collective-permute-start.6 = (bf16[2,256,256]{2,1,0:T(8,128)(2,1)S(1)}, bf16[2,256,256]{2,1,0:T(8,128)(2,1)S(1)}, u32[]{:S(2)}, u32[]{:S(2)}) collective-permute-start(bf16[2,256,256]{2,1,0:T(8,128)(2,1)S(1)} %get-tuple-element.45), channel_id=1, source_target_pairs={{0,6},{2,0},{4,2},{6,4},{1,7},{3,1},{5,3},{7,5},{8,14},{10,8},{12,... | collective-permute-start | bytes 786440 | tf_op jit(solution)/shard_map/ppermute | solution.py:633
  93.8 1.5 %collective-permute-start.8 = (bf16[2,128,256]{2,1,0:T(8,128)(2,1)S(1)}, bf16[2,128,256]{2,1,0:T(8,128)(2,1)S(1)}, u32[]{:S(2)}, u32[]{:S(2)}) collective-permute-start(bf16[2,128,256]{2,1,0:T(8,128)(2,1)S(1)} %get-tuple-element.47.refs_0_), channel_id=1, source_target_pairs={{0,1},{1,0},{2,3},{3,2},{4,5},{5,4},{6,7},{7,6},{8,9},{9,8},{10,11... | collective-permute-start | bytes 393224 | tf_op jit(solution)/shard_map/ppermute | solution.py:608
  95.3 0.0 collective-permute-done.9.low_other
  95.3 0.8 up_gradient.1.refs_3_
  96.1 0.1 collective-permute-done.8.refs_1_
  96.3 1.6 %down_gradient.1 = bf16[8,2,16,1152]{3,2,1,0:T(8,128)(2,1)} custom-call(s32[1]{0:T(128)} %bitcast.1.core.which, bf16[2,128,256]{2,1,0:T(8,128)(2,1)S(1)} %get-tuple-element.47.refs_0_, bf16[2,128,256]{2,1,0:T(8,128)(2,1)S(1)} %collective-permute-done.8.refs_1_, bf16[512,2048]{1,0:T(8,128)(2,1)S(1)} %copy-done.2, bf16[128,256]{1,0:T(8,128)(2,1)S(1)} %up_gradient.1.refs_3_), custom_call_target="tpu_custom_call" | custom-call | tf_op jit(solution)/shard_map/down_gradient/pallas_call | solution.py:471
  97.8 7.5 %all-to-all-start.1 = ((bf16[16,16,1152]{2,1,0:T(8,128)(2,1)}), bf16[16,16,1152]{2,1,0:T(8,128)(2,1)S(1)}, u32[]{:S(2)}, u32[]{:S(2)}) async-start(bf16[16,16,1152]{2,1,0:T(8,128)(2,1)} %bitcast.9), calls=%async_computation.1 | async-start | bytes 1179648 | tf_op jit(solution)/shard_map/all_to_all | solution.py:604
  105.4 0.0 collective-permute-done.5.part_2
  105.4 0.3 collective-permute-done.6.part_3
  105.7 1.6 %collective-permute-start.7 = (bf16[4,256,256]{2,1,0:T(8,128)(2,1)S(1)}, bf16[4,256,256]{2,1,0:T(8,128)(2,1)S(1)}, u32[]{:S(2)}, u32[]{:S(2)}) collective-permute-start(bf16[4,256,256]{2,1,0:T(8,128)(2,1)S(1)} %pick.1), channel_id=1, source_target_pairs={{0,1},{1,0},{2,3},{3,2},{4,5},{5,4},{6,7},{7,6},{8,9},{9,8},{10,11... | collective-permute-start | bytes 1572872 | tf_op jit(solution)/shard_map/ppermute | solution.py:608
  107.3 1.5 %collective-permute-done.7.other = bf16[4,256,256]{2,1,0:T(8,128)(2,1)S(1)} collective-permute-done((bf16[4,256,256]{2,1,0:T(8,128)(2,1)S(1)}, bf16[4,256,256]{2,1,0:T(8,128)(2,1)S(1)}, u32[]{:S(2)}, u32[]{:S(2)}) %collective-permute-start.7) | collective-permute-done | bytes 524320 | tf_op jit(solution)/shard_map/ppermute | solution.py:608
  108.9 1.1 arrive.1
  110.0 6.3 %all-to-all-done.1.parts = bf16[16,16,1152]{2,1,0:T(8,128)(2,1)S(1)} async-done(((bf16[16,16,1152]{2,1,0:T(8,128)(2,1)}), bf16[16,16,1152]{2,1,0:T(8,128)(2,1)S(1)}, u32[]{:S(2)}, u32[]{:S(2)}) %all-to-all-start.1) | async-done | bytes 589856 | tf_op jit(solution)/shard_map/all_to_all | solution.py:604
  116.2 0.1 sum_share.1.refs_0_
  116.3 0.1 collective-permute-start.10
  116.4 2.2 %collective-permute-start.11 = (bf16[16,1152]{1,0:T(8,128)(2,1)S(1)}, bf16[16,1152]{1,0:T(8,128)(2,1)S(1)}, u32[]{:S(2)}, u32[]{:S(2)}) collective-permute-start(bf16[16,1152]{1,0:T(8,128)(2,1)S(1)} %sum_share.1.refs_0_), channel_id=1, source_target_pairs={{0,4},{2,6},{4,0},{6,2},{1,5},{3,7},{5,1},{7,3},{8,12},{10,14},{12... | collective-permute-start | bytes 110600 | tf_op jit(solution)/shard_map/ppermute | solution.py:633
  118.6 2.0 %collective-permute-start.12 = (bf16[16,1152]{1,0:T(8,128)(2,1)S(1)}, bf16[16,1152]{1,0:T(8,128)(2,1)S(1)}, u32[]{:S(2)}, u32[]{:S(2)}) collective-permute-start(bf16[16,1152]{1,0:T(8,128)(2,1)S(1)} %sum_share.1.refs_0_), channel_id=1, source_target_pairs={{0,6},{2,0},{4,2},{6,4},{1,7},{3,1},{5,3},{7,5},{8,14},{10,8},{12,... | collective-permute-start | bytes 110600 | tf_op jit(solution)/shard_map/ppermute | solution.py:633
  120.5 0.0 collective-permute-done.10.refs_1_
  120.6 0.3 collective-permute-done.11.refs_2_
  120.8 0.8 collective-permute-done.12.refs_3_
  121.6 0.1 sum_chips.1
  121.7 14.2 %all_to_all.15 = bf16[16,16,1536]{2,1,0:T(8,128)(2,1)S(1)} all-to-all(bf16[16,16,1536]{2,1,0:T(8,128)(2,1)S(1)} %sum_chips.1), channel_id=1, replica_groups=mesh['x'=4,'z'=4,'y'=4,'core'=2] {'x','z'}, dimensions={0} | all-to-all | bytes 1572864 | tf_op jit(solution)/shard_map/all_to_all | solution.py:604
  136.0 4.6 %collective-permute-start.13 = (bf16[8,2,16,1536]{3,2,1,0:T(8,128)(2,1)S(1)}, bf16[8,2,16,1536]{3,2,1,0:T(8,128)(2,1)S(1)}, u32[]{:S(2)}, u32[]{:S(2)}) collective-permute-start(bf16[8,2,16,1536]{3,2,1,0:T(8,128)(2,1)S(1)} %bitcast.15), channel_id=1, source_target_pairs={{0,1},{1,0},{2,3},{3,2},{4,5},{5,4},{6,7},{7,6},{8,9},{9,8},{10,11... | collective-permute-start | bytes 2359304 | tf_op jit(solution)/shard_map/ppermute | solution.py:608
  140.5 1.2 place.2
  141.8 0.7 collective-permute-done.13.shares
  142.4 1.2 place.3
  (9 shorter events, 0.1 us)
Async XLA Ops:
  7.4 9.4 %copy-start = (bf16[1,256,4096]{2,1,0:T(8,128)(2,1)S(1)}, bf16[1,256,4096]{2,1,0:T(8,128)(2,1)}, u32[]{:S(2)}) copy-start(bf16[1,256,4096]{2,1,0:T(8,128)(2,1)} %param.10) | copy-start | bytes 6291460
  7.4 57.9 %copy-start.3 = (bf16[64,2048]{1,0:T(8,128)(2,1)S(1)}, bf16[64,2048]{1,0:T(8,128)(2,1)}, u32[]{:S(2)}) copy-start(bf16[64,2048]{1,0:T(8,128)(2,1)} %wq_up.3) | copy-start | bytes 786436
  7.5 57.9 %copy-start.5 = (s32[1,8]{1,0:T(1,128)S(1)}, s32[1,8]{1,0:T(1,128)}, u32[]{:S(2)}) copy-start(s32[1,8]{1,0:T(1,128)} %lengths.1) | copy-start | bytes 100
  7.5 57.8 %all-to-all-start = ((bf16[8,272,1024]{2,1,0:T(8,128)(2,1)}), bf16[8,272,1024]{2,1,0:T(8,128)(2,1)}, u32[]{:S(2)}, u32[]{:S(2)}) async-start(bf16[8,272,1024]{2,1,0:T(8,128)(2,1)} %get-tuple-element.33), calls=%async_computation | async-start | bytes 8912896 | tf_op jit(solution)/shard_map/all_to_all | solution.py:604
  13.6 3.3 %collective-permute-start = (bf16[256,2048]{1,0:T(8,128)(2,1)}, bf16[256,2048]{1,0:T(8,128)(2,1)S(1)}, u32[]{:S(2)}, u32[]{:S(2)}) collective-permute-start(bf16[256,2048]{1,0:T(8,128)(2,1)} %get-tuple-element.34), channel_id=1, source_target_pairs={{0,1},{1,0},{2,3},{3,2},{4,5},{5,4},{6,7},{7,6},{8,9},{9,8},{10,11... | collective-permute-start | bytes 3145736 | tf_op jit(solution)/shard_map/ppermute | solution.py:608
  17.0 1.3 copy-start.1
  65.3 1.0 copy-start.4
  81.5 14.8 %copy-start.2 = (bf16[512,2048]{1,0:T(8,128)(2,1)S(1)}, bf16[512,2048]{1,0:T(8,128)(2,1)}, u32[]{:S(2)}) copy-start(bf16[512,2048]{1,0:T(8,128)(2,1)} %copy-done.1) | copy-start | bytes 6291460
  81.5 6.5 %collective-permute-start.2 = (bf16[2,128,256]{2,1,0:T(8,128)(2,1)S(1)}, bf16[2,128,256]{2,1,0:T(8,128)(2,1)S(1)}, u32[]{:S(2)}, u32[]{:S(2)}) collective-permute-start(bf16[2,128,256]{2,1,0:T(8,128)(2,1)S(1)} %get-tuple-element.39), channel_id=1, source_target_pairs={{0,2},{2,4},{4,6},{6,0},{1,3},{3,5},{5,7},{7,1},{8,10},{10,12},{12... | collective-permute-start | bytes 393224 | tf_op jit(solution)/shard_map/ppermute | solution.py:633
  81.8 7.3 %collective-permute-start.3 = (bf16[2,128,256]{2,1,0:T(8,128)(2,1)S(1)}, bf16[2,128,256]{2,1,0:T(8,128)(2,1)S(1)}, u32[]{:S(2)}, u32[]{:S(2)}) collective-permute-start(bf16[2,128,256]{2,1,0:T(8,128)(2,1)S(1)} %get-tuple-element.40), channel_id=1, source_target_pairs={{0,4},{2,6},{4,0},{6,2},{1,5},{3,7},{5,1},{7,3},{8,12},{10,14},{12... | collective-permute-start | bytes 393224 | tf_op jit(solution)/shard_map/ppermute | solution.py:633
  83.6 6.4 %collective-permute-start.4 = (bf16[2,128,256]{2,1,0:T(8,128)(2,1)S(1)}, bf16[2,128,256]{2,1,0:T(8,128)(2,1)S(1)}, u32[]{:S(2)}, u32[]{:S(2)}) collective-permute-start(bf16[2,128,256]{2,1,0:T(8,128)(2,1)S(1)} %get-tuple-element.41), channel_id=1, source_target_pairs={{0,6},{2,0},{4,2},{6,4},{1,7},{3,1},{5,3},{7,5},{8,14},{10,8},{12,... | collective-permute-start | bytes 393224 | tf_op jit(solution)/shard_map/ppermute | solution.py:633
  84.3 10.9 %collective-permute-start.9 = (bf16[8,128,128]{2,1,0:T(8,128)(2,1)S(1)}, bf16[8,128,128]{2,1,0:T(8,128)(2,1)S(1)}, u32[]{:S(2)}, u32[]{:S(2)}) collective-permute-start(bf16[8,128,128]{2,1,0:T(8,128)(2,1)S(1)} %get-tuple-element.49.low), channel_id=1, source_target_pairs={{0,1},{1,0},{2,3},{3,2},{4,5},{5,4},{6,7},{7,6},{8,9},{9,8},{10,11... | collective-permute-start | bytes 786440 | tf_op jit(solution)/shard_map/ppermute | solution.py:608
  85.8 19.6 %collective-permute-start.1 = (bf16[2,256,256]{2,1,0:T(8,128)(2,1)S(1)}, bf16[2,256,256]{2,1,0:T(8,128)(2,1)S(1)}, u32[]{:S(2)}, u32[]{:S(2)}) collective-permute-start(bf16[2,256,256]{2,1,0:T(8,128)(2,1)S(1)} %get-tuple-element.37), channel_id=1, source_target_pairs={{0,2},{2,4},{4,6},{6,0},{1,3},{3,5},{5,7},{7,1},{8,10},{10,12},{12... | collective-permute-start | bytes 786440 | tf_op jit(solution)/shard_map/ppermute | solution.py:633
  90.2 15.2 %collective-permute-start.5 = (bf16[2,256,256]{2,1,0:T(8,128)(2,1)S(1)}, bf16[2,256,256]{2,1,0:T(8,128)(2,1)S(1)}, u32[]{:S(2)}, u32[]{:S(2)}) collective-permute-start(bf16[2,256,256]{2,1,0:T(8,128)(2,1)S(1)} %get-tuple-element.44), channel_id=1, source_target_pairs={{0,4},{2,6},{4,0},{6,2},{1,5},{3,7},{5,1},{7,3},{8,12},{10,14},{12... | collective-permute-start | bytes 786440 | tf_op jit(solution)/shard_map/ppermute | solution.py:633
  91.1 14.6 %collective-permute-start.6 = (bf16[2,256,256]{2,1,0:T(8,128)(2,1)S(1)}, bf16[2,256,256]{2,1,0:T(8,128)(2,1)S(1)}, u32[]{:S(2)}, u32[]{:S(2)}) collective-permute-start(bf16[2,256,256]{2,1,0:T(8,128)(2,1)S(1)} %get-tuple-element.45), channel_id=1, source_target_pairs={{0,6},{2,0},{4,2},{6,4},{1,7},{3,1},{5,3},{7,5},{8,14},{10,8},{12,... | collective-permute-start | bytes 786440 | tf_op jit(solution)/shard_map/ppermute | solution.py:633
  93.8 2.4 %collective-permute-start.8 = (bf16[2,128,256]{2,1,0:T(8,128)(2,1)S(1)}, bf16[2,128,256]{2,1,0:T(8,128)(2,1)S(1)}, u32[]{:S(2)}, u32[]{:S(2)}) collective-permute-start(bf16[2,128,256]{2,1,0:T(8,128)(2,1)S(1)} %get-tuple-element.47.refs_0_), channel_id=1, source_target_pairs={{0,1},{1,0},{2,3},{3,2},{4,5},{5,4},{6,7},{7,6},{8,9},{9,8},{10,11... | collective-permute-start | bytes 393224 | tf_op jit(solution)/shard_map/ppermute | solution.py:608
  97.8 18.4 %all-to-all-start.1 = ((bf16[16,16,1152]{2,1,0:T(8,128)(2,1)}), bf16[16,16,1152]{2,1,0:T(8,128)(2,1)S(1)}, u32[]{:S(2)}, u32[]{:S(2)}) async-start(bf16[16,16,1152]{2,1,0:T(8,128)(2,1)} %bitcast.9), calls=%async_computation.1 | async-start | bytes 1179648 | tf_op jit(solution)/shard_map/all_to_all | solution.py:604
  105.7 3.1 %collective-permute-start.7 = (bf16[4,256,256]{2,1,0:T(8,128)(2,1)S(1)}, bf16[4,256,256]{2,1,0:T(8,128)(2,1)S(1)}, u32[]{:S(2)}, u32[]{:S(2)}) collective-permute-start(bf16[4,256,256]{2,1,0:T(8,128)(2,1)S(1)} %pick.1), channel_id=1, source_target_pairs={{0,1},{1,0},{2,3},{3,2},{4,5},{5,4},{6,7},{7,6},{8,9},{9,8},{10,11... | collective-permute-start | bytes 1572872 | tf_op jit(solution)/shard_map/ppermute | solution.py:608
  116.3 4.2 %collective-permute-start.10 = (bf16[16,1152]{1,0:T(8,128)(2,1)S(1)}, bf16[16,1152]{1,0:T(8,128)(2,1)S(1)}, u32[]{:S(2)}, u32[]{:S(2)}) collective-permute-start(bf16[16,1152]{1,0:T(8,128)(2,1)S(1)} %sum_share.1.refs_0_), channel_id=1, source_target_pairs={{0,2},{2,4},{4,6},{6,0},{1,3},{3,5},{5,7},{7,1},{8,10},{10,12},{12... | collective-permute-start | bytes 110600 | tf_op jit(solution)/shard_map/ppermute | solution.py:633
  116.4 4.4 %collective-permute-start.11 = (bf16[16,1152]{1,0:T(8,128)(2,1)S(1)}, bf16[16,1152]{1,0:T(8,128)(2,1)S(1)}, u32[]{:S(2)}, u32[]{:S(2)}) collective-permute-start(bf16[16,1152]{1,0:T(8,128)(2,1)S(1)} %sum_share.1.refs_0_), channel_id=1, source_target_pairs={{0,4},{2,6},{4,0},{6,2},{1,5},{3,7},{5,1},{7,3},{8,12},{10,14},{12... | collective-permute-start | bytes 110600 | tf_op jit(solution)/shard_map/ppermute | solution.py:633
  118.6 3.0 %collective-permute-start.12 = (bf16[16,1152]{1,0:T(8,128)(2,1)S(1)}, bf16[16,1152]{1,0:T(8,128)(2,1)S(1)}, u32[]{:S(2)}, u32[]{:S(2)}) collective-permute-start(bf16[16,1152]{1,0:T(8,128)(2,1)S(1)} %sum_share.1.refs_0_), channel_id=1, source_target_pairs={{0,6},{2,0},{4,2},{6,4},{1,7},{3,1},{5,3},{7,5},{8,14},{10,8},{12,... | collective-permute-start | bytes 110600 | tf_op jit(solution)/shard_map/ppermute | solution.py:633
  136.0 6.5 %collective-permute-start.13 = (bf16[8,2,16,1536]{3,2,1,0:T(8,128)(2,1)S(1)}, bf16[8,2,16,1536]{3,2,1,0:T(8,128)(2,1)S(1)}, u32[]{:S(2)}, u32[]{:S(2)}) collective-permute-start(bf16[8,2,16,1536]{3,2,1,0:T(8,128)(2,1)S(1)} %bitcast.15), channel_id=1, source_target_pairs={{0,1},{1,0},{2,3},{3,2},{4,5},{5,4},{6,7},{7,6},{8,9},{9,8},{10,11... | collective-permute-start | bytes 2359304 | tf_op jit(solution)/shard_map/ppermute | solution.py:608

commit v13 on v11

--- a/solution.py
+++ b/solution.py
@@ -174,16 +174,15 @@
 
 
 def attention_kernel(
-    lengths, chip, core, packed, wq_up, wv_up, *refs
+    lengths, chip, packed, ups, *refs
 ):
-    *outs, dq_t, dv_t, low, q_t, k_t, v_t, g_t, dv, returned, out = refs[1:]
+    *outs, dq_t, dv_t, low, q_t, k_t, v_t, g_t, dv, returned, out = refs
     outs, backs = outs[: len(outs) // 2], outs[len(outs) // 2 :]
     length = out.shape[0]
     heads = out.shape[1] // HEAD_SIZE
     width = heads * HEAD_SIZE
     blocks = length // TILE
-    chip, core = chip[0], core[0]
-    own_columns = pl.ds(pl.multiple_of((chip * 2 + core) * width, width), width)
+    chip = chip[0]
     span = [slice(head * HEAD_SIZE, (head + 1) * HEAD_SIZE) for head in range(heads)]
 
     def columns(which, head):
@@ -258,9 +257,9 @@
     for head in range(heads):
         dv_t[span[head], :] = dv[head].astype(jnp.bfloat16).T
 
-    for part, (grads, weight) in enumerate(((dq_t, wq_up), (dv_t, wv_up))):
+    for part, grads in enumerate((dq_t, dv_t)):
         returned[part * RANK : (part + 1) * RANK, :] = (
-            ADAPTER_SCALE * dot(weight[:, own_columns], grads[...])
+            ADAPTER_SCALE * dot(ups[part * RANK : (part + 1) * RANK, :], grads[...])
         ).astype(jnp.bfloat16)
     for piece in range(low.shape[1] // LOW_ROWS):
         low[:, piece * LOW_ROWS : (piece + 1) * LOW_ROWS, :] = packed[
@@ -275,7 +274,7 @@
             outs[step][holder] = out[pl.ds(begin, rows), :]
 
 
-def attention(lengths, chip, core, packed, wq_up, wv_up, after):
+def attention(lengths, chip, packed, ups):
     seq_size = packed.shape[0]
     rows = packed.shape[1] - LOW_ROWS
     length = seq_size * rows
@@ -287,7 +286,7 @@
     grad_t = jax.ShapeDtypeStruct((width, length), jnp.bfloat16)
     return pl.pallas_call(
         attention_kernel,
-        in_specs=[SMEM] * 3 + [VMEM] * 4,
+        in_specs=[SMEM] * 2 + [VMEM] * 2,
         out_specs=[VMEM] * (3 + 2 * chips),
         scratch_shapes=[
             wide_t,
@@ -307,7 +306,7 @@
             flops=8 << 30, bytes_accessed=16 << 20, transcendentals=4 << 20
         ),
         name="attention",
-    )(lengths, chip, core, packed, wq_up, wv_up, after)
+    )(lengths, chip, packed, ups)
 
 
 def up_kernel(core, low, low_other, dq_t, dv_t, up, lows):
@@ -404,23 +403,29 @@
     )(*parts, *held)
 
 
-def halves_kernel(core, hidden, other, out, done):
+def halves_kernel(chip, core, hidden, other, wq_up, wv_up, out, ups):
     rows, half = other.shape
     out[:rows] = hidden[:, pl.ds(pl.multiple_of(core[0] * half, half), half)]
     out[rows:] = other[...]
-    done[...] = jnp.zeros_like(done)
-
-
-def halves(core, hidden, other):
+    width = ups.shape[1]
+    columns = pl.ds(pl.multiple_of((chip[0] * 2 + core[0]) * width, width), width)
+    ups[:RANK] = wq_up[:, columns]
+    ups[RANK:] = wv_up[:, columns]
+
+
+def halves(chip, core, hidden, other, wq_up, wv_up, width):
     rows, half = other.shape
     return pl.pallas_call(
         halves_kernel,
-        in_specs=[SMEM, VMEM, VMEM],
+        in_specs=[SMEM] * 2 + [VMEM] * 4,
         out_specs=[VMEM] * 2,
-        out_shape=[jax.ShapeDtypeStruct((2 * rows, half), hidden.dtype), DONE],
+        out_shape=[
+            jax.ShapeDtypeStruct((2 * rows, half), hidden.dtype),
+            jax.ShapeDtypeStruct((2 * RANK, width), wq_up.dtype),
+        ],
         compiler_params=pltpu.CompilerParams(vmem_limit_bytes=SMALL_VMEM),
         name="halves",
-    )(core, hidden, other)
+    )(chip, core, hidden, other, wq_up, wv_up)
 
 
 def down_kernel(core, *refs):
@@ -626,15 +631,14 @@
     )
     received = swap(packed, SEQ)
     hidden_other = to_other_core(hidden_leaving)
-    hidden_half, halves_done = halves(core, hidden[0], hidden_other)
+    hidden_half, ups = halves(
+        chip, core, hidden[0], hidden_other, query_up_weight, value_up_weight, width
+    )
     *outs, dq_t, dv_t, low = attention(
         document_length_list,
         chip,
-        core,
         received,
-        query_up_weight,
-        value_up_weight,
-        after=halves_done,
+        ups,
     )
     parts, backs = outs[:chips], outs[chips:]
 

time: 144 us -> 143 us (level)
    all_to_all x2, waiting for transfers between devices: 53.4 us -> 51.8 us  [swap(): return lax.all_to_all(x, axes, 0, 0, tiled=True)]
  transfers between devices with their start and end apart: 16 -> 16, of which waited for: 12 -> 12; matrix products, arithmetic and copies ran while one was open for 0% -> 0% of each run, Pallas kernels for 3% -> 4%
where the time goes in v13:
time: 143 us
  waiting for transfers between devices  62.7 us (44%)
  starting transfers between devices  34.1 us (24%)
  Pallas kernels  28.5 us (20%)
  blocking collectives  14.2 us (10%)
  local copies, waits for them, and re-layouts  2.29 us (2%)
    all_to_all x2, waiting for transfers between devices, swap(): return lax.all_to_all(x, axes, 0, 0, tiled=True)  51.8 us
    pallas_call x1, Pallas kernels, attention(): pl.pallas_call(attention_kernel, in_specs=[SMEM] * 2 + [VMEM] * 2, out_sp...  15.3 us
    all_to_all x1, blocking collectives, swap(): return lax.all_to_all(x, axes, 0, 0, tiled=True)  14.2 us
    all_to_all x2, starting transfers between devices, swap(): return lax.all_to_all(x, axes, 0, 0, tiled=True)  13.3 us
    ppermute x9, starting transfers between devices, to_chip(): return lax.ppermute(x, 'y', [(c, (c + step) % chips) for c in range(chips)])  11.8 us
    ppermute x5, starting transfers between devices, to_other_core(): return lax.ppermute(x, 'core', [(0, 1), (1, 0)])  8.94 us
    pallas_call x1, Pallas kernels, pack(): pl.pallas_call(pack_kernel, in_specs=[SMEM] + [ANY] * 9, out_specs=[ANY]...  6.78 us
    ppermute x5, waiting for transfers between devices, to_other_core(): return lax.ppermute(x, 'core', [(0, 1), (1, 0)])  5.48 us
  transfers between devices with their start and end apart: 16, of which 12 were waited for; matrix products, arithmetic and copies ran while one was open for 0% of the time, Pallas kernels for 4%

profile of v13, /device:TPU:1, one launch (start us, length us, event | category | flops | bytes accessed | tf_op | source)
XLA Modules:
  0.0 142.8 jit_solution(1977326802134049699)
XLA Ops:
  0.6 6.8 %pack.1 = (bf16[8,272,1024]{2,1,0:T(8,128)(2,1)}, bf16[256,2048]{1,0:T(8,128)(2,1)}) custom-call(s32[1]{0:T(128)} %bitcast.1.core.which, bf16[256,4096]{1,0:T(8,128)(2,1)} %bitcast.13, bf16[64,4096]{1,0:T(8,128)(2,1)} %bitcast.23, bf16[64,4096]{1,0:T(8,128)(2,1)} %bitcast.24, bf16[256,2048]{1,0:T(8,128)(2,1)} %bitcast.17, bf16[256,2048]{1,0:T(8,128)(2,1)} %bitcast.18, ...), custom_call_target="tpu_custom_call" | custom-call | tf_op jit(solution)/shard_map/pack/pallas_call | solution.py:147
  7.4 0.0 copy-start
  7.4 0.0 copy-start.3
  7.5 0.0 copy-start.5
  7.5 6.1 %all-to-all-start = ((bf16[8,272,1024]{2,1,0:T(8,128)(2,1)}), bf16[8,272,1024]{2,1,0:T(8,128)(2,1)}, u32[]{:S(2)}, u32[]{:S(2)}) async-start(bf16[8,272,1024]{2,1,0:T(8,128)(2,1)} %get-tuple-element.33), calls=%async_computation | async-start | bytes 8912896 | tf_op jit(solution)/shard_map/all_to_all | solution.py:588
  13.6 0.1 collective-permute-start
  13.7 3.2 %collective-permute-done.other = bf16[256,2048]{1,0:T(8,128)(2,1)S(1)} collective-permute-done((bf16[256,2048]{1,0:T(8,128)(2,1)}, bf16[256,2048]{1,0:T(8,128)(2,1)S(1)}, u32[]{:S(2)}, u32[]{:S(2)}) %collective-permute-start) | collective-permute-done | bytes 1048608 | tf_op jit(solution)/shard_map/ppermute | solution.py:592
  16.9 0.9 copy-done.4
  17.8 0.1 halves.1
  18.0 1.3 copy-done.1
  19.3 46.0 %all-to-all-done.packed = bf16[8,272,1024]{2,1,0:T(8,128)(2,1)} async-done(((bf16[8,272,1024]{2,1,0:T(8,128)(2,1)}), bf16[8,272,1024]{2,1,0:T(8,128)(2,1)}, u32[]{:S(2)}, u32[]{:S(2)}) %all-to-all-start) | async-done | bytes 4456480 | tf_op jit(solution)/shard_map/all_to_all | solution.py:588
  65.3 15.3 %attention.1 = (bf16[2,256,256]{2,1,0:T(8,128)(2,1)S(1)}, bf16[2,256,256]{2,1,0:T(8,128)(2,1)S(1)}, bf16[2,256,256]{2,1,0:T(8,128)(2,1)S(1)}, bf16[2,256,256]{2,...) custom-call(s32[1,8]{1,0:T(1,128)S(1)} %copy-done.5, ...), custom_call_target="tpu_custom_call" | custom-call | flops 8589934592 | bytes 16777216 | tf_op jit(solution)/shard_map/attention/pallas_call | solution.py:287
  80.6 0.4 collective-permute-start.2
  81.0 1.8 %collective-permute-start.3 = (bf16[2,128,256]{2,1,0:T(8,128)(2,1)S(1)}, bf16[2,128,256]{2,1,0:T(8,128)(2,1)S(1)}, u32[]{:S(2)}, u32[]{:S(2)}) collective-permute-start(bf16[2,128,256]{2,1,0:T(8,128)(2,1)S(1)} %get-tuple-element.40), channel_id=1, source_target_pairs={{0,4},{2,6},{4,0},{6,2},{1,5},{3,7},{5,1},{7,3},{8,12},{10,14},{12... | collective-permute-start | bytes 393224 | tf_op jit(solution)/shard_map/ppermute | solution.py:617
  82.7 0.9 collective-permute-start.4
  83.6 1.4 collective-permute-start.9
  85.0 0.9 collective-permute-start.1
  85.9 1.2 collective-permute-done.2.part_1
  87.1 1.2 collective-permute-done.3.part_2
  88.2 1.2 collective-permute-done.4.part_3
  89.4 0.1 sum_backs.1
  89.5 1.0 collective-permute-start.5
  90.5 2.7 %collective-permute-start.6 = (bf16[2,256,256]{2,1,0:T(8,128)(2,1)S(1)}, bf16[2,256,256]{2,1,0:T(8,128)(2,1)S(1)}, u32[]{:S(2)}, u32[]{:S(2)}) collective-permute-start(bf16[2,256,256]{2,1,0:T(8,128)(2,1)S(1)} %get-tuple-element.45), channel_id=1, source_target_pairs={{0,6},{2,0},{4,2},{6,4},{1,7},{3,1},{5,3},{7,5},{8,14},{10,8},{12,... | collective-permute-start | bytes 786440 | tf_op jit(solution)/shard_map/ppermute | solution.py:617
  93.2 1.4 collective-permute-start.8
  94.6 0.0 collective-permute-done.9.low_other
  94.6 0.9 up_gradient.1.refs_3_
  95.4 0.1 collective-permute-done.8.refs_1_
  95.6 1.6 %down_gradient.1 = bf16[8,2,16,1152]{3,2,1,0:T(8,128)(2,1)} custom-call(s32[1]{0:T(128)} %bitcast.1.core.which, bf16[2,128,256]{2,1,0:T(8,128)(2,1)S(1)} %get-tuple-element.47.refs_0_, bf16[2,128,256]{2,1,0:T(8,128)(2,1)S(1)} %collective-permute-done.8.refs_1_, bf16[512,2048]{1,0:T(8,128)(2,1)S(1)} %copy-done.2, bf16[128,256]{1,0:T(8,128)(2,1)S(1)} %up_gradient.1.refs_3_), custom_call_target="tpu_custom_call" | custom-call | tf_op jit(solution)/shard_map/down_gradient/pallas_call | solution.py:455
  97.1 7.2 %all-to-all-start.1 = ((bf16[16,16,1152]{2,1,0:T(8,128)(2,1)}), bf16[16,16,1152]{2,1,0:T(8,128)(2,1)S(1)}, u32[]{:S(2)}, u32[]{:S(2)}) async-start(bf16[16,16,1152]{2,1,0:T(8,128)(2,1)} %bitcast.9), calls=%async_computation.1 | async-start | bytes 1179648 | tf_op jit(solution)/shard_map/all_to_all | solution.py:588
  104.3 0.0 collective-permute-done.1.part_1
  104.3 0.0 collective-permute-done.5.part_2
  104.3 0.9 collective-permute-done.6.part_3
  105.3 1.5 %collective-permute-start.7 = (bf16[4,256,256]{2,1,0:T(8,128)(2,1)S(1)}, bf16[4,256,256]{2,1,0:T(8,128)(2,1)S(1)}, u32[]{:S(2)}, u32[]{:S(2)}) collective-permute-start(bf16[4,256,256]{2,1,0:T(8,128)(2,1)S(1)} %pick.1), channel_id=1, source_target_pairs={{0,1},{1,0},{2,3},{3,2},{4,5},{5,4},{6,7},{7,6},{8,9},{9,8},{10,11... | collective-permute-start | bytes 1572872 | tf_op jit(solution)/shard_map/ppermute | solution.py:592
  106.7 1.5 %collective-permute-done.7.other = bf16[4,256,256]{2,1,0:T(8,128)(2,1)S(1)} collective-permute-done((bf16[4,256,256]{2,1,0:T(8,128)(2,1)S(1)}, bf16[4,256,256]{2,1,0:T(8,128)(2,1)S(1)}, u32[]{:S(2)}, u32[]{:S(2)}) %collective-permute-start.7) | collective-permute-done | bytes 524320 | tf_op jit(solution)/shard_map/ppermute | solution.py:592
  108.3 1.1 arrive.1
  109.4 5.8 %all-to-all-done.1.parts = bf16[16,16,1152]{2,1,0:T(8,128)(2,1)S(1)} async-done(((bf16[16,16,1152]{2,1,0:T(8,128)(2,1)}), bf16[16,16,1152]{2,1,0:T(8,128)(2,1)S(1)}, u32[]{:S(2)}, u32[]{:S(2)}) %all-to-all-start.1) | async-done | bytes 589856 | tf_op jit(solution)/shard_map/all_to_all | solution.py:588
  115.2 0.1 sum_share.1.refs_0_
  115.3 0.1 collective-permute-start.10
  115.4 2.1 %collective-permute-start.11 = (bf16[16,1152]{1,0:T(8,128)(2,1)S(1)}, bf16[16,1152]{1,0:T(8,128)(2,1)S(1)}, u32[]{:S(2)}, u32[]{:S(2)}) collective-permute-start(bf16[16,1152]{1,0:T(8,128)(2,1)S(1)} %sum_share.1.refs_0_), channel_id=1, source_target_pairs={{0,4},{2,6},{4,0},{6,2},{1,5},{3,7},{5,1},{7,3},{8,12},{10,14},{12... | collective-permute-start | bytes 110600 | tf_op jit(solution)/shard_map/ppermute | solution.py:617
  117.5 2.0 %collective-permute-start.12 = (bf16[16,1152]{1,0:T(8,128)(2,1)S(1)}, bf16[16,1152]{1,0:T(8,128)(2,1)S(1)}, u32[]{:S(2)}, u32[]{:S(2)}) collective-permute-start(bf16[16,1152]{1,0:T(8,128)(2,1)S(1)} %sum_share.1.refs_0_), channel_id=1, source_target_pairs={{0,6},{2,0},{4,2},{6,4},{1,7},{3,1},{5,3},{7,5},{8,14},{10,8},{12,... | collective-permute-start | bytes 110600 | tf_op jit(solution)/shard_map/ppermute | solution.py:617
  119.5 0.3 collective-permute-done.11.refs_2_
  119.8 0.8 collective-permute-done.12.refs_3_
  120.6 0.1 sum_chips.1
  120.7 14.2 %all_to_all.15 = bf16[16,16,1536]{2,1,0:T(8,128)(2,1)S(1)} all-to-all(bf16[16,16,1536]{2,1,0:T(8,128)(2,1)S(1)} %sum_chips.1), channel_id=1, replica_groups=mesh['x'=4,'z'=4,'y'=4,'core'=2] {'x','z'}, dimensions={0} | all-to-all | bytes 1572864 | tf_op jit(solution)/shard_map/all_to_all | solution.py:588
  134.9 4.6 %collective-permute-start.13 = (bf16[8,2,16,1536]{3,2,1,0:T(8,128)(2,1)S(1)}, bf16[8,2,16,1536]{3,2,1,0:T(8,128)(2,1)S(1)}, u32[]{:S(2)}, u32[]{:S(2)}) collective-permute-start(bf16[8,2,16,1536]{3,2,1,0:T(8,128)(2,1)S(1)} %bitcast.15), channel_id=1, source_target_pairs={{0,1},{1,0},{2,3},{3,2},{4,5},{5,4},{6,7},{7,6},{8,9},{9,8},{10,11... | collective-permute-start | bytes 2359304 | tf_op jit(solution)/shard_map/ppermute | solution.py:592
  139.5 1.2 place.2
  140.7 0.7 collective-permute-done.13.shares
  141.4 1.2 place.3
  (9 shorter events, 0.1 us)
Async XLA Ops:
  7.4 9.4 %copy-start = (bf16[1,256,4096]{2,1,0:T(8,128)(2,1)S(1)}, bf16[1,256,4096]{2,1,0:T(8,128)(2,1)}, u32[]{:S(2)}) copy-start(bf16[1,256,4096]{2,1,0:T(8,128)(2,1)} %param.10) | copy-start | bytes 6291460
  7.4 9.4 %copy-start.3 = (bf16[64,2048]{1,0:T(8,128)(2,1)S(1)}, bf16[64,2048]{1,0:T(8,128)(2,1)}, u32[]{:S(2)}) copy-start(bf16[64,2048]{1,0:T(8,128)(2,1)} %wq_up.3) | copy-start | bytes 786436
  7.5 57.8 %copy-start.5 = (s32[1,8]{1,0:T(1,128)S(1)}, s32[1,8]{1,0:T(1,128)}, u32[]{:S(2)}) copy-start(s32[1,8]{1,0:T(1,128)} %lengths.1) | copy-start | bytes 100
  7.5 57.8 %all-to-all-start = ((bf16[8,272,1024]{2,1,0:T(8,128)(2,1)}), bf16[8,272,1024]{2,1,0:T(8,128)(2,1)}, u32[]{:S(2)}, u32[]{:S(2)}) async-start(bf16[8,272,1024]{2,1,0:T(8,128)(2,1)} %get-tuple-element.33), calls=%async_computation | async-start | bytes 8912896 | tf_op jit(solution)/shard_map/all_to_all | solution.py:588
  13.6 3.3 %collective-permute-start = (bf16[256,2048]{1,0:T(8,128)(2,1)}, bf16[256,2048]{1,0:T(8,128)(2,1)S(1)}, u32[]{:S(2)}, u32[]{:S(2)}) collective-permute-start(bf16[256,2048]{1,0:T(8,128)(2,1)} %get-tuple-element.34), channel_id=1, source_target_pairs={{0,1},{1,0},{2,3},{3,2},{4,5},{5,4},{6,7},{7,6},{8,9},{9,8},{10,11... | collective-permute-start | bytes 3145736 | tf_op jit(solution)/shard_map/ppermute | solution.py:592
  16.9 1.0 copy-start.4
  18.0 1.3 copy-start.1
  80.6 15.0 %copy-start.2 = (bf16[512,2048]{1,0:T(8,128)(2,1)S(1)}, bf16[512,2048]{1,0:T(8,128)(2,1)}, u32[]{:S(2)}) copy-start(bf16[512,2048]{1,0:T(8,128)(2,1)} %copy-done.1) | copy-start | bytes 6291460
  80.6 6.5 %collective-permute-start.2 = (bf16[2,128,256]{2,1,0:T(8,128)(2,1)S(1)}, bf16[2,128,256]{2,1,0:T(8,128)(2,1)S(1)}, u32[]{:S(2)}, u32[]{:S(2)}) collective-permute-start(bf16[2,128,256]{2,1,0:T(8,128)(2,1)S(1)} %get-tuple-element.39), channel_id=1, source_target_pairs={{0,2},{2,4},{4,6},{6,0},{1,3},{3,5},{5,7},{7,1},{8,10},{10,12},{12... | collective-permute-start | bytes 393224 | tf_op jit(solution)/shard_map/ppermute | solution.py:617
  81.0 7.3 %collective-permute-start.3 = (bf16[2,128,256]{2,1,0:T(8,128)(2,1)S(1)}, bf16[2,128,256]{2,1,0:T(8,128)(2,1)S(1)}, u32[]{:S(2)}, u32[]{:S(2)}) collective-permute-start(bf16[2,128,256]{2,1,0:T(8,128)(2,1)S(1)} %get-tuple-element.40), channel_id=1, source_target_pairs={{0,4},{2,6},{4,0},{6,2},{1,5},{3,7},{5,1},{7,3},{8,12},{10,14},{12... | collective-permute-start | bytes 393224 | tf_op jit(solution)/shard_map/ppermute | solution.py:617
  82.7 6.7 %collective-permute-start.4 = (bf16[2,128,256]{2,1,0:T(8,128)(2,1)S(1)}, bf16[2,128,256]{2,1,0:T(8,128)(2,1)S(1)}, u32[]{:S(2)}, u32[]{:S(2)}) collective-permute-start(bf16[2,128,256]{2,1,0:T(8,128)(2,1)S(1)} %get-tuple-element.41), channel_id=1, source_target_pairs={{0,6},{2,0},{4,2},{6,4},{1,7},{3,1},{5,3},{7,5},{8,14},{10,8},{12,... | collective-permute-start | bytes 393224 | tf_op jit(solution)/shard_map/ppermute | solution.py:617
  83.6 10.9 %collective-permute-start.9 = (bf16[8,128,128]{2,1,0:T(8,128)(2,1)S(1)}, bf16[8,128,128]{2,1,0:T(8,128)(2,1)S(1)}, u32[]{:S(2)}, u32[]{:S(2)}) collective-permute-start(bf16[8,128,128]{2,1,0:T(8,128)(2,1)S(1)} %get-tuple-element.49.low), channel_id=1, source_target_pairs={{0,1},{1,0},{2,3},{3,2},{4,5},{5,4},{6,7},{7,6},{8,9},{9,8},{10,11... | collective-permute-start | bytes 786440 | tf_op jit(solution)/shard_map/ppermute | solution.py:592
  85.0 19.3 %collective-permute-start.1 = (bf16[2,256,256]{2,1,0:T(8,128)(2,1)S(1)}, bf16[2,256,256]{2,1,0:T(8,128)(2,1)S(1)}, u32[]{:S(2)}, u32[]{:S(2)}) collective-permute-start(bf16[2,256,256]{2,1,0:T(8,128)(2,1)S(1)} %get-tuple-element.37), channel_id=1, source_target_pairs={{0,2},{2,4},{4,6},{6,0},{1,3},{3,5},{5,7},{7,1},{8,10},{10,12},{12... | collective-permute-start | bytes 786440 | tf_op jit(solution)/shard_map/ppermute | solution.py:617
  89.5 14.8 %collective-permute-start.5 = (bf16[2,256,256]{2,1,0:T(8,128)(2,1)S(1)}, bf16[2,256,256]{2,1,0:T(8,128)(2,1)S(1)}, u32[]{:S(2)}, u32[]{:S(2)}) collective-permute-start(bf16[2,256,256]{2,1,0:T(8,128)(2,1)S(1)} %get-tuple-element.44), channel_id=1, source_target_pairs={{0,4},{2,6},{4,0},{6,2},{1,5},{3,7},{5,1},{7,3},{8,12},{10,14},{12... | collective-permute-start | bytes 786440 | tf_op jit(solution)/shard_map/ppermute | solution.py:617
  90.5 14.7 %collective-permute-start.6 = (bf16[2,256,256]{2,1,0:T(8,128)(2,1)S(1)}, bf16[2,256,256]{2,1,0:T(8,128)(2,1)S(1)}, u32[]{:S(2)}, u32[]{:S(2)}) collective-permute-start(bf16[2,256,256]{2,1,0:T(8,128)(2,1)S(1)} %get-tuple-element.45), channel_id=1, source_target_pairs={{0,6},{2,0},{4,2},{6,4},{1,7},{3,1},{5,3},{7,5},{8,14},{10,8},{12,... | collective-permute-start | bytes 786440 | tf_op jit(solution)/shard_map/ppermute | solution.py:617
  93.2 2.3 %collective-permute-start.8 = (bf16[2,128,256]{2,1,0:T(8,128)(2,1)S(1)}, bf16[2,128,256]{2,1,0:T(8,128)(2,1)S(1)}, u32[]{:S(2)}, u32[]{:S(2)}) collective-permute-start(bf16[2,128,256]{2,1,0:T(8,128)(2,1)S(1)} %get-tuple-element.47.refs_0_), channel_id=1, source_target_pairs={{0,1},{1,0},{2,3},{3,2},{4,5},{5,4},{6,7},{7,6},{8,9},{9,8},{10,11... | collective-permute-start | bytes 393224 | tf_op jit(solution)/shard_map/ppermute | solution.py:592
  97.1 18.1 %all-to-all-start.1 = ((bf16[16,16,1152]{2,1,0:T(8,128)(2,1)}), bf16[16,16,1152]{2,1,0:T(8,128)(2,1)S(1)}, u32[]{:S(2)}, u32[]{:S(2)}) async-start(bf16[16,16,1152]{2,1,0:T(8,128)(2,1)} %bitcast.9), calls=%async_computation.1 | async-start | bytes 1179648 | tf_op jit(solution)/shard_map/all_to_all | solution.py:588
  105.3 3.0 %collective-permute-start.7 = (bf16[4,256,256]{2,1,0:T(8,128)(2,1)S(1)}, bf16[4,256,256]{2,1,0:T(8,128)(2,1)S(1)}, u32[]{:S(2)}, u32[]{:S(2)}) collective-permute-start(bf16[4,256,256]{2,1,0:T(8,128)(2,1)S(1)} %pick.1), channel_id=1, source_target_pairs={{0,1},{1,0},{2,3},{3,2},{4,5},{5,4},{6,7},{7,6},{8,9},{9,8},{10,11... | collective-permute-start | bytes 1572872 | tf_op jit(solution)/shard_map/ppermute | solution.py:592
  115.3 4.2 %collective-permute-start.10 = (bf16[16,1152]{1,0:T(8,128)(2,1)S(1)}, bf16[16,1152]{1,0:T(8,128)(2,1)S(1)}, u32[]{:S(2)}, u32[]{:S(2)}) collective-permute-start(bf16[16,1152]{1,0:T(8,128)(2,1)S(1)} %sum_share.1.refs_0_), channel_id=1, source_target_pairs={{0,2},{2,4},{4,6},{6,0},{1,3},{3,5},{5,7},{7,1},{8,10},{10,12},{12... | collective-permute-start | bytes 110600 | tf_op jit(solution)/shard_map/ppermute | solution.py:617
  115.4 4.4 %collective-permute-start.11 = (bf16[16,1152]{1,0:T(8,128)(2,1)S(1)}, bf16[16,1152]{1,0:T(8,128)(2,1)S(1)}, u32[]{:S(2)}, u32[]{:S(2)}) collective-permute-start(bf16[16,1152]{1,0:T(8,128)(2,1)S(1)} %sum_share.1.refs_0_), channel_id=1, source_target_pairs={{0,4},{2,6},{4,0},{6,2},{1,5},{3,7},{5,1},{7,3},{8,12},{10,14},{12... | collective-permute-start | bytes 110600 | tf_op jit(solution)/shard_map/ppermute | solution.py:617
  117.5 3.0 %collective-permute-start.12 = (bf16[16,1152]{1,0:T(8,128)(2,1)S(1)}, bf16[16,1152]{1,0:T(8,128)(2,1)S(1)}, u32[]{:S(2)}, u32[]{:S(2)}) collective-permute-start(bf16[16,1152]{1,0:T(8,128)(2,1)S(1)} %sum_share.1.refs_0_), channel_id=1, source_target_pairs={{0,6},{2,0},{4,2},{6,4},{1,7},{3,1},{5,3},{7,5},{8,14},{10,8},{12,... | collective-permute-start | bytes 110600 | tf_op jit(solution)/shard_map/ppermute | solution.py:617
  134.9 6.5 %collective-permute-start.13 = (bf16[8,2,16,1536]{3,2,1,0:T(8,128)(2,1)S(1)}, bf16[8,2,16,1536]{3,2,1,0:T(8,128)(2,1)S(1)}, u32[]{:S(2)}, u32[]{:S(2)}) collective-permute-start(bf16[8,2,16,1536]{3,2,1,0:T(8,128)(2,1)S(1)} %bitcast.15), channel_id=1, source_target_pairs={{0,1},{1,0},{2,3},{3,2},{4,5},{5,4},{6,7},{7,6},{8,9},{9,8},{10,11... | collective-permute-start | bytes 2359304 | tf_op jit(solution)/shard_map/ppermute | solution.py:592

commit v14 on v13

--- a/solution.py
+++ b/solution.py
@@ -89,7 +89,7 @@
         pltpu.make_async_copy(wv_up, wv_up_v, row_sems.at[2]),
         pltpu.make_async_copy(fv, fv_v, row_sems.at[3]),
     ]
-    for copy in downs + hiddens + through + whole:
+    for copy in downs + hiddens + whole:
         copy.start()
 
     def leave(device, begin, size, number):
@@ -103,6 +103,9 @@
     total = jnp.zeros((rows, 2 * RANK), jnp.float32)
     for index in range(HIDDEN_PARTS):
         hiddens[index].wait()
+        if index == 0:
+            for copy in through:
+                copy.start()
         total += dot_nt(hidden_v[:, part(index)], down_v[:, part(index)])
     low[...] = total.astype(jnp.bfloat16)
     half = other.shape[1]

time: 143 us -> 143 us (level)
  transfers between devices with their start and end apart: 16 -> 16, of which waited for: 12 -> 11; matrix products, arithmetic and copies ran while one was open for 0% -> 0% of each run, Pallas kernels for 4% -> 4%
where the time goes in v14:
time: 143 us; the launch traced here: 142 us
  waiting for transfers between devices  62.5 us (44%)
  starting transfers between devices  34.8 us (24%)
  Pallas kernels  27.4 us (19%)
  blocking collectives  14.2 us (10%)
  local copies, waits for them, and re-layouts  2.29 us (2%)
    all_to_all x2, waiting for transfers between devices, swap(): return lax.all_to_all(x, axes, 0, 0, tiled=True)  52.6 us
    pallas_call x1, Pallas kernels, attention(): pl.pallas_call(attention_kernel, in_specs=[SMEM] * 2 + [VMEM] * 2, out_sp...  14.8 us
    all_to_all x1, blocking collectives, swap(): return lax.all_to_all(x, axes, 0, 0, tiled=True)  14.2 us
    all_to_all x2, starting transfers between devices, swap(): return lax.all_to_all(x, axes, 0, 0, tiled=True)  14 us
    ppermute x9, starting transfers between devices, to_chip(): return lax.ppermute(x, 'y', [(c, (c + step) % chips) for c in range(chips)])  11.7 us
    ppermute x5, starting transfers between devices, to_other_core(): return lax.ppermute(x, 'core', [(0, 1), (1, 0)])  9.13 us
    pallas_call x1, Pallas kernels, pack(): pl.pallas_call(pack_kernel, in_specs=[SMEM] + [ANY] * 9, out_specs=[ANY]...  6.15 us
    ppermute x5, waiting for transfers between devices, to_other_core(): return lax.ppermute(x, 'core', [(0, 1), (1, 0)])  5.49 us
  transfers between devices with their start and end apart: 16, of which 11 were waited for; matrix products, arithmetic and copies ran while one was open for 0% of the time, Pallas kernels for 4%

profile of v14, /device:TPU:1, one launch (start us, length us, event | category | flops | bytes accessed | tf_op | source)
XLA Modules:
  0.0 142.2 jit_solution(10271368845719490586)
XLA Ops:
  0.6 6.1 %pack.1 = (bf16[8,272,1024]{2,1,0:T(8,128)(2,1)}, bf16[256,2048]{1,0:T(8,128)(2,1)}) custom-call(s32[1]{0:T(128)} %bitcast.1.core.which, bf16[256,4096]{1,0:T(8,128)(2,1)} %bitcast.13, bf16[64,4096]{1,0:T(8,128)(2,1)} %bitcast.23, bf16[64,4096]{1,0:T(8,128)(2,1)} %bitcast.24, bf16[256,2048]{1,0:T(8,128)(2,1)} %bitcast.17, bf16[256,2048]{1,0:T(8,128)(2,1)} %bitcast.18, ...), custom_call_target="tpu_custom_call" | custom-call | tf_op jit(solution)/shard_map/pack/pallas_call | solution.py:150
  6.8 0.0 copy-start
  6.8 0.0 copy-start.3
  6.8 0.0 copy-start.5
  6.8 6.1 %all-to-all-start = ((bf16[8,272,1024]{2,1,0:T(8,128)(2,1)}), bf16[8,272,1024]{2,1,0:T(8,128)(2,1)}, u32[]{:S(2)}, u32[]{:S(2)}) async-start(bf16[8,272,1024]{2,1,0:T(8,128)(2,1)} %get-tuple-element.33), calls=%async_computation | async-start | bytes 8912896 | tf_op jit(solution)/shard_map/all_to_all | solution.py:591
  12.9 0.1 collective-permute-start
  13.1 3.2 %collective-permute-done.other = bf16[256,2048]{1,0:T(8,128)(2,1)S(1)} collective-permute-done((bf16[256,2048]{1,0:T(8,128)(2,1)}, bf16[256,2048]{1,0:T(8,128)(2,1)S(1)}, u32[]{:S(2)}, u32[]{:S(2)}) %collective-permute-start) | collective-permute-done | bytes 1048608 | tf_op jit(solution)/shard_map/ppermute | solution.py:595
  16.2 0.9 copy-done.4
  17.2 0.1 halves.1
  17.4 1.3 copy-done.1
  18.7 46.0 %all-to-all-done.packed = bf16[8,272,1024]{2,1,0:T(8,128)(2,1)} async-done(((bf16[8,272,1024]{2,1,0:T(8,128)(2,1)}), bf16[8,272,1024]{2,1,0:T(8,128)(2,1)}, u32[]{:S(2)}, u32[]{:S(2)}) %all-to-all-start) | async-done | bytes 4456480 | tf_op jit(solution)/shard_map/all_to_all | solution.py:591
  64.7 14.8 %attention.1 = (bf16[2,256,256]{2,1,0:T(8,128)(2,1)S(1)}, bf16[2,256,256]{2,1,0:T(8,128)(2,1)S(1)}, bf16[2,256,256]{2,1,0:T(8,128)(2,1)S(1)}, bf16[2,256,256]{2,...) custom-call(s32[1,8]{1,0:T(1,128)S(1)} %copy-done.5, ...), custom_call_target="tpu_custom_call" | custom-call | flops 8589934592 | bytes 16777216 | tf_op jit(solution)/shard_map/attention/pallas_call | solution.py:290
  79.5 0.3 collective-permute-start.2
  79.9 1.8 %collective-permute-start.3 = (bf16[2,128,256]{2,1,0:T(8,128)(2,1)S(1)}, bf16[2,128,256]{2,1,0:T(8,128)(2,1)S(1)}, u32[]{:S(2)}, u32[]{:S(2)}) collective-permute-start(bf16[2,128,256]{2,1,0:T(8,128)(2,1)S(1)} %get-tuple-element.40), channel_id=1, source_target_pairs={{0,4},{2,6},{4,0},{6,2},{1,5},{3,7},{5,1},{7,3},{8,12},{10,14},{12... | collective-permute-start | bytes 393224 | tf_op jit(solution)/shard_map/ppermute | solution.py:620
  81.7 0.7 collective-permute-start.4
  82.4 1.4 %collective-permute-start.9 = (bf16[8,128,128]{2,1,0:T(8,128)(2,1)S(1)}, bf16[8,128,128]{2,1,0:T(8,128)(2,1)S(1)}, u32[]{:S(2)}, u32[]{:S(2)}) collective-permute-start(bf16[8,128,128]{2,1,0:T(8,128)(2,1)S(1)} %get-tuple-element.49.low), channel_id=1, source_target_pairs={{0,1},{1,0},{2,3},{3,2},{4,5},{5,4},{6,7},{7,6},{8,9},{9,8},{10,11... | collective-permute-start | bytes 786440 | tf_op jit(solution)/shard_map/ppermute | solution.py:595
  83.8 1.1 collective-permute-start.1
  84.9 1.2 collective-permute-done.2.part_1
  86.1 1.1 collective-permute-done.3.part_2
  87.2 1.0 collective-permute-done.4.part_3
  88.1 0.1 sum_backs.1
  88.2 1.0 collective-permute-start.5
  89.2 2.7 %collective-permute-start.6 = (bf16[2,256,256]{2,1,0:T(8,128)(2,1)S(1)}, bf16[2,256,256]{2,1,0:T(8,128)(2,1)S(1)}, u32[]{:S(2)}, u32[]{:S(2)}) collective-permute-start(bf16[2,256,256]{2,1,0:T(8,128)(2,1)S(1)} %get-tuple-element.45), channel_id=1, source_target_pairs={{0,6},{2,0},{4,2},{6,4},{1,7},{3,1},{5,3},{7,5},{8,14},{10,8},{12,... | collective-permute-start | bytes 786440 | tf_op jit(solution)/shard_map/ppermute | solution.py:620
  91.8 1.5 %collective-permute-start.8 = (bf16[2,128,256]{2,1,0:T(8,128)(2,1)S(1)}, bf16[2,128,256]{2,1,0:T(8,128)(2,1)S(1)}, u32[]{:S(2)}, u32[]{:S(2)}) collective-permute-start(bf16[2,128,256]{2,1,0:T(8,128)(2,1)S(1)} %get-tuple-element.47.refs_0_), channel_id=1, source_target_pairs={{0,1},{1,0},{2,3},{3,2},{4,5},{5,4},{6,7},{7,6},{8,9},{9,8},{10,11... | collective-permute-start | bytes 393224 | tf_op jit(solution)/shard_map/ppermute | solution.py:595
  93.3 0.0 collective-permute-done.9.low_other
  93.3 0.9 up_gradient.1.refs_3_
  94.2 0.1 collective-permute-done.8.refs_1_
  94.3 1.6 %down_gradient.1 = bf16[8,2,16,1152]{3,2,1,0:T(8,128)(2,1)} custom-call(s32[1]{0:T(128)} %bitcast.1.core.which, bf16[2,128,256]{2,1,0:T(8,128)(2,1)S(1)} %get-tuple-element.47.refs_0_, bf16[2,128,256]{2,1,0:T(8,128)(2,1)S(1)} %collective-permute-done.8.refs_1_, bf16[512,2048]{1,0:T(8,128)(2,1)S(1)} %copy-done.2, bf16[128,256]{1,0:T(8,128)(2,1)S(1)} %up_gradient.1.refs_3_), custom_call_target="tpu_custom_call" | custom-call | tf_op jit(solution)/shard_map/down_gradient/pallas_call | solution.py:458
  95.9 7.9 %all-to-all-start.1 = ((bf16[16,16,1152]{2,1,0:T(8,128)(2,1)}), bf16[16,16,1152]{2,1,0:T(8,128)(2,1)S(1)}, u32[]{:S(2)}, u32[]{:S(2)}) async-start(bf16[16,16,1152]{2,1,0:T(8,128)(2,1)} %bitcast.9), calls=%async_computation.1 | async-start | bytes 1179648 | tf_op jit(solution)/shard_map/all_to_all | solution.py:591
  103.8 0.0 collective-permute-done.1.part_1
  103.8 0.0 collective-permute-done.5.part_2
  103.8 0.0 collective-permute-done.6.part_3
  103.8 1.5 %collective-permute-start.7 = (bf16[4,256,256]{2,1,0:T(8,128)(2,1)S(1)}, bf16[4,256,256]{2,1,0:T(8,128)(2,1)S(1)}, u32[]{:S(2)}, u32[]{:S(2)}) collective-permute-start(bf16[4,256,256]{2,1,0:T(8,128)(2,1)S(1)} %pick.1), channel_id=1, source_target_pairs={{0,1},{1,0},{2,3},{3,2},{4,5},{5,4},{6,7},{7,6},{8,9},{9,8},{10,11... | collective-permute-start | bytes 1572872 | tf_op jit(solution)/shard_map/ppermute | solution.py:595
  105.4 1.5 %collective-permute-done.7.other = bf16[4,256,256]{2,1,0:T(8,128)(2,1)S(1)} collective-permute-done((bf16[4,256,256]{2,1,0:T(8,128)(2,1)S(1)}, bf16[4,256,256]{2,1,0:T(8,128)(2,1)S(1)}, u32[]{:S(2)}, u32[]{:S(2)}) %collective-permute-start.7) | collective-permute-done | bytes 524320 | tf_op jit(solution)/shard_map/ppermute | solution.py:595
  106.9 1.1 arrive.1
  108.0 6.6 %all-to-all-done.1.parts = bf16[16,16,1152]{2,1,0:T(8,128)(2,1)S(1)} async-done(((bf16[16,16,1152]{2,1,0:T(8,128)(2,1)}), bf16[16,16,1152]{2,1,0:T(8,128)(2,1)S(1)}, u32[]{:S(2)}, u32[]{:S(2)}) %all-to-all-start.1) | async-done | bytes 589856 | tf_op jit(solution)/shard_map/all_to_all | solution.py:591
  114.6 0.1 sum_share.1.refs_0_
  114.7 0.1 collective-permute-start.10
  114.8 2.2 %collective-permute-start.11 = (bf16[16,1152]{1,0:T(8,128)(2,1)S(1)}, bf16[16,1152]{1,0:T(8,128)(2,1)S(1)}, u32[]{:S(2)}, u32[]{:S(2)}) collective-permute-start(bf16[16,1152]{1,0:T(8,128)(2,1)S(1)} %sum_share.1.refs_0_), channel_id=1, source_target_pairs={{0,4},{2,6},{4,0},{6,2},{1,5},{3,7},{5,1},{7,3},{8,12},{10,14},{12... | collective-permute-start | bytes 110600 | tf_op jit(solution)/shard_map/ppermute | solution.py:620
  116.9 2.0 %collective-permute-start.12 = (bf16[16,1152]{1,0:T(8,128)(2,1)S(1)}, bf16[16,1152]{1,0:T(8,128)(2,1)S(1)}, u32[]{:S(2)}, u32[]{:S(2)}) collective-permute-start(bf16[16,1152]{1,0:T(8,128)(2,1)S(1)} %sum_share.1.refs_0_), channel_id=1, source_target_pairs={{0,6},{2,0},{4,2},{6,4},{1,7},{3,1},{5,3},{7,5},{8,14},{10,8},{12,... | collective-permute-start | bytes 110600 | tf_op jit(solution)/shard_map/ppermute | solution.py:620
  118.9 0.3 collective-permute-done.11.refs_2_
  119.2 0.8 collective-permute-done.12.refs_3_
  120.0 0.1 sum_chips.1
  120.1 14.2 %all_to_all.15 = bf16[16,16,1536]{2,1,0:T(8,128)(2,1)S(1)} all-to-all(bf16[16,16,1536]{2,1,0:T(8,128)(2,1)S(1)} %sum_chips.1), channel_id=1, replica_groups=mesh['x'=4,'z'=4,'y'=4,'core'=2] {'x','z'}, dimensions={0} | all-to-all | bytes 1572864 | tf_op jit(solution)/shard_map/all_to_all | solution.py:591
  134.3 4.6 %collective-permute-start.13 = (bf16[8,2,16,1536]{3,2,1,0:T(8,128)(2,1)S(1)}, bf16[8,2,16,1536]{3,2,1,0:T(8,128)(2,1)S(1)}, u32[]{:S(2)}, u32[]{:S(2)}) collective-permute-start(bf16[8,2,16,1536]{3,2,1,0:T(8,128)(2,1)S(1)} %bitcast.15), channel_id=1, source_target_pairs={{0,1},{1,0},{2,3},{3,2},{4,5},{5,4},{6,7},{7,6},{8,9},{9,8},{10,11... | collective-permute-start | bytes 2359304 | tf_op jit(solution)/shard_map/ppermute | solution.py:595
  138.9 1.2 place.2
  140.2 0.7 collective-permute-done.13.shares
  140.8 1.2 place.3
  (9 shorter events, 0.1 us)
Async XLA Ops:
  6.8 9.4 %copy-start = (bf16[1,256,4096]{2,1,0:T(8,128)(2,1)S(1)}, bf16[1,256,4096]{2,1,0:T(8,128)(2,1)}, u32[]{:S(2)}) copy-start(bf16[1,256,4096]{2,1,0:T(8,128)(2,1)} %param.10) | copy-start | bytes 6291460
  6.8 9.4 %copy-start.3 = (bf16[64,2048]{1,0:T(8,128)(2,1)S(1)}, bf16[64,2048]{1,0:T(8,128)(2,1)}, u32[]{:S(2)}) copy-start(bf16[64,2048]{1,0:T(8,128)(2,1)} %wq_up.3) | copy-start | bytes 786436
  6.8 57.8 %copy-start.5 = (s32[1,8]{1,0:T(1,128)S(1)}, s32[1,8]{1,0:T(1,128)}, u32[]{:S(2)}) copy-start(s32[1,8]{1,0:T(1,128)} %lengths.1) | copy-start | bytes 100
  6.8 57.8 %all-to-all-start = ((bf16[8,272,1024]{2,1,0:T(8,128)(2,1)}), bf16[8,272,1024]{2,1,0:T(8,128)(2,1)}, u32[]{:S(2)}, u32[]{:S(2)}) async-start(bf16[8,272,1024]{2,1,0:T(8,128)(2,1)} %get-tuple-element.33), calls=%async_computation | async-start | bytes 8912896 | tf_op jit(solution)/shard_map/all_to_all | solution.py:591
  12.9 3.3 %collective-permute-start = (bf16[256,2048]{1,0:T(8,128)(2,1)}, bf16[256,2048]{1,0:T(8,128)(2,1)S(1)}, u32[]{:S(2)}, u32[]{:S(2)}) collective-permute-start(bf16[256,2048]{1,0:T(8,128)(2,1)} %get-tuple-element.34), channel_id=1, source_target_pairs={{0,1},{1,0},{2,3},{3,2},{4,5},{5,4},{6,7},{7,6},{8,9},{9,8},{10,11... | collective-permute-start | bytes 3145736 | tf_op jit(solution)/shard_map/ppermute | solution.py:595
  16.2 1.0 copy-start.4
  17.3 1.3 copy-start.1
  79.5 14.8 %copy-start.2 = (bf16[512,2048]{1,0:T(8,128)(2,1)S(1)}, bf16[512,2048]{1,0:T(8,128)(2,1)}, u32[]{:S(2)}) copy-start(bf16[512,2048]{1,0:T(8,128)(2,1)} %copy-done.1) | copy-start | bytes 6291460
  79.5 6.5 %collective-permute-start.2 = (bf16[2,128,256]{2,1,0:T(8,128)(2,1)S(1)}, bf16[2,128,256]{2,1,0:T(8,128)(2,1)S(1)}, u32[]{:S(2)}, u32[]{:S(2)}) collective-permute-start(bf16[2,128,256]{2,1,0:T(8,128)(2,1)S(1)} %get-tuple-element.39), channel_id=1, source_target_pairs={{0,2},{2,4},{4,6},{6,0},{1,3},{3,5},{5,7},{7,1},{8,10},{10,12},{12... | collective-permute-start | bytes 393224 | tf_op jit(solution)/shard_map/ppermute | solution.py:620
  79.9 7.3 %collective-permute-start.3 = (bf16[2,128,256]{2,1,0:T(8,128)(2,1)S(1)}, bf16[2,128,256]{2,1,0:T(8,128)(2,1)S(1)}, u32[]{:S(2)}, u32[]{:S(2)}) collective-permute-start(bf16[2,128,256]{2,1,0:T(8,128)(2,1)S(1)} %get-tuple-element.40), channel_id=1, source_target_pairs={{0,4},{2,6},{4,0},{6,2},{1,5},{3,7},{5,1},{7,3},{8,12},{10,14},{12... | collective-permute-start | bytes 393224 | tf_op jit(solution)/shard_map/ppermute | solution.py:620
  81.7 6.5 %collective-permute-start.4 = (bf16[2,128,256]{2,1,0:T(8,128)(2,1)S(1)}, bf16[2,128,256]{2,1,0:T(8,128)(2,1)S(1)}, u32[]{:S(2)}, u32[]{:S(2)}) collective-permute-start(bf16[2,128,256]{2,1,0:T(8,128)(2,1)S(1)} %get-tuple-element.41), channel_id=1, source_target_pairs={{0,6},{2,0},{4,2},{6,4},{1,7},{3,1},{5,3},{7,5},{8,14},{10,8},{12,... | collective-permute-start | bytes 393224 | tf_op jit(solution)/shard_map/ppermute | solution.py:620
  82.4 10.9 %collective-permute-start.9 = (bf16[8,128,128]{2,1,0:T(8,128)(2,1)S(1)}, bf16[8,128,128]{2,1,0:T(8,128)(2,1)S(1)}, u32[]{:S(2)}, u32[]{:S(2)}) collective-permute-start(bf16[8,128,128]{2,1,0:T(8,128)(2,1)S(1)} %get-tuple-element.49.low), channel_id=1, source_target_pairs={{0,1},{1,0},{2,3},{3,2},{4,5},{5,4},{6,7},{7,6},{8,9},{9,8},{10,11... | collective-permute-start | bytes 786440 | tf_op jit(solution)/shard_map/ppermute | solution.py:595
  83.8 19.9 %collective-permute-start.1 = (bf16[2,256,256]{2,1,0:T(8,128)(2,1)S(1)}, bf16[2,256,256]{2,1,0:T(8,128)(2,1)S(1)}, u32[]{:S(2)}, u32[]{:S(2)}) collective-permute-start(bf16[2,256,256]{2,1,0:T(8,128)(2,1)S(1)} %get-tuple-element.37), channel_id=1, source_target_pairs={{0,2},{2,4},{4,6},{6,0},{1,3},{3,5},{5,7},{7,1},{8,10},{10,12},{12... | collective-permute-start | bytes 786440 | tf_op jit(solution)/shard_map/ppermute | solution.py:620
  88.2 15.6 %collective-permute-start.5 = (bf16[2,256,256]{2,1,0:T(8,128)(2,1)S(1)}, bf16[2,256,256]{2,1,0:T(8,128)(2,1)S(1)}, u32[]{:S(2)}, u32[]{:S(2)}) collective-permute-start(bf16[2,256,256]{2,1,0:T(8,128)(2,1)S(1)} %get-tuple-element.44), channel_id=1, source_target_pairs={{0,4},{2,6},{4,0},{6,2},{1,5},{3,7},{5,1},{7,3},{8,12},{10,14},{12... | collective-permute-start | bytes 786440 | tf_op jit(solution)/shard_map/ppermute | solution.py:620
  89.2 14.6 %collective-permute-start.6 = (bf16[2,256,256]{2,1,0:T(8,128)(2,1)S(1)}, bf16[2,256,256]{2,1,0:T(8,128)(2,1)S(1)}, u32[]{:S(2)}, u32[]{:S(2)}) collective-permute-start(bf16[2,256,256]{2,1,0:T(8,128)(2,1)S(1)} %get-tuple-element.45), channel_id=1, source_target_pairs={{0,6},{2,0},{4,2},{6,4},{1,7},{3,1},{5,3},{7,5},{8,14},{10,8},{12,... | collective-permute-start | bytes 786440 | tf_op jit(solution)/shard_map/ppermute | solution.py:620
  91.8 2.5 %collective-permute-start.8 = (bf16[2,128,256]{2,1,0:T(8,128)(2,1)S(1)}, bf16[2,128,256]{2,1,0:T(8,128)(2,1)S(1)}, u32[]{:S(2)}, u32[]{:S(2)}) collective-permute-start(bf16[2,128,256]{2,1,0:T(8,128)(2,1)S(1)} %get-tuple-element.47.refs_0_), channel_id=1, source_target_pairs={{0,1},{1,0},{2,3},{3,2},{4,5},{5,4},{6,7},{7,6},{8,9},{9,8},{10,11... | collective-permute-start | bytes 393224 | tf_op jit(solution)/shard_map/ppermute | solution.py:595
  95.9 18.8 %all-to-all-start.1 = ((bf16[16,16,1152]{2,1,0:T(8,128)(2,1)}), bf16[16,16,1152]{2,1,0:T(8,128)(2,1)S(1)}, u32[]{:S(2)}, u32[]{:S(2)}) async-start(bf16[16,16,1152]{2,1,0:T(8,128)(2,1)} %bitcast.9), calls=%async_computation.1 | async-start | bytes 1179648 | tf_op jit(solution)/shard_map/all_to_all | solution.py:591
  103.8 3.1 %collective-permute-start.7 = (bf16[4,256,256]{2,1,0:T(8,128)(2,1)S(1)}, bf16[4,256,256]{2,1,0:T(8,128)(2,1)S(1)}, u32[]{:S(2)}, u32[]{:S(2)}) collective-permute-start(bf16[4,256,256]{2,1,0:T(8,128)(2,1)S(1)} %pick.1), channel_id=1, source_target_pairs={{0,1},{1,0},{2,3},{3,2},{4,5},{5,4},{6,7},{7,6},{8,9},{9,8},{10,11... | collective-permute-start | bytes 1572872 | tf_op jit(solution)/shard_map/ppermute | solution.py:595
  114.7 4.2 %collective-permute-start.10 = (bf16[16,1152]{1,0:T(8,128)(2,1)S(1)}, bf16[16,1152]{1,0:T(8,128)(2,1)S(1)}, u32[]{:S(2)}, u32[]{:S(2)}) collective-permute-start(bf16[16,1152]{1,0:T(8,128)(2,1)S(1)} %sum_share.1.refs_0_), channel_id=1, source_target_pairs={{0,2},{2,4},{4,6},{6,0},{1,3},{3,5},{5,7},{7,1},{8,10},{10,12},{12... | collective-permute-start | bytes 110600 | tf_op jit(solution)/shard_map/ppermute | solution.py:620
  114.8 4.4 %collective-permute-start.11 = (bf16[16,1152]{1,0:T(8,128)(2,1)S(1)}, bf16[16,1152]{1,0:T(8,128)(2,1)S(1)}, u32[]{:S(2)}, u32[]{:S(2)}) collective-permute-start(bf16[16,1152]{1,0:T(8,128)(2,1)S(1)} %sum_share.1.refs_0_), channel_id=1, source_target_pairs={{0,4},{2,6},{4,0},{6,2},{1,5},{3,7},{5,1},{7,3},{8,12},{10,14},{12... | collective-permute-start | bytes 110600 | tf_op jit(solution)/shard_map/ppermute | solution.py:620
  116.9 3.0 %collective-permute-start.12 = (bf16[16,1152]{1,0:T(8,128)(2,1)S(1)}, bf16[16,1152]{1,0:T(8,128)(2,1)S(1)}, u32[]{:S(2)}, u32[]{:S(2)}) collective-permute-start(bf16[16,1152]{1,0:T(8,128)(2,1)S(1)} %sum_share.1.refs_0_), channel_id=1, source_target_pairs={{0,6},{2,0},{4,2},{6,4},{1,7},{3,1},{5,3},{7,5},{8,14},{10,8},{12,... | collective-permute-start | bytes 110600 | tf_op jit(solution)/shard_map/ppermute | solution.py:620
  134.3 6.5 %collective-permute-start.13 = (bf16[8,2,16,1536]{3,2,1,0:T(8,128)(2,1)S(1)}, bf16[8,2,16,1536]{3,2,1,0:T(8,128)(2,1)S(1)}, u32[]{:S(2)}, u32[]{:S(2)}) collective-permute-start(bf16[8,2,16,1536]{3,2,1,0:T(8,128)(2,1)S(1)} %bitcast.15), channel_id=1, source_target_pairs={{0,1},{1,0},{2,3},{3,2},{4,5},{5,4},{6,7},{7,6},{8,9},{9,8},{10,11... | collective-permute-start | bytes 2359304 | tf_op jit(solution)/shard_map/ppermute | solution.py:595

commit v15 on v14

--- a/solution.py
+++ b/solution.py
@@ -506,7 +506,7 @@
     total = total.astype(out.dtype)
     for device in range(out.shape[0]):
         out[device, :, :DOWN_COLS] = total
-    for step, part in enumerate(parts):
+    for step, part in zip((0, 2, 1, 3), parts):
         origin = lax.rem(chip + len(parts) - step, len(parts))
         begin = pl.multiple_of(DOWN_COLS + origin * UP_COLS, UP_COLS)
         for device in range(out.shape[0]):
@@ -646,7 +646,7 @@
     parts, backs = outs[:chips], outs[chips:]
 
     backs = [backs[0]] + [to_chip(backs[step], step) for step in range(1, chips)]
-    back, *held = sum_backs(backs, parts[-2:])
+    back, *held = sum_backs([backs[0], backs[2], backs[1], backs[3]], parts[-2:])
     parts = parts[:-2] + held
     back_other = to_other_core(back)
     parts = [parts[0]] + [to_chip(parts[step], step) for step in range(1, chips)]
@@ -658,7 +658,7 @@
 
     shares = swap(down.reshape((-1,) + down.shape[2:]), DP)
     share = sum_share(shares, after=[attended_done])
-    share = [share] + [to_chip(share, step) for step in range(1, chips)]
+    share = [share] + [to_chip(share, step) for step in (2, 1, 3)]
     shares = swap(sum_chips(chip, share, shares.shape[0]), DP)
     shares = shares.reshape(down.shape[:2] + shares.shape[1:])
     shares_other = to_other_core(shares)

time: 143 us -> 143 us (level)
  starting transfers between devices: 34.8 us -> 31.8 us
  waiting for transfers between devices: 62.5 us -> 65.4 us
    ppermute x9, starting transfers between devices: 11.7 us -> 9.52 us  [to_chip(): return lax.ppermute(x, 'y', [(c, (c + step) % chips) for c in range(chips)])]
    ppermute x9, waiting for transfers between devices: 4.34 us -> 6.43 us  [to_chip(): return lax.ppermute(x, 'y', [(c, (c + step) % chips) for c in range(chips)])]
  transfers between devices with their start and end apart: 16 -> 16, of which waited for: 11 -> 10; matrix products, arithmetic and copies ran while one was open for 0% -> 0% of each run, Pallas kernels for 4% -> 4%
where the time goes in v15:
time: 143 us; the launch traced here: 142 us
  waiting for transfers between devices  65.4 us (46%)
  starting transfers between devices  31.8 us (22%)
  Pallas kernels  27.5 us (19%)
  blocking collectives  14.2 us (10%)
  local copies, waits for them, and re-layouts  2.29 us (2%)
    all_to_all x2, waiting for transfers between devices, swap(): return lax.all_to_all(x, axes, 0, 0, tiled=True)  53.4 us
    pallas_call x1, Pallas kernels, attention(): pl.pallas_call(attention_kernel, in_specs=[SMEM] * 2 + [VMEM] * 2, out_sp...  14.9 us
    all_to_all x1, blocking collectives, swap(): return lax.all_to_all(x, axes, 0, 0, tiled=True)  14.2 us
    all_to_all x2, starting transfers between devices, swap(): return lax.all_to_all(x, axes, 0, 0, tiled=True)  13.7 us
    ppermute x9, starting transfers between devices, to_chip(): return lax.ppermute(x, 'y', [(c, (c + step) % chips) for c in range(chips)])  9.52 us
    ppermute x5, starting transfers between devices, to_other_core(): return lax.ppermute(x, 'core', [(0, 1), (1, 0)])  8.58 us
    ppermute x9, waiting for transfers between devices, to_chip(): return lax.ppermute(x, 'y', [(c, (c + step) % chips) for c in range(chips)])  6.43 us
    pallas_call x1, Pallas kernels, pack(): pl.pallas_call(pack_kernel, in_specs=[SMEM] + [ANY] * 9, out_specs=[ANY]...  6.15 us
  transfers between devices with their start and end apart: 16, of which 10 were waited for; matrix products, arithmetic and copies ran while one was open for 0% of the time, Pallas kernels for 4%

profile of v15, /device:TPU:1, one launch (start us, length us, event | category | flops | bytes accessed | tf_op | source)
XLA Modules:
  0.0 142.1 jit_solution(12587370784532583250)
XLA Ops:
  0.6 6.1 %pack.1 = (bf16[8,272,1024]{2,1,0:T(8,128)(2,1)}, bf16[256,2048]{1,0:T(8,128)(2,1)}) custom-call(s32[1]{0:T(128)} %bitcast.1.core.which, bf16[256,4096]{1,0:T(8,128)(2,1)} %bitcast.13, bf16[64,4096]{1,0:T(8,128)(2,1)} %bitcast.23, bf16[64,4096]{1,0:T(8,128)(2,1)} %bitcast.24, bf16[256,2048]{1,0:T(8,128)(2,1)} %bitcast.17, bf16[256,2048]{1,0:T(8,128)(2,1)} %bitcast.18, ...), custom_call_target="tpu_custom_call" | custom-call | tf_op jit(solution)/shard_map/pack/pallas_call | solution.py:150
  6.8 0.0 copy-start
  6.8 0.0 copy-start.3
  6.8 0.0 copy-start.5
  6.8 6.1 %all-to-all-start = ((bf16[8,272,1024]{2,1,0:T(8,128)(2,1)}), bf16[8,272,1024]{2,1,0:T(8,128)(2,1)}, u32[]{:S(2)}, u32[]{:S(2)}) async-start(bf16[8,272,1024]{2,1,0:T(8,128)(2,1)} %get-tuple-element.33), calls=%async_computation | async-start | bytes 8912896 | tf_op jit(solution)/shard_map/all_to_all | solution.py:591
  12.9 0.1 collective-permute-start
  13.1 3.2 %collective-permute-done.other = bf16[256,2048]{1,0:T(8,128)(2,1)S(1)} collective-permute-done((bf16[256,2048]{1,0:T(8,128)(2,1)}, bf16[256,2048]{1,0:T(8,128)(2,1)S(1)}, u32[]{:S(2)}, u32[]{:S(2)}) %collective-permute-start) | collective-permute-done | bytes 1048608 | tf_op jit(solution)/shard_map/ppermute | solution.py:595
  16.2 0.9 copy-done.4
  17.2 0.1 halves.1
  17.4 1.3 copy-done.1
  18.7 46.0 %all-to-all-done.packed = bf16[8,272,1024]{2,1,0:T(8,128)(2,1)} async-done(((bf16[8,272,1024]{2,1,0:T(8,128)(2,1)}), bf16[8,272,1024]{2,1,0:T(8,128)(2,1)}, u32[]{:S(2)}, u32[]{:S(2)}) %all-to-all-start) | async-done | bytes 4456480 | tf_op jit(solution)/shard_map/all_to_all | solution.py:591
  64.7 14.9 %attention.1 = (bf16[2,256,256]{2,1,0:T(8,128)(2,1)S(1)}, bf16[2,256,256]{2,1,0:T(8,128)(2,1)S(1)}, bf16[2,256,256]{2,1,0:T(8,128)(2,1)S(1)}, bf16[2,256,256]{2,...) custom-call(s32[1,8]{1,0:T(1,128)S(1)} %copy-done.5, ...), custom_call_target="tpu_custom_call" | custom-call | flops 8589934592 | bytes 16777216 | tf_op jit(solution)/shard_map/attention/pallas_call | solution.py:290
  79.5 0.5 collective-permute-start.2
  80.0 1.1 collective-permute-start.3
  81.1 1.6 %collective-permute-start.4 = (bf16[2,128,256]{2,1,0:T(8,128)(2,1)S(1)}, bf16[2,128,256]{2,1,0:T(8,128)(2,1)S(1)}, u32[]{:S(2)}, u32[]{:S(2)}) collective-permute-start(bf16[2,128,256]{2,1,0:T(8,128)(2,1)S(1)} %get-tuple-element.41), channel_id=1, source_target_pairs={{0,6},{2,0},{4,2},{6,4},{1,7},{3,1},{5,3},{7,5},{8,14},{10,8},{12,... | collective-permute-start | bytes 393224 | tf_op jit(solution)/shard_map/ppermute | solution.py:620
  82.7 1.4 %collective-permute-start.9 = (bf16[8,128,128]{2,1,0:T(8,128)(2,1)S(1)}, bf16[8,128,128]{2,1,0:T(8,128)(2,1)S(1)}, u32[]{:S(2)}, u32[]{:S(2)}) collective-permute-start(bf16[8,128,128]{2,1,0:T(8,128)(2,1)S(1)} %get-tuple-element.49.low), channel_id=1, source_target_pairs={{0,1},{1,0},{2,3},{3,2},{4,5},{5,4},{6,7},{7,6},{8,9},{9,8},{10,11... | collective-permute-start | bytes 786440 | tf_op jit(solution)/shard_map/ppermute | solution.py:595
  84.1 0.2 collective-permute-start.1
  84.3 0.8 collective-permute-done.2.part_1
  85.0 4.3 %collective-permute-done.3.part_2 = bf16[2,128,256]{2,1,0:T(8,128)(2,1)S(1)} collective-permute-done((bf16[2,128,256]{2,1,0:T(8,128)(2,1)S(1)}, bf16[2,128,256]{2,1,0:T(8,128)(2,1)S(1)}, u32[]{:S(2)}, u32[]{:S(2)}) %collective-permute-start.3) | collective-permute-done | bytes 131104 | tf_op jit(solution)/shard_map/ppermute | solution.py:620
  89.4 0.0 collective-permute-done.4.part_3
  89.4 0.1 sum_backs.1
  89.4 0.1 collective-permute-start.5
  89.5 2.0 %collective-permute-start.6 = (bf16[2,256,256]{2,1,0:T(8,128)(2,1)S(1)}, bf16[2,256,256]{2,1,0:T(8,128)(2,1)S(1)}, u32[]{:S(2)}, u32[]{:S(2)}) collective-permute-start(bf16[2,256,256]{2,1,0:T(8,128)(2,1)S(1)} %get-tuple-element.45), channel_id=1, source_target_pairs={{0,6},{2,0},{4,2},{6,4},{1,7},{3,1},{5,3},{7,5},{8,14},{10,8},{12,... | collective-permute-start | bytes 786440 | tf_op jit(solution)/shard_map/ppermute | solution.py:620
  91.6 1.7 %collective-permute-start.8 = (bf16[2,128,256]{2,1,0:T(8,128)(2,1)S(1)}, bf16[2,128,256]{2,1,0:T(8,128)(2,1)S(1)}, u32[]{:S(2)}, u32[]{:S(2)}) collective-permute-start(bf16[2,128,256]{2,1,0:T(8,128)(2,1)S(1)} %get-tuple-element.47.refs_0_), channel_id=1, source_target_pairs={{0,1},{1,0},{2,3},{3,2},{4,5},{5,4},{6,7},{7,6},{8,9},{9,8},{10,11... | collective-permute-start | bytes 393224 | tf_op jit(solution)/shard_map/ppermute | solution.py:595
  93.2 0.0 collective-permute-done.9.low_other
  93.2 0.9 up_gradient.1.refs_3_
  94.1 0.1 collective-permute-done.8.refs_1_
  94.2 1.6 %down_gradient.1 = bf16[8,2,16,1152]{3,2,1,0:T(8,128)(2,1)} custom-call(s32[1]{0:T(128)} %bitcast.1.core.which, bf16[2,128,256]{2,1,0:T(8,128)(2,1)S(1)} %get-tuple-element.47.refs_0_, bf16[2,128,256]{2,1,0:T(8,128)(2,1)S(1)} %collective-permute-done.8.refs_1_, bf16[512,2048]{1,0:T(8,128)(2,1)S(1)} %copy-done.2, bf16[128,256]{1,0:T(8,128)(2,1)S(1)} %up_gradient.1.refs_3_), custom_call_target="tpu_custom_call" | custom-call | tf_op jit(solution)/shard_map/down_gradient/pallas_call | solution.py:458
  95.8 7.6 %all-to-all-start.1 = ((bf16[16,16,1152]{2,1,0:T(8,128)(2,1)}), bf16[16,16,1152]{2,1,0:T(8,128)(2,1)S(1)}, u32[]{:S(2)}, u32[]{:S(2)}) async-start(bf16[16,16,1152]{2,1,0:T(8,128)(2,1)} %bitcast.9), calls=%async_computation.1 | async-start | bytes 1179648 | tf_op jit(solution)/shard_map/all_to_all | solution.py:591
  103.4 0.0 collective-permute-done.5.part_2
  103.4 0.0 collective-permute-done.6.part_3
  103.5 0.7 collective-permute-start.7
  104.2 1.5 %collective-permute-done.7.other = bf16[4,256,256]{2,1,0:T(8,128)(2,1)S(1)} collective-permute-done((bf16[4,256,256]{2,1,0:T(8,128)(2,1)S(1)}, bf16[4,256,256]{2,1,0:T(8,128)(2,1)S(1)}, u32[]{:S(2)}, u32[]{:S(2)}) %collective-permute-start.7) | collective-permute-done | bytes 524320 | tf_op jit(solution)/shard_map/ppermute | solution.py:595
  105.8 1.1 arrive.1
  106.9 7.4 %all-to-all-done.1.parts = bf16[16,16,1152]{2,1,0:T(8,128)(2,1)S(1)} async-done(((bf16[16,16,1152]{2,1,0:T(8,128)(2,1)}), bf16[16,16,1152]{2,1,0:T(8,128)(2,1)S(1)}, u32[]{:S(2)}, u32[]{:S(2)}) %all-to-all-start.1) | async-done | bytes 589856 | tf_op jit(solution)/shard_map/all_to_all | solution.py:591
  114.3 0.1 sum_share.1.refs_0_
  114.4 1.4 %collective-permute-start.10 = (bf16[16,1152]{1,0:T(8,128)(2,1)S(1)}, bf16[16,1152]{1,0:T(8,128)(2,1)S(1)}, u32[]{:S(2)}, u32[]{:S(2)}) collective-permute-start(bf16[16,1152]{1,0:T(8,128)(2,1)S(1)} %sum_share.1.refs_0_), channel_id=1, source_target_pairs={{0,4},{2,6},{4,0},{6,2},{1,5},{3,7},{5,1},{7,3},{8,12},{10,14},{12... | collective-permute-start | bytes 110600 | tf_op jit(solution)/shard_map/ppermute | solution.py:620
  115.8 0.0 collective-permute-start.11
  115.8 2.7 %collective-permute-start.12 = (bf16[16,1152]{1,0:T(8,128)(2,1)S(1)}, bf16[16,1152]{1,0:T(8,128)(2,1)S(1)}, u32[]{:S(2)}, u32[]{:S(2)}) collective-permute-start(bf16[16,1152]{1,0:T(8,128)(2,1)S(1)} %sum_share.1.refs_0_), channel_id=1, source_target_pairs={{0,6},{2,0},{4,2},{6,4},{1,7},{3,1},{5,3},{7,5},{8,14},{10,8},{12,... | collective-permute-start | bytes 110600 | tf_op jit(solution)/shard_map/ppermute | solution.py:620
  118.5 0.3 collective-permute-done.10.refs_1_
  118.8 1.1 collective-permute-done.11.refs_2_
  119.8 0.0 collective-permute-done.12.refs_3_
  119.8 0.1 sum_chips.1
  119.9 14.2 %all_to_all.15 = bf16[16,16,1536]{2,1,0:T(8,128)(2,1)S(1)} all-to-all(bf16[16,16,1536]{2,1,0:T(8,128)(2,1)S(1)} %sum_chips.1), channel_id=1, replica_groups=mesh['x'=4,'z'=4,'y'=4,'core'=2] {'x','z'}, dimensions={0} | all-to-all | bytes 1572864 | tf_op jit(solution)/shard_map/all_to_all | solution.py:591
  134.1 4.6 %collective-permute-start.13 = (bf16[8,2,16,1536]{3,2,1,0:T(8,128)(2,1)S(1)}, bf16[8,2,16,1536]{3,2,1,0:T(8,128)(2,1)S(1)}, u32[]{:S(2)}, u32[]{:S(2)}) collective-permute-start(bf16[8,2,16,1536]{3,2,1,0:T(8,128)(2,1)S(1)} %bitcast.15), channel_id=1, source_target_pairs={{0,1},{1,0},{2,3},{3,2},{4,5},{5,4},{6,7},{7,6},{8,9},{9,8},{10,11... | collective-permute-start | bytes 2359304 | tf_op jit(solution)/shard_map/ppermute | solution.py:595
  138.8 1.2 place.2
  140.0 0.7 collective-permute-done.13.shares
  140.7 1.2 place.3
  (9 shorter events, 0.1 us)
Async XLA Ops:
  6.8 9.4 %copy-start = (bf16[1,256,4096]{2,1,0:T(8,128)(2,1)S(1)}, bf16[1,256,4096]{2,1,0:T(8,128)(2,1)}, u32[]{:S(2)}) copy-start(bf16[1,256,4096]{2,1,0:T(8,128)(2,1)} %param.10) | copy-start | bytes 6291460
  6.8 9.4 %copy-start.3 = (bf16[64,2048]{1,0:T(8,128)(2,1)S(1)}, bf16[64,2048]{1,0:T(8,128)(2,1)}, u32[]{:S(2)}) copy-start(bf16[64,2048]{1,0:T(8,128)(2,1)} %wq_up.3) | copy-start | bytes 786436
  6.8 57.8 %copy-start.5 = (s32[1,8]{1,0:T(1,128)S(1)}, s32[1,8]{1,0:T(1,128)}, u32[]{:S(2)}) copy-start(s32[1,8]{1,0:T(1,128)} %lengths.1) | copy-start | bytes 100
  6.8 57.8 %all-to-all-start = ((bf16[8,272,1024]{2,1,0:T(8,128)(2,1)}), bf16[8,272,1024]{2,1,0:T(8,128)(2,1)}, u32[]{:S(2)}, u32[]{:S(2)}) async-start(bf16[8,272,1024]{2,1,0:T(8,128)(2,1)} %get-tuple-element.33), calls=%async_computation | async-start | bytes 8912896 | tf_op jit(solution)/shard_map/all_to_all | solution.py:591
  12.9 3.3 %collective-permute-start = (bf16[256,2048]{1,0:T(8,128)(2,1)}, bf16[256,2048]{1,0:T(8,128)(2,1)S(1)}, u32[]{:S(2)}, u32[]{:S(2)}) collective-permute-start(bf16[256,2048]{1,0:T(8,128)(2,1)} %get-tuple-element.34), channel_id=1, source_target_pairs={{0,1},{1,0},{2,3},{3,2},{4,5},{5,4},{6,7},{7,6},{8,9},{9,8},{10,11... | collective-permute-start | bytes 3145736 | tf_op jit(solution)/shard_map/ppermute | solution.py:595
  16.2 1.0 copy-start.4
  17.3 1.3 copy-start.1
  79.5 14.7 %copy-start.2 = (bf16[512,2048]{1,0:T(8,128)(2,1)S(1)}, bf16[512,2048]{1,0:T(8,128)(2,1)}, u32[]{:S(2)}) copy-start(bf16[512,2048]{1,0:T(8,128)(2,1)} %copy-done.1) | copy-start | bytes 6291460
  79.5 5.5 %collective-permute-start.2 = (bf16[2,128,256]{2,1,0:T(8,128)(2,1)S(1)}, bf16[2,128,256]{2,1,0:T(8,128)(2,1)S(1)}, u32[]{:S(2)}, u32[]{:S(2)}) collective-permute-start(bf16[2,128,256]{2,1,0:T(8,128)(2,1)S(1)} %get-tuple-element.39), channel_id=1, source_target_pairs={{0,4},{2,6},{4,0},{6,2},{1,5},{3,7},{5,1},{7,3},{8,12},{10,14},{12... | collective-permute-start | bytes 393224 | tf_op jit(solution)/shard_map/ppermute | solution.py:620
  80.0 9.4 %collective-permute-start.3 = (bf16[2,128,256]{2,1,0:T(8,128)(2,1)S(1)}, bf16[2,128,256]{2,1,0:T(8,128)(2,1)S(1)}, u32[]{:S(2)}, u32[]{:S(2)}) collective-permute-start(bf16[2,128,256]{2,1,0:T(8,128)(2,1)S(1)} %get-tuple-element.40), channel_id=1, source_target_pairs={{0,2},{2,4},{4,6},{6,0},{1,3},{3,5},{5,7},{7,1},{8,10},{10,12},{12... | collective-permute-start | bytes 393224 | tf_op jit(solution)/shard_map/ppermute | solution.py:620
  81.1 8.3 %collective-permute-start.4 = (bf16[2,128,256]{2,1,0:T(8,128)(2,1)S(1)}, bf16[2,128,256]{2,1,0:T(8,128)(2,1)S(1)}, u32[]{:S(2)}, u32[]{:S(2)}) collective-permute-start(bf16[2,128,256]{2,1,0:T(8,128)(2,1)S(1)} %get-tuple-element.41), channel_id=1, source_target_pairs={{0,6},{2,0},{4,2},{6,4},{1,7},{3,1},{5,3},{7,5},{8,14},{10,8},{12,... | collective-permute-start | bytes 393224 | tf_op jit(solution)/shard_map/ppermute | solution.py:620
  82.7 10.6 %collective-permute-start.9 = (bf16[8,128,128]{2,1,0:T(8,128)(2,1)S(1)}, bf16[8,128,128]{2,1,0:T(8,128)(2,1)S(1)}, u32[]{:S(2)}, u32[]{:S(2)}) collective-permute-start(bf16[8,128,128]{2,1,0:T(8,128)(2,1)S(1)} %get-tuple-element.49.low), channel_id=1, source_target_pairs={{0,1},{1,0},{2,3},{3,2},{4,5},{5,4},{6,7},{7,6},{8,9},{9,8},{10,11... | collective-permute-start | bytes 786440 | tf_op jit(solution)/shard_map/ppermute | solution.py:595
  84.1 19.3 %collective-permute-start.1 = (bf16[2,256,256]{2,1,0:T(8,128)(2,1)S(1)}, bf16[2,256,256]{2,1,0:T(8,128)(2,1)S(1)}, u32[]{:S(2)}, u32[]{:S(2)}) collective-permute-start(bf16[2,256,256]{2,1,0:T(8,128)(2,1)S(1)} %get-tuple-element.37), channel_id=1, source_target_pairs={{0,2},{2,4},{4,6},{6,0},{1,3},{3,5},{5,7},{7,1},{8,10},{10,12},{12... | collective-permute-start | bytes 786440 | tf_op jit(solution)/shard_map/ppermute | solution.py:620
  89.4 14.0 %collective-permute-start.5 = (bf16[2,256,256]{2,1,0:T(8,128)(2,1)S(1)}, bf16[2,256,256]{2,1,0:T(8,128)(2,1)S(1)}, u32[]{:S(2)}, u32[]{:S(2)}) collective-permute-start(bf16[2,256,256]{2,1,0:T(8,128)(2,1)S(1)} %get-tuple-element.44), channel_id=1, source_target_pairs={{0,4},{2,6},{4,0},{6,2},{1,5},{3,7},{5,1},{7,3},{8,12},{10,14},{12... | collective-permute-start | bytes 786440 | tf_op jit(solution)/shard_map/ppermute | solution.py:620
  89.5 13.9 %collective-permute-start.6 = (bf16[2,256,256]{2,1,0:T(8,128)(2,1)S(1)}, bf16[2,256,256]{2,1,0:T(8,128)(2,1)S(1)}, u32[]{:S(2)}, u32[]{:S(2)}) collective-permute-start(bf16[2,256,256]{2,1,0:T(8,128)(2,1)S(1)} %get-tuple-element.45), channel_id=1, source_target_pairs={{0,6},{2,0},{4,2},{6,4},{1,7},{3,1},{5,3},{7,5},{8,14},{10,8},{12,... | collective-permute-start | bytes 786440 | tf_op jit(solution)/shard_map/ppermute | solution.py:620
  91.6 2.7 %collective-permute-start.8 = (bf16[2,128,256]{2,1,0:T(8,128)(2,1)S(1)}, bf16[2,128,256]{2,1,0:T(8,128)(2,1)S(1)}, u32[]{:S(2)}, u32[]{:S(2)}) collective-permute-start(bf16[2,128,256]{2,1,0:T(8,128)(2,1)S(1)} %get-tuple-element.47.refs_0_), channel_id=1, source_target_pairs={{0,1},{1,0},{2,3},{3,2},{4,5},{5,4},{6,7},{7,6},{8,9},{9,8},{10,11... | collective-permute-start | bytes 393224 | tf_op jit(solution)/shard_map/ppermute | solution.py:595
  95.8 18.5 %all-to-all-start.1 = ((bf16[16,16,1152]{2,1,0:T(8,128)(2,1)}), bf16[16,16,1152]{2,1,0:T(8,128)(2,1)S(1)}, u32[]{:S(2)}, u32[]{:S(2)}) async-start(bf16[16,16,1152]{2,1,0:T(8,128)(2,1)} %bitcast.9), calls=%async_computation.1 | async-start | bytes 1179648 | tf_op jit(solution)/shard_map/all_to_all | solution.py:591
  103.5 2.3 %collective-permute-start.7 = (bf16[4,256,256]{2,1,0:T(8,128)(2,1)S(1)}, bf16[4,256,256]{2,1,0:T(8,128)(2,1)S(1)}, u32[]{:S(2)}, u32[]{:S(2)}) collective-permute-start(bf16[4,256,256]{2,1,0:T(8,128)(2,1)S(1)} %pick.1), channel_id=1, source_target_pairs={{0,1},{1,0},{2,3},{3,2},{4,5},{5,4},{6,7},{7,6},{8,9},{9,8},{10,11... | collective-permute-start | bytes 1572872 | tf_op jit(solution)/shard_map/ppermute | solution.py:595
  114.4 4.4 %collective-permute-start.10 = (bf16[16,1152]{1,0:T(8,128)(2,1)S(1)}, bf16[16,1152]{1,0:T(8,128)(2,1)S(1)}, u32[]{:S(2)}, u32[]{:S(2)}) collective-permute-start(bf16[16,1152]{1,0:T(8,128)(2,1)S(1)} %sum_share.1.refs_0_), channel_id=1, source_target_pairs={{0,4},{2,6},{4,0},{6,2},{1,5},{3,7},{5,1},{7,3},{8,12},{10,14},{12... | collective-permute-start | bytes 110600 | tf_op jit(solution)/shard_map/ppermute | solution.py:620
  115.8 4.0 %collective-permute-start.11 = (bf16[16,1152]{1,0:T(8,128)(2,1)S(1)}, bf16[16,1152]{1,0:T(8,128)(2,1)S(1)}, u32[]{:S(2)}, u32[]{:S(2)}) collective-permute-start(bf16[16,1152]{1,0:T(8,128)(2,1)S(1)} %sum_share.1.refs_0_), channel_id=1, source_target_pairs={{0,2},{2,4},{4,6},{6,0},{1,3},{3,5},{5,7},{7,1},{8,10},{10,12},{12... | collective-permute-start | bytes 110600 | tf_op jit(solution)/shard_map/ppermute | solution.py:620
  115.8 4.0 %collective-permute-start.12 = (bf16[16,1152]{1,0:T(8,128)(2,1)S(1)}, bf16[16,1152]{1,0:T(8,128)(2,1)S(1)}, u32[]{:S(2)}, u32[]{:S(2)}) collective-permute-start(bf16[16,1152]{1,0:T(8,128)(2,1)S(1)} %sum_share.1.refs_0_), channel_id=1, source_target_pairs={{0,6},{2,0},{4,2},{6,4},{1,7},{3,1},{5,3},{7,5},{8,14},{10,8},{12,... | collective-permute-start | bytes 110600 | tf_op jit(solution)/shard_map/ppermute | solution.py:620
  134.1 6.5 %collective-permute-start.13 = (bf16[8,2,16,1536]{3,2,1,0:T(8,128)(2,1)S(1)}, bf16[8,2,16,1536]{3,2,1,0:T(8,128)(2,1)S(1)}, u32[]{:S(2)}, u32[]{:S(2)}) collective-permute-start(bf16[8,2,16,1536]{3,2,1,0:T(8,128)(2,1)S(1)} %bitcast.15), channel_id=1, source_target_pairs={{0,1},{1,0},{2,3},{3,2},{4,5},{5,4},{6,7},{7,6},{8,9},{9,8},{10,11... | collective-permute-start | bytes 2359304 | tf_op jit(solution)/shard_map/ppermute | solution.py:595
